TPU v7x, 32 devices: a whole 2x2x4 slice. The times are simulated.
32 devices in a mesh: grp: 4 (over x, core), mem: 8 (over z, y).
Axes of the slice: x: 2, y: 2, z: 4, core: 2. Of those that a mesh axis runs over, the one named last changes fastest.
Arguments:
- rhs: float32 [96, 448, 384], P('grp', 'mem'), may hold values from -6 to 6
- conductivity: float32 [96, 448], P('grp', 'mem'), may hold values from 0.2 to 5
- local_inverse: bfloat16 [65536, 2048], P(('grp', 'mem')), may hold values from -0.125 to 0.125
- coarse_basis: float32 [96, 448, 16], P('grp', 'mem'), may hold values from -0.5 to 0.5
- coarse_inverse: float32 [512, 512], P(('grp', 'mem')), may hold values from -3 to 8, as said below
Outputs:
- solution: float32 [96, 448, 384], P('grp', 'mem')
Inputs may be any that keep to these rules, and one draw needn't show every extreme that they name: coarse_inverse is symmetric up to rounding, with a positive diagonal.
All inputs are finite; a program needn't handle non-finite values.
Results may differ from a plain program's by a relative error of at most 0.0005.
Values may be sent and summed in bfloat16 or wider, within the bound.
No kernel may reach another device: no remote copies, remote signals or barrier semaphores. Data moves between devices by JAX's collectives and lax.ppermute only.
A program may use at most 128 MiB of HBM per device.

v0:
```python
import jax
import jax.numpy as jnp
from jax import lax
from jax.sharding import PartitionSpec as P

OV = 4
ITERS = 2


def padded(block, sides, width):
    for axis, dim in sides:
        count = lax.axis_size(axis)
        forward = [(i, i + 1) for i in range(count - 1)]
        backward = [(target, source) for source, target in forward]
        low = lax.ppermute(
            lax.slice_in_dim(block, block.shape[dim] - width, None, axis=dim), axis, forward
        )
        high = lax.ppermute(lax.slice_in_dim(block, 0, width, axis=dim), axis, backward)
        block = jnp.concatenate([low, block, high], axis=dim)
    return block


def apply_operator(field_pad, conduct_pad):
    center = field_pad[1:-1, 1:-1]
    conduct_mid = conduct_pad[1:-1, 1:-1]
    neighbour_fields = (
        field_pad[2:, 1:-1],
        field_pad[:-2, 1:-1],
        field_pad[1:-1, 2:],
        field_pad[1:-1, :-2],
    )
    neighbour_conduct = (
        conduct_pad[2:, 1:-1],
        conduct_pad[:-2, 1:-1],
        conduct_pad[1:-1, 2:],
        conduct_pad[1:-1, :-2],
    )
    summed = jnp.zeros(center.shape, jnp.float32)
    for other_field, other_conduct in zip(neighbour_fields, neighbour_conduct):
        face = 0.5 * (conduct_mid + other_conduct)
        summed = summed + face[:, :, None] * (center - other_field)
    return summed


def on_device(rhs, conductivity, local_inverse, coarse_basis, coarse_inverse):
    own_x, own_y, columns = rhs.shape
    modes = coarse_basis.shape[2]
    span_x = own_x + 2 * OV
    span_y = own_y + 2 * OV
    owned_inverse = local_inverse.reshape(span_x, span_y, span_x * span_y)[
        OV : OV + own_x, OV : OV + own_y
    ]
    owned_inverse = owned_inverse.reshape(own_x * own_y, span_x * span_y)
    basis_flat = coarse_basis.reshape(own_x * own_y, modes)
    conduct_pad = padded(conductivity, (("grp", 0), ("mem", 1)), 1)
    solution = jnp.zeros(rhs.shape, jnp.float32)
    for sweep in range(ITERS):
        solution_pad = padded(solution, (("grp", 0), ("mem", 1)), 1)
        residual = rhs - apply_operator(solution_pad, conduct_pad)
        rounded = residual.astype(jnp.bfloat16)
        extended = padded(rounded, (("grp", 0), ("mem", 1)), OV)
        flat_rows = extended.reshape(span_x * span_y, columns)
        fine_part = jnp.dot(owned_inverse, flat_rows, preferred_element_type=jnp.float32).reshape(
            own_x, own_y, columns
        )
        restricted = lax.dot_general(
            basis_flat,
            residual.reshape(own_x * own_y, columns),
            (((0,), (0,)), ((), ())),
            precision=lax.Precision.HIGHEST,
            preferred_element_type=jnp.float32,
        )
        group_block = lax.all_gather(restricted, "mem", axis=0, tiled=True)
        lifted = jnp.dot(
            coarse_inverse,
            lax.all_gather(group_block, "grp", axis=0, tiled=True),
            precision=lax.Precision.HIGHEST,
            preferred_element_type=jnp.float32,
        )
        coarse_part = jnp.dot(
            basis_flat, lifted, precision=lax.Precision.HIGHEST, preferred_element_type=jnp.float32
        ).reshape(own_x, own_y, columns)
        solution = solution + fine_part + coarse_part
    return solution


def solution(mesh):
    placed = (
        P("grp", "mem", None),
        P("grp", "mem"),
        P(("grp", "mem"), None),
        P("grp", "mem", None),
        P(("grp", "mem"), None),
    )
    return jax.shard_map(
        on_device, mesh=mesh, in_specs=placed, out_specs=P("grp", "mem", None), check_vma=False
    )
```

profile of v0, /device:TPU:0, one launch (start us, length us, event | category | flops | bytes accessed | tf_op | source)
XLA Modules:
  0.0 182.4 jit_solution(9934167536577995836)
XLA Ops:
  0.0 2.4 %collective-permute-start.3 = (f32[1,56,384]{2,1,0:T(8,128)S(1)}, f32[1,56,384]{2,1,0:T(8,128)S(1)}, u32[]{:S(2)}, u32[]{:S(2)}) collective-permute-start(f32[1,56,384]{2,1,0:T(8,128)S(1)} %broadcast.15), channel_id=1, source_target_pairs={{0,8},{8,16},{16,24},{1,9},{9,17},{17,25},{2,10},{10,18},{18,26},{... | collective-permute-start | bytes 258056 | tf_op jit(solution)/shard_map/ppermute | solution.py:15
  2.4 1.3 collective-permute-start.1
  4.4 5.1 %collective-permute-start.2 = (f32[1,56]{1,0:T(1,128)S(1)}, f32[1,56]{1,0:T(1,128)S(1)}, u32[]{:S(2)}, u32[]{:S(2)}) collective-permute-start(f32[1,56]{1,0:T(1,128)S(1)} %get-tuple-element.29), channel_id=1, source_target_pairs={{0,8},{8,16},{16,24},{1,9},{9,17},{17,25},{2,10},{10,18},{18,26},{... | collective-permute-start | bytes 680 | tf_op jit(solution)/shard_map/ppermute | solution.py:15
  9.5 1.3 collective-permute-start
  11.9 5.9 %slice.148 = bf16[24,56,2048]{2,1,0:T(8,128)(2,1)S(1)} slice(bf16[32,64,2048]{2,1,0:T(8,128)(2,1)} %bitcast.50), slice={[4:28], [4:60], [0:2048]} | slice | bytes 11010048 | tf_op jit(solution)/shard_map/slice | solution.py:50
  19.2 4.7 %collective-permute-start.6 = (f32[26,1]{1,0:T(8,128)S(1)}, f32[26,1]{1,0:T(8,128)S(1)}, u32[]{:S(2)}, u32[]{:S(2)}) collective-permute-start(f32[26,1]{1,0:T(8,128)S(1)} %get-tuple-element.24), channel_id=1, source_target_pairs={{0,1},{1,2},{2,3},{3,4},{4,5},{5,6},{6,7},{8,9},{9,10},{10,11},{11... | collective-permute-start | bytes 320 | tf_op jit(solution)/shard_map/ppermute | solution.py:15
  24.2 1.3 collective-permute-start.5
  25.5 5.0 %collective-permute-start.7 = (f32[26,1,384]{2,1,0:T(1,128)S(1)}, f32[26,1,384]{2,1,0:T(1,128)S(1)}, u32[]{:S(2)}, u32[]{:S(2)}) collective-permute-start(f32[26,1,384]{2,1,0:T(1,128)S(1)} %get-tuple-element.12), channel_id=1, source_target_pairs={{0,1},{1,2},{2,3},{3,4},{4,5},{5,6},{6,7},{8,9},{9,10},{10,11},{11... | collective-permute-start | bytes 119816 | tf_op jit(solution)/shard_map/ppermute | solution.py:15
  30.6 1.6 collective-permute-done.7
  32.2 3.1 %fusion.34 = (bf16[24,56,384]{2,1,0:T(8,128)(2,1)S(1)}, f32[24,56,384]{2,1,0:T(8,128)S(1)}) fusion(f32[24,56,384]{2,1,0:T(8,128)S(1)} %copy-done.1, f32[24,56,384]{2,1,0:T(8,128)S(1)} %broadcast_in_dim.2, f32[1,56,384]{2,1,0:T(8,128)S(1)} %collective-permute-done.1, f32[1,56,384]{2,1,0:T(8,128)S(1)} %collective-permute-done.3, ...), kind=kLoop, calls=%fused_computation.78 | loop fusion | flops 9805824 | bytes 7498752 | tf_op jit(solution)/shard_map/convert_element_type | solution.py:60
  36.5 34.0 %all_gather.12 = f32[128,384]{1,0:T(8,128)S(1)} all-gather(f32[16,384]{1,0:T(8,128)S(1)} %convolution_bitcast_fusion.1), channel_id=1, replica_groups=mesh['grp'=4,'mem'=8] {'mem'}, dimensions={0}, use_global_device_ids=true | all-gather | bytes 221184 | tf_op jit(solution)/shard_map/all_gather | solution.py:73
  70.6 1.3 collective-permute-start.8
  73.2 15.4 %all_gather.13 = f32[512,384]{1,0:T(8,128)S(1)} all-gather(f32[128,384]{1,0:T(8,128)S(1)} %all_gather.12), channel_id=1, replica_groups=mesh['grp'=4,'mem'=8] {'grp'}, dimensions={0}, use_global_device_ids=true | all-gather | bytes 983040 | tf_op jit(solution)/shard_map/all_gather | solution.py:76
  89.2 1.3 collective-permute-start.10
  90.5 1.5 collective-permute-start.11
  92.0 1.9 %fusion.41 = f32[384,1344]{0,1:T(8,128)S(1)} fusion(f32[384,16]{0,1:T(8,128)S(1)} %fusion.40, f32[1344,16]{0,1:T(8,128)S(1)} %reshape.35), kind=kOutput, calls=%fused_computation.84 | convolution fusion | flops 99090432 | bytes 2174976 | tf_op jit(solution)/shard_map/dot_general | solution.py:80
  93.9 3.6 %collective-permute-done.11 = bf16[32,4,384]{2,1,0:T(4,128)(2,1)S(1)} collective-permute-done((bf16[32,4,384]{2,1,0:T(4,128)(2,1)S(1)}, bf16[32,4,384]{2,1,0:T(4,128)(2,1)S(1)}, u32[]{:S(2)}, u32[]{:S(2)}) %collective-permute-start.11) | collective-permute-done | bytes 98336 | tf_op jit(solution)/shard_map/ppermute | solution.py:18
  98.3 3.2 %convolution_add_fusion = f32[384,1344]{0,1:T(8,128)S(1)} fusion(f32[384,1344]{0,1:T(8,128)S(1)} %fusion.41, bf16[1344,2048]{1,0:T(8,128)(2,1)S(1)} %bitcast.48, bf16[2048,384]{1,0:T(8,128)(2,1)S(1)} %bitcast.52), kind=kOutput, calls=%fused_computation | convolution fusion | flops 2114445312 | bytes 11206656 | tf_op jit(solution)/shard_map/dot_general | solution.py:63
  101.5 1.5 collective-permute-start.13
  104.3 1.9 %collective-permute-done.12 = f32[1,56,384]{2,1,0:T(8,128)S(1)} collective-permute-done((f32[1,56,384]{2,1,0:T(8,128)S(1)}, f32[1,56,384]{2,1,0:T(8,128)S(1)}, u32[]{:S(2)}, u32[]{:S(2)}) %collective-permute-start.12) | collective-permute-done | bytes 86048 | tf_op jit(solution)/shard_map/ppermute | solution.py:18
  107.5 4.5 %collective-permute-start.15 = (f32[26,1,384]{2,1,0:T(1,128)S(1)}, f32[26,1,384]{2,1,0:T(1,128)S(1)}, u32[]{:S(2)}, u32[]{:S(2)}) collective-permute-start(f32[26,1,384]{2,1,0:T(1,128)S(1)} %get-tuple-element.10), channel_id=1, source_target_pairs={{0,1},{1,2},{2,3},{3,4},{4,5},{5,6},{6,7},{8,9},{9,10},{10,11},{11... | collective-permute-start | bytes 119816 | tf_op jit(solution)/shard_map/ppermute | solution.py:15
  112.1 1.7 collective-permute-done.15
  113.8 3.4 %fusion.32 = (bf16[24,56,384]{2,1,0:T(8,128)(2,1)S(1)}, f32[24,56,384]{2,1,0:T(8,128)S(1)}) fusion(f32[24,56,384]{2,1,0:T(8,128)S(1)} %copy-done.1, f32[24,56,384]{2,1,0:T(8,128)S(1)} %bitcast.45, f32[1,56,384]{2,1,0:T(8,128)S(1)} %collective-permute-done.12, f32[1,56,384]{2,1,0:T(8,128)S(1)} %collective-permute-done.13, ...), kind=kLoop, calls=%fused_computation.77 | loop fusion | flops 10838016 | bytes 7498752 | tf_op jit(solution)/shard_map/convert_element_type | solution.py:60
  118.5 33.1 %all_gather.14 = f32[128,384]{1,0:T(8,128)S(1)} all-gather(f32[16,384]{1,0:T(8,128)S(1)} %convolution_bitcast_fusion), channel_id=1, replica_groups=mesh['grp'=4,'mem'=8] {'mem'}, dimensions={0}, use_global_device_ids=true | all-gather | bytes 221184 | tf_op jit(solution)/shard_map/all_gather | solution.py:73
  151.6 1.3 collective-permute-start.16
  154.2 13.7 %all_gather.15 = f32[512,384]{1,0:T(8,128)S(1)} all-gather(f32[128,384]{1,0:T(8,128)S(1)} %all_gather.14), channel_id=1, replica_groups=mesh['grp'=4,'mem'=8] {'grp'}, dimensions={0}, use_global_device_ids=true | all-gather | bytes 983040 | tf_op jit(solution)/shard_map/all_gather | solution.py:76
  168.5 1.3 collective-permute-start.18
  169.8 1.5 collective-permute-start.19
  171.4 1.8 %fusion.43 = f32[384,1344]{0,1:T(8,128)S(1)} fusion(f32[384,16]{0,1:T(8,128)S(1)} %fusion.42, f32[1344,16]{0,1:T(8,128)S(1)} %reshape.35), kind=kOutput, calls=%fused_computation.86 | convolution fusion | flops 99090432 | bytes 2174976 | tf_op jit(solution)/shard_map/dot_general | solution.py:80
  173.2 3.6 %collective-permute-done.19 = bf16[32,4,384]{2,1,0:T(4,128)(2,1)S(1)} collective-permute-done((bf16[32,4,384]{2,1,0:T(4,128)(2,1)S(1)}, bf16[32,4,384]{2,1,0:T(4,128)(2,1)S(1)}, u32[]{:S(2)}, u32[]{:S(2)}) %collective-permute-start.19) | collective-permute-done | bytes 98336 | tf_op jit(solution)/shard_map/ppermute | solution.py:18
  177.7 3.1 %fusion.44 = f32[384,1344]{0,1:T(8,128)S(1)} fusion(bf16[1344,2048]{1,0:T(8,128)(2,1)S(1)} %bitcast.49, bf16[2048,384]{1,0:T(8,128)(2,1)S(1)} %bitcast.53), kind=kOutput, calls=%fused_computation.87 | convolution fusion | flops 2113929216 | bytes 9142272 | tf_op jit(solution)/shard_map/dot_general | solution.py:63
  180.8 1.6 add_add_fusion
  (49 shorter events, 14.4 us)
Async XLA Ops:
  0.0 88.6 %copy-start = (f32[16,512]{1,0:T(8,128)S(1)}, f32[16,512]{1,0:T(8,128)}, u32[]{:S(2)}) copy-start(f32[16,512]{1,0:T(8,128)} %param.9) | copy-start | bytes 98308
  0.0 23.9 %collective-permute-start.3 = (f32[1,56,384]{2,1,0:T(8,128)S(1)}, f32[1,56,384]{2,1,0:T(8,128)S(1)}, u32[]{:S(2)}, u32[]{:S(2)}) collective-permute-start(f32[1,56,384]{2,1,0:T(8,128)S(1)} %broadcast.15), channel_id=1, source_target_pairs={{0,8},{8,16},{16,24},{1,9},{9,17},{17,25},{2,10},{10,18},{18,26},{... | collective-permute-start | bytes 258056 | tf_op jit(solution)/shard_map/ppermute | solution.py:15
  2.4 21.6 %collective-permute-start.1 = (f32[1,56,384]{2,1,0:T(8,128)S(1)}, f32[1,56,384]{2,1,0:T(8,128)S(1)}, u32[]{:S(2)}, u32[]{:S(2)}) collective-permute-start(f32[1,56,384]{2,1,0:T(8,128)S(1)} %broadcast.15), channel_id=1, source_target_pairs={{8,0},{16,8},{24,16},{9,1},{17,9},{25,17},{10,2},{18,10},{26,18},{... | collective-permute-start | bytes 258056 | tf_op jit(solution)/shard_map/ppermute | solution.py:18
  4.4 13.4 %collective-permute-start.2 = (f32[1,56]{1,0:T(1,128)S(1)}, f32[1,56]{1,0:T(1,128)S(1)}, u32[]{:S(2)}, u32[]{:S(2)}) collective-permute-start(f32[1,56]{1,0:T(1,128)S(1)} %get-tuple-element.29), channel_id=1, source_target_pairs={{0,8},{8,16},{16,24},{1,9},{9,17},{17,25},{2,10},{10,18},{18,26},{... | collective-permute-start | bytes 680 | tf_op jit(solution)/shard_map/ppermute | solution.py:15
  9.5 8.3 %collective-permute-start = (f32[1,56]{1,0:T(1,128)S(1)}, f32[1,56]{1,0:T(1,128)S(1)}, u32[]{:S(2)}, u32[]{:S(2)}) collective-permute-start(f32[1,56]{1,0:T(1,128)S(1)} %get-tuple-element.30), channel_id=1, source_target_pairs={{8,0},{16,8},{24,16},{9,1},{17,9},{25,17},{10,2},{18,10},{26,18},{... | collective-permute-start | bytes 680 | tf_op jit(solution)/shard_map/ppermute | solution.py:18
  11.9 5.9 %copy-start.3 = (f32[24,56]{1,0:T(8,128)S(1)}, f32[24,56]{1,0:T(8,128)}, u32[]{:S(2)}) copy-start(f32[24,56]{1,0:T(8,128)} %param.6) | copy-start | bytes 16132
  17.9 12.5 %collective-permute-start.4 = (f32[26,1]{1,0:T(8,128)S(1)}, f32[26,1]{1,0:T(8,128)S(1)}, u32[]{:S(2)}, u32[]{:S(2)}) collective-permute-start(f32[26,1]{1,0:T(8,128)S(1)} %get-tuple-element.23), channel_id=1, source_target_pairs={{1,0},{2,1},{3,2},{4,3},{5,4},{6,5},{7,6},{9,8},{10,9},{11,10},{12... | collective-permute-start | bytes 320 | tf_op jit(solution)/shard_map/ppermute | solution.py:18
  19.2 13.0 %copy-start.1 = (f32[24,56,384]{2,1,0:T(8,128)S(1)}, f32[24,56,384]{2,1,0:T(8,128)}, u32[]{:S(2)}) copy-start(f32[24,56,384]{2,1,0:T(8,128)} %param.5) | copy-start | bytes 6193156
  19.2 11.2 %collective-permute-start.6 = (f32[26,1]{1,0:T(8,128)S(1)}, f32[26,1]{1,0:T(8,128)S(1)}, u32[]{:S(2)}, u32[]{:S(2)}) collective-permute-start(f32[26,1]{1,0:T(8,128)S(1)} %get-tuple-element.24), channel_id=1, source_target_pairs={{0,1},{1,2},{2,3},{3,4},{4,5},{5,6},{6,7},{8,9},{9,10},{10,11},{11... | collective-permute-start | bytes 320 | tf_op jit(solution)/shard_map/ppermute | solution.py:15
  24.2 6.4 %collective-permute-start.5 = (f32[26,1,384]{2,1,0:T(1,128)S(1)}, f32[26,1,384]{2,1,0:T(1,128)S(1)}, u32[]{:S(2)}, u32[]{:S(2)}) collective-permute-start(f32[26,1,384]{2,1,0:T(1,128)S(1)} %get-tuple-element.11), channel_id=1, source_target_pairs={{1,0},{2,1},{3,2},{4,3},{5,4},{6,5},{7,6},{9,8},{10,9},{11,10},{12... | collective-permute-start | bytes 119816 | tf_op jit(solution)/shard_map/ppermute | solution.py:18
  25.5 6.7 %collective-permute-start.7 = (f32[26,1,384]{2,1,0:T(1,128)S(1)}, f32[26,1,384]{2,1,0:T(1,128)S(1)}, u32[]{:S(2)}, u32[]{:S(2)}) collective-permute-start(f32[26,1,384]{2,1,0:T(1,128)S(1)} %get-tuple-element.12), channel_id=1, source_target_pairs={{0,1},{1,2},{2,3},{3,4},{4,5},{5,6},{6,7},{8,9},{9,10},{10,11},{11... | collective-permute-start | bytes 119816 | tf_op jit(solution)/shard_map/ppermute | solution.py:15
  32.2 3.1 %copy-start.2 = (f32[24,56,16]{1,2,0:T(8,128)S(1)}, f32[24,56,16]{1,2,0:T(8,128)}, u32[]{:S(2)}) copy-start(f32[24,56,16]{1,2,0:T(8,128)} %param.8) | copy-start | bytes 258052
  70.6 18.5 %collective-permute-start.8 = (bf16[4,56,384]{2,1,0:T(8,128)(2,1)S(1)}, bf16[4,56,384]{2,1,0:T(8,128)(2,1)S(1)}, u32[]{:S(2)}, u32[]{:S(2)}) collective-permute-start(bf16[4,56,384]{2,1,0:T(8,128)(2,1)S(1)} %get-tuple-element.21), channel_id=1, source_target_pairs={{0,8},{8,16},{16,24},{1,9},{9,17},{17,25},{2,10},{10,18},{18,26},{... | collective-permute-start | bytes 516104 | tf_op jit(solution)/shard_map/ppermute | solution.py:15
  71.9 17.2 %collective-permute-start.9 = (bf16[4,56,384]{2,1,0:T(8,128)(2,1)S(1)}, bf16[4,56,384]{2,1,0:T(8,128)(2,1)S(1)}, u32[]{:S(2)}, u32[]{:S(2)}) collective-permute-start(bf16[4,56,384]{2,1,0:T(8,128)(2,1)S(1)} %get-tuple-element.22), channel_id=1, source_target_pairs={{8,0},{16,8},{24,16},{9,1},{17,9},{25,17},{10,2},{18,10},{26,18},{... | collective-permute-start | bytes 516104 | tf_op jit(solution)/shard_map/ppermute | solution.py:18
  89.2 4.7 %collective-permute-start.10 = (bf16[32,4,384]{2,1,0:T(4,128)(2,1)S(1)}, bf16[32,4,384]{2,1,0:T(4,128)(2,1)S(1)}, u32[]{:S(2)}, u32[]{:S(2)}) collective-permute-start(bf16[32,4,384]{2,1,0:T(4,128)(2,1)S(1)} %get-tuple-element.17), channel_id=1, source_target_pairs={{0,1},{1,2},{2,3},{3,4},{4,5},{5,6},{6,7},{8,9},{9,10},{10,11},{11... | collective-permute-start | bytes 294920 | tf_op jit(solution)/shard_map/ppermute | solution.py:15
  90.5 6.9 %collective-permute-start.11 = (bf16[32,4,384]{2,1,0:T(4,128)(2,1)S(1)}, bf16[32,4,384]{2,1,0:T(4,128)(2,1)S(1)}, u32[]{:S(2)}, u32[]{:S(2)}) collective-permute-start(bf16[32,4,384]{2,1,0:T(4,128)(2,1)S(1)} %get-tuple-element.18), channel_id=1, source_target_pairs={{1,0},{2,1},{3,2},{4,3},{5,4},{6,5},{7,6},{9,8},{10,9},{11,10},{12... | collective-permute-start | bytes 294920 | tf_op jit(solution)/shard_map/ppermute | solution.py:18
  101.5 2.8 %collective-permute-start.13 = (f32[1,56,384]{2,1,0:T(8,128)S(1)}, f32[1,56,384]{2,1,0:T(8,128)S(1)}, u32[]{:S(2)}, u32[]{:S(2)}) collective-permute-start(f32[1,56,384]{2,1,0:T(8,128)S(1)} %get-tuple-element.13), channel_id=1, source_target_pairs={{0,8},{8,16},{16,24},{1,9},{9,17},{17,25},{2,10},{10,18},{18,26},{... | collective-permute-start | bytes 258056 | tf_op jit(solution)/shard_map/ppermute | solution.py:15
  103.0 3.2 %collective-permute-start.12 = (f32[1,56,384]{2,1,0:T(8,128)S(1)}, f32[1,56,384]{2,1,0:T(8,128)S(1)}, u32[]{:S(2)}, u32[]{:S(2)}) collective-permute-start(f32[1,56,384]{2,1,0:T(8,128)S(1)} %get-tuple-element.14), channel_id=1, source_target_pairs={{8,0},{16,8},{24,16},{9,1},{17,9},{25,17},{10,2},{18,10},{26,18},{... | collective-permute-start | bytes 258056 | tf_op jit(solution)/shard_map/ppermute | solution.py:18
  106.2 5.9 %collective-permute-start.14 = (f32[26,1,384]{2,1,0:T(1,128)S(1)}, f32[26,1,384]{2,1,0:T(1,128)S(1)}, u32[]{:S(2)}, u32[]{:S(2)}) collective-permute-start(f32[26,1,384]{2,1,0:T(1,128)S(1)} %get-tuple-element.9), channel_id=1, source_target_pairs={{1,0},{2,1},{3,2},{4,3},{5,4},{6,5},{7,6},{9,8},{10,9},{11,10},{12... | collective-permute-start | bytes 119816 | tf_op jit(solution)/shard_map/ppermute | solution.py:18
  107.5 6.3 %collective-permute-start.15 = (f32[26,1,384]{2,1,0:T(1,128)S(1)}, f32[26,1,384]{2,1,0:T(1,128)S(1)}, u32[]{:S(2)}, u32[]{:S(2)}) collective-permute-start(f32[26,1,384]{2,1,0:T(1,128)S(1)} %get-tuple-element.10), channel_id=1, source_target_pairs={{0,1},{1,2},{2,3},{3,4},{4,5},{5,6},{6,7},{8,9},{9,10},{10,11},{11... | collective-permute-start | bytes 119816 | tf_op jit(solution)/shard_map/ppermute | solution.py:15
  151.6 16.8 %collective-permute-start.16 = (bf16[4,56,384]{2,1,0:T(8,128)(2,1)S(1)}, bf16[4,56,384]{2,1,0:T(8,128)(2,1)S(1)}, u32[]{:S(2)}, u32[]{:S(2)}) collective-permute-start(bf16[4,56,384]{2,1,0:T(8,128)(2,1)S(1)} %get-tuple-element.19), channel_id=1, source_target_pairs={{0,8},{8,16},{16,24},{1,9},{9,17},{17,25},{2,10},{10,18},{18,26},{... | collective-permute-start | bytes 516104 | tf_op jit(solution)/shard_map/ppermute | solution.py:15
  152.9 15.5 %collective-permute-start.17 = (bf16[4,56,384]{2,1,0:T(8,128)(2,1)S(1)}, bf16[4,56,384]{2,1,0:T(8,128)(2,1)S(1)}, u32[]{:S(2)}, u32[]{:S(2)}) collective-permute-start(bf16[4,56,384]{2,1,0:T(8,128)(2,1)S(1)} %get-tuple-element.20), channel_id=1, source_target_pairs={{8,0},{16,8},{24,16},{9,1},{17,9},{25,17},{10,2},{18,10},{26,18},{... | collective-permute-start | bytes 516104 | tf_op jit(solution)/shard_map/ppermute | solution.py:18
  168.5 4.7 %collective-permute-start.18 = (bf16[32,4,384]{2,1,0:T(4,128)(2,1)S(1)}, bf16[32,4,384]{2,1,0:T(4,128)(2,1)S(1)}, u32[]{:S(2)}, u32[]{:S(2)}) collective-permute-start(bf16[32,4,384]{2,1,0:T(4,128)(2,1)S(1)} %get-tuple-element.15), channel_id=1, source_target_pairs={{0,1},{1,2},{2,3},{3,4},{4,5},{5,6},{6,7},{8,9},{9,10},{10,11},{11... | collective-permute-start | bytes 294920 | tf_op jit(solution)/shard_map/ppermute | solution.py:15
  169.8 6.9 %collective-permute-start.19 = (bf16[32,4,384]{2,1,0:T(4,128)(2,1)S(1)}, bf16[32,4,384]{2,1,0:T(4,128)(2,1)S(1)}, u32[]{:S(2)}, u32[]{:S(2)}) collective-permute-start(bf16[32,4,384]{2,1,0:T(4,128)(2,1)S(1)} %get-tuple-element.16), channel_id=1, source_target_pairs={{1,0},{2,1},{3,2},{4,3},{5,4},{6,5},{7,6},{9,8},{10,9},{11,10},{12... | collective-permute-start | bytes 294920 | tf_op jit(solution)/shard_map/ppermute | solution.py:18
where the time goes:
time: 183 us; the launch traced here: 182 us
  blocking collectives  96.2 us (53%)
  starting transfers between devices  41.6 us (23%)
  matrix products  13.5 us (7%)
  waiting for transfers between devices  12.4 us (7%)
  other arithmetic  10.3 us (6%)
  local copies, waits for them, and re-layouts  8 us (4%)
    all_gather x2, blocking collectives, on_device(): group_block = lax.all_gather(restricted, 'mem', axis=0, tiled=True)  67.1 us
    all_gather x2, blocking collectives, on_device(): lax.all_gather(group_block, 'grp', axis=0, tiled=True)  29.1 us
    ppermute x10, starting transfers between devices, padded(): lax.ppermute(lax.slice_in_dim(block, block.shape[dim] - width, None, axis...  28.3 us
    ppermute x10, starting transfers between devices, padded(): lax.ppermute(lax.slice_in_dim(block, 0, width, axis=dim), axis, backward)  13.3 us
    ppermute x10, waiting for transfers between devices, padded(): lax.ppermute(lax.slice_in_dim(block, 0, width, axis=dim), axis, backward)  9.04 us
    convert_element_type x2, other arithmetic, on_device(): rounded = residual.astype(jnp.bfloat16)  6.48 us
    dot_general x2, matrix products, on_device(): jnp.dot(owned_inverse, flat_rows, preferred_element_type=jnp.float32)  6.24 us
    slice x1, local copies, waits for them, and re-layouts, on_device(): local_inverse.reshape(span_x, span_y, span_x * span_y)  5.87 us
  transfers between devices with their start and end apart: 20, of which 5 were waited for; matrix products, arithmetic and copies ran while one was open for 7% of the time, Pallas kernels for 0%

commit v1 on v0

v1 whole, which is shorter than its diff:
```python
import jax
import jax.numpy as jnp
from jax import lax
from jax.sharding import PartitionSpec as P

OV = 4
ITERS = 2
AXES = ("grp", "mem")
EXACT = lax.Precision.HIGHEST


def neighbour_pairs(count, first):
    pairs = [(i, i + 1) for i in range(first, count - 1, 2)]
    return pairs + [(j, i) for i, j in pairs]


def edges(low_edge, high_edge, axis):
    count = lax.axis_size(axis)
    even = lax.axis_index(axis) % 2 == 0
    first = lax.ppermute(
        jnp.where(even, high_edge, low_edge), axis, neighbour_pairs(count, 0)
    )
    second = lax.ppermute(
        jnp.where(even, low_edge, high_edge), axis, neighbour_pairs(count, 1)
    )
    return jnp.where(even, second, first), jnp.where(even, first, second)


def dim_edges(block, axis, dim, width):
    size = block.shape[dim]
    low_edge = lax.slice_in_dim(block, 0, width, axis=dim)
    high_edge = lax.slice_in_dim(block, size - width, size, axis=dim)
    return edges(low_edge, high_edge, axis)


def padded(block, axis, dim, width):
    low, high = dim_edges(block, axis, dim, width)
    return jnp.concatenate([low, block, high], axis=dim)


def power_of_two(count):
    return count & (count - 1) == 0


def masks():
    members, groups = lax.axis_size("mem"), lax.axis_size("grp")
    mem_bits = [1 << k for k in range(members.bit_length() - 1)]
    grp_bits = [members << k for k in range(groups.bit_length() - 1)]
    return mem_bits[:0:-1] + grp_bits[:1], mem_bits[:1] + grp_bits[1:]


def swap(value, bit):
    total = lax.axis_size("grp") * lax.axis_size("mem")
    return lax.ppermute(value, AXES, [(i, i ^ bit) for i in range(total)])


def gathered(value, bits):
    for bit in bits:
        value = jnp.concatenate([value, swap(value, bit)], axis=0)
    return value


def coarse_solve(inverse_rows, restricted, modes):
    gather_bits, sum_bits = masks()
    sources = gathered(restricted, gather_bits)
    shares = lax.dot_general(
        inverse_rows,
        sources,
        (((0,), (0,)), ((), ())),
        precision=EXACT,
        preferred_element_type=jnp.float32,
    )
    me = lax.axis_index(AXES)
    targets = [0]
    for bit in sum_bits[::-1]:
        targets = targets + [t ^ bit for t in targets]
    parts = [
        lax.dynamic_slice_in_dim(shares, (me ^ target) * modes, modes, 0) for target in targets
    ]
    for bit in sum_bits:
        half = len(parts) // 2
        got = swap(jnp.concatenate(parts[half:], axis=0), bit)
        parts = [
            part + got[k * modes : (k + 1) * modes] for k, part in enumerate(parts[:half])
        ]
    return parts[0]


def on_device(rhs, conductivity, local_inverse, coarse_basis, coarse_inverse):
    own_x, own_y, columns = rhs.shape
    modes = coarse_basis.shape[2]
    span_x = own_x + 2 * OV
    span_y = own_y + 2 * OV
    cells = own_x * own_y
    owned_inverse = local_inverse[OV * span_y : (OV + own_x) * span_y]
    basis_flat = coarse_basis.reshape(cells, modes)

    below, above = dim_edges(conductivity, "grp", 0, 1)
    left, right = dim_edges(conductivity, "mem", 1, 1)
    conduct_x = jnp.concatenate([below, conductivity, above], axis=0)
    conduct_y = jnp.concatenate([left, conductivity, right], axis=1)
    faces_x = 0.5 * (conduct_x[1:] + conduct_x[:-1])[:, :, None]
    faces_y = 0.5 * (conduct_y[:, 1:] + conduct_y[:, :-1])[:, :, None]

    def residual_of(solution):
        along_x = padded(solution, "grp", 0, 1)
        along_y = padded(solution, "mem", 1, 1)
        summed = faces_x[1:] * (solution - along_x[2:])
        summed = summed + faces_x[:-1] * (solution - along_x[:-2])
        summed = summed + faces_y[:, 1:] * (solution - along_y[:, 2:])
        summed = summed + faces_y[:, :-1] * (solution - along_y[:, :-2])
        return rhs - summed

    def fine(residual):
        extended = padded(residual.astype(jnp.bfloat16), "grp", 0, OV)
        extended = padded(extended, "mem", 1, OV)
        product = jnp.dot(
            owned_inverse,
            extended.reshape(span_x * span_y, columns),
            preferred_element_type=jnp.float32,
        )
        return product.reshape(own_x, span_y, columns)[:, OV : OV + own_y]

    inverse_rows = gathered(coarse_inverse, masks()[0])

    def coarse(residual):
        restricted = lax.dot_general(
            basis_flat,
            residual.reshape(cells, columns),
            (((0,), (0,)), ((), ())),
            precision=EXACT,
            preferred_element_type=jnp.float32,
        )
        lifted = coarse_solve(inverse_rows, restricted, modes)
        return jnp.dot(
            basis_flat, lifted, precision=EXACT, preferred_element_type=jnp.float32
        ).reshape(own_x, own_y, columns)

    solution = fine(rhs) + coarse(rhs)
    for sweep in range(ITERS - 1):
        residual = residual_of(solution)
        solution = solution + fine(residual) + coarse(residual)
    return solution


def solution(mesh):
    placed = (
        P("grp", "mem", None),
        P("grp", "mem"),
        P(("grp", "mem"), None),
        P("grp", "mem", None),
        P(("grp", "mem"), None),
    )
    return jax.shard_map(
        on_device, mesh=mesh, in_specs=placed, out_specs=P("grp", "mem", None), check_vma=False
    )
```

time: 183 us -> 106 us (0.58)
  blocking collectives: 96.2 us -> 0 us
  other arithmetic: 10.3 us -> 19.7 us
  matrix products: 13.5 us -> 19 us
  starting transfers between devices: 41.6 us -> 44.5 us
    all_gather x4 -> x0, blocking collectives: 96.2 us -> none  [the longest x2 67.1 us: on_device(): group_block = lax.all_gather(restricted, 'mem', axis=0, tiled=True)]
    slice x6 -> x1, local copies, waits for them, and re-layouts: 6.73 us -> 0.01 us  [residual_of(): summed = faces_x[1:] * (solution - along_x[2:])]
    dot_general x8, matrix products: 13.5 us -> 19 us  [the longest x2 6.69 us: fine(): jnp.dot(owned_inverse, extended.reshape(span_x * span_y, columns), prefer...]
    dot_general x0 -> x2, local copies, waits for them, and re-layouts: none -> 5.08 us  [fine(): jnp.dot(owned_inverse, extended.reshape(span_x * span_y, columns), prefer...]
    add x1 -> x4, other arithmetic: 1.6 us -> 6.06 us  [the longest x1 3.92 us: on_device(): solution = solution + fine(residual) + coarse(residual)]
    convert_element_type x2, other arithmetic: 6.48 us -> 2.18 us  [fine(): extended = padded(residual.astype(jnp.bfloat16), 'grp', 0, OV)]
    select_n x0 -> x17, other arithmetic: none -> 4.12 us  [the longest x6 3.19 us: edges(): jnp.where(even, low_edge, high_edge)]
    concatenate x3 -> x11, other arithmetic: 1.8 us -> 5.74 us  [the longest x6 3.22 us: gathered(): value = jnp.concatenate([value, swap(value, bit)], axis=0)]
  transfers between devices with their start and end apart: 20 -> 29, of which waited for: 5 -> 9; matrix products, arithmetic and copies ran while one was open for 7% -> 23% of each run, Pallas kernels for 0% -> 0%
where the time goes in v1:
time: 106 us; the launch traced here: 104 us
  starting transfers between devices  44.5 us (42%)
  other arithmetic  19.7 us (19%)
  matrix products  19 us (18%)
  waiting for transfers between devices  12.1 us (11%)
  local copies, waits for them, and re-layouts  7.91 us (7%)
    ppermute x8, starting transfers between devices, edges(): lax.ppermute(jnp.where(even, high_edge, low_edge), axis, neighbour_pairs(...  19.2 us
    ppermute x13, starting transfers between devices, swap(): return lax.ppermute(value, AXES, [(i, i ^ bit) for i in range(total)])  18.5 us
    ppermute x13, waiting for transfers between devices, swap(): return lax.ppermute(value, AXES, [(i, i ^ bit) for i in range(total)])  11.7 us
    ppermute x8, starting transfers between devices, edges(): lax.ppermute(jnp.where(even, low_edge, high_edge), axis, neighbour_pairs(...  6.78 us
    dot_general x2, matrix products, fine(): jnp.dot(owned_inverse, extended.reshape(span_x * span_y, columns), prefer...  6.69 us
    dot_general x2, matrix products, coarse(): jnp.dot(basis_flat, lifted, precision=EXACT, preferred_element_type=jnp.f...  5.75 us
    dot_general x2, local copies, waits for them, and re-layouts, fine(): jnp.dot(owned_inverse, extended.reshape(span_x * span_y, columns), prefer...  5.08 us
    dot_general x2, matrix products, coarse(): lax.dot_general(basis_flat, residual.reshape(cells, columns), (((0,), (0,...  4.9 us
  transfers between devices with their start and end apart: 29, of which 9 were waited for; matrix products, arithmetic and copies ran while one was open for 23% of the time, Pallas kernels for 0%

profile of v1, /device:TPU:0, one launch (start us, length us, event | category | flops | bytes accessed | tf_op | source)
XLA Modules:
  0.0 103.7 jit_solution(14167921224305859674)
XLA Ops:
  0.0 1.4 %broadcast_select_fusion.24 = (f32[1,56]{1,0:T(1,128)}, f32[1,56]{1,0:T(1,128)}) fusion(pred[]{:T(512)S(6)} %eq.22, f32[24,56]{1,0:T(8,128)} %param.6), kind=kLoop, calls=%fused_computation.115 | loop fusion | flops 112 | bytes 897 | tf_op jit(solution)/shard_map/jit(_where)/select_n | solution.py:24
  1.4 1.1 %collective-permute-start.13 = (f32[1,56]{1,0:T(1,128)}, f32[1,56]{1,0:T(1,128)}, u32[]{:S(2)}, u32[]{:S(2)}) collective-permute-start(f32[1,56]{1,0:T(1,128)} %get-tuple-element.41), channel_id=1, source_target_pairs={{8,16},{16,8},{9,17},{17,9},{10,18},{18,10},{11,19},{19,11},{12,20... | collective-permute-start | bytes 680 | tf_op jit(solution)/shard_map/ppermute | solution.py:23
  2.6 3.9 %collective-permute-start.12 = (f32[1,56]{1,0:T(1,128)}, f32[1,56]{1,0:T(1,128)}, u32[]{:S(2)}, u32[]{:S(2)}) collective-permute-start(f32[1,56]{1,0:T(1,128)} %get-tuple-element.42), channel_id=1, source_target_pairs={{0,8},{16,24},{8,0},{24,16},{1,9},{17,25},{9,1},{25,17},{2,10},{18... | collective-permute-start | bytes 680 | tf_op jit(solution)/shard_map/ppermute | solution.py:20
  6.5 1.5 %slice_select_fusion.2 = (f32[24,1]{1,0:T(8,128)}, f32[24,1]{1,0:T(8,128)}) fusion(f32[24,56]{1,0:T(8,128)} %param.6, pred[]{:T(512)S(6)} %eq.21), kind=kLoop, calls=%fused_computation.101 | loop fusion | flops 48 | bytes 385 | tf_op jit(solution)/shard_map/jit(_where)/select_n | solution.py:24
  7.9 1.2 %collective-permute-start.17 = (f32[24,1]{1,0:T(8,128)}, f32[24,1]{1,0:T(8,128)}, u32[]{:S(2)}, u32[]{:S(2)}) collective-permute-start(f32[24,1]{1,0:T(8,128)} %get-tuple-element.45), channel_id=1, source_target_pairs={{1,2},{3,4},{5,6},{2,1},{4,3},{6,5},{9,10},{11,12},{13,14},{10,9},... | collective-permute-start | bytes 296 | tf_op jit(solution)/shard_map/ppermute | solution.py:23
  9.2 3.8 %collective-permute-start.16 = (f32[24,1]{1,0:T(8,128)}, f32[24,1]{1,0:T(8,128)}, u32[]{:S(2)}, u32[]{:S(2)}) collective-permute-start(f32[24,1]{1,0:T(8,128)} %get-tuple-element.46), channel_id=1, source_target_pairs={{0,1},{2,3},{4,5},{6,7},{1,0},{3,2},{5,4},{7,6},{8,9},{10,11},{12,... | collective-permute-start | bytes 296 | tf_op jit(solution)/shard_map/ppermute | solution.py:20
  12.9 2.6 %collective-permute-start.4 = (f32[16,512]{1,0:T(8,128)}, f32[16,512]{1,0:T(8,128)}, u32[]{:S(2)}, u32[]{:S(2)}) collective-permute-start(f32[16,512]{1,0:T(8,128)} %param.9), channel_id=1, source_target_pairs={{0,4},{1,5},{2,6},{3,7},{4,0},{5,1},{6,2},{7,3},{8,12},{9,13},{10,... | collective-permute-start | bytes 98312 | tf_op jit(solution)/shard_map/ppermute | solution.py:54
  16.3 1.0 copy.11
  17.3 3.7 %convolution_bitcast_fusion.1 = f32[16,384]{1,0:T(8,128)} fusion(f32[24,56,16]{1,2,0:T(8,128)} %param.8, f32[24,56,384]{2,1,0:T(8,128)} %param.5), kind=kOutput, calls=%fused_computation.28 | convolution fusion | flops 99090432 | bytes 2174976 | tf_op jit(solution)/shard_map/dot_general | solution.py:127
  24.0 1.3 %collective-permute-start.1 = (bf16[4,56,384]{2,1,0:T(8,128)(2,1)S(1)}, bf16[4,56,384]{2,1,0:T(8,128)(2,1)S(1)}, u32[]{:S(2)}, u32[]{:S(2)}) collective-permute-start(bf16[4,56,384]{2,1,0:T(8,128)(2,1)S(1)} %get-tuple-element.20), channel_id=1, source_target_pairs={{0,8},{16,24},{8,0},{24,16},{1,9},{17,25},{9,1},{25,17},{2,10},{18... | collective-permute-start | bytes 516104 | tf_op jit(solution)/shard_map/ppermute | solution.py:20
  27.6 1.6 %collective-permute-start.8 = (f32[32,384]{1,0:T(8,128)S(1)}, f32[32,384]{1,0:T(8,128)S(1)}, u32[]{:S(2)}, u32[]{:S(2)}) collective-permute-start(f32[32,384]{1,0:T(8,128)S(1)} %pad_maximum_fusion.16), channel_id=1, source_target_pairs={{0,2},{1,3},{2,0},{3,1},{4,6},{5,7},{6,4},{7,5},{8,10},{9,11},{10,... | collective-permute-start | bytes 147464 | tf_op jit(solution)/shard_map/ppermute | solution.py:54
  32.4 1.8 %collective-permute-done.5 = f32[32,512]{1,0:T(8,128)S(1)} collective-permute-done((f32[32,512]{1,0:T(8,128)S(1)}, f32[32,512]{1,0:T(8,128)S(1)}, u32[]{:S(2)}, u32[]{:S(2)}) %collective-permute-start.5) | collective-permute-done | bytes 65568 | tf_op jit(solution)/shard_map/ppermute | solution.py:54
  37.6 3.6 %collective-permute-start.10 = (f32[32,384]{1,0:T(8,128)S(1)}, f32[32,384]{1,0:T(8,128)S(1)}, u32[]{:S(2)}, u32[]{:S(2)}) collective-permute-start(f32[32,384]{1,0:T(8,128)S(1)} %pad_maximum_fusion.17), channel_id=1, source_target_pairs={{0,1},{1,0},{2,3},{3,2},{4,5},{5,4},{6,7},{7,6},{8,9},{9,8},{10,11... | collective-permute-start | bytes 147464 | tf_op jit(solution)/shard_map/ppermute | solution.py:54
  42.1 1.7 %collective-permute-done.10 = f32[32,384]{1,0:T(8,128)S(1)} collective-permute-done((f32[32,384]{1,0:T(8,128)S(1)}, f32[32,384]{1,0:T(8,128)S(1)}, u32[]{:S(2)}, u32[]{:S(2)}) %collective-permute-start.10) | collective-permute-done | bytes 49184 | tf_op jit(solution)/shard_map/ppermute | solution.py:54
  44.3 2.6 %fusion.4 = f32[1536,384]{0,1:T(8,128)S(1)} fusion(bf16[2048,384]{1,0:T(8,128)(2,1)S(1)} %bitcast.63, bf16[2048,2048]{1,0:T(8,128)(2,1)S(1)} %copy-done.5), kind=kOutput, calls=%fused_computation.4 | convolution fusion | flops 2415919104 | bytes 10223616 | tf_op jit(solution)/shard_map/dot_general | solution.py:117
  47.0 2.0 %copy.10 = f32[1536,384]{1,0:T(8,128)} copy(f32[1536,384]{0,1:T(8,128)S(1)} %fusion.4) | data formatting | bytes 4718592 | tf_op jit(solution)/shard_map/dot_general | solution.py:117
  48.9 2.6 %fusion.43 = f32[384,1344]{0,1:T(8,128)S(1)} fusion(f32[1344,16]{0,1:T(8,128)S(1)} %reshape.71, f32[16,384]{1,0:T(8,128)S(1)} %collective-permute-done.11, f32[32,384]{1,0:T(8,128)S(1)} %collective-permute-done.10, f32[512,384]{1,0:T(8,128)} %copy-done.3, s32[]{:T(128)S(6)} %select_n.203), kind=kOutput, calls=%fused_computation.90 | convolution fusion | flops 99102720 | bytes 2228228 | tf_op jit(solution)/shard_map/dot_general | solution.py:135
  51.6 2.1 %slice_add_fusion.1 = f32[24,56,384]{2,1,0:T(8,128)S(1)} fusion(f32[24,56,384]{2,1,0:T(8,128)S(1)} %bitcast.61, f32[24,64,384]{2,1,0:T(8,128)} %bitcast.59), kind=kLoop, calls=%fused_computation.24 | loop fusion | flops 516096 | bytes 6193152 | tf_op jit(solution)/shard_map/add | solution.py:139
  53.8 2.6 %collective-permute-start.18 = (f32[24,1,384]{2,1,0:T(1,128)S(1)}, f32[24,1,384]{2,1,0:T(1,128)S(1)}, u32[]{:S(2)}, u32[]{:S(2)}) collective-permute-start(f32[24,1,384]{2,1,0:T(1,128)S(1)} %get-tuple-element.15), channel_id=1, source_target_pairs={{0,1},{2,3},{4,5},{6,7},{1,0},{3,2},{5,4},{7,6},{8,9},{10,11},{12,... | collective-permute-start | bytes 110600 | tf_op jit(solution)/shard_map/ppermute | solution.py:20
  58.5 2.1 %fusion.53 = (bf16[24,56,384]{2,1,0:T(8,128)(2,1)S(1)}, f32[24,56,384]{2,1,0:T(8,128)S(1)}) fusion(f32[24,56,384]{2,1,0:T(8,128)S(1)} %copy-done.1, f32[24,56,384]{2,1,0:T(8,128)S(1)} %slice_add_fusion.1, f32[24,1,384]{2,1,0:T(1,128)S(1)} %bitcast.75, f32[24,56]{1,0:T(8,128)S(1)} %get-tuple-element.44, f32[24,1,384]{2,1,0:T(1,128)S(1)} %bitcast.74, ...), kind=kLoop, calls=%fused_computation.119 | loop fusion | flops 8773632 | bytes 7492608 | tf_op jit(solution)/shard_map/convert_element_type | solution.py:115
  60.6 1.2 %convolution_bitcast_fusion = f32[16,384]{1,0:T(8,128)S(1)} fusion(f32[24,56,384]{2,1,0:T(8,128)S(1)} %get-tuple-element.9, f32[24,56,16]{1,2,0:T(8,128)S(1)} %copy-done.2), kind=kOutput, calls=%fused_computation.27 | convolution fusion | flops 99090432 | bytes 2174976 | tf_op jit(solution)/shard_map/dot_general | solution.py:127
  61.8 6.3 %collective-permute-start.24 = (f32[16,384]{1,0:T(8,128)S(1)}, f32[16,384]{1,0:T(8,128)S(1)}, u32[]{:S(2)}, u32[]{:S(2)}) collective-permute-start(f32[16,384]{1,0:T(8,128)S(1)} %convolution_bitcast_fusion), channel_id=1, source_target_pairs={{0,4},{1,5},{2,6},{3,7},{4,0},{5,1},{6,2},{7,3},{8,12},{9,13},{10,... | collective-permute-start | bytes 73736 | tf_op jit(solution)/shard_map/ppermute | solution.py:54
  69.0 5.2 %collective-permute-start.21 = (bf16[4,56,384]{2,1,0:T(8,128)(2,1)S(1)}, bf16[4,56,384]{2,1,0:T(8,128)(2,1)S(1)}, u32[]{:S(2)}, u32[]{:S(2)}) collective-permute-start(bf16[4,56,384]{2,1,0:T(8,128)(2,1)S(1)} %get-tuple-element.18), channel_id=1, source_target_pairs={{0,8},{16,24},{8,0},{24,16},{1,9},{17,25},{9,1},{25,17},{2,10},{18... | collective-permute-start | bytes 516104 | tf_op jit(solution)/shard_map/ppermute | solution.py:20
  74.1 1.9 %collective-permute-start.25 = (f32[32,384]{1,0:T(8,128)S(1)}, f32[32,384]{1,0:T(8,128)S(1)}, u32[]{:S(2)}, u32[]{:S(2)}) collective-permute-start(f32[32,384]{1,0:T(8,128)S(1)} %pad_maximum_fusion.18), channel_id=1, source_target_pairs={{0,2},{1,3},{2,0},{3,1},{4,6},{5,7},{6,4},{7,5},{8,10},{9,11},{10,... | collective-permute-start | bytes 147464 | tf_op jit(solution)/shard_map/ppermute | solution.py:54
  76.1 2.2 %collective-permute-done.25 = f32[32,384]{1,0:T(8,128)S(1)} collective-permute-done((f32[32,384]{1,0:T(8,128)S(1)}, f32[32,384]{1,0:T(8,128)S(1)}, u32[]{:S(2)}, u32[]{:S(2)}) %collective-permute-start.25) | collective-permute-done | bytes 49184 | tf_op jit(solution)/shard_map/ppermute | solution.py:54
  78.4 1.2 %collective-permute-done.26 = f32[64,384]{1,0:T(8,128)S(1)} collective-permute-done((f32[64,384]{1,0:T(8,128)S(1)}, f32[64,384]{1,0:T(8,128)S(1)}, u32[]{:S(2)}, u32[]{:S(2)}) %collective-permute-start.26) | collective-permute-done | bytes 98336 | tf_op jit(solution)/shard_map/ppermute | solution.py:54
  81.2 3.5 %collective-permute-done.27 = f32[32,384]{1,0:T(8,128)S(1)} collective-permute-done((f32[32,384]{1,0:T(8,128)S(1)}, f32[32,384]{1,0:T(8,128)S(1)}, u32[]{:S(2)}, u32[]{:S(2)}) %collective-permute-start.27) | collective-permute-done | bytes 49184 | tf_op jit(solution)/shard_map/ppermute | solution.py:54
  85.1 2.0 %collective-permute-start.23 = (bf16[32,4,384]{2,1,0:T(4,128)(2,1)S(1)}, bf16[32,4,384]{2,1,0:T(4,128)(2,1)S(1)}, u32[]{:S(2)}, u32[]{:S(2)}) collective-permute-start(bf16[32,4,384]{2,1,0:T(4,128)(2,1)S(1)} %bitcast.81), channel_id=1, source_target_pairs={{0,1},{2,3},{4,5},{6,7},{1,0},{3,2},{5,4},{7,6},{8,9},{10,11},{12,... | collective-permute-start | bytes 294920 | tf_op jit(solution)/shard_map/ppermute | solution.py:20
  88.5 3.1 %fusion.40 = f32[384,1344]{0,1:T(8,128)} fusion(f32[1344,16]{0,1:T(8,128)S(1)} %reshape.71, f32[16,384]{1,0:T(8,128)S(1)} %collective-permute-done.28, f32[32,384]{1,0:T(8,128)S(1)} %collective-permute-done.27, f32[512,384]{1,0:T(8,128)S(1)} %fusion.31, s32[]{:T(128)S(6)} %select_n.203), kind=kOutput, calls=%fused_computation.86 | convolution fusion | flops 99102720 | bytes 2228228 | tf_op jit(solution)/shard_map/dot_general | solution.py:135
  92.6 4.0 %fusion.7 = f32[1536,384]{0,1:T(8,128)} fusion(bf16[2048,384]{1,0:T(8,128)(2,1)S(1)} %bitcast.64, bf16[2048,2048]{1,0:T(8,128)(2,1)S(1)} %bitcast.85), kind=kOutput, calls=%fused_computation.5 | convolution fusion | flops 2415919104 | bytes 10223616 | tf_op jit(solution)/shard_map/dot_general | solution.py:117
  96.6 3.1 %copy.14 = f32[1536,384]{1,0:T(8,128)} copy(f32[1536,384]{0,1:T(8,128)} %fusion.7) | data formatting | bytes 4718592 | tf_op jit(solution)/shard_map/dot_general | solution.py:117
  99.8 3.9 %fusion.10 = f32[24,56,384]{2,1,0:T(8,128)} fusion(f32[24,56,384]{2,1,0:T(8,128)} %bitcast.62, f32[24,56,384]{2,1,0:T(8,128)S(1)} %slice_add_fusion.1, f32[24,64,384]{2,1,0:T(8,128)} %bitcast.60), kind=kLoop, calls=%fused_computation.7 | loop fusion | flops 1032192 | bytes 8257536 | tf_op jit(solution)/shard_map/add | solution.py:142
  (99 shorter events, 21.4 us)
Async XLA Ops:
  0.0 21.0 %copy-start = (f32[24,56,384]{2,1,0:T(8,128)S(1)}, f32[24,56,384]{2,1,0:T(8,128)}, u32[]{:S(2)}) copy-start(f32[24,56,384]{2,1,0:T(8,128)} %param.5) | copy-start | bytes 6193156
  1.4 22.6 %collective-permute-start.13 = (f32[1,56]{1,0:T(1,128)}, f32[1,56]{1,0:T(1,128)}, u32[]{:S(2)}, u32[]{:S(2)}) collective-permute-start(f32[1,56]{1,0:T(1,128)} %get-tuple-element.41), channel_id=1, source_target_pairs={{8,16},{16,8},{9,17},{17,9},{10,18},{18,10},{11,19},{19,11},{12,20... | collective-permute-start | bytes 680 | tf_op jit(solution)/shard_map/ppermute | solution.py:23
  2.6 22.8 %collective-permute-start.12 = (f32[1,56]{1,0:T(1,128)}, f32[1,56]{1,0:T(1,128)}, u32[]{:S(2)}, u32[]{:S(2)}) collective-permute-start(f32[1,56]{1,0:T(1,128)} %get-tuple-element.42), channel_id=1, source_target_pairs={{0,8},{16,24},{8,0},{24,16},{1,9},{17,25},{9,1},{25,17},{2,10},{18... | collective-permute-start | bytes 680 | tf_op jit(solution)/shard_map/ppermute | solution.py:20
  7.9 13.4 %collective-permute-start.17 = (f32[24,1]{1,0:T(8,128)}, f32[24,1]{1,0:T(8,128)}, u32[]{:S(2)}, u32[]{:S(2)}) collective-permute-start(f32[24,1]{1,0:T(8,128)} %get-tuple-element.45), channel_id=1, source_target_pairs={{1,2},{3,4},{5,6},{2,1},{4,3},{6,5},{9,10},{11,12},{13,14},{10,9},... | collective-permute-start | bytes 296 | tf_op jit(solution)/shard_map/ppermute | solution.py:23
  9.2 12.5 %collective-permute-start.16 = (f32[24,1]{1,0:T(8,128)}, f32[24,1]{1,0:T(8,128)}, u32[]{:S(2)}, u32[]{:S(2)}) collective-permute-start(f32[24,1]{1,0:T(8,128)} %get-tuple-element.46), channel_id=1, source_target_pairs={{0,1},{2,3},{4,5},{6,7},{1,0},{3,2},{5,4},{7,6},{8,9},{10,11},{12,... | collective-permute-start | bytes 296 | tf_op jit(solution)/shard_map/ppermute | solution.py:20
  12.9 16.2 %collective-permute-start.4 = (f32[16,512]{1,0:T(8,128)}, f32[16,512]{1,0:T(8,128)}, u32[]{:S(2)}, u32[]{:S(2)}) collective-permute-start(f32[16,512]{1,0:T(8,128)} %param.9), channel_id=1, source_target_pairs={{0,4},{1,5},{2,6},{3,7},{4,0},{5,1},{6,2},{7,3},{8,12},{9,13},{10,... | collective-permute-start | bytes 98312 | tf_op jit(solution)/shard_map/ppermute | solution.py:54
  21.3 5.5 %collective-permute-start.7 = (f32[16,384]{1,0:T(8,128)}, f32[16,384]{1,0:T(8,128)S(1)}, u32[]{:S(2)}, u32[]{:S(2)}) collective-permute-start(f32[16,384]{1,0:T(8,128)} %convolution_bitcast_fusion.1), channel_id=1, source_target_pairs={{0,4},{1,5},{2,6},{3,7},{4,0},{5,1},{6,2},{7,3},{8,12},{9,13},{10,... | collective-permute-start | bytes 73736 | tf_op jit(solution)/shard_map/ppermute | solution.py:54
  21.7 13.5 %collective-permute-start = (bf16[4,56,384]{2,1,0:T(8,128)(2,1)S(1)}, bf16[4,56,384]{2,1,0:T(8,128)(2,1)S(1)}, u32[]{:S(2)}, u32[]{:S(2)}) collective-permute-start(bf16[4,56,384]{2,1,0:T(8,128)(2,1)S(1)} %get-tuple-element.19), channel_id=1, source_target_pairs={{8,16},{16,8},{9,17},{17,9},{10,18},{18,10},{11,19},{19,11},{12,20... | collective-permute-start | bytes 516104 | tf_op jit(solution)/shard_map/ppermute | solution.py:23
  24.0 11.2 %collective-permute-start.1 = (bf16[4,56,384]{2,1,0:T(8,128)(2,1)S(1)}, bf16[4,56,384]{2,1,0:T(8,128)(2,1)S(1)}, u32[]{:S(2)}, u32[]{:S(2)}) collective-permute-start(bf16[4,56,384]{2,1,0:T(8,128)(2,1)S(1)} %get-tuple-element.20), channel_id=1, source_target_pairs={{0,8},{16,24},{8,0},{24,16},{1,9},{17,25},{9,1},{25,17},{2,10},{18... | collective-permute-start | bytes 516104 | tf_op jit(solution)/shard_map/ppermute | solution.py:20
  27.6 4.1 %collective-permute-start.8 = (f32[32,384]{1,0:T(8,128)S(1)}, f32[32,384]{1,0:T(8,128)S(1)}, u32[]{:S(2)}, u32[]{:S(2)}) collective-permute-start(f32[32,384]{1,0:T(8,128)S(1)} %pad_maximum_fusion.16), channel_id=1, source_target_pairs={{0,2},{1,3},{2,0},{3,1},{4,6},{5,7},{6,4},{7,5},{8,10},{9,11},{10,... | collective-permute-start | bytes 147464 | tf_op jit(solution)/shard_map/ppermute | solution.py:54
  29.9 4.3 %collective-permute-start.5 = (f32[32,512]{1,0:T(8,128)S(1)}, f32[32,512]{1,0:T(8,128)S(1)}, u32[]{:S(2)}, u32[]{:S(2)}) collective-permute-start(f32[32,512]{1,0:T(8,128)S(1)} %pad_maximum_fusion.15), channel_id=1, source_target_pairs={{0,2},{1,3},{2,0},{3,1},{4,6},{5,7},{6,4},{7,5},{8,10},{9,11},{10,... | collective-permute-start | bytes 196616 | tf_op jit(solution)/shard_map/ppermute | solution.py:54
  32.4 4.3 %collective-permute-start.9 = (f32[64,384]{1,0:T(8,128)S(1)}, f32[64,384]{1,0:T(8,128)S(1)}, u32[]{:S(2)}, u32[]{:S(2)}) collective-permute-start(f32[64,384]{1,0:T(8,128)S(1)} %pad_maximum_fusion.13), channel_id=1, source_target_pairs={{0,8},{1,9},{2,10},{3,11},{4,12},{5,13},{6,14},{7,15},{8,0},{9,1},... | collective-permute-start | bytes 294920 | tf_op jit(solution)/shard_map/ppermute | solution.py:54
  35.1 1.6 %collective-permute-start.6 = (f32[64,512]{1,0:T(8,128)S(1)}, f32[64,512]{1,0:T(8,128)S(1)}, u32[]{:S(2)}, u32[]{:S(2)}) collective-permute-start(f32[64,512]{1,0:T(8,128)S(1)} %pad_maximum_fusion.6), channel_id=1, source_target_pairs={{0,8},{1,9},{2,10},{3,11},{4,12},{5,13},{6,14},{7,15},{8,0},{9,1},... | collective-permute-start | bytes 393224 | tf_op jit(solution)/shard_map/ppermute | solution.py:54
  35.4 5.8 %collective-permute-start.3 = (bf16[32,4,384]{2,1,0:T(4,128)(2,1)S(1)}, bf16[32,4,384]{2,1,0:T(4,128)(2,1)S(1)}, u32[]{:S(2)}, u32[]{:S(2)}) collective-permute-start(bf16[32,4,384]{2,1,0:T(4,128)(2,1)S(1)} %bitcast.78), channel_id=1, source_target_pairs={{0,1},{2,3},{4,5},{6,7},{1,0},{3,2},{5,4},{7,6},{8,9},{10,11},{12,... | collective-permute-start | bytes 294920 | tf_op jit(solution)/shard_map/ppermute | solution.py:20
  35.9 5.3 %collective-permute-start.2 = (bf16[32,4,384]{2,1,0:T(4,128)(2,1)S(1)}, bf16[32,4,384]{2,1,0:T(4,128)(2,1)S(1)}, u32[]{:S(2)}, u32[]{:S(2)}) collective-permute-start(bf16[32,4,384]{2,1,0:T(4,128)(2,1)S(1)} %get-tuple-element.10), channel_id=1, source_target_pairs={{1,2},{3,4},{5,6},{2,1},{4,3},{6,5},{9,10},{11,12},{13,14},{10,9},... | collective-permute-start | bytes 294920 | tf_op jit(solution)/shard_map/ppermute | solution.py:23
  37.6 6.2 %collective-permute-start.10 = (f32[32,384]{1,0:T(8,128)S(1)}, f32[32,384]{1,0:T(8,128)S(1)}, u32[]{:S(2)}, u32[]{:S(2)}) collective-permute-start(f32[32,384]{1,0:T(8,128)S(1)} %pad_maximum_fusion.17), channel_id=1, source_target_pairs={{0,1},{1,0},{2,3},{3,2},{4,5},{5,4},{6,7},{7,6},{8,9},{9,8},{10,11... | collective-permute-start | bytes 147464 | tf_op jit(solution)/shard_map/ppermute | solution.py:54
  43.8 5.2 %collective-permute-start.11 = (f32[16,384]{1,0:T(8,128)S(1)}, f32[16,384]{1,0:T(8,128)S(1)}, u32[]{:S(2)}, u32[]{:S(2)}) collective-permute-start(f32[16,384]{1,0:T(8,128)S(1)} %slice_add_fusion.4), channel_id=1, source_target_pairs={{0,16},{1,17},{2,18},{3,19},{4,20},{5,21},{6,22},{7,23},{8,24},{9,... | collective-permute-start | bytes 73736 | tf_op jit(solution)/shard_map/ppermute | solution.py:54
  53.8 4.5 %collective-permute-start.18 = (f32[24,1,384]{2,1,0:T(1,128)S(1)}, f32[24,1,384]{2,1,0:T(1,128)S(1)}, u32[]{:S(2)}, u32[]{:S(2)}) collective-permute-start(f32[24,1,384]{2,1,0:T(1,128)S(1)} %get-tuple-element.15), channel_id=1, source_target_pairs={{0,1},{2,3},{4,5},{6,7},{1,0},{3,2},{5,4},{7,6},{8,9},{10,11},{12,... | collective-permute-start | bytes 110600 | tf_op jit(solution)/shard_map/ppermute | solution.py:20
  56.4 1.9 %collective-permute-start.19 = (f32[24,1,384]{2,1,0:T(1,128)S(1)}, f32[24,1,384]{2,1,0:T(1,128)S(1)}, u32[]{:S(2)}, u32[]{:S(2)}) collective-permute-start(f32[24,1,384]{2,1,0:T(1,128)S(1)} %get-tuple-element.16), channel_id=1, source_target_pairs={{1,2},{3,4},{5,6},{2,1},{4,3},{6,5},{9,10},{11,12},{13,14},{10,9},... | collective-permute-start | bytes 110600 | tf_op jit(solution)/shard_map/ppermute | solution.py:23
  57.1 1.3 %collective-permute-start.14 = (f32[1,56,384]{2,1,0:T(8,128)S(1)}, f32[1,56,384]{2,1,0:T(8,128)S(1)}, u32[]{:S(2)}, u32[]{:S(2)}) collective-permute-start(f32[1,56,384]{2,1,0:T(8,128)S(1)} %get-tuple-element.13), channel_id=1, source_target_pairs={{0,8},{16,24},{8,0},{24,16},{1,9},{17,25},{9,1},{25,17},{2,10},{18... | collective-permute-start | bytes 258056 | tf_op jit(solution)/shard_map/ppermute | solution.py:20
  57.1 1.3 %collective-permute-start.15 = (f32[1,56,384]{2,1,0:T(8,128)S(1)}, f32[1,56,384]{2,1,0:T(8,128)S(1)}, u32[]{:S(2)}, u32[]{:S(2)}) collective-permute-start(f32[1,56,384]{2,1,0:T(8,128)S(1)} %get-tuple-element.14), channel_id=1, source_target_pairs={{8,16},{16,8},{9,17},{17,9},{10,18},{18,10},{11,19},{19,11},{12,20... | collective-permute-start | bytes 258056 | tf_op jit(solution)/shard_map/ppermute | solution.py:23
  58.5 34.1 %slice-start = ((s8[8388608]{0:T(1024)(128)(4,1)}), s8[4194304]{0:T(1024)(128)(4,1)S(1)}, s32[]{:S(2)}) async-start(s8[8388608]{0:T(1024)(128)(4,1)} %bitcast.84), calls=%async_computation | async-start | bytes 8388608
  61.8 12.3 %collective-permute-start.24 = (f32[16,384]{1,0:T(8,128)S(1)}, f32[16,384]{1,0:T(8,128)S(1)}, u32[]{:S(2)}, u32[]{:S(2)}) collective-permute-start(f32[16,384]{1,0:T(8,128)S(1)} %convolution_bitcast_fusion), channel_id=1, source_target_pairs={{0,4},{1,5},{2,6},{3,7},{4,0},{5,1},{6,2},{7,3},{8,12},{9,13},{10,... | collective-permute-start | bytes 73736 | tf_op jit(solution)/shard_map/ppermute | solution.py:54
  68.1 24.5 %slice-start.1 = ((s8[8388608]{0:T(1024)(128)(4,1)}), s8[4194304]{0:T(1024)(128)(4,1)S(1)}, s32[]{:S(2)}) async-start(s8[8388608]{0:T(1024)(128)(4,1)} %bitcast.84), calls=%async_computation.1 | async-start | bytes 8388608
  68.2 10.2 %collective-permute-start.20 = (bf16[4,56,384]{2,1,0:T(8,128)(2,1)S(1)}, bf16[4,56,384]{2,1,0:T(8,128)(2,1)S(1)}, u32[]{:S(2)}, u32[]{:S(2)}) collective-permute-start(bf16[4,56,384]{2,1,0:T(8,128)(2,1)S(1)} %get-tuple-element.17), channel_id=1, source_target_pairs={{8,16},{16,8},{9,17},{17,9},{10,18},{18,10},{11,19},{19,11},{12,20... | collective-permute-start | bytes 516104 | tf_op jit(solution)/shard_map/ppermute | solution.py:23
  69.0 9.4 %collective-permute-start.21 = (bf16[4,56,384]{2,1,0:T(8,128)(2,1)S(1)}, bf16[4,56,384]{2,1,0:T(8,128)(2,1)S(1)}, u32[]{:S(2)}, u32[]{:S(2)}) collective-permute-start(bf16[4,56,384]{2,1,0:T(8,128)(2,1)S(1)} %get-tuple-element.18), channel_id=1, source_target_pairs={{0,8},{16,24},{8,0},{24,16},{1,9},{17,25},{9,1},{25,17},{2,10},{18... | collective-permute-start | bytes 516104 | tf_op jit(solution)/shard_map/ppermute | solution.py:20
  74.1 4.2 %collective-permute-start.25 = (f32[32,384]{1,0:T(8,128)S(1)}, f32[32,384]{1,0:T(8,128)S(1)}, u32[]{:S(2)}, u32[]{:S(2)}) collective-permute-start(f32[32,384]{1,0:T(8,128)S(1)} %pad_maximum_fusion.18), channel_id=1, source_target_pairs={{0,2},{1,3},{2,0},{3,1},{4,6},{5,7},{6,4},{7,5},{8,10},{9,11},{10,... | collective-permute-start | bytes 147464 | tf_op jit(solution)/shard_map/ppermute | solution.py:54
  78.3 1.4 %collective-permute-start.26 = (f32[64,384]{1,0:T(8,128)S(1)}, f32[64,384]{1,0:T(8,128)S(1)}, u32[]{:S(2)}, u32[]{:S(2)}) collective-permute-start(f32[64,384]{1,0:T(8,128)S(1)} %pad_maximum_fusion.14), channel_id=1, source_target_pairs={{0,8},{1,9},{2,10},{3,11},{4,12},{5,13},{6,14},{7,15},{8,0},{9,1},... | collective-permute-start | bytes 294920 | tf_op jit(solution)/shard_map/ppermute | solution.py:54
  80.5 4.2 %collective-permute-start.27 = (f32[32,384]{1,0:T(8,128)S(1)}, f32[32,384]{1,0:T(8,128)S(1)}, u32[]{:S(2)}, u32[]{:S(2)}) collective-permute-start(f32[32,384]{1,0:T(8,128)S(1)} %pad_maximum_fusion.19), channel_id=1, source_target_pairs={{0,1},{1,0},{2,3},{3,2},{4,5},{5,4},{6,7},{7,6},{8,9},{9,8},{10,11... | collective-permute-start | bytes 147464 | tf_op jit(solution)/shard_map/ppermute | solution.py:54
  84.7 3.8 %collective-permute-start.28 = (f32[16,384]{1,0:T(8,128)S(1)}, f32[16,384]{1,0:T(8,128)S(1)}, u32[]{:S(2)}, u32[]{:S(2)}) collective-permute-start(f32[16,384]{1,0:T(8,128)S(1)} %slice_add_fusion.2), channel_id=1, source_target_pairs={{0,16},{1,17},{2,18},{3,19},{4,20},{5,21},{6,22},{7,23},{8,24},{9,... | collective-permute-start | bytes 73736 | tf_op jit(solution)/shard_map/ppermute | solution.py:54
  85.1 6.5 %collective-permute-start.23 = (bf16[32,4,384]{2,1,0:T(4,128)(2,1)S(1)}, bf16[32,4,384]{2,1,0:T(4,128)(2,1)S(1)}, u32[]{:S(2)}, u32[]{:S(2)}) collective-permute-start(bf16[32,4,384]{2,1,0:T(4,128)(2,1)S(1)} %bitcast.81), channel_id=1, source_target_pairs={{0,1},{2,3},{4,5},{6,7},{1,0},{3,2},{5,4},{7,6},{8,9},{10,11},{12,... | collective-permute-start | bytes 294920 | tf_op jit(solution)/shard_map/ppermute | solution.py:20
  87.1 4.6 %collective-permute-start.22 = (bf16[32,4,384]{2,1,0:T(4,128)(2,1)S(1)}, bf16[32,4,384]{2,1,0:T(4,128)(2,1)S(1)}, u32[]{:S(2)}, u32[]{:S(2)}) collective-permute-start(bf16[32,4,384]{2,1,0:T(4,128)(2,1)S(1)} %get-tuple-element.5), channel_id=1, source_target_pairs={{1,2},{3,4},{5,6},{2,1},{4,3},{6,5},{9,10},{11,12},{13,14},{10,9},... | collective-permute-start | bytes 294920 | tf_op jit(solution)/shard_map/ppermute | solution.py:23
  (5 other events, 41.3 us)

commit v2 on v1

v2 whole, which is shorter than its diff:
```python
import functools

import jax
import jax.numpy as jnp
from jax import lax
from jax.experimental import pallas as pl
from jax.experimental.pallas import tpu as pltpu
from jax.sharding import PartitionSpec as P

OV = 4
ITERS = 2
LANES = 128
AXES = ("grp", "mem")
EXACT = lax.Precision.HIGHEST
F32 = jnp.float32
BF16 = jnp.bfloat16


def neighbour_pairs(count, first):
    pairs = [(i, i + 1) for i in range(first, count - 1, 2)]
    return pairs + [(j, i) for i, j in pairs]


def edges(low_edge, high_edge, axis):
    count = lax.axis_size(axis)
    even = lax.axis_index(axis) % 2 == 0
    first = lax.ppermute(jnp.where(even, high_edge, low_edge), axis, neighbour_pairs(count, 0))
    second = lax.ppermute(jnp.where(even, low_edge, high_edge), axis, neighbour_pairs(count, 1))
    return jnp.where(even, second, first), jnp.where(even, first, second)


def masks():
    members, groups = lax.axis_size("mem"), lax.axis_size("grp")
    mem_bits = [1 << k for k in range(members.bit_length() - 1)]
    grp_bits = [members << k for k in range(groups.bit_length() - 1)]
    return mem_bits[:0:-1] + grp_bits[:1], mem_bits[:1] + grp_bits[1:]


def swap(value, bit):
    total = lax.axis_size("grp") * lax.axis_size("mem")
    return lax.ppermute(value, AXES, [(i, i ^ bit) for i in range(total)])


def gathered(value, bits):
    for bit in bits:
        value = jnp.concatenate([value, swap(value, bit)], axis=0)
    return value


def summed_shares(inverse_rows, sources, modes):
    shares = lax.dot_general(
        inverse_rows,
        sources,
        (((0,), (0,)), ((), ())),
        precision=EXACT,
        preferred_element_type=F32,
    )
    sum_bits = masks()[1]
    me = lax.axis_index(AXES)
    targets = [0]
    for bit in sum_bits[::-1]:
        targets = targets + [t ^ bit for t in targets]
    parts = [
        lax.dynamic_slice_in_dim(shares, (me ^ target) * modes, modes, 0) for target in targets
    ]
    for bit in sum_bits:
        half = len(parts) // 2
        got = swap(jnp.concatenate(parts[half:], axis=0), bit)
        parts = [part + got[k * modes : (k + 1) * modes] for k, part in enumerate(parts[:half])]
    return parts[0]


def survey(block, basis, step, low_ref, high_ref, side_ref, sum_ref):
    rows, own_y, columns = block.shape

    @pl.when(step == 0)
    def _():
        low_ref[...] = block.astype(BF16)
        sum_ref[...] = jnp.zeros_like(sum_ref)

    @pl.when(step == pl.num_programs(0) - 1)
    def _():
        high_ref[...] = block.astype(BF16)

    first = lax.broadcasted_iota(jnp.int32, (rows, 2 * OV, columns), 1) < OV
    side_ref[...] = jnp.where(first, block[:, : 2 * OV], block[:, own_y - 2 * OV :]).astype(BF16)
    sum_ref[...] += lax.dot_general(
        basis,
        block.reshape(rows * own_y, columns),
        (((0,), (0,)), ((), ())),
        precision=EXACT,
        preferred_element_type=F32,
    )


def start_kernel(block_ref, basis_ref, low_ref, high_ref, side_ref, sum_ref):
    survey(
        block_ref[...], basis_ref[...], pl.program_id(0), low_ref, high_ref, side_ref, sum_ref
    )


def residual_kernel(
    rhs_ref,
    now_ref,
    before_ref,
    after_ref,
    below_ref,
    above_ref,
    left_ref,
    right_ref,
    heat_ref,
    heat_before_ref,
    heat_after_ref,
    basis_ref,
    out_ref,
    low_ref,
    high_ref,
    side_ref,
    sum_ref,
):
    step = pl.program_id(0)
    last = pl.num_programs(0) - 1
    rows, own_y, columns = now_ref.shape
    wide = columns + LANES

    def spread(heat):
        return jnp.concatenate([heat] * (columns // LANES), axis=1)

    def row(index):
        return jnp.concatenate([now_ref[index], heat_ref[index]], axis=1)

    before = jnp.concatenate([before_ref[0], heat_before_ref[0]], axis=1)
    after = jnp.concatenate([after_ref[0], heat_after_ref[0]], axis=1)
    before = jnp.where(step == 0, below_ref[0], before)
    after = jnp.where(step == last, above_ref[0], after)
    place = lax.broadcasted_iota(jnp.int32, (own_y, wide), 0)
    for index in range(rows):
        here = row(index)
        up = row(index + 1) if index + 1 < rows else after
        down = row(index - 1) if index else before
        right = jnp.where(
            place == own_y - 1, right_ref[0, index : index + 1], pltpu.roll(here, own_y - 1, 0)
        )
        left = jnp.where(place == 0, left_ref[0, index : index + 1], pltpu.roll(here, 1, 0))
        summed = jnp.zeros((own_y, columns), F32)
        for other in (up, down, right, left):
            face = 0.5 * (here[:, columns:] + other[:, columns:])
            summed = summed + spread(face) * (here[:, :columns] - other[:, :columns])
        out_ref[index] = rhs_ref[index] - summed
    survey(out_ref[...], basis_ref[...], step, low_ref, high_ref, side_ref, sum_ref)


def fine_kernel(
    has_base,
    inverse_ref,
    block_ref,
    low_ref,
    high_ref,
    side_ref,
    basis_ref,
    lifted_ref,
    *refs,
):
    if has_base:
        base_ref, out_ref, window, wide, product = refs
    else:
        heat_ref, out_ref, first_ref, last_ref, left_ref, right_ref, window, wide, product = refs
    step = pl.program_id(0)
    own_x, own_y, columns = block_ref.shape
    span_y = own_y + 2 * OV
    rows = out_ref.shape[0]

    @pl.when(step == 0)
    def _():
        def place(index, values):
            wide[OV : OV + own_y, :] = values
            sides = side_ref[index].astype(F32)
            wide[:OV, :] = sides[:OV]
            wide[OV + own_y :, :] = sides[OV:]
            start = index * span_y
            if not isinstance(index, int):
                start = pl.multiple_of(start, span_y)
            window[pl.ds(start, span_y), :] = wide[...].astype(BF16)

        for index in range(OV):
            place(index, low_ref[index].astype(F32))
            place(OV + own_x + index, high_ref[index].astype(F32))

        @pl.loop(0, own_x, unroll=4)
        def _(index):
            place(OV + index, block_ref[index])

    product[...] = jnp.dot(inverse_ref[...], window[...], preferred_element_type=F32)
    coarse = jnp.dot(basis_ref[...], lifted_ref[...], precision=EXACT, preferred_element_type=F32)
    for index in range(rows):
        value = product[index * span_y + OV : index * span_y + OV + own_y, :]
        value = value + coarse[index * own_y : (index + 1) * own_y]
        if has_base:
            value = base_ref[index] + value
        out_ref[index] = value
    if not has_base:
        final = pl.num_programs(0) - 1

        @pl.when(step == 0)
        def _():
            first_ref[0] = jnp.concatenate([out_ref[0], heat_ref[0]], axis=1)

        @pl.when(step == final)
        def _():
            last_ref[0] = jnp.concatenate([out_ref[rows - 1], heat_ref[rows - 1]], axis=1)

        for index in range(rows):
            for ref, at in ((left_ref, 0), (right_ref, own_y - 1)):
                ref[0, index : index + 1, :columns] = out_ref[index, at : at + 1]
                ref[0, index : index + 1, columns:] = heat_ref[index, at : at + 1]


def whole(shape):
    return pl.BlockSpec(shape, lambda i: (0,) * len(shape))


def tiles(shape):
    return pl.BlockSpec(shape, lambda i: (i,) + (0,) * (len(shape) - 1))


def shape_of(shape, kind):
    return jax.ShapeDtypeStruct(shape, kind)


def on_device(rhs, conductivity, local_inverse, coarse_basis, coarse_inverse):
    own_x, own_y, columns = rhs.shape
    modes = coarse_basis.shape[2]
    span_x = own_x + 2 * OV
    span_y = own_y + 2 * OV
    local = span_x * span_y
    cells = own_x * own_y
    steps = own_x // OV
    basis_flat = coarse_basis.reshape(cells, modes)
    heat = jnp.broadcast_to(conductivity[:, :, None], (own_x, own_y, LANES))
    params = pltpu.CompilerParams(vmem_limit_bytes=32 * 2**20)

    block = (OV, own_y, columns)
    basis_block = tiles((OV * own_y, modes))
    survey_shapes = [
        shape_of(block, BF16),
        shape_of(block, BF16),
        shape_of((own_x, 2 * OV, columns), BF16),
        shape_of((modes, columns), F32),
    ]
    survey_specs = [
        whole(block),
        whole(block),
        tiles((OV, 2 * OV, columns)),
        whole((modes, columns)),
    ]

    def surveyed_start():
        return pl.pallas_call(
            start_kernel,
            grid=(steps,),
            in_specs=[tiles(block), basis_block],
            out_specs=survey_specs,
            out_shape=survey_shapes,
            compiler_params=params,
        )(rhs, basis_flat)

    def surveyed_residual(now, around):
        below, above, left, right = around

        def before(size):
            return pl.BlockSpec((1, own_y, size), lambda i: (jnp.maximum(i * OV - 1, 0), 0, 0))

        def after(size):
            return pl.BlockSpec(
                (1, own_y, size), lambda i: (jnp.minimum(i * OV + OV, own_x - 1), 0, 0)
            )

        edge = columns + LANES
        return pl.pallas_call(
            residual_kernel,
            grid=(steps,),
            in_specs=[
                tiles(block),
                tiles(block),
                before(columns),
                after(columns),
                whole((1, own_y, edge)),
                whole((1, own_y, edge)),
                tiles((1, OV, edge)),
                tiles((1, OV, edge)),
                tiles((OV, own_y, LANES)),
                before(LANES),
                after(LANES),
                basis_block,
            ],
            out_specs=[tiles(block)] + survey_specs,
            out_shape=[shape_of(rhs.shape, F32)] + survey_shapes,
            compiler_params=params,
        )(rhs, now, now, now, below, above, left, right, heat, heat, heat, basis_flat)

    def window_margins(low_edge, high_edge, sides):
        low, high = edges(low_edge, high_edge, "grp")
        corners = [jnp.concatenate([m[:, :OV], m[:, -OV:]], axis=1) for m in (low, high)]
        sides = jnp.concatenate([corners[0], sides, corners[1]], axis=0)
        left, right = edges(sides[:, :OV], sides[:, OV:], "mem")
        return low, high, jnp.concatenate([left, right], axis=1)

    def improved(values, margins, lifted, now):
        low, high, sides = margins
        edge = columns + LANES
        in_specs = [
            pl.BlockSpec((OV * span_y, local), lambda i: (i + 1, 0)),
            whole(rhs.shape),
            whole(block),
            whole(block),
            whole((span_x, 2 * OV, columns)),
            basis_block,
            whole((modes, columns)),
        ]
        out_specs = [tiles(block)]
        out_shape = [shape_of(rhs.shape, F32)]
        if now is None:
            in_specs.append(tiles((OV, own_y, LANES)))
            out_specs += [whole((1, own_y, edge))] * 2 + [tiles((1, OV, edge))] * 2
            out_shape += [shape_of((1, own_y, edge), F32)] * 2
            out_shape += [shape_of((steps, OV, edge), F32)] * 2
        else:
            in_specs.append(tiles(block))
        return pl.pallas_call(
            functools.partial(fine_kernel, now is not None),
            grid=(steps,),
            in_specs=in_specs,
            out_specs=out_specs,
            out_shape=out_shape,
            scratch_shapes=[
                pltpu.VMEM((local, columns), BF16),
                pltpu.VMEM((span_y, columns), F32),
                pltpu.VMEM((OV * span_y, columns), F32),
            ],
            compiler_params=params,
        )(
            local_inverse,
            values,
            low,
            high,
            sides,
            basis_flat,
            lifted,
            heat if now is None else now,
        )

    gather_bits = masks()[0]
    *to_send, restricted = surveyed_start()
    sources = gathered(jnp.concatenate([restricted, coarse_inverse], axis=1), gather_bits)
    inverse_rows = sources[:, columns:]
    margins = window_margins(*to_send)
    lifted = summed_shares(inverse_rows, sources[:, :columns], modes)
    now, first, final, left, right = improved(rhs, margins, lifted, None)
    for sweep in range(ITERS - 1):
        around = edges(first, final, "grp") + edges(left, right, "mem")
        residual, *to_send, restricted = surveyed_residual(now, around)
        sources = gathered(restricted, gather_bits)
        margins = window_margins(*to_send)
        lifted = summed_shares(inverse_rows, sources, modes)
        now = improved(residual, margins, lifted, now)[0]
    return now


def solution(mesh):
    placed = (
        P("grp", "mem", None),
        P("grp", "mem"),
        P(("grp", "mem"), None),
        P("grp", "mem", None),
        P(("grp", "mem"), None),
    )
    return jax.shard_map(
        on_device, mesh=mesh, in_specs=placed, out_specs=P("grp", "mem", None), check_vma=False
    )
```

time: 106 us -> 92.7 us (0.87); the launches traced: 104 us -> 92.3 us
  Pallas kernels: 0 us -> 20.5 us
  other arithmetic: 19.7 us -> 0.9 us
  matrix products: 19 us -> 1.64 us
  waiting for transfers between devices: 12.1 us -> 22.7 us
  starting transfers between devices: 44.5 us -> 39.7 us
  local copies, waits for them, and re-layouts: 7.91 us -> 6.49 us
    pallas_call x0 -> x4, Pallas kernels: none -> 20.5 us  [the longest x2 13.9 us: improved(): pl.pallas_call(functools.partial(fine_kernel, now is not None), grid=(ste...]
    dot_general x8 -> x2, matrix products: 19 us -> 1.64 us  [summed_shares(): lax.dot_general(inverse_rows, sources, (((0,), (0,)), ((), ())), precisio...]
    ppermute x8 -> x6, starting transfers between devices: 19.2 us -> 8.52 us  [edges(): lax.ppermute(jnp.where(even, high_edge, low_edge), axis, neighbour_pairs(...]
    ppermute x13 -> x10, starting transfers between devices: 18.5 us -> 27.2 us  [swap(): return lax.ppermute(value, AXES, [(i, i ^ bit) for i in range(total)])]
    ppermute x8 -> x6, waiting for transfers between devices: 0.42 us -> 6.68 us  [edges(): lax.ppermute(jnp.where(even, high_edge, low_edge), axis, neighbour_pairs(...]
    add x4, other arithmetic: 6.06 us -> 0.02 us  [summed_shares(): part + got[k * modes:(k + 1) * modes]]
    dot_general x2 -> x0, local copies, waits for them, and re-layouts: 5.08 us -> none  [fine(): jnp.dot(owned_inverse, extended.reshape(span_x * span_y, columns), prefer...]
    ppermute x13 -> x10, waiting for transfers between devices: 11.7 us -> 16 us  [swap(): return lax.ppermute(value, AXES, [(i, i ^ bit) for i in range(total)])]
  transfers between devices with their start and end apart: 29 -> 22, of which waited for: 9 -> 11; matrix products, arithmetic and copies ran while one was open for 23% -> 3% of each run, Pallas kernels for 0% -> 0%
where the time goes in v2:
time: 92.7 us; the launch traced here: 92.3 us
  starting transfers between devices  39.7 us (43%)
  waiting for transfers between devices  22.7 us (24%)
  Pallas kernels  20.5 us (22%)
  local copies, waits for them, and re-layouts  6.49 us (7%)
  matrix products  1.64 us (2%)
    ppermute x10, starting transfers between devices, swap(): return lax.ppermute(value, AXES, [(i, i ^ bit) for i in range(total)])  27.2 us
    ppermute x10, waiting for transfers between devices, swap(): return lax.ppermute(value, AXES, [(i, i ^ bit) for i in range(total)])  16 us
    pallas_call x2, Pallas kernels, improved(): pl.pallas_call(functools.partial(fine_kernel, now is not None), grid=(ste...  13.9 us
    ppermute x6, starting transfers between devices, edges(): lax.ppermute(jnp.where(even, high_edge, low_edge), axis, neighbour_pairs(...  8.52 us
    ppermute x6, waiting for transfers between devices, edges(): lax.ppermute(jnp.where(even, high_edge, low_edge), axis, neighbour_pairs(...  6.68 us
    unnamed x16, local copies, waits for them, and re-layouts  6.17 us
    pallas_call x1, Pallas kernels, surveyed_residual(): pl.pallas_call(residual_kernel, grid=(steps,), in_specs=[tiles(block), ti...  4.32 us
    ppermute x6, starting transfers between devices, edges(): lax.ppermute(jnp.where(even, low_edge, high_edge), axis, neighbour_pairs(...  3.99 us
  transfers between devices with their start and end apart: 22, of which 11 were waited for; matrix products, arithmetic and copies ran while one was open for 3% of the time, Pallas kernels for 0%

profile of v2, /device:TPU:0, one launch (start us, length us, event | category | flops | bytes accessed | tf_op | source)
XLA Modules:
  0.0 92.3 jit_solution(6319474061751308054)
XLA Ops:
  0.0 1.2 %copy.6 = f32[24,56,16]{2,1,0:T(8,128)S(1)} copy(f32[24,56,16]{1,2,0:T(8,128)} %param.8) | data formatting | bytes 172032 | tf_op args[3]
  1.2 1.6 %copy-done.1 = f32[24,56,384]{2,1,0:T(8,128)S(1)} copy-done((f32[24,56,384]{2,1,0:T(8,128)S(1)}, f32[24,56,384]{2,1,0:T(8,128)}, u32[]{:S(2)}) %copy-start.1) | copy-done | bytes 2064408
  2.8 2.3 %shard_map.55 = (bf16[4,56,384]{2,1,0:T(8,128)(2,1)S(1)}, bf16[4,56,384]{2,1,0:T(8,128)(2,1)S(1)}, bf16[24,8,384]{2,1,0:T(8,128)(2,1)S(1)}, f32[16,384]{1,0:T(8,128)S(1)}) custom-call(f32[24,56,384]{2,1,0:T(8,128)S(1)} %copy-done.1, f32[1344,16]{1,0:T(8,128)S(1)} %bitcast.19), custom_call_target="tpu_custom_call" | custom-call | tf_op jit(solution)/shard_map/pallas_call | solution.py:258
  5.1 4.1 %collective-permute-start.4 = (f32[16,896]{1,0:T(8,128)S(1)}, f32[16,896]{1,0:T(8,128)S(1)}, u32[]{:S(2)}, u32[]{:S(2)}) collective-permute-start(f32[16,896]{1,0:T(8,128)S(1)} %constant_dynamic-update-slice_fusion), channel_id=1, source_target_pairs={{0,4},{1,5},{2,6},{3,7},{4,0},{5,1},{6,2},{7,3},{8,12},{9,13},{10,... | collective-permute-start | bytes 172040 | tf_op jit(solution)/shard_map/ppermute | solution.py:41
  9.2 2.8 %collective-permute-done.4 = f32[16,896]{1,0:T(8,128)S(1)} collective-permute-done((f32[16,896]{1,0:T(8,128)S(1)}, f32[16,896]{1,0:T(8,128)S(1)}, u32[]{:S(2)}, u32[]{:S(2)}) %collective-permute-start.4) | collective-permute-done | bytes 57376 | tf_op jit(solution)/shard_map/ppermute | solution.py:41
  12.0 1.4 %collective-permute-start.5 = (f32[32,896]{1,0:T(8,128)S(1)}, f32[32,896]{1,0:T(8,128)S(1)}, u32[]{:S(2)}, u32[]{:S(2)}) collective-permute-start(f32[32,896]{1,0:T(8,128)S(1)} %pad_maximum_fusion.4), channel_id=1, source_target_pairs={{0,2},{1,3},{2,0},{3,1},{4,6},{5,7},{6,4},{7,5},{8,10},{9,11},{10,... | collective-permute-start | bytes 344072 | tf_op jit(solution)/shard_map/ppermute | solution.py:41
  13.4 0.7 collective-permute-start
  14.2 2.7 %collective-permute-done.5 = f32[32,896]{1,0:T(8,128)S(1)} collective-permute-done((f32[32,896]{1,0:T(8,128)S(1)}, f32[32,896]{1,0:T(8,128)S(1)}, u32[]{:S(2)}, u32[]{:S(2)}) %collective-permute-start.5) | collective-permute-done | bytes 114720 | tf_op jit(solution)/shard_map/ppermute | solution.py:41
  18.1 3.8 %collective-permute-start.3 = (bf16[32,4,384]{2,1,0:T(4,128)(2,1)S(1)}, bf16[32,4,384]{2,1,0:T(4,128)(2,1)S(1)}, u32[]{:S(2)}, u32[]{:S(2)}) collective-permute-start(bf16[32,4,384]{2,1,0:T(4,128)(2,1)S(1)} %get-tuple-element.56), channel_id=1, source_target_pairs={{0,1},{2,3},{4,5},{6,7},{1,0},{3,2},{5,4},{7,6},{8,9},{10,11},{12,... | collective-permute-start | bytes 294920 | tf_op jit(solution)/shard_map/ppermute | solution.py:27
  22.0 0.8 fusion.2
  23.0 2.0 %collective-permute-done.3 = bf16[32,4,384]{2,1,0:T(4,128)(2,1)S(1)} collective-permute-done((bf16[32,4,384]{2,1,0:T(4,128)(2,1)S(1)}, bf16[32,4,384]{2,1,0:T(4,128)(2,1)S(1)}, u32[]{:S(2)}, u32[]{:S(2)}) %collective-permute-start.3) | collective-permute-done | bytes 98336 | tf_op jit(solution)/shard_map/ppermute | solution.py:27
  25.0 2.3 %collective-permute-done.7 = f32[32,384]{1,0:T(8,128)S(1)} collective-permute-done((f32[32,384]{1,0:T(8,128)S(1)}, f32[32,384]{1,0:T(8,128)S(1)}, u32[]{:S(2)}, u32[]{:S(2)}) %collective-permute-start.7) | collective-permute-done | bytes 49184 | tf_op jit(solution)/shard_map/ppermute | solution.py:41
  27.3 4.1 %collective-permute-start.8 = (f32[16,384]{1,0:T(8,128)S(1)}, f32[16,384]{1,0:T(8,128)S(1)}, u32[]{:S(2)}, u32[]{:S(2)}) collective-permute-start(f32[16,384]{1,0:T(8,128)S(1)} %slice_add_fusion.2), channel_id=1, source_target_pairs={{0,16},{1,17},{2,18},{3,19},{4,20},{5,21},{6,22},{7,23},{8,24},{9,... | collective-permute-start | bytes 73736 | tf_op jit(solution)/shard_map/ppermute | solution.py:41
  31.5 1.7 %collective-permute-done.8 = f32[16,384]{1,0:T(8,128)S(1)} collective-permute-done((f32[16,384]{1,0:T(8,128)S(1)}, f32[16,384]{1,0:T(8,128)S(1)}, u32[]{:S(2)}, u32[]{:S(2)}) %collective-permute-start.8) | collective-permute-done | bytes 24608 | tf_op jit(solution)/shard_map/ppermute | solution.py:41
  33.5 3.4 %copy-done = bf16[2048,2048]{1,0:T(8,128)(2,1)S(1)} copy-done((bf16[2048,2048]{1,0:T(8,128)(2,1)S(1)}, bf16[2048,2048]{1,0:T(8,128)(2,1)}, u32[]{:S(2)}) %copy-start) | copy-done | bytes 8388632
  36.8 6.6 %shard_map.56 = (f32[24,56,384]{2,1,0:T(8,128)S(1)}, f32[1,56,512]{2,1,0:T(8,128)S(1)}, f32[1,56,512]{2,1,0:T(8,128)S(1)}, f32[6,4,512]{2,1,0:T(4,128)S(1)}, f32[6,4,512]{2,1,0:T(4,128)S(1)}) custom-call(bf16[2048,2048]{1,0:T(8,128)(2,1)S(1)} %copy-done, f32[24,56,384]{2,1,0:T(8,128)S(1)} %copy-done.2, bf16[4,56,384]{2,1,0:T(8,128)(2,1)S(1)} %get-tuple-element.42.low_ref, ...), custom_call_target="tpu_custom_call" | custom-call | tf_op jit(solution)/shard_map/pallas_call | solution.py:329
  43.4 1.2 %collective-permute-start.12 = (f32[6,4,512]{2,1,0:T(4,128)S(1)}, f32[6,4,512]{2,1,0:T(4,128)S(1)}, u32[]{:S(2)}, u32[]{:S(2)}) collective-permute-start(f32[6,4,512]{2,1,0:T(4,128)S(1)} %bitcast.37), channel_id=1, source_target_pairs={{0,1},{2,3},{4,5},{6,7},{1,0},{3,2},{5,4},{7,6},{8,9},{10,11},{12,... | collective-permute-start | bytes 147464 | tf_op jit(solution)/shard_map/ppermute | solution.py:27
  45.4 0.7 collective-permute-start.9
  46.1 1.5 %collective-permute-done.12 = f32[6,4,512]{2,1,0:T(4,128)S(1)} collective-permute-done((f32[6,4,512]{2,1,0:T(4,128)S(1)}, f32[6,4,512]{2,1,0:T(4,128)S(1)}, u32[]{:S(2)}, u32[]{:S(2)}) %collective-permute-start.12) | collective-permute-done | bytes 49184 | tf_op jit(solution)/shard_map/ppermute | solution.py:27
  47.7 4.3 %shard_map.57 = (f32[24,56,384]{2,1,0:T(8,128)S(1)}, bf16[4,56,384]{2,1,0:T(8,128)(2,1)S(1)}, bf16[4,56,384]{2,1,0:T(8,128)(2,1)S(1)}, bf16[24,8,384]{2,1,0:T(8,128)(2,1)S(1)}, f32[16,384]{1,0:T(8,128)S(1)}) custom-call(f32[24,56,384]{2,1,0:T(8,128)S(1)} %copy-done.2, f32[24,56,384]{2,1,0:T(8,128)S(1)} %get-tuple-element.23.now_ref.before_ref.after_ref.refs_0_, ...), custom_call_target="tpu_custom_call" | custom-call | tf_op jit(solution)/shard_map/pallas_call | solution.py:279
  52.0 6.3 %collective-permute-start.17 = (f32[16,384]{1,0:T(8,128)S(1)}, f32[16,384]{1,0:T(8,128)S(1)}, u32[]{:S(2)}, u32[]{:S(2)}) collective-permute-start(f32[16,384]{1,0:T(8,128)S(1)} %get-tuple-element.32), channel_id=1, source_target_pairs={{0,4},{1,5},{2,6},{3,7},{4,0},{5,1},{6,2},{7,3},{8,12},{9,13},{10,... | collective-permute-start | bytes 73736 | tf_op jit(solution)/shard_map/ppermute | solution.py:41
  58.3 1.8 %collective-permute-done.17 = f32[16,384]{1,0:T(8,128)S(1)} collective-permute-done((f32[16,384]{1,0:T(8,128)S(1)}, f32[16,384]{1,0:T(8,128)S(1)}, u32[]{:S(2)}, u32[]{:S(2)}) %collective-permute-start.17) | collective-permute-done | bytes 24608 | tf_op jit(solution)/shard_map/ppermute | solution.py:41
  60.1 2.3 %collective-permute-start.18 = (f32[32,384]{1,0:T(8,128)S(1)}, f32[32,384]{1,0:T(8,128)S(1)}, u32[]{:S(2)}, u32[]{:S(2)}) collective-permute-start(f32[32,384]{1,0:T(8,128)S(1)} %pad_maximum_fusion.7), channel_id=1, source_target_pairs={{0,2},{1,3},{2,0},{3,1},{4,6},{5,7},{6,4},{7,5},{8,10},{9,11},{10,... | collective-permute-start | bytes 147464 | tf_op jit(solution)/shard_map/ppermute | solution.py:41
  62.4 2.1 %collective-permute-done.18 = f32[32,384]{1,0:T(8,128)S(1)} collective-permute-done((f32[32,384]{1,0:T(8,128)S(1)}, f32[32,384]{1,0:T(8,128)S(1)}, u32[]{:S(2)}, u32[]{:S(2)}) %collective-permute-start.18) | collective-permute-done | bytes 49184 | tf_op jit(solution)/shard_map/ppermute | solution.py:41
  64.5 1.8 %collective-permute-start.19 = (f32[64,384]{1,0:T(8,128)S(1)}, f32[64,384]{1,0:T(8,128)S(1)}, u32[]{:S(2)}, u32[]{:S(2)}) collective-permute-start(f32[64,384]{1,0:T(8,128)S(1)} %pad_maximum_fusion.5), channel_id=1, source_target_pairs={{0,8},{1,9},{2,10},{3,11},{4,12},{5,13},{6,14},{7,15},{8,0},{9,1},... | collective-permute-start | bytes 294920 | tf_op jit(solution)/shard_map/ppermute | solution.py:41
  67.2 0.8 fusion
  68.1 1.5 %collective-permute-start.20 = (f32[32,384]{1,0:T(8,128)S(1)}, f32[32,384]{1,0:T(8,128)S(1)}, u32[]{:S(2)}, u32[]{:S(2)}) collective-permute-start(f32[32,384]{1,0:T(8,128)S(1)} %pad_maximum_fusion.8), channel_id=1, source_target_pairs={{0,1},{1,0},{2,3},{3,2},{4,5},{5,4},{6,7},{7,6},{8,9},{9,8},{10,11... | collective-permute-start | bytes 147464 | tf_op jit(solution)/shard_map/ppermute | solution.py:41
  69.7 2.5 %collective-permute-done.20 = f32[32,384]{1,0:T(8,128)S(1)} collective-permute-done((f32[32,384]{1,0:T(8,128)S(1)}, f32[32,384]{1,0:T(8,128)S(1)}, u32[]{:S(2)}, u32[]{:S(2)}) %collective-permute-start.20) | collective-permute-done | bytes 49184 | tf_op jit(solution)/shard_map/ppermute | solution.py:41
  72.2 5.3 %collective-permute-start.21 = (f32[16,384]{1,0:T(8,128)S(1)}, f32[16,384]{1,0:T(8,128)S(1)}, u32[]{:S(2)}, u32[]{:S(2)}) collective-permute-start(f32[16,384]{1,0:T(8,128)S(1)} %slice_add_fusion), channel_id=1, source_target_pairs={{0,16},{1,17},{2,18},{3,19},{4,20},{5,21},{6,22},{7,23},{8,24},{9,... | collective-permute-start | bytes 73736 | tf_op jit(solution)/shard_map/ppermute | solution.py:41
  78.4 3.3 %collective-permute-start.16 = (bf16[32,4,384]{2,1,0:T(4,128)(2,1)S(1)}, bf16[32,4,384]{2,1,0:T(4,128)(2,1)S(1)}, u32[]{:S(2)}, u32[]{:S(2)}) collective-permute-start(bf16[32,4,384]{2,1,0:T(4,128)(2,1)S(1)} %get-tuple-element.52), channel_id=1, source_target_pairs={{0,1},{2,3},{4,5},{6,7},{1,0},{3,2},{5,4},{7,6},{8,9},{10,11},{12,... | collective-permute-start | bytes 294920 | tf_op jit(solution)/shard_map/ppermute | solution.py:27
  81.7 3.2 %collective-permute-done.16 = bf16[32,4,384]{2,1,0:T(4,128)(2,1)S(1)} collective-permute-done((bf16[32,4,384]{2,1,0:T(4,128)(2,1)S(1)}, bf16[32,4,384]{2,1,0:T(4,128)(2,1)S(1)}, u32[]{:S(2)}, u32[]{:S(2)}) %collective-permute-start.16) | collective-permute-done | bytes 98336 | tf_op jit(solution)/shard_map/ppermute | solution.py:27
  85.0 7.3 %shard_map.58 = f32[24,56,384]{2,1,0:T(8,128)} custom-call(bf16[2048,2048]{1,0:T(8,128)(2,1)S(1)} %bitcast.18, f32[24,56,384]{2,1,0:T(8,128)S(1)} %get-tuple-element.28.block_ref, bf16[4,56,384]{2,1,0:T(8,128)(2,1)S(1)} %get-tuple-element.38.low_ref, bf16[4,56,384]{2,1,0:T(8,128)(2,1)S(1)} %get-tuple-element.37.high_ref, ...), custom_call_target="tpu_custom_call" | custom-call | tf_op jit(solution)/shard_map/pallas_call | solution.py:329
  (69 shorter events, 4.8 us)
Async XLA Ops:
  0.0 5.1 %copy-start.3 = (f32[16,512]{1,0:T(8,128)S(1)}, f32[16,512]{1,0:T(8,128)}, u32[]{:S(2)}) copy-start(f32[16,512]{1,0:T(8,128)} %param.9) | copy-start | bytes 98308
  1.2 1.6 %copy-start.1 = (f32[24,56,384]{2,1,0:T(8,128)S(1)}, f32[24,56,384]{2,1,0:T(8,128)}, u32[]{:S(2)}) copy-start(f32[24,56,384]{2,1,0:T(8,128)} %rhs_ref.1) | copy-start | bytes 6193156
  5.1 6.9 %collective-permute-start.4 = (f32[16,896]{1,0:T(8,128)S(1)}, f32[16,896]{1,0:T(8,128)S(1)}, u32[]{:S(2)}, u32[]{:S(2)}) collective-permute-start(f32[16,896]{1,0:T(8,128)S(1)} %constant_dynamic-update-slice_fusion), channel_id=1, source_target_pairs={{0,4},{1,5},{2,6},{3,7},{4,0},{5,1},{6,2},{7,3},{8,12},{9,13},{10,... | collective-permute-start | bytes 172040 | tf_op jit(solution)/shard_map/ppermute | solution.py:41
  12.0 4.9 %collective-permute-start.5 = (f32[32,896]{1,0:T(8,128)S(1)}, f32[32,896]{1,0:T(8,128)S(1)}, u32[]{:S(2)}, u32[]{:S(2)}) collective-permute-start(f32[32,896]{1,0:T(8,128)S(1)} %pad_maximum_fusion.4), channel_id=1, source_target_pairs={{0,2},{1,3},{2,0},{3,1},{4,6},{5,7},{6,4},{7,5},{8,10},{9,11},{10,... | collective-permute-start | bytes 344072 | tf_op jit(solution)/shard_map/ppermute | solution.py:41
  13.4 3.8 %collective-permute-start.1 = (bf16[4,56,384]{2,1,0:T(8,128)(2,1)S(1)}, bf16[4,56,384]{2,1,0:T(8,128)(2,1)S(1)}, u32[]{:S(2)}, u32[]{:S(2)}) collective-permute-start(bf16[4,56,384]{2,1,0:T(8,128)(2,1)S(1)} %get-tuple-element.43), channel_id=1, source_target_pairs={{0,8},{16,24},{8,0},{24,16},{1,9},{17,25},{9,1},{25,17},{2,10},{18... | collective-permute-start | bytes 516104 | tf_op jit(solution)/shard_map/ppermute | solution.py:27
  13.4 3.8 %collective-permute-start = (bf16[4,56,384]{2,1,0:T(8,128)(2,1)S(1)}, bf16[4,56,384]{2,1,0:T(8,128)(2,1)S(1)}, u32[]{:S(2)}, u32[]{:S(2)}) collective-permute-start(bf16[4,56,384]{2,1,0:T(8,128)(2,1)S(1)} %get-tuple-element.44), channel_id=1, source_target_pairs={{8,16},{16,8},{9,17},{17,9},{10,18},{18,10},{11,19},{19,11},{12,20... | collective-permute-start | bytes 516104 | tf_op jit(solution)/shard_map/ppermute | solution.py:28
  16.8 5.1 %collective-permute-start.6 = (f32[64,896]{1,0:T(8,128)S(1)}, f32[64,896]{1,0:T(8,128)S(1)}, u32[]{:S(2)}, u32[]{:S(2)}) collective-permute-start(f32[64,896]{1,0:T(8,128)S(1)} %pad_maximum_fusion.1), channel_id=1, source_target_pairs={{0,8},{1,9},{2,10},{3,11},{4,12},{5,13},{6,14},{7,15},{8,0},{9,1},... | collective-permute-start | bytes 688136 | tf_op jit(solution)/shard_map/ppermute | solution.py:41
  17.3 15.9 %copy-start.4 = (f32[24,56]{1,0:T(8,128)S(1)}, f32[24,56]{1,0:T(8,128)}, u32[]{:S(2)}) copy-start(f32[24,56]{1,0:T(8,128)} %param.6) | copy-start | bytes 16132
  17.5 5.5 %collective-permute-start.2 = (bf16[32,4,384]{2,1,0:T(4,128)(2,1)S(1)}, bf16[32,4,384]{2,1,0:T(4,128)(2,1)S(1)}, u32[]{:S(2)}, u32[]{:S(2)}) collective-permute-start(bf16[32,4,384]{2,1,0:T(4,128)(2,1)S(1)} %get-tuple-element.55), channel_id=1, source_target_pairs={{1,2},{3,4},{5,6},{2,1},{4,3},{6,5},{9,10},{11,12},{13,14},{10,9},... | collective-permute-start | bytes 294920 | tf_op jit(solution)/shard_map/ppermute | solution.py:28
  18.1 15.3 %copy-start.2 = (f32[24,56,384]{2,1,0:T(8,128)S(1)}, f32[24,56,384]{2,1,0:T(8,128)}, u32[]{:S(2)}) copy-start(f32[24,56,384]{2,1,0:T(8,128)} %rhs_ref.1) | copy-start | bytes 6193156
  18.1 6.8 %collective-permute-start.3 = (bf16[32,4,384]{2,1,0:T(4,128)(2,1)S(1)}, bf16[32,4,384]{2,1,0:T(4,128)(2,1)S(1)}, u32[]{:S(2)}, u32[]{:S(2)}) collective-permute-start(bf16[32,4,384]{2,1,0:T(4,128)(2,1)S(1)} %get-tuple-element.56), channel_id=1, source_target_pairs={{0,1},{2,3},{4,5},{6,7},{1,0},{3,2},{5,4},{7,6},{8,9},{10,11},{12,... | collective-permute-start | bytes 294920 | tf_op jit(solution)/shard_map/ppermute | solution.py:27
  22.9 4.4 %collective-permute-start.7 = (f32[32,384]{1,0:T(8,128)S(1)}, f32[32,384]{1,0:T(8,128)S(1)}, u32[]{:S(2)}, u32[]{:S(2)}) collective-permute-start(f32[32,384]{1,0:T(8,128)S(1)} %pad_maximum_fusion.6), channel_id=1, source_target_pairs={{0,1},{1,0},{2,3},{3,2},{4,5},{5,4},{6,7},{7,6},{8,9},{9,8},{10,11... | collective-permute-start | bytes 147464 | tf_op jit(solution)/shard_map/ppermute | solution.py:41
  27.3 5.9 %collective-permute-start.8 = (f32[16,384]{1,0:T(8,128)S(1)}, f32[16,384]{1,0:T(8,128)S(1)}, u32[]{:S(2)}, u32[]{:S(2)}) collective-permute-start(f32[16,384]{1,0:T(8,128)S(1)} %slice_add_fusion.2), channel_id=1, source_target_pairs={{0,16},{1,17},{2,18},{3,19},{4,20},{5,21},{6,22},{7,23},{8,24},{9,... | collective-permute-start | bytes 73736 | tf_op jit(solution)/shard_map/ppermute | solution.py:41
  33.5 3.4 %copy-start = (bf16[2048,2048]{1,0:T(8,128)(2,1)S(1)}, bf16[2048,2048]{1,0:T(8,128)(2,1)}, u32[]{:S(2)}) copy-start(bf16[2048,2048]{1,0:T(8,128)(2,1)} %inverse_ref.3) | copy-start | bytes 25165828
  43.4 4.2 %collective-permute-start.12 = (f32[6,4,512]{2,1,0:T(4,128)S(1)}, f32[6,4,512]{2,1,0:T(4,128)S(1)}, u32[]{:S(2)}, u32[]{:S(2)}) collective-permute-start(f32[6,4,512]{2,1,0:T(4,128)S(1)} %bitcast.37), channel_id=1, source_target_pairs={{0,1},{2,3},{4,5},{6,7},{1,0},{3,2},{5,4},{7,6},{8,9},{10,11},{12,... | collective-permute-start | bytes 147464 | tf_op jit(solution)/shard_map/ppermute | solution.py:27
  44.6 3.0 %collective-permute-start.11 = (f32[6,4,512]{2,1,0:T(4,128)S(1)}, f32[6,4,512]{2,1,0:T(4,128)S(1)}, u32[]{:S(2)}, u32[]{:S(2)}) collective-permute-start(f32[6,4,512]{2,1,0:T(4,128)S(1)} %bitcast.36), channel_id=1, source_target_pairs={{1,2},{3,4},{5,6},{2,1},{4,3},{6,5},{9,10},{11,12},{13,14},{10,9},... | collective-permute-start | bytes 147464 | tf_op jit(solution)/shard_map/ppermute | solution.py:28
  45.3 2.3 %collective-permute-start.10 = (f32[1,56,512]{2,1,0:T(8,128)S(1)}, f32[1,56,512]{2,1,0:T(8,128)S(1)}, u32[]{:S(2)}, u32[]{:S(2)}) collective-permute-start(f32[1,56,512]{2,1,0:T(8,128)S(1)} %get-tuple-element.47), channel_id=1, source_target_pairs={{0,8},{16,24},{8,0},{24,16},{1,9},{17,25},{9,1},{25,17},{2,10},{18... | collective-permute-start | bytes 344072 | tf_op jit(solution)/shard_map/ppermute | solution.py:27
  45.4 2.2 %collective-permute-start.9 = (f32[1,56,512]{2,1,0:T(8,128)S(1)}, f32[1,56,512]{2,1,0:T(8,128)S(1)}, u32[]{:S(2)}, u32[]{:S(2)}) collective-permute-start(f32[1,56,512]{2,1,0:T(8,128)S(1)} %get-tuple-element.48), channel_id=1, source_target_pairs={{8,16},{16,8},{9,17},{17,9},{10,18},{18,10},{11,19},{19,11},{12,20... | collective-permute-start | bytes 344072 | tf_op jit(solution)/shard_map/ppermute | solution.py:28
  47.7 37.3 %slice-start = ((s8[8388608]{0:T(1024)(128)(4,1)}), s8[4194304]{0:T(1024)(128)(4,1)S(1)}, s32[]{:S(2)}) async-start(s8[8388608]{0:T(1024)(128)(4,1)} %bitcast.17), calls=%async_computation | async-start | bytes 8388608
  47.7 37.3 %slice-start.1 = ((s8[8388608]{0:T(1024)(128)(4,1)}), s8[4194304]{0:T(1024)(128)(4,1)S(1)}, s32[]{:S(2)}) async-start(s8[8388608]{0:T(1024)(128)(4,1)} %bitcast.17), calls=%async_computation.1 | async-start | bytes 8388608
  52.0 8.1 %collective-permute-start.17 = (f32[16,384]{1,0:T(8,128)S(1)}, f32[16,384]{1,0:T(8,128)S(1)}, u32[]{:S(2)}, u32[]{:S(2)}) collective-permute-start(f32[16,384]{1,0:T(8,128)S(1)} %get-tuple-element.32), channel_id=1, source_target_pairs={{0,4},{1,5},{2,6},{3,7},{4,0},{5,1},{6,2},{7,3},{8,12},{9,13},{10,... | collective-permute-start | bytes 73736 | tf_op jit(solution)/shard_map/ppermute | solution.py:41
  60.1 4.3 %collective-permute-start.18 = (f32[32,384]{1,0:T(8,128)S(1)}, f32[32,384]{1,0:T(8,128)S(1)}, u32[]{:S(2)}, u32[]{:S(2)}) collective-permute-start(f32[32,384]{1,0:T(8,128)S(1)} %pad_maximum_fusion.7), channel_id=1, source_target_pairs={{0,2},{1,3},{2,0},{3,1},{4,6},{5,7},{6,4},{7,5},{8,10},{9,11},{10,... | collective-permute-start | bytes 147464 | tf_op jit(solution)/shard_map/ppermute | solution.py:41
  64.5 2.7 %collective-permute-start.19 = (f32[64,384]{1,0:T(8,128)S(1)}, f32[64,384]{1,0:T(8,128)S(1)}, u32[]{:S(2)}, u32[]{:S(2)}) collective-permute-start(f32[64,384]{1,0:T(8,128)S(1)} %pad_maximum_fusion.5), channel_id=1, source_target_pairs={{0,8},{1,9},{2,10},{3,11},{4,12},{5,13},{6,14},{7,15},{8,0},{9,1},... | collective-permute-start | bytes 294920 | tf_op jit(solution)/shard_map/ppermute | solution.py:41
  66.3 3.2 %collective-permute-start.14 = (bf16[4,56,384]{2,1,0:T(8,128)(2,1)S(1)}, bf16[4,56,384]{2,1,0:T(8,128)(2,1)S(1)}, u32[]{:S(2)}, u32[]{:S(2)}) collective-permute-start(bf16[4,56,384]{2,1,0:T(8,128)(2,1)S(1)} %get-tuple-element.39), channel_id=1, source_target_pairs={{0,8},{16,24},{8,0},{24,16},{1,9},{17,25},{9,1},{25,17},{2,10},{18... | collective-permute-start | bytes 516104 | tf_op jit(solution)/shard_map/ppermute | solution.py:27
  66.4 3.2 %collective-permute-start.13 = (bf16[4,56,384]{2,1,0:T(8,128)(2,1)S(1)}, bf16[4,56,384]{2,1,0:T(8,128)(2,1)S(1)}, u32[]{:S(2)}, u32[]{:S(2)}) collective-permute-start(bf16[4,56,384]{2,1,0:T(8,128)(2,1)S(1)} %get-tuple-element.40), channel_id=1, source_target_pairs={{8,16},{16,8},{9,17},{17,9},{10,18},{18,10},{11,19},{19,11},{12,20... | collective-permute-start | bytes 516104 | tf_op jit(solution)/shard_map/ppermute | solution.py:28
  68.1 4.2 %collective-permute-start.20 = (f32[32,384]{1,0:T(8,128)S(1)}, f32[32,384]{1,0:T(8,128)S(1)}, u32[]{:S(2)}, u32[]{:S(2)}) collective-permute-start(f32[32,384]{1,0:T(8,128)S(1)} %pad_maximum_fusion.8), channel_id=1, source_target_pairs={{0,1},{1,0},{2,3},{3,2},{4,5},{5,4},{6,7},{7,6},{8,9},{9,8},{10,11... | collective-permute-start | bytes 147464 | tf_op jit(solution)/shard_map/ppermute | solution.py:41
  72.2 9.4 %collective-permute-start.21 = (f32[16,384]{1,0:T(8,128)S(1)}, f32[16,384]{1,0:T(8,128)S(1)}, u32[]{:S(2)}, u32[]{:S(2)}) collective-permute-start(f32[16,384]{1,0:T(8,128)S(1)} %slice_add_fusion), channel_id=1, source_target_pairs={{0,16},{1,17},{2,18},{3,19},{4,20},{5,21},{6,22},{7,23},{8,24},{9,... | collective-permute-start | bytes 73736 | tf_op jit(solution)/shard_map/ppermute | solution.py:41
  77.7 4.0 %collective-permute-start.15 = (bf16[32,4,384]{2,1,0:T(4,128)(2,1)S(1)}, bf16[32,4,384]{2,1,0:T(4,128)(2,1)S(1)}, u32[]{:S(2)}, u32[]{:S(2)}) collective-permute-start(bf16[32,4,384]{2,1,0:T(4,128)(2,1)S(1)} %get-tuple-element.51), channel_id=1, source_target_pairs={{1,2},{3,4},{5,6},{2,1},{4,3},{6,5},{9,10},{11,12},{13,14},{10,9},... | collective-permute-start | bytes 294920 | tf_op jit(solution)/shard_map/ppermute | solution.py:28
  78.4 6.5 %collective-permute-start.16 = (bf16[32,4,384]{2,1,0:T(4,128)(2,1)S(1)}, bf16[32,4,384]{2,1,0:T(4,128)(2,1)S(1)}, u32[]{:S(2)}, u32[]{:S(2)}) collective-permute-start(bf16[32,4,384]{2,1,0:T(4,128)(2,1)S(1)} %get-tuple-element.52), channel_id=1, source_target_pairs={{0,1},{2,3},{4,5},{6,7},{1,0},{3,2},{5,4},{7,6},{8,9},{10,11},{12,... | collective-permute-start | bytes 294920 | tf_op jit(solution)/shard_map/ppermute | solution.py:27

commit v3 on v1

v3 whole, which is shorter than its diff:
```python
import functools

import jax
import jax.numpy as jnp
from jax import lax
from jax.experimental import pallas as pl
from jax.experimental.pallas import tpu as pltpu
from jax.sharding import PartitionSpec as P

OV = 4
ITERS = 2
LANES = 128
AXES = ("grp", "mem")
EXACT = lax.Precision.HIGHEST
F32 = jnp.float32
BF16 = jnp.bfloat16


def neighbour_pairs(count, first):
    pairs = [(i, i + 1) for i in range(first, count - 1, 2)]
    return pairs + [(j, i) for i, j in pairs]


def edges(low_edge, high_edge, axis):
    count = lax.axis_size(axis)
    even = lax.axis_index(axis) % 2 == 0
    first = lax.ppermute(jnp.where(even, high_edge, low_edge), axis, neighbour_pairs(count, 0))
    second = lax.ppermute(jnp.where(even, low_edge, high_edge), axis, neighbour_pairs(count, 1))
    return jnp.where(even, second, first), jnp.where(even, first, second)


def masks():
    members, groups = lax.axis_size("mem"), lax.axis_size("grp")
    mem_bits = [1 << k for k in range(members.bit_length() - 1)]
    grp_bits = [members << k for k in range(groups.bit_length() - 1)]
    return mem_bits[:0:-1] + grp_bits[:1], mem_bits[:1] + grp_bits[1:]


def swap(value, bit):
    total = lax.axis_size("grp") * lax.axis_size("mem")
    return lax.ppermute(value, AXES, [(i, i ^ bit) for i in range(total)])


def gathered(value, bits):
    for bit in bits:
        value = jnp.concatenate([value, swap(value, bit)], axis=0)
    return value


def summed_shares(inverse_rows, sources, modes):
    shares = lax.dot_general(
        inverse_rows,
        sources,
        (((0,), (0,)), ((), ())),
        precision=EXACT,
        preferred_element_type=F32,
    )
    sum_bits = masks()[1]
    me = lax.axis_index(AXES)
    targets = [0]
    for bit in sum_bits[::-1]:
        targets = targets + [t ^ bit for t in targets]
    parts = [
        lax.dynamic_slice_in_dim(shares, (me ^ target) * modes, modes, 0) for target in targets
    ]
    for bit in sum_bits:
        half = len(parts) // 2
        got = swap(jnp.concatenate(parts[half:], axis=0), bit)
        parts = [part + got[k * modes : (k + 1) * modes] for k, part in enumerate(parts[:half])]
    return parts[0]


def split(values):
    high = values.astype(BF16)
    rest = values - high.astype(F32)
    middle = rest.astype(BF16)
    return high, middle, (rest - middle.astype(F32)).astype(BF16)


def product(a, b):
    return jnp.dot(a, b, preferred_element_type=F32)


def modes_of(basis_ref, first, rows):
    return split(jnp.concatenate([basis_ref[first + k] for k in range(rows)], axis=1))


def restrict(basis_ref, first, block):
    rows, own_y, columns = block.shape
    high, middle, low = modes_of(basis_ref, first, rows)
    modes = high.shape[0]
    block_high, block_middle, block_low = split(block.reshape(rows * own_y, columns))
    three = product(jnp.concatenate([high, middle, low], axis=0), block_high)
    two = product(jnp.concatenate([high, middle], axis=0), block_middle)
    one = product(high, block_low)
    return one + (two[modes:] + three[2 * modes :]) + (two[:modes] + three[modes : 2 * modes]) + three[:modes]


def survey(block, basis_ref, first, low_ref, high_ref, side_ref):
    rows, own_y, columns = block.shape
    if first == 0:
        low_ref[...] = block[:OV].astype(BF16)
    if first + rows == side_ref.shape[0]:
        high_ref[...] = block[rows - OV :].astype(BF16)
    left = lax.broadcasted_iota(jnp.int32, (rows, 2 * OV, columns), 1) < OV
    side_ref[first : first + rows] = jnp.where(
        left, block[:, : 2 * OV], block[:, own_y - 2 * OV :]
    ).astype(BF16)
    return restrict(basis_ref, first, block)


def start_kernel(rhs_ref, basis_ref, low_ref, high_ref, side_ref, sum_ref, held, arrived):
    own_x = held.shape[0]
    copies = [
        pltpu.make_async_copy(
            rhs_ref.at[pl.ds(first, OV)], held.at[pl.ds(first, OV)], arrived.at[first // OV]
        )
        for first in range(0, own_x, OV)
    ]
    for copy in copies:
        copy.start()
    total = jnp.zeros(sum_ref.shape, F32)
    for first in range(0, own_x, OV):
        copies[first // OV].wait()
        block = held[first : first + OV]
        total = total + survey(block, basis_ref, first, low_ref, high_ref, side_ref)
    sum_ref[...] = total


def residual_kernel(
    rhs_ref,
    now_ref,
    below_ref,
    above_ref,
    left_ref,
    right_ref,
    heat_ref,
    basis_ref,
    out_ref,
    low_ref,
    high_ref,
    side_ref,
    sum_ref,
):
    own_x, own_y, columns = now_ref.shape
    place = lax.broadcasted_iota(jnp.int32, (own_y, columns), 0)
    place_heat = place[:, :LANES]

    def flux(values, heat, other, other_heat):
        face = 0.5 * (heat + other_heat)
        return jnp.concatenate([face] * (columns // LANES), axis=1) * (values - other)

    def parts(row):
        return row[:, :columns], row[:, columns:]

    here, heat = now_ref[0], heat_ref[0]
    before = flux(*parts(below_ref[0]), here, heat)
    total = jnp.zeros(sum_ref.shape, F32)
    for index in range(own_x):
        if index + 1 < own_x:
            after, after_heat = now_ref[index + 1], heat_ref[index + 1]
        else:
            after, after_heat = parts(above_ref[0])
        across = flux(here, heat, after, after_heat)
        right, right_heat = parts(right_ref[index // OV, index % OV : index % OV + 1])
        left, left_heat = parts(left_ref[index // OV, index % OV : index % OV + 1])
        right = jnp.where(place == own_y - 1, right, pltpu.roll(here, own_y - 1, 0))
        right_heat = jnp.where(place_heat == own_y - 1, right_heat, pltpu.roll(heat, own_y - 1, 0))
        along = flux(here, heat, right, right_heat)
        entering = jnp.where(
            place == 0, flux(left, left_heat, here[:1], heat[:1]), pltpu.roll(along, 1, 0)
        )
        out_ref[index] = rhs_ref[index] - ((across - before) + (along - entering))
        here, heat, before = after, after_heat, across
        if index % OV == OV - 1:
            first = index + 1 - OV
            block = out_ref[first : first + OV]
            total = total + survey(block, basis_ref, first, low_ref, high_ref, side_ref)
    sum_ref[...] = total


def fine_kernel(
    last,
    inverse_ref,
    block_ref,
    low_ref,
    high_ref,
    side_ref,
    basis_ref,
    lifted_ref,
    extra_ref,
    out_ref,
    *refs,
):
    if last:
        rows_held, window, wide, solved, arrived, result, left_for = refs
    else:
        first_ref, last_ref, left_ref, right_ref, rows_held, window, wide, solved, arrived = refs
        result = out_ref
    own_x, own_y, columns = block_ref.shape
    span_y = own_y + 2 * OV
    rows = solved.shape[0] // span_y
    copies = []
    for first in range(0, own_x, rows):
        count = rows * span_y
        copies.append(
            pltpu.make_async_copy(
                inverse_ref.at[pl.ds((OV + first) * span_y, count)],
                rows_held.at[pl.ds(first * span_y, count)],
                arrived.at[first // rows],
            )
        )
        copies[-1].start()

    def place(index, values):
        wide[OV : OV + own_y, :] = values
        sides = side_ref[index].astype(F32)
        wide[:OV, :] = sides[:OV]
        wide[OV + own_y :, :] = sides[OV:]
        window[index * span_y : (index + 1) * span_y, :] = wide[...].astype(BF16)

    for index in range(OV):
        place(index, low_ref[index].astype(F32))
        place(OV + own_x + index, high_ref[index].astype(F32))
    for index in range(own_x):
        place(OV + index, block_ref[index])

    high, middle, low = split(lifted_ref[...])
    lifted = jnp.concatenate([high, middle, high, low, middle, high], axis=0)
    sends = []
    for first in range(0, own_x, rows):
        copies[first // rows].wait()
        solved[...] = product(
            rows_held[first * span_y : (first + rows) * span_y, :], window[...]
        )
        high, middle, low = modes_of(basis_ref, first, rows)
        coarse = lax.dot_general(
            jnp.concatenate([high, high, middle, high, middle, low], axis=0),
            lifted,
            (((0,), (0,)), ((), ())),
            preferred_element_type=F32,
        )
        for k in range(rows):
            value = solved[k * span_y + OV : k * span_y + OV + own_y, :]
            value = value + coarse[k * own_y : (k + 1) * own_y]
            if last:
                value = extra_ref[first + k] + value
            result[first + k] = value
        if last:
            sends.append(
                pltpu.make_async_copy(
                    result.at[pl.ds(first, rows)],
                    out_ref.at[pl.ds(first, rows)],
                    left_for.at[first // rows],
                )
            )
            sends[-1].start()
        else:
            for index in range(first, first + rows):
                for ref, at in ((left_ref, 0), (right_ref, own_y - 1)):
                    row = pl.ds(index % OV, 1)
                    ref[index // OV, row, :columns] = result[index, at : at + 1]
                    ref[index // OV, row, columns:] = extra_ref[index, at : at + 1]
    for send in sends:
        send.wait()
    if not last:
        first_ref[0] = jnp.concatenate([result[0], extra_ref[0]], axis=1)
        last_ref[0] = jnp.concatenate([result[own_x - 1], extra_ref[own_x - 1]], axis=1)


def shape_of(shape, kind):
    return jax.ShapeDtypeStruct(shape, kind)


def on_device(rhs, conductivity, local_inverse, coarse_basis, coarse_inverse):
    own_x, own_y, columns = rhs.shape
    modes = coarse_basis.shape[2]
    span_x = own_x + 2 * OV
    span_y = own_y + 2 * OV
    local = span_x * span_y
    basis = jnp.transpose(coarse_basis, (0, 2, 1))
    heat = jnp.broadcast_to(conductivity[:, :, None], (own_x, own_y, LANES))
    params = pltpu.CompilerParams(vmem_limit_bytes=40 * 2**20)
    group = 2 * OV if own_x % (2 * OV) == 0 else OV
    in_vmem = pl.BlockSpec(memory_space=pltpu.VMEM)
    in_hbm = pl.BlockSpec(memory_space=pltpu.HBM)

    survey_shapes = [
        shape_of((OV, own_y, columns), BF16),
        shape_of((OV, own_y, columns), BF16),
        shape_of((own_x, 2 * OV, columns), BF16),
        shape_of((modes, columns), F32),
    ]

    def surveyed_start():
        return pl.pallas_call(
            start_kernel,
            in_specs=[in_hbm, in_vmem],
            out_specs=[in_vmem] * 4,
            out_shape=survey_shapes,
            scratch_shapes=[
                pltpu.VMEM(rhs.shape, F32),
                pltpu.SemaphoreType.DMA((own_x // OV,)),
            ],
            compiler_params=params,
        )(rhs, basis)

    def surveyed_residual(now, around):
        return pl.pallas_call(
            residual_kernel,
            in_specs=[in_vmem] * 8,
            out_specs=[in_vmem] * 5,
            out_shape=[shape_of(rhs.shape, F32)] + survey_shapes,
            compiler_params=params,
        )(rhs, now, *around, heat, basis)

    def window_margins(low_edge, high_edge, sides):
        low, high = edges(low_edge, high_edge, "grp")
        corners = [jnp.concatenate([m[:, :OV], m[:, -OV:]], axis=1) for m in (low, high)]
        sides = jnp.concatenate([corners[0], sides, corners[1]], axis=0)
        left, right = edges(sides[:, :OV], sides[:, OV:], "mem")
        return low, high, jnp.concatenate([left, right], axis=1)

    def improved(values, margins, lifted, now):
        last = now is not None
        edge = columns + LANES
        out_shape = [shape_of(rhs.shape, F32)]
        scratch = [
            pltpu.VMEM((own_x * span_y, local), BF16),
            pltpu.VMEM((local, columns), BF16),
            pltpu.VMEM((span_y, columns), F32),
            pltpu.VMEM((group * span_y, columns), F32),
            pltpu.SemaphoreType.DMA((own_x // group,)),
        ]
        if last:
            out_specs = [in_hbm]
            scratch += [pltpu.VMEM(rhs.shape, F32), pltpu.SemaphoreType.DMA((own_x // group,))]
        else:
            out_specs = [in_vmem] * 5
            out_shape += [shape_of((1, own_y, edge), F32)] * 2
            out_shape += [shape_of((own_x // OV, OV, edge), F32)] * 2
        return pl.pallas_call(
            functools.partial(fine_kernel, last),
            in_specs=[in_hbm] + [in_vmem] * 7,
            out_specs=out_specs,
            out_shape=out_shape,
            scratch_shapes=scratch,
            compiler_params=params,
        )(local_inverse, values, *margins, basis, lifted, now if last else heat)

    gather_bits = masks()[0]
    *to_send, restricted = surveyed_start()
    sources = gathered(jnp.concatenate([restricted, coarse_inverse], axis=1), gather_bits)
    inverse_rows = sources[:, columns:]
    margins = window_margins(*to_send)
    lifted = summed_shares(inverse_rows, sources[:, :columns], modes)
    now, first, final, left, right = improved(rhs, margins, lifted, None)
    for sweep in range(ITERS - 1):
        around = edges(first, final, "grp") + edges(left, right, "mem")
        residual, *to_send, restricted = surveyed_residual(now, around)
        sources = gathered(restricted, gather_bits)
        margins = window_margins(*to_send)
        lifted = summed_shares(inverse_rows, sources, modes)
        now = improved(residual, margins, lifted, now)[0]
    return now


def solution(mesh):
    placed = (
        P("grp", "mem", None),
        P("grp", "mem"),
        P(("grp", "mem"), None),
        P("grp", "mem", None),
        P(("grp", "mem"), None),
    )
    return jax.shard_map(
        on_device, mesh=mesh, in_specs=placed, out_specs=P("grp", "mem", None), check_vma=False
    )
```

time: 106 us -> 88.5 us (0.83); the launches traced: 104 us -> 88.1 us
  other arithmetic: 19.7 us -> 0.9 us
  matrix products: 19 us -> 1.65 us
  Pallas kernels: 0 us -> 14.6 us
  waiting for transfers between devices: 12.1 us -> 22.6 us
  starting transfers between devices: 44.5 us -> 39.9 us
    dot_general x8 -> x2, matrix products: 19 us -> 1.65 us  [summed_shares(): lax.dot_general(inverse_rows, sources, (((0,), (0,)), ((), ())), precisio...]
    pallas_call x0 -> x4, Pallas kernels: none -> 14.6 us  [the longest x2 11 us: improved(): pl.pallas_call(functools.partial(fine_kernel, last), in_specs=[in_hbm] +...]
    ppermute x8 -> x6, starting transfers between devices: 19.2 us -> 8.51 us  [edges(): lax.ppermute(jnp.where(even, high_edge, low_edge), axis, neighbour_pairs(...]
    ppermute x13 -> x10, starting transfers between devices: 18.5 us -> 27.2 us  [swap(): return lax.ppermute(value, AXES, [(i, i ^ bit) for i in range(total)])]
    ppermute x8 -> x6, waiting for transfers between devices: 0.42 us -> 6.65 us  [edges(): lax.ppermute(jnp.where(even, high_edge, low_edge), axis, neighbour_pairs(...]
    add x4, other arithmetic: 6.06 us -> 0.02 us  [summed_shares(): part + got[k * modes:(k + 1) * modes]]
    dot_general x2 -> x0, local copies, waits for them, and re-layouts: 5.08 us -> none  [fine(): jnp.dot(owned_inverse, extended.reshape(span_x * span_y, columns), prefer...]
    unnamed x20 -> x21, local copies, waits for them, and re-layouts: 2.6 us -> 7.5 us
  transfers between devices with their start and end apart: 29 -> 22, of which waited for: 9 -> 11; matrix products, arithmetic and copies ran while one was open for 23% -> 3% of each run, Pallas kernels for 0% -> 0%
where the time goes in v3:
time: 88.5 us; the launch traced here: 88.1 us
  starting transfers between devices  39.9 us (45%)
  waiting for transfers between devices  22.6 us (26%)
  Pallas kernels  14.6 us (16%)
  local copies, waits for them, and re-layouts  7.81 us (9%)
  matrix products  1.65 us (2%)
  other arithmetic  0.9 us (1%)
    ppermute x10, starting transfers between devices, swap(): return lax.ppermute(value, AXES, [(i, i ^ bit) for i in range(total)])  27.2 us
    ppermute x10, waiting for transfers between devices, swap(): return lax.ppermute(value, AXES, [(i, i ^ bit) for i in range(total)])  16 us
    pallas_call x2, Pallas kernels, improved(): pl.pallas_call(functools.partial(fine_kernel, last), in_specs=[in_hbm] +...  11 us
    ppermute x6, starting transfers between devices, edges(): lax.ppermute(jnp.where(even, high_edge, low_edge), axis, neighbour_pairs(...  8.51 us
    unnamed x21, local copies, waits for them, and re-layouts  7.5 us
    ppermute x6, waiting for transfers between devices, edges(): lax.ppermute(jnp.where(even, high_edge, low_edge), axis, neighbour_pairs(...  6.65 us
    ppermute x6, starting transfers between devices, edges(): lax.ppermute(jnp.where(even, low_edge, high_edge), axis, neighbour_pairs(...  4.17 us
    pallas_call x1, Pallas kernels, surveyed_residual(): pl.pallas_call(residual_kernel, in_specs=[in_vmem] * 8, out_specs=[in_vme...  1.87 us
  transfers between devices with their start and end apart: 22, of which 11 were waited for; matrix products, arithmetic and copies ran while one was open for 3% of the time, Pallas kernels for 0%

profile of v3, /device:TPU:0, one launch (start us, length us, event | category | flops | bytes accessed | tf_op | source)
XLA Modules:
  0.0 88.1 jit_solution(13504030663622120014)
XLA Ops:
  0.0 1.6 %copy-done.2 = f32[24,56,384]{2,1,0:T(8,128)S(1)} copy-done((f32[24,56,384]{2,1,0:T(8,128)S(1)}, f32[24,56,384]{2,1,0:T(8,128)}, u32[]{:S(2)}) %copy-start.2) | copy-done | bytes 2064408
  1.6 0.9 %copy-done.6 = f32[24,56,16]{1,2,0:T(8,128)S(1)} copy-done((f32[24,56,16]{1,2,0:T(8,128)S(1)}, f32[24,56,16]{1,2,0:T(8,128)}, u32[]{:S(2)}) %copy-start.6) | copy-done | bytes 86040
  2.5 1.8 %shard_map.55 = (bf16[4,56,384]{2,1,0:T(8,128)(2,1)S(1)}, bf16[4,56,384]{2,1,0:T(8,128)(2,1)S(1)}, bf16[24,8,384]{2,1,0:T(8,128)(2,1)S(1)}, f32[16,384]{1,0:T(8,128)S(1)}) custom-call(f32[24,56,384]{2,1,0:T(8,128)S(1)} %copy-done.2, f32[24,16,56]{2,1,0:T(8,128)S(1)} %bitcast.17), custom_call_target="tpu_custom_call" | custom-call | tf_op jit(solution)/shard_map/pallas_call | solution.py:296
  4.4 4.1 %collective-permute-start.4 = (f32[16,896]{1,0:T(8,128)S(1)}, f32[16,896]{1,0:T(8,128)S(1)}, u32[]{:S(2)}, u32[]{:S(2)}) collective-permute-start(f32[16,896]{1,0:T(8,128)S(1)} %constant_dynamic-update-slice_fusion), channel_id=1, source_target_pairs={{0,4},{1,5},{2,6},{3,7},{4,0},{5,1},{6,2},{7,3},{8,12},{9,13},{10,... | collective-permute-start | bytes 172040 | tf_op jit(solution)/shard_map/ppermute | solution.py:41
  8.5 2.8 %collective-permute-done.4 = f32[16,896]{1,0:T(8,128)S(1)} collective-permute-done((f32[16,896]{1,0:T(8,128)S(1)}, f32[16,896]{1,0:T(8,128)S(1)}, u32[]{:S(2)}, u32[]{:S(2)}) %collective-permute-start.4) | collective-permute-done | bytes 57376 | tf_op jit(solution)/shard_map/ppermute | solution.py:41
  11.2 1.4 %collective-permute-start.5 = (f32[32,896]{1,0:T(8,128)S(1)}, f32[32,896]{1,0:T(8,128)S(1)}, u32[]{:S(2)}, u32[]{:S(2)}) collective-permute-start(f32[32,896]{1,0:T(8,128)S(1)} %pad_maximum_fusion.4), channel_id=1, source_target_pairs={{0,2},{1,3},{2,0},{3,1},{4,6},{5,7},{6,4},{7,5},{8,10},{9,11},{10,... | collective-permute-start | bytes 344072 | tf_op jit(solution)/shard_map/ppermute | solution.py:41
  13.4 2.7 %collective-permute-done.5 = f32[32,896]{1,0:T(8,128)S(1)} collective-permute-done((f32[32,896]{1,0:T(8,128)S(1)}, f32[32,896]{1,0:T(8,128)S(1)}, u32[]{:S(2)}, u32[]{:S(2)}) %collective-permute-start.5) | collective-permute-done | bytes 114720 | tf_op jit(solution)/shard_map/ppermute | solution.py:41
  17.4 3.8 %collective-permute-start.3 = (bf16[32,4,384]{2,1,0:T(4,128)(2,1)S(1)}, bf16[32,4,384]{2,1,0:T(4,128)(2,1)S(1)}, u32[]{:S(2)}, u32[]{:S(2)}) collective-permute-start(bf16[32,4,384]{2,1,0:T(4,128)(2,1)S(1)} %get-tuple-element.56), channel_id=1, source_target_pairs={{0,1},{2,3},{4,5},{6,7},{1,0},{3,2},{5,4},{7,6},{8,9},{10,11},{12,... | collective-permute-start | bytes 294920 | tf_op jit(solution)/shard_map/ppermute | solution.py:27
  21.3 0.8 fusion.2
  22.2 2.0 %collective-permute-done.3 = bf16[32,4,384]{2,1,0:T(4,128)(2,1)S(1)} collective-permute-done((bf16[32,4,384]{2,1,0:T(4,128)(2,1)S(1)}, bf16[32,4,384]{2,1,0:T(4,128)(2,1)S(1)}, u32[]{:S(2)}, u32[]{:S(2)}) %collective-permute-start.3) | collective-permute-done | bytes 98336 | tf_op jit(solution)/shard_map/ppermute | solution.py:27
  24.3 2.3 %collective-permute-done.7 = f32[32,384]{1,0:T(8,128)S(1)} collective-permute-done((f32[32,384]{1,0:T(8,128)S(1)}, f32[32,384]{1,0:T(8,128)S(1)}, u32[]{:S(2)}, u32[]{:S(2)}) %collective-permute-start.7) | collective-permute-done | bytes 49184 | tf_op jit(solution)/shard_map/ppermute | solution.py:41
  26.6 4.1 %collective-permute-start.8 = (f32[16,384]{1,0:T(8,128)S(1)}, f32[16,384]{1,0:T(8,128)S(1)}, u32[]{:S(2)}, u32[]{:S(2)}) collective-permute-start(f32[16,384]{1,0:T(8,128)S(1)} %slice_add_fusion.2), channel_id=1, source_target_pairs={{0,16},{1,17},{2,18},{3,19},{4,20},{5,21},{6,22},{7,23},{8,24},{9,... | collective-permute-start | bytes 73736 | tf_op jit(solution)/shard_map/ppermute | solution.py:41
  30.8 1.7 %collective-permute-done.8 = f32[16,384]{1,0:T(8,128)S(1)} collective-permute-done((f32[16,384]{1,0:T(8,128)S(1)}, f32[16,384]{1,0:T(8,128)S(1)}, u32[]{:S(2)}, u32[]{:S(2)}) %collective-permute-start.8) | collective-permute-done | bytes 24608 | tf_op jit(solution)/shard_map/ppermute | solution.py:41
  32.8 3.4 %copy-done = bf16[2048,2048]{1,0:T(8,128)(2,1)S(1)} copy-done((bf16[2048,2048]{1,0:T(8,128)(2,1)S(1)}, bf16[2048,2048]{1,0:T(8,128)(2,1)}, u32[]{:S(2)}) %copy-start) | copy-done | bytes 8388632
  36.2 5.1 %shard_map.56 = (f32[24,56,384]{2,1,0:T(8,128)S(1)}, f32[1,56,512]{2,1,0:T(8,128)S(1)}, f32[1,56,512]{2,1,0:T(8,128)S(1)}, f32[6,4,512]{2,1,0:T(4,128)S(1)}, f32[6,4,512]{2,1,0:T(4,128)S(1)}) custom-call(bf16[2048,2048]{1,0:T(8,128)(2,1)S(1)} %copy-done, f32[24,56,384]{2,1,0:T(8,128)S(1)} %copy-done.3, bf16[4,56,384]{2,1,0:T(8,128)(2,1)S(1)} %get-tuple-element.42.low_ref, ...), custom_call_target="tpu_custom_call" | custom-call | tf_op jit(solution)/shard_map/pallas_call | solution.py:342
  41.3 1.2 %collective-permute-start.12 = (f32[6,4,512]{2,1,0:T(4,128)S(1)}, f32[6,4,512]{2,1,0:T(4,128)S(1)}, u32[]{:S(2)}, u32[]{:S(2)}) collective-permute-start(f32[6,4,512]{2,1,0:T(4,128)S(1)} %bitcast.35), channel_id=1, source_target_pairs={{0,1},{2,3},{4,5},{6,7},{1,0},{3,2},{5,4},{7,6},{8,9},{10,11},{12,... | collective-permute-start | bytes 147464 | tf_op jit(solution)/shard_map/ppermute | solution.py:27
  43.9 1.5 %collective-permute-done.12 = f32[6,4,512]{2,1,0:T(4,128)S(1)} collective-permute-done((f32[6,4,512]{2,1,0:T(4,128)S(1)}, f32[6,4,512]{2,1,0:T(4,128)S(1)}, u32[]{:S(2)}, u32[]{:S(2)}) %collective-permute-start.12) | collective-permute-done | bytes 49184 | tf_op jit(solution)/shard_map/ppermute | solution.py:27
  45.5 1.9 %shard_map.57 = (f32[24,56,384]{2,1,0:T(8,128)S(1)}, bf16[4,56,384]{2,1,0:T(8,128)(2,1)S(1)}, bf16[4,56,384]{2,1,0:T(8,128)(2,1)S(1)}, bf16[24,8,384]{2,1,0:T(8,128)(2,1)S(1)}, f32[16,384]{1,0:T(8,128)S(1)}) custom-call(f32[24,56,384]{2,1,0:T(8,128)S(1)} %copy-done.3, f32[24,56,384]{2,1,0:T(8,128)S(1)} %get-tuple-element.23.now_ref.extra_ref, ...), custom_call_target="tpu_custom_call" | custom-call | tf_op jit(solution)/shard_map/pallas_call | solution.py:309
  47.4 6.3 %collective-permute-start.17 = (f32[16,384]{1,0:T(8,128)S(1)}, f32[16,384]{1,0:T(8,128)S(1)}, u32[]{:S(2)}, u32[]{:S(2)}) collective-permute-start(f32[16,384]{1,0:T(8,128)S(1)} %get-tuple-element.32), channel_id=1, source_target_pairs={{0,4},{1,5},{2,6},{3,7},{4,0},{5,1},{6,2},{7,3},{8,12},{9,13},{10,... | collective-permute-start | bytes 73736 | tf_op jit(solution)/shard_map/ppermute | solution.py:41
  53.7 1.8 %collective-permute-done.17 = f32[16,384]{1,0:T(8,128)S(1)} collective-permute-done((f32[16,384]{1,0:T(8,128)S(1)}, f32[16,384]{1,0:T(8,128)S(1)}, u32[]{:S(2)}, u32[]{:S(2)}) %collective-permute-start.17) | collective-permute-done | bytes 24608 | tf_op jit(solution)/shard_map/ppermute | solution.py:41
  55.5 2.3 %collective-permute-start.18 = (f32[32,384]{1,0:T(8,128)S(1)}, f32[32,384]{1,0:T(8,128)S(1)}, u32[]{:S(2)}, u32[]{:S(2)}) collective-permute-start(f32[32,384]{1,0:T(8,128)S(1)} %pad_maximum_fusion.7), channel_id=1, source_target_pairs={{0,2},{1,3},{2,0},{3,1},{4,6},{5,7},{6,4},{7,5},{8,10},{9,11},{10,... | collective-permute-start | bytes 147464 | tf_op jit(solution)/shard_map/ppermute | solution.py:41
  57.8 2.1 %collective-permute-done.18 = f32[32,384]{1,0:T(8,128)S(1)} collective-permute-done((f32[32,384]{1,0:T(8,128)S(1)}, f32[32,384]{1,0:T(8,128)S(1)}, u32[]{:S(2)}, u32[]{:S(2)}) %collective-permute-start.18) | collective-permute-done | bytes 49184 | tf_op jit(solution)/shard_map/ppermute | solution.py:41
  59.8 1.8 %collective-permute-start.19 = (f32[64,384]{1,0:T(8,128)S(1)}, f32[64,384]{1,0:T(8,128)S(1)}, u32[]{:S(2)}, u32[]{:S(2)}) collective-permute-start(f32[64,384]{1,0:T(8,128)S(1)} %pad_maximum_fusion.5), channel_id=1, source_target_pairs={{0,8},{1,9},{2,10},{3,11},{4,12},{5,13},{6,14},{7,15},{8,0},{9,1},... | collective-permute-start | bytes 294920 | tf_op jit(solution)/shard_map/ppermute | solution.py:41
  62.6 0.8 fusion
  63.5 1.5 %collective-permute-start.20 = (f32[32,384]{1,0:T(8,128)S(1)}, f32[32,384]{1,0:T(8,128)S(1)}, u32[]{:S(2)}, u32[]{:S(2)}) collective-permute-start(f32[32,384]{1,0:T(8,128)S(1)} %pad_maximum_fusion.8), channel_id=1, source_target_pairs={{0,1},{1,0},{2,3},{3,2},{4,5},{5,4},{6,7},{7,6},{8,9},{9,8},{10,11... | collective-permute-start | bytes 147464 | tf_op jit(solution)/shard_map/ppermute | solution.py:41
  65.1 2.5 %collective-permute-done.20 = f32[32,384]{1,0:T(8,128)S(1)} collective-permute-done((f32[32,384]{1,0:T(8,128)S(1)}, f32[32,384]{1,0:T(8,128)S(1)}, u32[]{:S(2)}, u32[]{:S(2)}) %collective-permute-start.20) | collective-permute-done | bytes 49184 | tf_op jit(solution)/shard_map/ppermute | solution.py:41
  67.6 5.3 %collective-permute-start.21 = (f32[16,384]{1,0:T(8,128)S(1)}, f32[16,384]{1,0:T(8,128)S(1)}, u32[]{:S(2)}, u32[]{:S(2)}) collective-permute-start(f32[16,384]{1,0:T(8,128)S(1)} %slice_add_fusion), channel_id=1, source_target_pairs={{0,16},{1,17},{2,18},{3,19},{4,20},{5,21},{6,22},{7,23},{8,24},{9,... | collective-permute-start | bytes 73736 | tf_op jit(solution)/shard_map/ppermute | solution.py:41
  73.1 0.8 collective-permute-start.15
  73.9 3.3 %collective-permute-start.16 = (bf16[32,4,384]{2,1,0:T(4,128)(2,1)S(1)}, bf16[32,4,384]{2,1,0:T(4,128)(2,1)S(1)}, u32[]{:S(2)}, u32[]{:S(2)}) collective-permute-start(bf16[32,4,384]{2,1,0:T(4,128)(2,1)S(1)} %get-tuple-element.52), channel_id=1, source_target_pairs={{0,1},{2,3},{4,5},{6,7},{1,0},{3,2},{5,4},{7,6},{8,9},{10,11},{12,... | collective-permute-start | bytes 294920 | tf_op jit(solution)/shard_map/ppermute | solution.py:27
  77.2 3.1 %collective-permute-done.16 = bf16[32,4,384]{2,1,0:T(4,128)(2,1)S(1)} collective-permute-done((bf16[32,4,384]{2,1,0:T(4,128)(2,1)S(1)}, bf16[32,4,384]{2,1,0:T(4,128)(2,1)S(1)}, u32[]{:S(2)}, u32[]{:S(2)}) %collective-permute-start.16) | collective-permute-done | bytes 98336 | tf_op jit(solution)/shard_map/ppermute | solution.py:27
  80.5 1.6 %copy-done.5 = f32[24,56,384]{2,1,0:T(8,128)S(1)} copy-done((f32[24,56,384]{2,1,0:T(8,128)S(1)}, f32[24,56,384]{2,1,0:T(8,128)}, u32[]{:S(2)}) %copy-start.5) | copy-done | bytes 2064408
  82.1 5.9 %shard_map.58 = f32[24,56,384]{2,1,0:T(8,128)} custom-call(bf16[2048,2048]{1,0:T(8,128)(2,1)S(1)} %copy-done.1, f32[24,56,384]{2,1,0:T(8,128)S(1)} %get-tuple-element.28.block_ref, bf16[4,56,384]{2,1,0:T(8,128)(2,1)S(1)} %get-tuple-element.38.low_ref, bf16[4,56,384]{2,1,0:T(8,128)(2,1)S(1)} %get-tuple-element.37.high_ref, ...), custom_call_target="tpu_custom_call" | custom-call | tf_op jit(solution)/shard_map/pallas_call | solution.py:342
  (73 shorter events, 5.4 us)
Async XLA Ops:
  0.0 1.6 %copy-start.2 = (f32[24,56,384]{2,1,0:T(8,128)S(1)}, f32[24,56,384]{2,1,0:T(8,128)}, u32[]{:S(2)}) copy-start(f32[24,56,384]{2,1,0:T(8,128)} %rhs_ref.3) | copy-start | bytes 6193156
  1.6 0.9 %copy-start.6 = (f32[24,56,16]{1,2,0:T(8,128)S(1)}, f32[24,56,16]{1,2,0:T(8,128)}, u32[]{:S(2)}) copy-start(f32[24,56,16]{1,2,0:T(8,128)} %param.8) | copy-start | bytes 258052
  2.5 1.8 %copy-start.8 = (f32[16,512]{1,0:T(8,128)S(1)}, f32[16,512]{1,0:T(8,128)}, u32[]{:S(2)}) copy-start(f32[16,512]{1,0:T(8,128)} %param.9) | copy-start | bytes 98308
  4.4 6.9 %collective-permute-start.4 = (f32[16,896]{1,0:T(8,128)S(1)}, f32[16,896]{1,0:T(8,128)S(1)}, u32[]{:S(2)}, u32[]{:S(2)}) collective-permute-start(f32[16,896]{1,0:T(8,128)S(1)} %constant_dynamic-update-slice_fusion), channel_id=1, source_target_pairs={{0,4},{1,5},{2,6},{3,7},{4,0},{5,1},{6,2},{7,3},{8,12},{9,13},{10,... | collective-permute-start | bytes 172040 | tf_op jit(solution)/shard_map/ppermute | solution.py:41
  11.2 4.9 %collective-permute-start.5 = (f32[32,896]{1,0:T(8,128)S(1)}, f32[32,896]{1,0:T(8,128)S(1)}, u32[]{:S(2)}, u32[]{:S(2)}) collective-permute-start(f32[32,896]{1,0:T(8,128)S(1)} %pad_maximum_fusion.4), channel_id=1, source_target_pairs={{0,2},{1,3},{2,0},{3,1},{4,6},{5,7},{6,4},{7,5},{8,10},{9,11},{10,... | collective-permute-start | bytes 344072 | tf_op jit(solution)/shard_map/ppermute | solution.py:41
  12.6 3.8 %collective-permute-start.1 = (bf16[4,56,384]{2,1,0:T(8,128)(2,1)S(1)}, bf16[4,56,384]{2,1,0:T(8,128)(2,1)S(1)}, u32[]{:S(2)}, u32[]{:S(2)}) collective-permute-start(bf16[4,56,384]{2,1,0:T(8,128)(2,1)S(1)} %get-tuple-element.43), channel_id=1, source_target_pairs={{0,8},{16,24},{8,0},{24,16},{1,9},{17,25},{9,1},{25,17},{2,10},{18... | collective-permute-start | bytes 516104 | tf_op jit(solution)/shard_map/ppermute | solution.py:27
  12.7 3.8 %collective-permute-start = (bf16[4,56,384]{2,1,0:T(8,128)(2,1)S(1)}, bf16[4,56,384]{2,1,0:T(8,128)(2,1)S(1)}, u32[]{:S(2)}, u32[]{:S(2)}) collective-permute-start(bf16[4,56,384]{2,1,0:T(8,128)(2,1)S(1)} %get-tuple-element.44), channel_id=1, source_target_pairs={{8,16},{16,8},{9,17},{17,9},{10,18},{18,10},{11,19},{19,11},{12,20... | collective-permute-start | bytes 516104 | tf_op jit(solution)/shard_map/ppermute | solution.py:28
  16.1 5.1 %collective-permute-start.6 = (f32[64,896]{1,0:T(8,128)S(1)}, f32[64,896]{1,0:T(8,128)S(1)}, u32[]{:S(2)}, u32[]{:S(2)}) collective-permute-start(f32[64,896]{1,0:T(8,128)S(1)} %pad_maximum_fusion.1), channel_id=1, source_target_pairs={{0,8},{1,9},{2,10},{3,11},{4,12},{5,13},{6,14},{7,15},{8,0},{9,1},... | collective-permute-start | bytes 688136 | tf_op jit(solution)/shard_map/ppermute | solution.py:41
  16.6 15.9 %copy-start.9 = (f32[24,56]{1,0:T(8,128)S(1)}, f32[24,56]{1,0:T(8,128)}, u32[]{:S(2)}) copy-start(f32[24,56]{1,0:T(8,128)} %param.6) | copy-start | bytes 16132
  16.7 5.5 %collective-permute-start.2 = (bf16[32,4,384]{2,1,0:T(4,128)(2,1)S(1)}, bf16[32,4,384]{2,1,0:T(4,128)(2,1)S(1)}, u32[]{:S(2)}, u32[]{:S(2)}) collective-permute-start(bf16[32,4,384]{2,1,0:T(4,128)(2,1)S(1)} %get-tuple-element.55), channel_id=1, source_target_pairs={{1,2},{3,4},{5,6},{2,1},{4,3},{6,5},{9,10},{11,12},{13,14},{10,9},... | collective-permute-start | bytes 294920 | tf_op jit(solution)/shard_map/ppermute | solution.py:28
  17.4 15.3 %copy-start.3 = (f32[24,56,384]{2,1,0:T(8,128)S(1)}, f32[24,56,384]{2,1,0:T(8,128)}, u32[]{:S(2)}) copy-start(f32[24,56,384]{2,1,0:T(8,128)} %rhs_ref.3) | copy-start | bytes 6193156
  17.4 15.3 %copy-start.7 = (f32[24,56,16]{1,2,0:T(8,128)S(1)}, f32[24,56,16]{1,2,0:T(8,128)}, u32[]{:S(2)}) copy-start(f32[24,56,16]{1,2,0:T(8,128)} %param.8) | copy-start | bytes 258052
  17.4 6.8 %collective-permute-start.3 = (bf16[32,4,384]{2,1,0:T(4,128)(2,1)S(1)}, bf16[32,4,384]{2,1,0:T(4,128)(2,1)S(1)}, u32[]{:S(2)}, u32[]{:S(2)}) collective-permute-start(bf16[32,4,384]{2,1,0:T(4,128)(2,1)S(1)} %get-tuple-element.56), channel_id=1, source_target_pairs={{0,1},{2,3},{4,5},{6,7},{1,0},{3,2},{5,4},{7,6},{8,9},{10,11},{12,... | collective-permute-start | bytes 294920 | tf_op jit(solution)/shard_map/ppermute | solution.py:27
  22.2 4.4 %collective-permute-start.7 = (f32[32,384]{1,0:T(8,128)S(1)}, f32[32,384]{1,0:T(8,128)S(1)}, u32[]{:S(2)}, u32[]{:S(2)}) collective-permute-start(f32[32,384]{1,0:T(8,128)S(1)} %pad_maximum_fusion.6), channel_id=1, source_target_pairs={{0,1},{1,0},{2,3},{3,2},{4,5},{5,4},{6,7},{7,6},{8,9},{9,8},{10,11... | collective-permute-start | bytes 147464 | tf_op jit(solution)/shard_map/ppermute | solution.py:41
  26.6 5.9 %collective-permute-start.8 = (f32[16,384]{1,0:T(8,128)S(1)}, f32[16,384]{1,0:T(8,128)S(1)}, u32[]{:S(2)}, u32[]{:S(2)}) collective-permute-start(f32[16,384]{1,0:T(8,128)S(1)} %slice_add_fusion.2), channel_id=1, source_target_pairs={{0,16},{1,17},{2,18},{3,19},{4,20},{5,21},{6,22},{7,23},{8,24},{9,... | collective-permute-start | bytes 73736 | tf_op jit(solution)/shard_map/ppermute | solution.py:41
  32.8 3.4 %copy-start = (bf16[2048,2048]{1,0:T(8,128)(2,1)S(1)}, bf16[2048,2048]{1,0:T(8,128)(2,1)}, u32[]{:S(2)}) copy-start(bf16[2048,2048]{1,0:T(8,128)(2,1)} %inverse_ref.3) | copy-start | bytes 25165828
  41.2 6.1 %copy-start.4 = (f32[24,56,384]{2,1,0:T(8,128)}, f32[24,56,384]{2,1,0:T(8,128)S(1)}, u32[]{:S(2)}) copy-start(f32[24,56,384]{2,1,0:T(8,128)S(1)} %get-tuple-element.23.now_ref.extra_ref) | copy-start | bytes 6193156
  41.3 4.2 %collective-permute-start.12 = (f32[6,4,512]{2,1,0:T(4,128)S(1)}, f32[6,4,512]{2,1,0:T(4,128)S(1)}, u32[]{:S(2)}, u32[]{:S(2)}) collective-permute-start(f32[6,4,512]{2,1,0:T(4,128)S(1)} %bitcast.35), channel_id=1, source_target_pairs={{0,1},{2,3},{4,5},{6,7},{1,0},{3,2},{5,4},{7,6},{8,9},{10,11},{12,... | collective-permute-start | bytes 147464 | tf_op jit(solution)/shard_map/ppermute | solution.py:27
  42.5 3.0 %collective-permute-start.11 = (f32[6,4,512]{2,1,0:T(4,128)S(1)}, f32[6,4,512]{2,1,0:T(4,128)S(1)}, u32[]{:S(2)}, u32[]{:S(2)}) collective-permute-start(f32[6,4,512]{2,1,0:T(4,128)S(1)} %bitcast.34), channel_id=1, source_target_pairs={{1,2},{3,4},{5,6},{2,1},{4,3},{6,5},{9,10},{11,12},{13,14},{10,9},... | collective-permute-start | bytes 147464 | tf_op jit(solution)/shard_map/ppermute | solution.py:28
  43.1 2.3 %collective-permute-start.10 = (f32[1,56,512]{2,1,0:T(8,128)S(1)}, f32[1,56,512]{2,1,0:T(8,128)S(1)}, u32[]{:S(2)}, u32[]{:S(2)}) collective-permute-start(f32[1,56,512]{2,1,0:T(8,128)S(1)} %get-tuple-element.47), channel_id=1, source_target_pairs={{0,8},{16,24},{8,0},{24,16},{1,9},{17,25},{9,1},{25,17},{2,10},{18... | collective-permute-start | bytes 344072 | tf_op jit(solution)/shard_map/ppermute | solution.py:27
  43.2 2.2 %collective-permute-start.9 = (f32[1,56,512]{2,1,0:T(8,128)S(1)}, f32[1,56,512]{2,1,0:T(8,128)S(1)}, u32[]{:S(2)}, u32[]{:S(2)}) collective-permute-start(f32[1,56,512]{2,1,0:T(8,128)S(1)} %get-tuple-element.48), channel_id=1, source_target_pairs={{8,16},{16,8},{9,17},{17,9},{10,18},{18,10},{11,19},{19,11},{12,20... | collective-permute-start | bytes 344072 | tf_op jit(solution)/shard_map/ppermute | solution.py:28
  45.5 35.0 %copy-start.1 = (bf16[2048,2048]{1,0:T(8,128)(2,1)S(1)}, bf16[2048,2048]{1,0:T(8,128)(2,1)}, u32[]{:S(2)}) copy-start(bf16[2048,2048]{1,0:T(8,128)(2,1)} %inverse_ref.3) | copy-start | bytes 25165828
  47.4 8.1 %collective-permute-start.17 = (f32[16,384]{1,0:T(8,128)S(1)}, f32[16,384]{1,0:T(8,128)S(1)}, u32[]{:S(2)}, u32[]{:S(2)}) collective-permute-start(f32[16,384]{1,0:T(8,128)S(1)} %get-tuple-element.32), channel_id=1, source_target_pairs={{0,4},{1,5},{2,6},{3,7},{4,0},{5,1},{6,2},{7,3},{8,12},{9,13},{10,... | collective-permute-start | bytes 73736 | tf_op jit(solution)/shard_map/ppermute | solution.py:41
  55.5 4.4 %collective-permute-start.18 = (f32[32,384]{1,0:T(8,128)S(1)}, f32[32,384]{1,0:T(8,128)S(1)}, u32[]{:S(2)}, u32[]{:S(2)}) collective-permute-start(f32[32,384]{1,0:T(8,128)S(1)} %pad_maximum_fusion.7), channel_id=1, source_target_pairs={{0,2},{1,3},{2,0},{3,1},{4,6},{5,7},{6,4},{7,5},{8,10},{9,11},{10,... | collective-permute-start | bytes 147464 | tf_op jit(solution)/shard_map/ppermute | solution.py:41
  59.8 2.7 %collective-permute-start.19 = (f32[64,384]{1,0:T(8,128)S(1)}, f32[64,384]{1,0:T(8,128)S(1)}, u32[]{:S(2)}, u32[]{:S(2)}) collective-permute-start(f32[64,384]{1,0:T(8,128)S(1)} %pad_maximum_fusion.5), channel_id=1, source_target_pairs={{0,8},{1,9},{2,10},{3,11},{4,12},{5,13},{6,14},{7,15},{8,0},{9,1},... | collective-permute-start | bytes 294920 | tf_op jit(solution)/shard_map/ppermute | solution.py:41
  61.7 3.2 %collective-permute-start.14 = (bf16[4,56,384]{2,1,0:T(8,128)(2,1)S(1)}, bf16[4,56,384]{2,1,0:T(8,128)(2,1)S(1)}, u32[]{:S(2)}, u32[]{:S(2)}) collective-permute-start(bf16[4,56,384]{2,1,0:T(8,128)(2,1)S(1)} %get-tuple-element.39), channel_id=1, source_target_pairs={{0,8},{16,24},{8,0},{24,16},{1,9},{17,25},{9,1},{25,17},{2,10},{18... | collective-permute-start | bytes 516104 | tf_op jit(solution)/shard_map/ppermute | solution.py:27
  61.8 3.2 %collective-permute-start.13 = (bf16[4,56,384]{2,1,0:T(8,128)(2,1)S(1)}, bf16[4,56,384]{2,1,0:T(8,128)(2,1)S(1)}, u32[]{:S(2)}, u32[]{:S(2)}) collective-permute-start(bf16[4,56,384]{2,1,0:T(8,128)(2,1)S(1)} %get-tuple-element.40), channel_id=1, source_target_pairs={{8,16},{16,8},{9,17},{17,9},{10,18},{18,10},{11,19},{19,11},{12,20... | collective-permute-start | bytes 516104 | tf_op jit(solution)/shard_map/ppermute | solution.py:28
  63.5 4.2 %collective-permute-start.20 = (f32[32,384]{1,0:T(8,128)S(1)}, f32[32,384]{1,0:T(8,128)S(1)}, u32[]{:S(2)}, u32[]{:S(2)}) collective-permute-start(f32[32,384]{1,0:T(8,128)S(1)} %pad_maximum_fusion.8), channel_id=1, source_target_pairs={{0,1},{1,0},{2,3},{3,2},{4,5},{5,4},{6,7},{7,6},{8,9},{9,8},{10,11... | collective-permute-start | bytes 147464 | tf_op jit(solution)/shard_map/ppermute | solution.py:41
  67.6 9.6 %collective-permute-start.21 = (f32[16,384]{1,0:T(8,128)S(1)}, f32[16,384]{1,0:T(8,128)S(1)}, u32[]{:S(2)}, u32[]{:S(2)}) collective-permute-start(f32[16,384]{1,0:T(8,128)S(1)} %slice_add_fusion), channel_id=1, source_target_pairs={{0,16},{1,17},{2,18},{3,19},{4,20},{5,21},{6,22},{7,23},{8,24},{9,... | collective-permute-start | bytes 73736 | tf_op jit(solution)/shard_map/ppermute | solution.py:41
  73.1 4.2 %collective-permute-start.15 = (bf16[32,4,384]{2,1,0:T(4,128)(2,1)S(1)}, bf16[32,4,384]{2,1,0:T(4,128)(2,1)S(1)}, u32[]{:S(2)}, u32[]{:S(2)}) collective-permute-start(bf16[32,4,384]{2,1,0:T(4,128)(2,1)S(1)} %get-tuple-element.51), channel_id=1, source_target_pairs={{1,2},{3,4},{5,6},{2,1},{4,3},{6,5},{9,10},{11,12},{13,14},{10,9},... | collective-permute-start | bytes 294920 | tf_op jit(solution)/shard_map/ppermute | solution.py:28
  73.9 6.4 %collective-permute-start.16 = (bf16[32,4,384]{2,1,0:T(4,128)(2,1)S(1)}, bf16[32,4,384]{2,1,0:T(4,128)(2,1)S(1)}, u32[]{:S(2)}, u32[]{:S(2)}) collective-permute-start(bf16[32,4,384]{2,1,0:T(4,128)(2,1)S(1)} %get-tuple-element.52), channel_id=1, source_target_pairs={{0,1},{2,3},{4,5},{6,7},{1,0},{3,2},{5,4},{7,6},{8,9},{10,11},{12,... | collective-permute-start | bytes 294920 | tf_op jit(solution)/shard_map/ppermute | solution.py:27
  80.5 1.6 %copy-start.5 = (f32[24,56,384]{2,1,0:T(8,128)S(1)}, f32[24,56,384]{2,1,0:T(8,128)}, u32[]{:S(2)}) copy-start(f32[24,56,384]{2,1,0:T(8,128)} %copy-done.4) | copy-start | bytes 6193156

commit v4 on v3

--- a/solution.py
+++ b/solution.py
@@ -280,7 +280,10 @@
     local = span_x * span_y
     basis = jnp.transpose(coarse_basis, (0, 2, 1))
     heat = jnp.broadcast_to(conductivity[:, :, None], (own_x, own_y, LANES))
-    params = pltpu.CompilerParams(vmem_limit_bytes=40 * 2**20)
+
+    def params(mebibytes):
+        return pltpu.CompilerParams(vmem_limit_bytes=mebibytes * 2**20)
+
     group = 2 * OV if own_x % (2 * OV) == 0 else OV
     in_vmem = pl.BlockSpec(memory_space=pltpu.VMEM)
     in_hbm = pl.BlockSpec(memory_space=pltpu.HBM)
@@ -302,8 +305,8 @@
                 pltpu.VMEM(rhs.shape, F32),
                 pltpu.SemaphoreType.DMA((own_x // OV,)),
             ],
-            compiler_params=params,
-        )(rhs, basis)
+            compiler_params=params(8),
+        )(pltpu.with_memory_space_constraint(rhs, pltpu.HBM), basis)
 
     def surveyed_residual(now, around):
         return pl.pallas_call(
@@ -311,7 +314,7 @@
             in_specs=[in_vmem] * 8,
             out_specs=[in_vmem] * 5,
             out_shape=[shape_of(rhs.shape, F32)] + survey_shapes,
-            compiler_params=params,
+            compiler_params=params(16),
         )(rhs, now, *around, heat, basis)
 
     def window_margins(low_edge, high_edge, sides):
@@ -345,8 +348,15 @@
             out_specs=out_specs,
             out_shape=out_shape,
             scratch_shapes=scratch,
-            compiler_params=params,
-        )(local_inverse, values, *margins, basis, lifted, now if last else heat)
+            compiler_params=params(24),
+        )(
+            pltpu.with_memory_space_constraint(local_inverse, pltpu.HBM),
+            values,
+            *margins,
+            basis,
+            lifted,
+            now if last else heat,
+        )
 
     gather_bits = masks()[0]
     *to_send, restricted = surveyed_start()

time: 88.5 us -> 83.8 us (0.947)
  local copies, waits for them, and re-layouts: 7.81 us -> 1.27 us
  Pallas kernels: 14.6 us -> 16.6 us
    unnamed x21 -> x11, local copies, waits for them, and re-layouts: 7.5 us -> 0.95 us
    pallas_call x2, Pallas kernels: 11 us -> 12.6 us  [improved(): pl.pallas_call(functools.partial(fine_kernel, last), in_specs=[in_hbm] +...]
where the time goes in v4:
time: 83.8 us; the launch traced here: 83.5 us
  starting transfers between devices  39.9 us (48%)
  waiting for transfers between devices  22.7 us (27%)
  Pallas kernels  16.6 us (20%)
  matrix products  1.64 us (2%)
  local copies, waits for them, and re-layouts  1.27 us (2%)
  other arithmetic  0.9 us (1%)
    ppermute x10, starting transfers between devices, swap(): return lax.ppermute(value, AXES, [(i, i ^ bit) for i in range(total)])  27.2 us
    ppermute x10, waiting for transfers between devices, swap(): return lax.ppermute(value, AXES, [(i, i ^ bit) for i in range(total)])  16 us
    pallas_call x2, Pallas kernels, improved(): pl.pallas_call(functools.partial(fine_kernel, last), in_specs=[in_hbm] +...  12.6 us
    ppermute x6, starting transfers between devices, edges(): lax.ppermute(jnp.where(even, high_edge, low_edge), axis, neighbour_pairs(...  8.52 us
    ppermute x6, waiting for transfers between devices, edges(): lax.ppermute(jnp.where(even, high_edge, low_edge), axis, neighbour_pairs(...  6.65 us
    ppermute x6, starting transfers between devices, edges(): lax.ppermute(jnp.where(even, low_edge, high_edge), axis, neighbour_pairs(...  4.17 us
    pallas_call x1, Pallas kernels, surveyed_start(): pl.pallas_call(start_kernel, in_specs=[in_hbm, in_vmem], out_specs=[in_vm...  2.04 us
    pallas_call x1, Pallas kernels, surveyed_residual(): pl.pallas_call(residual_kernel, in_specs=[in_vmem] * 8, out_specs=[in_vme...  1.89 us
  transfers between devices with their start and end apart: 22, of which 11 were waited for; matrix products, arithmetic and copies ran while one was open for 3% of the time, Pallas kernels for 0%

profile of v4, /device:TPU:0, one launch (start us, length us, event | category | flops | bytes accessed | tf_op | source)
XLA Modules:
  0.0 83.5 jit_solution(16437535384500715647)
XLA Ops:
  0.0 0.9 %copy-done.1 = f32[24,56,16]{1,2,0:T(8,128)S(1)} copy-done((f32[24,56,16]{1,2,0:T(8,128)S(1)}, f32[24,56,16]{1,2,0:T(8,128)}, u32[]{:S(2)}) %copy-start.1) | copy-done | bytes 86040
  0.9 2.0 %shard_map.55 = (bf16[4,56,384]{2,1,0:T(8,128)(2,1)S(1)}, bf16[4,56,384]{2,1,0:T(8,128)(2,1)S(1)}, bf16[24,8,384]{2,1,0:T(8,128)(2,1)S(1)}, f32[16,384]{1,0:T(8,128)S(1)}) custom-call(f32[24,56,384]{2,1,0:T(8,128)} %rhs_ref.3, f32[24,16,56]{2,1,0:T(8,128)S(1)} %bitcast.17), custom_call_target="tpu_custom_call" | custom-call | tf_op jit(solution)/shard_map/pallas_call | solution.py:299
  3.0 4.1 %collective-permute-start.4 = (f32[16,896]{1,0:T(8,128)S(1)}, f32[16,896]{1,0:T(8,128)S(1)}, u32[]{:S(2)}, u32[]{:S(2)}) collective-permute-start(f32[16,896]{1,0:T(8,128)S(1)} %constant_dynamic-update-slice_fusion), channel_id=1, source_target_pairs={{0,4},{1,5},{2,6},{3,7},{4,0},{5,1},{6,2},{7,3},{8,12},{9,13},{10,... | collective-permute-start | bytes 172040 | tf_op jit(solution)/shard_map/ppermute | solution.py:41
  7.1 2.8 %collective-permute-done.4 = f32[16,896]{1,0:T(8,128)S(1)} collective-permute-done((f32[16,896]{1,0:T(8,128)S(1)}, f32[16,896]{1,0:T(8,128)S(1)}, u32[]{:S(2)}, u32[]{:S(2)}) %collective-permute-start.4) | collective-permute-done | bytes 57376 | tf_op jit(solution)/shard_map/ppermute | solution.py:41
  9.9 1.4 %collective-permute-start.5 = (f32[32,896]{1,0:T(8,128)S(1)}, f32[32,896]{1,0:T(8,128)S(1)}, u32[]{:S(2)}, u32[]{:S(2)}) collective-permute-start(f32[32,896]{1,0:T(8,128)S(1)} %pad_maximum_fusion.4), channel_id=1, source_target_pairs={{0,2},{1,3},{2,0},{3,1},{4,6},{5,7},{6,4},{7,5},{8,10},{9,11},{10,... | collective-permute-start | bytes 344072 | tf_op jit(solution)/shard_map/ppermute | solution.py:41
  11.4 0.7 collective-permute-start
  12.1 2.7 %collective-permute-done.5 = f32[32,896]{1,0:T(8,128)S(1)} collective-permute-done((f32[32,896]{1,0:T(8,128)S(1)}, f32[32,896]{1,0:T(8,128)S(1)}, u32[]{:S(2)}, u32[]{:S(2)}) %collective-permute-start.5) | collective-permute-done | bytes 114720 | tf_op jit(solution)/shard_map/ppermute | solution.py:41
  15.4 0.7 collective-permute-start.2
  16.1 3.8 %collective-permute-start.3 = (bf16[32,4,384]{2,1,0:T(4,128)(2,1)S(1)}, bf16[32,4,384]{2,1,0:T(4,128)(2,1)S(1)}, u32[]{:S(2)}, u32[]{:S(2)}) collective-permute-start(bf16[32,4,384]{2,1,0:T(4,128)(2,1)S(1)} %get-tuple-element.56), channel_id=1, source_target_pairs={{0,1},{2,3},{4,5},{6,7},{1,0},{3,2},{5,4},{7,6},{8,9},{10,11},{12,... | collective-permute-start | bytes 294920 | tf_op jit(solution)/shard_map/ppermute | solution.py:27
  20.0 0.8 fusion.2
  20.9 2.0 %collective-permute-done.3 = bf16[32,4,384]{2,1,0:T(4,128)(2,1)S(1)} collective-permute-done((bf16[32,4,384]{2,1,0:T(4,128)(2,1)S(1)}, bf16[32,4,384]{2,1,0:T(4,128)(2,1)S(1)}, u32[]{:S(2)}, u32[]{:S(2)}) %collective-permute-start.3) | collective-permute-done | bytes 98336 | tf_op jit(solution)/shard_map/ppermute | solution.py:27
  22.9 2.3 %collective-permute-done.7 = f32[32,384]{1,0:T(8,128)S(1)} collective-permute-done((f32[32,384]{1,0:T(8,128)S(1)}, f32[32,384]{1,0:T(8,128)S(1)}, u32[]{:S(2)}, u32[]{:S(2)}) %collective-permute-start.7) | collective-permute-done | bytes 49184 | tf_op jit(solution)/shard_map/ppermute | solution.py:41
  25.2 4.1 %collective-permute-start.8 = (f32[16,384]{1,0:T(8,128)S(1)}, f32[16,384]{1,0:T(8,128)S(1)}, u32[]{:S(2)}, u32[]{:S(2)}) collective-permute-start(f32[16,384]{1,0:T(8,128)S(1)} %slice_add_fusion.2), channel_id=1, source_target_pairs={{0,16},{1,17},{2,18},{3,19},{4,20},{5,21},{6,22},{7,23},{8,24},{9,... | collective-permute-start | bytes 73736 | tf_op jit(solution)/shard_map/ppermute | solution.py:41
  29.5 1.7 %collective-permute-done.8 = f32[16,384]{1,0:T(8,128)S(1)} collective-permute-done((f32[16,384]{1,0:T(8,128)S(1)}, f32[16,384]{1,0:T(8,128)S(1)}, u32[]{:S(2)}, u32[]{:S(2)}) %collective-permute-start.8) | collective-permute-done | bytes 24608 | tf_op jit(solution)/shard_map/ppermute | solution.py:41
  31.4 5.9 %shard_map.56 = (f32[24,56,384]{2,1,0:T(8,128)S(1)}, f32[1,56,512]{2,1,0:T(8,128)S(1)}, f32[1,56,512]{2,1,0:T(8,128)S(1)}, f32[6,4,512]{2,1,0:T(4,128)S(1)}, f32[6,4,512]{2,1,0:T(4,128)S(1)}) custom-call(bf16[2048,2048]{1,0:T(8,128)(2,1)} %inverse_ref.3, f32[24,56,384]{2,1,0:T(8,128)S(1)} %copy-done, bf16[4,56,384]{2,1,0:T(8,128)(2,1)S(1)} %get-tuple-element.42.low_ref, ...), custom_call_target="tpu_custom_call" | custom-call | tf_op jit(solution)/shard_map/pallas_call | solution.py:345
  37.3 1.2 %collective-permute-start.12 = (f32[6,4,512]{2,1,0:T(4,128)S(1)}, f32[6,4,512]{2,1,0:T(4,128)S(1)}, u32[]{:S(2)}, u32[]{:S(2)}) collective-permute-start(f32[6,4,512]{2,1,0:T(4,128)S(1)} %bitcast.35), channel_id=1, source_target_pairs={{0,1},{2,3},{4,5},{6,7},{1,0},{3,2},{5,4},{7,6},{8,9},{10,11},{12,... | collective-permute-start | bytes 147464 | tf_op jit(solution)/shard_map/ppermute | solution.py:27
  39.3 0.7 collective-permute-start.9
  40.0 1.5 %collective-permute-done.12 = f32[6,4,512]{2,1,0:T(4,128)S(1)} collective-permute-done((f32[6,4,512]{2,1,0:T(4,128)S(1)}, f32[6,4,512]{2,1,0:T(4,128)S(1)}, u32[]{:S(2)}, u32[]{:S(2)}) %collective-permute-start.12) | collective-permute-done | bytes 49184 | tf_op jit(solution)/shard_map/ppermute | solution.py:27
  41.6 1.9 %shard_map.57 = (f32[24,56,384]{2,1,0:T(8,128)S(1)}, bf16[4,56,384]{2,1,0:T(8,128)(2,1)S(1)}, bf16[4,56,384]{2,1,0:T(8,128)(2,1)S(1)}, bf16[24,8,384]{2,1,0:T(8,128)(2,1)S(1)}, f32[16,384]{1,0:T(8,128)S(1)}) custom-call(f32[24,56,384]{2,1,0:T(8,128)S(1)} %copy-done, f32[24,56,384]{2,1,0:T(8,128)S(1)} %get-tuple-element.23.now_ref.extra_ref, ...), custom_call_target="tpu_custom_call" | custom-call | tf_op jit(solution)/shard_map/pallas_call | solution.py:312
  43.5 6.3 %collective-permute-start.17 = (f32[16,384]{1,0:T(8,128)S(1)}, f32[16,384]{1,0:T(8,128)S(1)}, u32[]{:S(2)}, u32[]{:S(2)}) collective-permute-start(f32[16,384]{1,0:T(8,128)S(1)} %get-tuple-element.32), channel_id=1, source_target_pairs={{0,4},{1,5},{2,6},{3,7},{4,0},{5,1},{6,2},{7,3},{8,12},{9,13},{10,... | collective-permute-start | bytes 73736 | tf_op jit(solution)/shard_map/ppermute | solution.py:41
  49.7 1.8 %collective-permute-done.17 = f32[16,384]{1,0:T(8,128)S(1)} collective-permute-done((f32[16,384]{1,0:T(8,128)S(1)}, f32[16,384]{1,0:T(8,128)S(1)}, u32[]{:S(2)}, u32[]{:S(2)}) %collective-permute-start.17) | collective-permute-done | bytes 24608 | tf_op jit(solution)/shard_map/ppermute | solution.py:41
  51.5 2.3 %collective-permute-start.18 = (f32[32,384]{1,0:T(8,128)S(1)}, f32[32,384]{1,0:T(8,128)S(1)}, u32[]{:S(2)}, u32[]{:S(2)}) collective-permute-start(f32[32,384]{1,0:T(8,128)S(1)} %pad_maximum_fusion.7), channel_id=1, source_target_pairs={{0,2},{1,3},{2,0},{3,1},{4,6},{5,7},{6,4},{7,5},{8,10},{9,11},{10,... | collective-permute-start | bytes 147464 | tf_op jit(solution)/shard_map/ppermute | solution.py:41
  53.8 2.1 %collective-permute-done.18 = f32[32,384]{1,0:T(8,128)S(1)} collective-permute-done((f32[32,384]{1,0:T(8,128)S(1)}, f32[32,384]{1,0:T(8,128)S(1)}, u32[]{:S(2)}, u32[]{:S(2)}) %collective-permute-start.18) | collective-permute-done | bytes 49184 | tf_op jit(solution)/shard_map/ppermute | solution.py:41
  55.9 1.8 %collective-permute-start.19 = (f32[64,384]{1,0:T(8,128)S(1)}, f32[64,384]{1,0:T(8,128)S(1)}, u32[]{:S(2)}, u32[]{:S(2)}) collective-permute-start(f32[64,384]{1,0:T(8,128)S(1)} %pad_maximum_fusion.5), channel_id=1, source_target_pairs={{0,8},{1,9},{2,10},{3,11},{4,12},{5,13},{6,14},{7,15},{8,0},{9,1},... | collective-permute-start | bytes 294920 | tf_op jit(solution)/shard_map/ppermute | solution.py:41
  58.7 0.8 fusion
  59.5 1.5 %collective-permute-start.20 = (f32[32,384]{1,0:T(8,128)S(1)}, f32[32,384]{1,0:T(8,128)S(1)}, u32[]{:S(2)}, u32[]{:S(2)}) collective-permute-start(f32[32,384]{1,0:T(8,128)S(1)} %pad_maximum_fusion.8), channel_id=1, source_target_pairs={{0,1},{1,0},{2,3},{3,2},{4,5},{5,4},{6,7},{7,6},{8,9},{9,8},{10,11... | collective-permute-start | bytes 147464 | tf_op jit(solution)/shard_map/ppermute | solution.py:41
  61.1 2.6 %collective-permute-done.20 = f32[32,384]{1,0:T(8,128)S(1)} collective-permute-done((f32[32,384]{1,0:T(8,128)S(1)}, f32[32,384]{1,0:T(8,128)S(1)}, u32[]{:S(2)}, u32[]{:S(2)}) %collective-permute-start.20) | collective-permute-done | bytes 49184 | tf_op jit(solution)/shard_map/ppermute | solution.py:41
  63.7 5.3 %collective-permute-start.21 = (f32[16,384]{1,0:T(8,128)S(1)}, f32[16,384]{1,0:T(8,128)S(1)}, u32[]{:S(2)}, u32[]{:S(2)}) collective-permute-start(f32[16,384]{1,0:T(8,128)S(1)} %slice_add_fusion), channel_id=1, source_target_pairs={{0,16},{1,17},{2,18},{3,19},{4,20},{5,21},{6,22},{7,23},{8,24},{9,... | collective-permute-start | bytes 73736 | tf_op jit(solution)/shard_map/ppermute | solution.py:41
  69.1 0.8 %collective-permute-start.15 = (bf16[32,4,384]{2,1,0:T(4,128)(2,1)S(1)}, bf16[32,4,384]{2,1,0:T(4,128)(2,1)S(1)}, u32[]{:S(2)}, u32[]{:S(2)}) collective-permute-start(bf16[32,4,384]{2,1,0:T(4,128)(2,1)S(1)} %get-tuple-element.51), channel_id=1, source_target_pairs={{1,2},{3,4},{5,6},{2,1},{4,3},{6,5},{9,10},{11,12},{13,14},{10,9},... | collective-permute-start | bytes 294920 | tf_op jit(solution)/shard_map/ppermute | solution.py:28
  70.0 3.3 %collective-permute-start.16 = (bf16[32,4,384]{2,1,0:T(4,128)(2,1)S(1)}, bf16[32,4,384]{2,1,0:T(4,128)(2,1)S(1)}, u32[]{:S(2)}, u32[]{:S(2)}) collective-permute-start(bf16[32,4,384]{2,1,0:T(4,128)(2,1)S(1)} %get-tuple-element.52), channel_id=1, source_target_pairs={{0,1},{2,3},{4,5},{6,7},{1,0},{3,2},{5,4},{7,6},{8,9},{10,11},{12,... | collective-permute-start | bytes 294920 | tf_op jit(solution)/shard_map/ppermute | solution.py:27
  73.3 3.1 %collective-permute-done.16 = bf16[32,4,384]{2,1,0:T(4,128)(2,1)S(1)} collective-permute-done((bf16[32,4,384]{2,1,0:T(4,128)(2,1)S(1)}, bf16[32,4,384]{2,1,0:T(4,128)(2,1)S(1)}, u32[]{:S(2)}, u32[]{:S(2)}) %collective-permute-start.16) | collective-permute-done | bytes 98336 | tf_op jit(solution)/shard_map/ppermute | solution.py:27
  76.6 6.8 %shard_map.58 = f32[24,56,384]{2,1,0:T(8,128)} custom-call(bf16[2048,2048]{1,0:T(8,128)(2,1)} %inverse_ref.3, f32[24,56,384]{2,1,0:T(8,128)S(1)} %get-tuple-element.28.block_ref, bf16[4,56,384]{2,1,0:T(8,128)(2,1)S(1)} %get-tuple-element.38.low_ref, bf16[4,56,384]{2,1,0:T(8,128)(2,1)S(1)} %get-tuple-element.37.high_ref, ...), custom_call_target="tpu_custom_call" | custom-call | tf_op jit(solution)/shard_map/pallas_call | solution.py:345
  (63 shorter events, 3.4 us)
Async XLA Ops:
  0.0 0.9 %copy-start.1 = (f32[24,56,16]{1,2,0:T(8,128)S(1)}, f32[24,56,16]{1,2,0:T(8,128)}, u32[]{:S(2)}) copy-start(f32[24,56,16]{1,2,0:T(8,128)} %param.8) | copy-start | bytes 258052
  0.9 2.1 %copy-start.3 = (f32[16,512]{1,0:T(8,128)S(1)}, f32[16,512]{1,0:T(8,128)}, u32[]{:S(2)}) copy-start(f32[16,512]{1,0:T(8,128)} %param.9) | copy-start | bytes 98308
  3.0 6.9 %collective-permute-start.4 = (f32[16,896]{1,0:T(8,128)S(1)}, f32[16,896]{1,0:T(8,128)S(1)}, u32[]{:S(2)}, u32[]{:S(2)}) collective-permute-start(f32[16,896]{1,0:T(8,128)S(1)} %constant_dynamic-update-slice_fusion), channel_id=1, source_target_pairs={{0,4},{1,5},{2,6},{3,7},{4,0},{5,1},{6,2},{7,3},{8,12},{9,13},{10,... | collective-permute-start | bytes 172040 | tf_op jit(solution)/shard_map/ppermute | solution.py:41
  9.9 4.9 %collective-permute-start.5 = (f32[32,896]{1,0:T(8,128)S(1)}, f32[32,896]{1,0:T(8,128)S(1)}, u32[]{:S(2)}, u32[]{:S(2)}) collective-permute-start(f32[32,896]{1,0:T(8,128)S(1)} %pad_maximum_fusion.4), channel_id=1, source_target_pairs={{0,2},{1,3},{2,0},{3,1},{4,6},{5,7},{6,4},{7,5},{8,10},{9,11},{10,... | collective-permute-start | bytes 344072 | tf_op jit(solution)/shard_map/ppermute | solution.py:41
  11.3 3.8 %collective-permute-start.1 = (bf16[4,56,384]{2,1,0:T(8,128)(2,1)S(1)}, bf16[4,56,384]{2,1,0:T(8,128)(2,1)S(1)}, u32[]{:S(2)}, u32[]{:S(2)}) collective-permute-start(bf16[4,56,384]{2,1,0:T(8,128)(2,1)S(1)} %get-tuple-element.43), channel_id=1, source_target_pairs={{0,8},{16,24},{8,0},{24,16},{1,9},{17,25},{9,1},{25,17},{2,10},{18... | collective-permute-start | bytes 516104 | tf_op jit(solution)/shard_map/ppermute | solution.py:27
  11.4 3.8 %collective-permute-start = (bf16[4,56,384]{2,1,0:T(8,128)(2,1)S(1)}, bf16[4,56,384]{2,1,0:T(8,128)(2,1)S(1)}, u32[]{:S(2)}, u32[]{:S(2)}) collective-permute-start(bf16[4,56,384]{2,1,0:T(8,128)(2,1)S(1)} %get-tuple-element.44), channel_id=1, source_target_pairs={{8,16},{16,8},{9,17},{17,9},{10,18},{18,10},{11,19},{19,11},{12,20... | collective-permute-start | bytes 516104 | tf_op jit(solution)/shard_map/ppermute | solution.py:28
  14.8 5.1 %collective-permute-start.6 = (f32[64,896]{1,0:T(8,128)S(1)}, f32[64,896]{1,0:T(8,128)S(1)}, u32[]{:S(2)}, u32[]{:S(2)}) collective-permute-start(f32[64,896]{1,0:T(8,128)S(1)} %pad_maximum_fusion.1), channel_id=1, source_target_pairs={{0,8},{1,9},{2,10},{3,11},{4,12},{5,13},{6,14},{7,15},{8,0},{9,1},... | collective-permute-start | bytes 688136 | tf_op jit(solution)/shard_map/ppermute | solution.py:41
  15.3 15.9 %copy-start.4 = (f32[24,56]{1,0:T(8,128)S(1)}, f32[24,56]{1,0:T(8,128)}, u32[]{:S(2)}) copy-start(f32[24,56]{1,0:T(8,128)} %param.6) | copy-start | bytes 16132
  15.4 5.5 %collective-permute-start.2 = (bf16[32,4,384]{2,1,0:T(4,128)(2,1)S(1)}, bf16[32,4,384]{2,1,0:T(4,128)(2,1)S(1)}, u32[]{:S(2)}, u32[]{:S(2)}) collective-permute-start(bf16[32,4,384]{2,1,0:T(4,128)(2,1)S(1)} %get-tuple-element.55), channel_id=1, source_target_pairs={{1,2},{3,4},{5,6},{2,1},{4,3},{6,5},{9,10},{11,12},{13,14},{10,9},... | collective-permute-start | bytes 294920 | tf_op jit(solution)/shard_map/ppermute | solution.py:28
  16.1 15.3 %copy-start = (f32[24,56,384]{2,1,0:T(8,128)S(1)}, f32[24,56,384]{2,1,0:T(8,128)}, u32[]{:S(2)}) copy-start(f32[24,56,384]{2,1,0:T(8,128)} %rhs_ref.3) | copy-start | bytes 6193156
  16.1 15.3 %copy-start.2 = (f32[24,56,16]{1,2,0:T(8,128)S(1)}, f32[24,56,16]{1,2,0:T(8,128)}, u32[]{:S(2)}) copy-start(f32[24,56,16]{1,2,0:T(8,128)} %param.8) | copy-start | bytes 258052
  16.1 6.8 %collective-permute-start.3 = (bf16[32,4,384]{2,1,0:T(4,128)(2,1)S(1)}, bf16[32,4,384]{2,1,0:T(4,128)(2,1)S(1)}, u32[]{:S(2)}, u32[]{:S(2)}) collective-permute-start(bf16[32,4,384]{2,1,0:T(4,128)(2,1)S(1)} %get-tuple-element.56), channel_id=1, source_target_pairs={{0,1},{2,3},{4,5},{6,7},{1,0},{3,2},{5,4},{7,6},{8,9},{10,11},{12,... | collective-permute-start | bytes 294920 | tf_op jit(solution)/shard_map/ppermute | solution.py:27
  20.8 4.4 %collective-permute-start.7 = (f32[32,384]{1,0:T(8,128)S(1)}, f32[32,384]{1,0:T(8,128)S(1)}, u32[]{:S(2)}, u32[]{:S(2)}) collective-permute-start(f32[32,384]{1,0:T(8,128)S(1)} %pad_maximum_fusion.6), channel_id=1, source_target_pairs={{0,1},{1,0},{2,3},{3,2},{4,5},{5,4},{6,7},{7,6},{8,9},{9,8},{10,11... | collective-permute-start | bytes 147464 | tf_op jit(solution)/shard_map/ppermute | solution.py:41
  25.2 5.9 %collective-permute-start.8 = (f32[16,384]{1,0:T(8,128)S(1)}, f32[16,384]{1,0:T(8,128)S(1)}, u32[]{:S(2)}, u32[]{:S(2)}) collective-permute-start(f32[16,384]{1,0:T(8,128)S(1)} %slice_add_fusion.2), channel_id=1, source_target_pairs={{0,16},{1,17},{2,18},{3,19},{4,20},{5,21},{6,22},{7,23},{8,24},{9,... | collective-permute-start | bytes 73736 | tf_op jit(solution)/shard_map/ppermute | solution.py:41
  37.3 4.2 %collective-permute-start.12 = (f32[6,4,512]{2,1,0:T(4,128)S(1)}, f32[6,4,512]{2,1,0:T(4,128)S(1)}, u32[]{:S(2)}, u32[]{:S(2)}) collective-permute-start(f32[6,4,512]{2,1,0:T(4,128)S(1)} %bitcast.35), channel_id=1, source_target_pairs={{0,1},{2,3},{4,5},{6,7},{1,0},{3,2},{5,4},{7,6},{8,9},{10,11},{12,... | collective-permute-start | bytes 147464 | tf_op jit(solution)/shard_map/ppermute | solution.py:27
  38.5 3.0 %collective-permute-start.11 = (f32[6,4,512]{2,1,0:T(4,128)S(1)}, f32[6,4,512]{2,1,0:T(4,128)S(1)}, u32[]{:S(2)}, u32[]{:S(2)}) collective-permute-start(f32[6,4,512]{2,1,0:T(4,128)S(1)} %bitcast.34), channel_id=1, source_target_pairs={{1,2},{3,4},{5,6},{2,1},{4,3},{6,5},{9,10},{11,12},{13,14},{10,9},... | collective-permute-start | bytes 147464 | tf_op jit(solution)/shard_map/ppermute | solution.py:28
  39.2 2.3 %collective-permute-start.10 = (f32[1,56,512]{2,1,0:T(8,128)S(1)}, f32[1,56,512]{2,1,0:T(8,128)S(1)}, u32[]{:S(2)}, u32[]{:S(2)}) collective-permute-start(f32[1,56,512]{2,1,0:T(8,128)S(1)} %get-tuple-element.47), channel_id=1, source_target_pairs={{0,8},{16,24},{8,0},{24,16},{1,9},{17,25},{9,1},{25,17},{2,10},{18... | collective-permute-start | bytes 344072 | tf_op jit(solution)/shard_map/ppermute | solution.py:27
  39.3 2.2 %collective-permute-start.9 = (f32[1,56,512]{2,1,0:T(8,128)S(1)}, f32[1,56,512]{2,1,0:T(8,128)S(1)}, u32[]{:S(2)}, u32[]{:S(2)}) collective-permute-start(f32[1,56,512]{2,1,0:T(8,128)S(1)} %get-tuple-element.48), channel_id=1, source_target_pairs={{8,16},{16,8},{9,17},{17,9},{10,18},{18,10},{11,19},{19,11},{12,20... | collective-permute-start | bytes 344072 | tf_op jit(solution)/shard_map/ppermute | solution.py:28
  43.5 8.1 %collective-permute-start.17 = (f32[16,384]{1,0:T(8,128)S(1)}, f32[16,384]{1,0:T(8,128)S(1)}, u32[]{:S(2)}, u32[]{:S(2)}) collective-permute-start(f32[16,384]{1,0:T(8,128)S(1)} %get-tuple-element.32), channel_id=1, source_target_pairs={{0,4},{1,5},{2,6},{3,7},{4,0},{5,1},{6,2},{7,3},{8,12},{9,13},{10,... | collective-permute-start | bytes 73736 | tf_op jit(solution)/shard_map/ppermute | solution.py:41
  51.5 4.4 %collective-permute-start.18 = (f32[32,384]{1,0:T(8,128)S(1)}, f32[32,384]{1,0:T(8,128)S(1)}, u32[]{:S(2)}, u32[]{:S(2)}) collective-permute-start(f32[32,384]{1,0:T(8,128)S(1)} %pad_maximum_fusion.7), channel_id=1, source_target_pairs={{0,2},{1,3},{2,0},{3,1},{4,6},{5,7},{6,4},{7,5},{8,10},{9,11},{10,... | collective-permute-start | bytes 147464 | tf_op jit(solution)/shard_map/ppermute | solution.py:41
  55.9 2.7 %collective-permute-start.19 = (f32[64,384]{1,0:T(8,128)S(1)}, f32[64,384]{1,0:T(8,128)S(1)}, u32[]{:S(2)}, u32[]{:S(2)}) collective-permute-start(f32[64,384]{1,0:T(8,128)S(1)} %pad_maximum_fusion.5), channel_id=1, source_target_pairs={{0,8},{1,9},{2,10},{3,11},{4,12},{5,13},{6,14},{7,15},{8,0},{9,1},... | collective-permute-start | bytes 294920 | tf_op jit(solution)/shard_map/ppermute | solution.py:41
  57.8 3.2 %collective-permute-start.14 = (bf16[4,56,384]{2,1,0:T(8,128)(2,1)S(1)}, bf16[4,56,384]{2,1,0:T(8,128)(2,1)S(1)}, u32[]{:S(2)}, u32[]{:S(2)}) collective-permute-start(bf16[4,56,384]{2,1,0:T(8,128)(2,1)S(1)} %get-tuple-element.39), channel_id=1, source_target_pairs={{0,8},{16,24},{8,0},{24,16},{1,9},{17,25},{9,1},{25,17},{2,10},{18... | collective-permute-start | bytes 516104 | tf_op jit(solution)/shard_map/ppermute | solution.py:27
  57.9 3.1 %collective-permute-start.13 = (bf16[4,56,384]{2,1,0:T(8,128)(2,1)S(1)}, bf16[4,56,384]{2,1,0:T(8,128)(2,1)S(1)}, u32[]{:S(2)}, u32[]{:S(2)}) collective-permute-start(bf16[4,56,384]{2,1,0:T(8,128)(2,1)S(1)} %get-tuple-element.40), channel_id=1, source_target_pairs={{8,16},{16,8},{9,17},{17,9},{10,18},{18,10},{11,19},{19,11},{12,20... | collective-permute-start | bytes 516104 | tf_op jit(solution)/shard_map/ppermute | solution.py:28
  59.5 4.2 %collective-permute-start.20 = (f32[32,384]{1,0:T(8,128)S(1)}, f32[32,384]{1,0:T(8,128)S(1)}, u32[]{:S(2)}, u32[]{:S(2)}) collective-permute-start(f32[32,384]{1,0:T(8,128)S(1)} %pad_maximum_fusion.8), channel_id=1, source_target_pairs={{0,1},{1,0},{2,3},{3,2},{4,5},{5,4},{6,7},{7,6},{8,9},{9,8},{10,11... | collective-permute-start | bytes 147464 | tf_op jit(solution)/shard_map/ppermute | solution.py:41
  63.7 9.6 %collective-permute-start.21 = (f32[16,384]{1,0:T(8,128)S(1)}, f32[16,384]{1,0:T(8,128)S(1)}, u32[]{:S(2)}, u32[]{:S(2)}) collective-permute-start(f32[16,384]{1,0:T(8,128)S(1)} %slice_add_fusion), channel_id=1, source_target_pairs={{0,16},{1,17},{2,18},{3,19},{4,20},{5,21},{6,22},{7,23},{8,24},{9,... | collective-permute-start | bytes 73736 | tf_op jit(solution)/shard_map/ppermute | solution.py:41
  69.1 4.2 %collective-permute-start.15 = (bf16[32,4,384]{2,1,0:T(4,128)(2,1)S(1)}, bf16[32,4,384]{2,1,0:T(4,128)(2,1)S(1)}, u32[]{:S(2)}, u32[]{:S(2)}) collective-permute-start(bf16[32,4,384]{2,1,0:T(4,128)(2,1)S(1)} %get-tuple-element.51), channel_id=1, source_target_pairs={{1,2},{3,4},{5,6},{2,1},{4,3},{6,5},{9,10},{11,12},{13,14},{10,9},... | collective-permute-start | bytes 294920 | tf_op jit(solution)/shard_map/ppermute | solution.py:28
  70.0 6.4 %collective-permute-start.16 = (bf16[32,4,384]{2,1,0:T(4,128)(2,1)S(1)}, bf16[32,4,384]{2,1,0:T(4,128)(2,1)S(1)}, u32[]{:S(2)}, u32[]{:S(2)}) collective-permute-start(bf16[32,4,384]{2,1,0:T(4,128)(2,1)S(1)} %get-tuple-element.52), channel_id=1, source_target_pairs={{0,1},{2,3},{4,5},{6,7},{1,0},{3,2},{5,4},{7,6},{8,9},{10,11},{12,... | collective-permute-start | bytes 294920 | tf_op jit(solution)/shard_map/ppermute | solution.py:27

commit v5 on v4

--- a/solution.py
+++ b/solution.py
@@ -9,6 +9,7 @@
 
 OV = 4
 ITERS = 2
+AHEAD = 2
 LANES = 128
 AXES = ("grp", "mem")
 EXACT = lax.Precision.HIGHEST
@@ -16,17 +17,13 @@
 BF16 = jnp.bfloat16
 
 
-def neighbour_pairs(count, first):
-    pairs = [(i, i + 1) for i in range(first, count - 1, 2)]
-    return pairs + [(j, i) for i, j in pairs]
-
-
 def edges(low_edge, high_edge, axis):
     count = lax.axis_size(axis)
-    even = lax.axis_index(axis) % 2 == 0
-    first = lax.ppermute(jnp.where(even, high_edge, low_edge), axis, neighbour_pairs(count, 0))
-    second = lax.ppermute(jnp.where(even, low_edge, high_edge), axis, neighbour_pairs(count, 1))
-    return jnp.where(even, second, first), jnp.where(even, first, second)
+    index = lax.axis_index(axis)
+    up = [(i, (i + 1) % count) for i in range(count)]
+    low = lax.ppermute(high_edge, axis, up)
+    high = lax.ppermute(low_edge, axis, [(j, i) for i, j in up])
+    return jnp.where(index == 0, 0, low), jnp.where(index == count - 1, 0, high)
 
 
 def masks():
@@ -179,38 +176,28 @@
     sum_ref[...] = total
 
 
-def fine_kernel(
-    last,
-    inverse_ref,
-    block_ref,
-    low_ref,
-    high_ref,
-    side_ref,
-    basis_ref,
-    lifted_ref,
-    extra_ref,
-    out_ref,
-    *refs,
-):
-    if last:
-        rows_held, window, wide, solved, arrived, result, left_for = refs
-    else:
-        first_ref, last_ref, left_ref, right_ref, rows_held, window, wide, solved, arrived = refs
-        result = out_ref
+def fine_kernel(fetch, inverse_ref, block_ref, low_ref, high_ref, side_ref, out_ref, *refs):
     own_x, own_y, columns = block_ref.shape
     span_y = own_y + 2 * OV
-    rows = solved.shape[0] // span_y
     copies = []
-    for first in range(0, own_x, rows):
-        count = rows * span_y
-        copies.append(
-            pltpu.make_async_copy(
-                inverse_ref.at[pl.ds((OV + first) * span_y, count)],
-                rows_held.at[pl.ds(first * span_y, count)],
-                arrived.at[first // rows],
+    if fetch:
+        rows_held, window, wide, solved, arrived = refs
+        rows = solved.shape[0] // span_y
+        for first in range(0, own_x, rows):
+            count = rows * span_y
+            copies.append(
+                pltpu.make_async_copy(
+                    inverse_ref.at[pl.ds((OV + first) * span_y, count)],
+                    rows_held.at[pl.ds(first * span_y, count)],
+                    arrived.at[first // rows],
+                )
             )
-        )
-        copies[-1].start()
+        for copy in copies[:AHEAD]:
+            copy.start()
+    else:
+        rows_held = inverse_ref
+        window, wide, solved = refs
+        rows = solved.shape[0] // span_y
 
     def place(index, values):
         wide[OV : OV + own_y, :] = values
@@ -225,42 +212,55 @@
     for index in range(own_x):
         place(OV + index, block_ref[index])
 
+    for first in range(0, own_x, rows):
+        if fetch:
+            copies[first // rows].wait()
+            for copy in copies[first // rows + AHEAD : first // rows + AHEAD + 1]:
+                copy.start()
+        solved[...] = product(
+            rows_held[first * span_y : (first + rows) * span_y, :], window[...]
+        )
+        for k in range(rows):
+            out_ref[first + k] = solved[k * span_y + OV : k * span_y + OV + own_y, :]
+
+
+def update_kernel(last, fine_ref, basis_ref, lifted_ref, extra_ref, out_ref, *refs):
+    own_x, own_y, columns = fine_ref.shape
+    if last:
+        result, left_for = refs
+    else:
+        first_ref, last_ref, left_ref, right_ref = refs
+        result = out_ref
     high, middle, low = split(lifted_ref[...])
     lifted = jnp.concatenate([high, middle, high, low, middle, high], axis=0)
     sends = []
-    for first in range(0, own_x, rows):
-        copies[first // rows].wait()
-        solved[...] = product(
-            rows_held[first * span_y : (first + rows) * span_y, :], window[...]
-        )
-        high, middle, low = modes_of(basis_ref, first, rows)
+    for first in range(0, own_x, OV):
+        high, middle, low = modes_of(basis_ref, first, OV)
         coarse = lax.dot_general(
             jnp.concatenate([high, high, middle, high, middle, low], axis=0),
             lifted,
             (((0,), (0,)), ((), ())),
             preferred_element_type=F32,
         )
-        for k in range(rows):
-            value = solved[k * span_y + OV : k * span_y + OV + own_y, :]
-            value = value + coarse[k * own_y : (k + 1) * own_y]
+        for k in range(OV):
+            value = fine_ref[first + k] + coarse[k * own_y : (k + 1) * own_y]
             if last:
                 value = extra_ref[first + k] + value
             result[first + k] = value
         if last:
             sends.append(
                 pltpu.make_async_copy(
-                    result.at[pl.ds(first, rows)],
-                    out_ref.at[pl.ds(first, rows)],
-                    left_for.at[first // rows],
+                    result.at[pl.ds(first, OV)],
+                    out_ref.at[pl.ds(first, OV)],
+                    left_for.at[first // OV],
                 )
             )
             sends[-1].start()
         else:
-            for index in range(first, first + rows):
+            for k in range(OV):
                 for ref, at in ((left_ref, 0), (right_ref, own_y - 1)):
-                    row = pl.ds(index % OV, 1)
-                    ref[index // OV, row, :columns] = result[index, at : at + 1]
-                    ref[index // OV, row, columns:] = extra_ref[index, at : at + 1]
+                    ref[first // OV, k : k + 1, :columns] = result[first + k, at : at + 1]
+                    ref[first // OV, k : k + 1, columns:] = extra_ref[first + k, at : at + 1]
     for send in sends:
         send.wait()
     if not last:
@@ -324,54 +324,72 @@
         left, right = edges(sides[:, :OV], sides[:, OV:], "mem")
         return low, high, jnp.concatenate([left, right], axis=1)
 
-    def improved(values, margins, lifted, now):
+    held = (own_x * span_y, local)
+
+    def fine(rows, values, margins):
+        fetch = rows.shape != held
+        out_shape = [shape_of(rhs.shape, F32)]
+        scratch = [
+            pltpu.VMEM((local, columns), BF16),
+            pltpu.VMEM((span_y, columns), F32),
+            pltpu.VMEM((group * span_y, columns), F32),
+        ]
+        if fetch:
+            rows = pltpu.with_memory_space_constraint(rows, pltpu.HBM)
+            out_shape.append(shape_of(held, BF16))
+            scratch.append(pltpu.SemaphoreType.DMA((own_x // group,)))
+        result = pl.pallas_call(
+            functools.partial(fine_kernel, fetch),
+            in_specs=[in_hbm if fetch else in_vmem] + [in_vmem] * 4,
+            out_specs=[in_vmem] * len(out_shape),
+            out_shape=out_shape,
+            scratch_shapes=scratch,
+            compiler_params=params(24),
+            cost_estimate=pl.CostEstimate(
+                flops=2 * held[0] * local * columns,
+                bytes_accessed=2 * held[0] * local,
+                transcendentals=0,
+            ),
+        )(rows, values, *margins)
+        return result if fetch else (*result, rows)
+
+    def updated(solved, lifted, now):
         last = now is not None
         edge = columns + LANES
         out_shape = [shape_of(rhs.shape, F32)]
-        scratch = [
-            pltpu.VMEM((own_x * span_y, local), BF16),
-            pltpu.VMEM((local, columns), BF16),
-            pltpu.VMEM((span_y, columns), F32),
-            pltpu.VMEM((group * span_y, columns), F32),
-            pltpu.SemaphoreType.DMA((own_x // group,)),
-        ]
         if last:
             out_specs = [in_hbm]
-            scratch += [pltpu.VMEM(rhs.shape, F32), pltpu.SemaphoreType.DMA((own_x // group,))]
+            scratch = [pltpu.VMEM(rhs.shape, F32), pltpu.SemaphoreType.DMA((own_x // OV,))]
         else:
             out_specs = [in_vmem] * 5
             out_shape += [shape_of((1, own_y, edge), F32)] * 2
             out_shape += [shape_of((own_x // OV, OV, edge), F32)] * 2
+            scratch = []
         return pl.pallas_call(
-            functools.partial(fine_kernel, last),
-            in_specs=[in_hbm] + [in_vmem] * 7,
+            functools.partial(update_kernel, last),
+            in_specs=[in_vmem] * 4,
             out_specs=out_specs,
             out_shape=out_shape,
             scratch_shapes=scratch,
-            compiler_params=params(24),
-        )(
-            pltpu.with_memory_space_constraint(local_inverse, pltpu.HBM),
-            values,
-            *margins,
-            basis,
-            lifted,
-            now if last else heat,
-        )
+            compiler_params=params(16),
+        )(solved, basis, lifted, now if last else heat)
 
     gather_bits = masks()[0]
     *to_send, restricted = surveyed_start()
     sources = gathered(jnp.concatenate([restricted, coarse_inverse], axis=1), gather_bits)
     inverse_rows = sources[:, columns:]
     margins = window_margins(*to_send)
+    solved, rows = fine(local_inverse, rhs, margins)
     lifted = summed_shares(inverse_rows, sources[:, :columns], modes)
-    now, first, final, left, right = improved(rhs, margins, lifted, None)
+    now, first, final, left, right = updated(solved, lifted, None)
     for sweep in range(ITERS - 1):
         around = edges(first, final, "grp") + edges(left, right, "mem")
         residual, *to_send, restricted = surveyed_residual(now, around)
         sources = gathered(restricted, gather_bits)
         margins = window_margins(*to_send)
+        solved, rows = fine(rows, residual, margins)
         lifted = summed_shares(inverse_rows, sources, modes)
-        now = improved(residual, margins, lifted, now)[0]
+        now = updated(solved, lifted, now)[0]
     return now
 
 

time: 83.8 us -> 76.1 us (0.908)
  starting transfers between devices: 39.9 us -> 28.1 us
  waiting for transfers between devices: 22.7 us -> 28.2 us
  Pallas kernels: 16.6 us -> 15.4 us
    ppermute x10, starting transfers between devices: 27.2 us -> 8.48 us  [swap(): return lax.ppermute(value, AXES, [(i, i ^ bit) for i in range(total)])]
    ppermute x12, waiting for transfers between devices: 6.67 us -> 14.2 us  [the longest x6 12.6 us: edges(): low = lax.ppermute(high_edge, axis, up)]
    ppermute x12, starting transfers between devices: 12.7 us -> 19.6 us  [the longest x6 17.1 us: edges(): high = lax.ppermute(low_edge, axis, [(j, i) for i, j in up])]
    ppermute x10, waiting for transfers between devices: 16 us -> 14.1 us  [swap(): return lax.ppermute(value, AXES, [(i, i ^ bit) for i in range(total)])]
    pallas_call x2 -> x4, Pallas kernels: 12.6 us -> 11.5 us  [the longest x2 9.18 us: fine(): pl.pallas_call(functools.partial(fine_kernel, fetch), in_specs=[in_hbm if...]
  transfers between devices with their start and end apart: 22 -> 22, of which waited for: 11 -> 13; matrix products, arithmetic and copies ran while one was open for 3% -> 2% of each run, Pallas kernels for 0% -> 7%
where the time goes in v5:
time: 76.1 us; the launch traced here: 76 us
  waiting for transfers between devices  28.2 us (37%)
  starting transfers between devices  28.1 us (37%)
  Pallas kernels  15.4 us (20%)
  matrix products  1.66 us (2%)
  local copies, waits for them, and re-layouts  1.41 us (2%)
    ppermute x6, starting transfers between devices, edges(): high = lax.ppermute(low_edge, axis, [(j, i) for i, j in up])  17.1 us
    ppermute x10, waiting for transfers between devices, swap(): return lax.ppermute(value, AXES, [(i, i ^ bit) for i in range(total)])  14.1 us
    ppermute x6, waiting for transfers between devices, edges(): low = lax.ppermute(high_edge, axis, up)  12.6 us
    pallas_call x2, Pallas kernels, fine(): pl.pallas_call(functools.partial(fine_kernel, fetch), in_specs=[in_hbm if...  9.18 us
    ppermute x10, starting transfers between devices, swap(): return lax.ppermute(value, AXES, [(i, i ^ bit) for i in range(total)])  8.48 us
    ppermute x6, starting transfers between devices, edges(): low = lax.ppermute(high_edge, axis, up)  2.51 us
    pallas_call x2, Pallas kernels, updated(): pl.pallas_call(functools.partial(update_kernel, last), in_specs=[in_vmem]...  2.32 us
    pallas_call x1, Pallas kernels, surveyed_start(): pl.pallas_call(start_kernel, in_specs=[in_hbm, in_vmem], out_specs=[in_vm...  2.04 us
  transfers between devices with their start and end apart: 22, of which 13 were waited for; matrix products, arithmetic and copies ran while one was open for 2% of the time, Pallas kernels for 7%

profile of v5, /device:TPU:0, one launch (start us, length us, event | category | flops | bytes accessed | tf_op | source)
XLA Modules:
  0.0 76.0 jit_solution(15929466238329801269)
XLA Ops:
  0.0 0.9 %copy-done.1 = f32[24,56,16]{1,2,0:T(8,128)S(1)} copy-done((f32[24,56,16]{1,2,0:T(8,128)S(1)}, f32[24,56,16]{1,2,0:T(8,128)}, u32[]{:S(2)}) %copy-start.1) | copy-done | bytes 86040
  0.9 2.0 %shard_map.55 = (bf16[4,56,384]{2,1,0:T(8,128)(2,1)S(1)}, bf16[4,56,384]{2,1,0:T(8,128)(2,1)S(1)}, bf16[24,8,384]{2,1,0:T(8,128)(2,1)S(1)}, f32[16,384]{1,0:T(8,128)S(1)}) custom-call(f32[24,56,384]{2,1,0:T(8,128)} %rhs_ref.3, f32[24,16,56]{2,1,0:T(8,128)S(1)} %bitcast.1), custom_call_target="tpu_custom_call" | custom-call | tf_op jit(solution)/shard_map/pallas_call | solution.py:299
  3.0 4.1 %collective-permute-start.4 = (f32[16,896]{1,0:T(8,128)S(1)}, f32[16,896]{1,0:T(8,128)S(1)}, u32[]{:S(2)}, u32[]{:S(2)}) collective-permute-start(f32[16,896]{1,0:T(8,128)S(1)} %constant_dynamic-update-slice_fusion), channel_id=1, source_target_pairs={{0,4},{1,5},{2,6},{3,7},{4,0},{5,1},{6,2},{7,3},{8,12},{9,13},{10,... | collective-permute-start | bytes 172040 | tf_op jit(solution)/shard_map/ppermute | solution.py:38
  7.1 1.7 %collective-permute-start.1 = (bf16[4,56,384]{2,1,0:T(8,128)(2,1)S(1)}, bf16[4,56,384]{2,1,0:T(8,128)(2,1)S(1)}, u32[]{:S(2)}, u32[]{:S(2)}) collective-permute-start(bf16[4,56,384]{2,1,0:T(8,128)(2,1)S(1)} %get-tuple-element.22), channel_id=1, source_target_pairs={{8,0},{16,8},{24,16},{0,24},{9,1},{17,9},{25,17},{1,25},{10,2},{18... | collective-permute-start | bytes 516104 | tf_op jit(solution)/shard_map/ppermute | solution.py:25
  8.9 1.0 %collective-permute-done.4 = f32[16,896]{1,0:T(8,128)S(1)} collective-permute-done((f32[16,896]{1,0:T(8,128)S(1)}, f32[16,896]{1,0:T(8,128)S(1)}, u32[]{:S(2)}, u32[]{:S(2)}) %collective-permute-start.4) | collective-permute-done | bytes 57376 | tf_op jit(solution)/shard_map/ppermute | solution.py:38
  9.9 1.4 %collective-permute-start.5 = (f32[32,896]{1,0:T(8,128)S(1)}, f32[32,896]{1,0:T(8,128)S(1)}, u32[]{:S(2)}, u32[]{:S(2)}) collective-permute-start(f32[32,896]{1,0:T(8,128)S(1)} %pad_maximum_fusion.4), channel_id=1, source_target_pairs={{0,2},{1,3},{2,0},{3,1},{4,6},{5,7},{6,4},{7,5},{8,10},{9,11},{10,... | collective-permute-start | bytes 344072 | tf_op jit(solution)/shard_map/ppermute | solution.py:38
  11.3 0.7 collective-permute-done
  12.0 0.8 %collective-permute-done.1 = bf16[4,56,384]{2,1,0:T(8,128)(2,1)S(1)} collective-permute-done((bf16[4,56,384]{2,1,0:T(8,128)(2,1)S(1)}, bf16[4,56,384]{2,1,0:T(8,128)(2,1)S(1)}, u32[]{:S(2)}, u32[]{:S(2)}) %collective-permute-start.1) | collective-permute-done | bytes 172064 | tf_op jit(solution)/shard_map/ppermute | solution.py:25
  13.0 1.6 %collective-permute-start.2 = (bf16[32,4,384]{2,1,0:T(4,128)(2,1)S(1)}, bf16[32,4,384]{2,1,0:T(4,128)(2,1)S(1)}, u32[]{:S(2)}, u32[]{:S(2)}) collective-permute-start(bf16[32,4,384]{2,1,0:T(4,128)(2,1)S(1)} %get-tuple-element.43), channel_id=1, source_target_pairs={{0,1},{1,2},{2,3},{3,4},{4,5},{5,6},{6,7},{7,0},{8,9},{9,10},{10,1... | collective-permute-start | bytes 294920 | tf_op jit(solution)/shard_map/ppermute | solution.py:24
  14.6 3.2 %collective-permute-start.3 = (bf16[32,4,384]{2,1,0:T(4,128)(2,1)S(1)}, bf16[32,4,384]{2,1,0:T(4,128)(2,1)S(1)}, u32[]{:S(2)}, u32[]{:S(2)}) collective-permute-start(bf16[32,4,384]{2,1,0:T(4,128)(2,1)S(1)} %get-tuple-element.44), channel_id=1, source_target_pairs={{1,0},{2,1},{3,2},{4,3},{5,4},{6,5},{7,6},{0,7},{9,8},{10,9},{11,1... | collective-permute-start | bytes 294920 | tf_op jit(solution)/shard_map/ppermute | solution.py:25
  17.8 0.6 collective-permute-start.6
  18.4 3.0 %collective-permute-done.2 = bf16[32,4,384]{2,1,0:T(4,128)(2,1)S(1)} collective-permute-done((bf16[32,4,384]{2,1,0:T(4,128)(2,1)S(1)}, bf16[32,4,384]{2,1,0:T(4,128)(2,1)S(1)}, u32[]{:S(2)}, u32[]{:S(2)}) %collective-permute-start.2) | collective-permute-done | bytes 98336 | tf_op jit(solution)/shard_map/ppermute | solution.py:24
  21.4 0.8 %collective-permute-done.3 = bf16[32,4,384]{2,1,0:T(4,128)(2,1)S(1)} collective-permute-done((bf16[32,4,384]{2,1,0:T(4,128)(2,1)S(1)}, bf16[32,4,384]{2,1,0:T(4,128)(2,1)S(1)}, u32[]{:S(2)}, u32[]{:S(2)}) %collective-permute-start.3) | collective-permute-done | bytes 98336 | tf_op jit(solution)/shard_map/ppermute | solution.py:25
  22.3 0.8 %fusion.2 = f32[512,384]{1,0:T(8,128)S(1)} fusion(f32[128,896]{1,0:T(8,128)S(1)} %pad_maximum_fusion, f32[64,896]{1,0:T(8,128)S(1)} %collective-permute-done.6, f32[32,896]{1,0:T(8,128)S(1)} %collective-permute-done.5, f32[16,896]{1,0:T(8,128)S(1)} %collective-permute-done.4, f32[16,896]{1,0:T(8,128)S(1)} %constant_dynamic-update-slice_fusion), kind=kOutput, calls=%fused_computation.3 | convolution fusion | flops 302137344 | bytes 1507328 | tf_op jit(solution)/shard_map/dot_general | solution.py:48
  23.7 3.7 %collective-permute-done.7 = f32[32,384]{1,0:T(8,128)S(1)} collective-permute-done((f32[32,384]{1,0:T(8,128)S(1)}, f32[32,384]{1,0:T(8,128)S(1)}, u32[]{:S(2)}, u32[]{:S(2)}) %collective-permute-start.7) | collective-permute-done | bytes 49184 | tf_op jit(solution)/shard_map/ppermute | solution.py:38
  27.3 1.6 %collective-permute-start.8 = (f32[16,384]{1,0:T(8,128)S(1)}, f32[16,384]{1,0:T(8,128)S(1)}, u32[]{:S(2)}, u32[]{:S(2)}) collective-permute-start(f32[16,384]{1,0:T(8,128)S(1)} %slice_add_fusion.2), channel_id=1, source_target_pairs={{0,16},{1,17},{2,18},{3,19},{4,20},{5,21},{6,22},{7,23},{8,24},{9,... | collective-permute-start | bytes 73736 | tf_op jit(solution)/shard_map/ppermute | solution.py:38
  28.9 5.5 %shard_map.56 = (f32[24,56,384]{2,1,0:T(8,128)S(1)}, bf16[1536,2048]{1,0:T(8,128)(2,1)S(1)}) custom-call(bf16[2048,2048]{1,0:T(8,128)(2,1)} %inverse_ref.1, f32[24,56,384]{2,1,0:T(8,128)S(1)} %copy-done, bf16[4,56,384]{2,1,0:T(8,128)(2,1)S(1)} %broadcast_select_fusion.3.low_ref, bf16[4,56,384]{2,1,0:T(8,128)(2,1)S(1)} %broadcast_select_fusion.1.high_ref, ...), custom_call_target="tpu_custom_call" | custom-call | flops 2415919104 | bytes 6291456 | tf_op jit(solution)/shard_map/pallas_call | solution.py:341
  34.7 0.6 shard_map.57
  35.7 4.4 %collective-permute-start.12 = (f32[6,4,512]{2,1,0:T(4,128)S(1)}, f32[6,4,512]{2,1,0:T(4,128)S(1)}, u32[]{:S(2)}, u32[]{:S(2)}) collective-permute-start(f32[6,4,512]{2,1,0:T(4,128)S(1)} %get-tuple-element.31), channel_id=1, source_target_pairs={{1,0},{2,1},{3,2},{4,3},{5,4},{6,5},{7,6},{0,7},{9,8},{10,9},{11,1... | collective-permute-start | bytes 147464 | tf_op jit(solution)/shard_map/ppermute | solution.py:25
  40.1 1.7 %collective-permute-start.10 = (f32[1,56,512]{2,1,0:T(8,128)S(1)}, f32[1,56,512]{2,1,0:T(8,128)S(1)}, u32[]{:S(2)}, u32[]{:S(2)}) collective-permute-start(f32[1,56,512]{2,1,0:T(8,128)S(1)} %get-tuple-element.29), channel_id=1, source_target_pairs={{8,0},{16,8},{24,16},{0,24},{9,1},{17,9},{25,17},{1,25},{10,2},{18... | collective-permute-start | bytes 344072 | tf_op jit(solution)/shard_map/ppermute | solution.py:25
  42.2 2.5 %collective-permute-done.9 = f32[1,56,512]{2,1,0:T(8,128)S(1)} collective-permute-done((f32[1,56,512]{2,1,0:T(8,128)S(1)}, f32[1,56,512]{2,1,0:T(8,128)S(1)}, u32[]{:S(2)}, u32[]{:S(2)}) %collective-permute-start.9) | collective-permute-done | bytes 114720 | tf_op jit(solution)/shard_map/ppermute | solution.py:24
  44.7 1.8 %shard_map.58 = (f32[24,56,384]{2,1,0:T(8,128)S(1)}, bf16[4,56,384]{2,1,0:T(8,128)(2,1)S(1)}, bf16[4,56,384]{2,1,0:T(8,128)(2,1)S(1)}, bf16[24,8,384]{2,1,0:T(8,128)(2,1)S(1)}, f32[16,384]{1,0:T(8,128)S(1)}) custom-call(f32[24,56,384]{2,1,0:T(8,128)S(1)} %copy-done, f32[24,56,384]{2,1,0:T(8,128)S(1)} %get-tuple-element.27.now_ref.extra_ref, ...), custom_call_target="tpu_custom_call" | custom-call | tf_op jit(solution)/shard_map/pallas_call | solution.py:312
  46.6 4.7 %collective-permute-done.17 = f32[16,384]{1,0:T(8,128)S(1)} collective-permute-done((f32[16,384]{1,0:T(8,128)S(1)}, f32[16,384]{1,0:T(8,128)S(1)}, u32[]{:S(2)}, u32[]{:S(2)}) %collective-permute-start.17) | collective-permute-done | bytes 24608 | tf_op jit(solution)/shard_map/ppermute | solution.py:38
  51.3 4.1 %collective-permute-done.18 = f32[32,384]{1,0:T(8,128)S(1)} collective-permute-done((f32[32,384]{1,0:T(8,128)S(1)}, f32[32,384]{1,0:T(8,128)S(1)}, u32[]{:S(2)}, u32[]{:S(2)}) %collective-permute-start.18) | collective-permute-done | bytes 49184 | tf_op jit(solution)/shard_map/ppermute | solution.py:38
  56.0 1.3 %collective-permute-start.14 = (bf16[4,56,384]{2,1,0:T(8,128)(2,1)S(1)}, bf16[4,56,384]{2,1,0:T(8,128)(2,1)S(1)}, u32[]{:S(2)}, u32[]{:S(2)}) collective-permute-start(bf16[4,56,384]{2,1,0:T(8,128)(2,1)S(1)} %get-tuple-element.34), channel_id=1, source_target_pairs={{8,0},{16,8},{24,16},{0,24},{9,1},{17,9},{25,17},{1,25},{10,2},{18... | collective-permute-start | bytes 516104 | tf_op jit(solution)/shard_map/ppermute | solution.py:25
  57.3 0.8 %fusion = f32[512,384]{1,0:T(8,128)S(1)} fusion(f32[128,896]{1,0:T(8,128)S(1)} %pad_maximum_fusion, f32[64,384]{1,0:T(8,128)S(1)} %collective-permute-done.19, f32[32,384]{1,0:T(8,128)S(1)} %collective-permute-done.18, f32[16,384]{1,0:T(8,128)S(1)} %collective-permute-done.17, f32[16,384]{1,0:T(8,128)S(1)} %get-tuple-element.36), kind=kOutput, calls=%fused_computation.1 | convolution fusion | flops 302137344 | bytes 1245184 | tf_op jit(solution)/shard_map/dot_general | solution.py:48
  58.2 3.4 %collective-permute-done.13 = bf16[4,56,384]{2,1,0:T(8,128)(2,1)S(1)} collective-permute-done((bf16[4,56,384]{2,1,0:T(8,128)(2,1)S(1)}, bf16[4,56,384]{2,1,0:T(8,128)(2,1)S(1)}, u32[]{:S(2)}, u32[]{:S(2)}) %collective-permute-start.13) | collective-permute-done | bytes 172064 | tf_op jit(solution)/shard_map/ppermute | solution.py:24
  61.8 0.5 collective-permute-done.20
  62.8 4.7 %collective-permute-start.16 = (bf16[32,4,384]{2,1,0:T(4,128)(2,1)S(1)}, bf16[32,4,384]{2,1,0:T(4,128)(2,1)S(1)}, u32[]{:S(2)}, u32[]{:S(2)}) collective-permute-start(bf16[32,4,384]{2,1,0:T(4,128)(2,1)S(1)} %get-tuple-element.42), channel_id=1, source_target_pairs={{1,0},{2,1},{3,2},{4,3},{5,4},{6,5},{7,6},{0,7},{9,8},{10,9},{11,1... | collective-permute-start | bytes 294920 | tf_op jit(solution)/shard_map/ppermute | solution.py:25
  67.5 2.7 %collective-permute-done.15 = bf16[32,4,384]{2,1,0:T(4,128)(2,1)S(1)} collective-permute-done((bf16[32,4,384]{2,1,0:T(4,128)(2,1)S(1)}, bf16[32,4,384]{2,1,0:T(4,128)(2,1)S(1)}, u32[]{:S(2)}, u32[]{:S(2)}) %collective-permute-start.15) | collective-permute-done | bytes 98336 | tf_op jit(solution)/shard_map/ppermute | solution.py:24
  70.4 3.7 %shard_map.59.fine_ref = f32[24,56,384]{2,1,0:T(8,128)S(1)} custom-call(bf16[1536,2048]{1,0:T(8,128)(2,1)S(1)} %get-tuple-element.24.inverse_ref, f32[24,56,384]{2,1,0:T(8,128)S(1)} %get-tuple-element.32.block_ref, bf16[4,56,384]{2,1,0:T(8,128)(2,1)S(1)} %broadcast_select_fusion.2.low_ref, bf16[4,56,384]{2,1,0:T(8,128)(2,1)S(1)} %broadcast_select_fusion.high_ref, ...), custom_call_target="tpu_custom_call" | custom-call | flops 2415919104 | bytes 6291456 | tf_op jit(solution)/shard_map/pallas_call | solution.py:341
  74.1 1.7 %shard_map.60 = f32[24,56,384]{2,1,0:T(8,128)} custom-call(f32[24,56,384]{2,1,0:T(8,128)S(1)} %shard_map.59.fine_ref, f32[24,16,56]{2,1,0:T(8,128)S(1)} %bitcast.4, f32[16,384]{1,0:T(8,128)S(1)} %fusion.18.lifted_ref, f32[24,56,384]{2,1,0:T(8,128)S(1)} %get-tuple-element.27.now_ref.extra_ref), custom_call_target="tpu_custom_call" | custom-call | tf_op jit(solution)/shard_map/pallas_call | solution.py:368
  (68 shorter events, 3.3 us)
Async XLA Ops:
  0.0 0.9 %copy-start.1 = (f32[24,56,16]{1,2,0:T(8,128)S(1)}, f32[24,56,16]{1,2,0:T(8,128)}, u32[]{:S(2)}) copy-start(f32[24,56,16]{1,2,0:T(8,128)} %param.8) | copy-start | bytes 258052
  0.9 2.1 %copy-start.3 = (f32[16,512]{1,0:T(8,128)S(1)}, f32[16,512]{1,0:T(8,128)}, u32[]{:S(2)}) copy-start(f32[16,512]{1,0:T(8,128)} %param.9) | copy-start | bytes 98308
  3.0 6.9 %collective-permute-start.4 = (f32[16,896]{1,0:T(8,128)S(1)}, f32[16,896]{1,0:T(8,128)S(1)}, u32[]{:S(2)}, u32[]{:S(2)}) collective-permute-start(f32[16,896]{1,0:T(8,128)S(1)} %constant_dynamic-update-slice_fusion), channel_id=1, source_target_pairs={{0,4},{1,5},{2,6},{3,7},{4,0},{5,1},{6,2},{7,3},{8,12},{9,13},{10,... | collective-permute-start | bytes 172040 | tf_op jit(solution)/shard_map/ppermute | solution.py:38
  7.1 4.8 %collective-permute-start = (bf16[4,56,384]{2,1,0:T(8,128)(2,1)S(1)}, bf16[4,56,384]{2,1,0:T(8,128)(2,1)S(1)}, u32[]{:S(2)}, u32[]{:S(2)}) collective-permute-start(bf16[4,56,384]{2,1,0:T(8,128)(2,1)S(1)} %get-tuple-element.21), channel_id=1, source_target_pairs={{0,8},{8,16},{16,24},{24,0},{1,9},{9,17},{17,25},{25,1},{2,10},{10... | collective-permute-start | bytes 516104 | tf_op jit(solution)/shard_map/ppermute | solution.py:24
  7.1 5.7 %collective-permute-start.1 = (bf16[4,56,384]{2,1,0:T(8,128)(2,1)S(1)}, bf16[4,56,384]{2,1,0:T(8,128)(2,1)S(1)}, u32[]{:S(2)}, u32[]{:S(2)}) collective-permute-start(bf16[4,56,384]{2,1,0:T(8,128)(2,1)S(1)} %get-tuple-element.22), channel_id=1, source_target_pairs={{8,0},{16,8},{24,16},{0,24},{9,1},{17,9},{25,17},{1,25},{10,2},{18... | collective-permute-start | bytes 516104 | tf_op jit(solution)/shard_map/ppermute | solution.py:25
  9.9 7.9 %collective-permute-start.5 = (f32[32,896]{1,0:T(8,128)S(1)}, f32[32,896]{1,0:T(8,128)S(1)}, u32[]{:S(2)}, u32[]{:S(2)}) collective-permute-start(f32[32,896]{1,0:T(8,128)S(1)} %pad_maximum_fusion.4), channel_id=1, source_target_pairs={{0,2},{1,3},{2,0},{3,1},{4,6},{5,7},{6,4},{7,5},{8,10},{9,11},{10,... | collective-permute-start | bytes 344072 | tf_op jit(solution)/shard_map/ppermute | solution.py:38
  13.0 15.9 %copy-start = (f32[24,56,384]{2,1,0:T(8,128)S(1)}, f32[24,56,384]{2,1,0:T(8,128)}, u32[]{:S(2)}) copy-start(f32[24,56,384]{2,1,0:T(8,128)} %rhs_ref.3) | copy-start | bytes 6193156
  13.0 8.4 %collective-permute-start.2 = (bf16[32,4,384]{2,1,0:T(4,128)(2,1)S(1)}, bf16[32,4,384]{2,1,0:T(4,128)(2,1)S(1)}, u32[]{:S(2)}, u32[]{:S(2)}) collective-permute-start(bf16[32,4,384]{2,1,0:T(4,128)(2,1)S(1)} %get-tuple-element.43), channel_id=1, source_target_pairs={{0,1},{1,2},{2,3},{3,4},{4,5},{5,6},{6,7},{7,0},{8,9},{9,10},{10,1... | collective-permute-start | bytes 294920 | tf_op jit(solution)/shard_map/ppermute | solution.py:24
  14.6 7.6 %collective-permute-start.3 = (bf16[32,4,384]{2,1,0:T(4,128)(2,1)S(1)}, bf16[32,4,384]{2,1,0:T(4,128)(2,1)S(1)}, u32[]{:S(2)}, u32[]{:S(2)}) collective-permute-start(bf16[32,4,384]{2,1,0:T(4,128)(2,1)S(1)} %get-tuple-element.44), channel_id=1, source_target_pairs={{1,0},{2,1},{3,2},{4,3},{5,4},{6,5},{7,6},{0,7},{9,8},{10,9},{11,1... | collective-permute-start | bytes 294920 | tf_op jit(solution)/shard_map/ppermute | solution.py:25
  17.8 4.5 %collective-permute-start.6 = (f32[64,896]{1,0:T(8,128)S(1)}, f32[64,896]{1,0:T(8,128)S(1)}, u32[]{:S(2)}, u32[]{:S(2)}) collective-permute-start(f32[64,896]{1,0:T(8,128)S(1)} %pad_maximum_fusion.1), channel_id=1, source_target_pairs={{0,8},{1,9},{2,10},{3,11},{4,12},{5,13},{6,14},{7,15},{8,0},{9,1},... | collective-permute-start | bytes 688136 | tf_op jit(solution)/shard_map/ppermute | solution.py:38
  23.2 4.2 %collective-permute-start.7 = (f32[32,384]{1,0:T(8,128)S(1)}, f32[32,384]{1,0:T(8,128)S(1)}, u32[]{:S(2)}, u32[]{:S(2)}) collective-permute-start(f32[32,384]{1,0:T(8,128)S(1)} %pad_maximum_fusion.6), channel_id=1, source_target_pairs={{0,1},{1,0},{2,3},{3,2},{4,5},{5,4},{6,7},{7,6},{8,9},{9,8},{10,11... | collective-permute-start | bytes 147464 | tf_op jit(solution)/shard_map/ppermute | solution.py:38
  27.3 7.1 %copy-start.4 = (f32[24,56]{1,0:T(8,128)S(1)}, f32[24,56]{1,0:T(8,128)}, u32[]{:S(2)}) copy-start(f32[24,56]{1,0:T(8,128)} %param.6) | copy-start | bytes 16132
  27.3 7.3 %copy-start.2 = (f32[24,56,16]{1,2,0:T(8,128)S(1)}, f32[24,56,16]{1,2,0:T(8,128)}, u32[]{:S(2)}) copy-start(f32[24,56,16]{1,2,0:T(8,128)} %param.8) | copy-start | bytes 258052
  27.3 7.0 %collective-permute-start.8 = (f32[16,384]{1,0:T(8,128)S(1)}, f32[16,384]{1,0:T(8,128)S(1)}, u32[]{:S(2)}, u32[]{:S(2)}) collective-permute-start(f32[16,384]{1,0:T(8,128)S(1)} %slice_add_fusion.2), channel_id=1, source_target_pairs={{0,16},{1,17},{2,18},{3,19},{4,20},{5,21},{6,22},{7,23},{8,24},{9,... | collective-permute-start | bytes 73736 | tf_op jit(solution)/shard_map/ppermute | solution.py:38
  35.3 6.8 %collective-permute-start.11 = (f32[6,4,512]{2,1,0:T(4,128)S(1)}, f32[6,4,512]{2,1,0:T(4,128)S(1)}, u32[]{:S(2)}, u32[]{:S(2)}) collective-permute-start(f32[6,4,512]{2,1,0:T(4,128)S(1)} %get-tuple-element.30), channel_id=1, source_target_pairs={{0,1},{1,2},{2,3},{3,4},{4,5},{5,6},{6,7},{7,0},{8,9},{9,10},{10,1... | collective-permute-start | bytes 147464 | tf_op jit(solution)/shard_map/ppermute | solution.py:24
  35.7 6.5 %collective-permute-start.12 = (f32[6,4,512]{2,1,0:T(4,128)S(1)}, f32[6,4,512]{2,1,0:T(4,128)S(1)}, u32[]{:S(2)}, u32[]{:S(2)}) collective-permute-start(f32[6,4,512]{2,1,0:T(4,128)S(1)} %get-tuple-element.31), channel_id=1, source_target_pairs={{1,0},{2,1},{3,2},{4,3},{5,4},{6,5},{7,6},{0,7},{9,8},{10,9},{11,1... | collective-permute-start | bytes 147464 | tf_op jit(solution)/shard_map/ppermute | solution.py:25
  40.1 4.6 %collective-permute-start.9 = (f32[1,56,512]{2,1,0:T(8,128)S(1)}, f32[1,56,512]{2,1,0:T(8,128)S(1)}, u32[]{:S(2)}, u32[]{:S(2)}) collective-permute-start(f32[1,56,512]{2,1,0:T(8,128)S(1)} %get-tuple-element.28), channel_id=1, source_target_pairs={{0,8},{8,16},{16,24},{24,0},{1,9},{9,17},{17,25},{25,1},{2,10},{10... | collective-permute-start | bytes 344072 | tf_op jit(solution)/shard_map/ppermute | solution.py:24
  40.1 4.6 %collective-permute-start.10 = (f32[1,56,512]{2,1,0:T(8,128)S(1)}, f32[1,56,512]{2,1,0:T(8,128)S(1)}, u32[]{:S(2)}, u32[]{:S(2)}) collective-permute-start(f32[1,56,512]{2,1,0:T(8,128)S(1)} %get-tuple-element.29), channel_id=1, source_target_pairs={{8,0},{16,8},{24,16},{0,24},{9,1},{17,9},{25,17},{1,25},{10,2},{18... | collective-permute-start | bytes 344072 | tf_op jit(solution)/shard_map/ppermute | solution.py:25
  46.6 4.7 %collective-permute-start.17 = (f32[16,384]{1,0:T(8,128)S(1)}, f32[16,384]{1,0:T(8,128)S(1)}, u32[]{:S(2)}, u32[]{:S(2)}) collective-permute-start(f32[16,384]{1,0:T(8,128)S(1)} %get-tuple-element.36), channel_id=1, source_target_pairs={{0,4},{1,5},{2,6},{3,7},{4,0},{5,1},{6,2},{7,3},{8,12},{9,13},{10,... | collective-permute-start | bytes 73736 | tf_op jit(solution)/shard_map/ppermute | solution.py:38
  51.3 4.1 %collective-permute-start.18 = (f32[32,384]{1,0:T(8,128)S(1)}, f32[32,384]{1,0:T(8,128)S(1)}, u32[]{:S(2)}, u32[]{:S(2)}) collective-permute-start(f32[32,384]{1,0:T(8,128)S(1)} %pad_maximum_fusion.7), channel_id=1, source_target_pairs={{0,2},{1,3},{2,0},{3,1},{4,6},{5,7},{6,4},{7,5},{8,10},{9,11},{10,... | collective-permute-start | bytes 147464 | tf_op jit(solution)/shard_map/ppermute | solution.py:38
  55.4 1.9 %collective-permute-start.19 = (f32[64,384]{1,0:T(8,128)S(1)}, f32[64,384]{1,0:T(8,128)S(1)}, u32[]{:S(2)}, u32[]{:S(2)}) collective-permute-start(f32[64,384]{1,0:T(8,128)S(1)} %pad_maximum_fusion.5), channel_id=1, source_target_pairs={{0,8},{1,9},{2,10},{3,11},{4,12},{5,13},{6,14},{7,15},{8,0},{9,1},... | collective-permute-start | bytes 294920 | tf_op jit(solution)/shard_map/ppermute | solution.py:38
  55.5 6.2 %collective-permute-start.13 = (bf16[4,56,384]{2,1,0:T(8,128)(2,1)S(1)}, bf16[4,56,384]{2,1,0:T(8,128)(2,1)S(1)}, u32[]{:S(2)}, u32[]{:S(2)}) collective-permute-start(bf16[4,56,384]{2,1,0:T(8,128)(2,1)S(1)} %get-tuple-element.33), channel_id=1, source_target_pairs={{0,8},{8,16},{16,24},{24,0},{1,9},{9,17},{17,25},{25,1},{2,10},{10... | collective-permute-start | bytes 516104 | tf_op jit(solution)/shard_map/ppermute | solution.py:24
  56.0 5.7 %collective-permute-start.14 = (bf16[4,56,384]{2,1,0:T(8,128)(2,1)S(1)}, bf16[4,56,384]{2,1,0:T(8,128)(2,1)S(1)}, u32[]{:S(2)}, u32[]{:S(2)}) collective-permute-start(bf16[4,56,384]{2,1,0:T(8,128)(2,1)S(1)} %get-tuple-element.34), channel_id=1, source_target_pairs={{8,0},{16,8},{24,16},{0,24},{9,1},{17,9},{25,17},{1,25},{10,2},{18... | collective-permute-start | bytes 516104 | tf_op jit(solution)/shard_map/ppermute | solution.py:25
  58.2 4.2 %collective-permute-start.20 = (f32[32,384]{1,0:T(8,128)S(1)}, f32[32,384]{1,0:T(8,128)S(1)}, u32[]{:S(2)}, u32[]{:S(2)}) collective-permute-start(f32[32,384]{1,0:T(8,128)S(1)} %pad_maximum_fusion.8), channel_id=1, source_target_pairs={{0,1},{1,0},{2,3},{3,2},{4,5},{5,4},{6,7},{7,6},{8,9},{9,8},{10,11... | collective-permute-start | bytes 147464 | tf_op jit(solution)/shard_map/ppermute | solution.py:38
  62.3 5.2 %collective-permute-start.21 = (f32[16,384]{1,0:T(8,128)S(1)}, f32[16,384]{1,0:T(8,128)S(1)}, u32[]{:S(2)}, u32[]{:S(2)}) collective-permute-start(f32[16,384]{1,0:T(8,128)S(1)} %slice_add_fusion), channel_id=1, source_target_pairs={{0,16},{1,17},{2,18},{3,19},{4,20},{5,21},{6,22},{7,23},{8,24},{9,... | collective-permute-start | bytes 73736 | tf_op jit(solution)/shard_map/ppermute | solution.py:38
  62.7 7.5 %collective-permute-start.15 = (bf16[32,4,384]{2,1,0:T(4,128)(2,1)S(1)}, bf16[32,4,384]{2,1,0:T(4,128)(2,1)S(1)}, u32[]{:S(2)}, u32[]{:S(2)}) collective-permute-start(bf16[32,4,384]{2,1,0:T(4,128)(2,1)S(1)} %get-tuple-element.41), channel_id=1, source_target_pairs={{0,1},{1,2},{2,3},{3,4},{4,5},{5,6},{6,7},{7,0},{8,9},{9,10},{10,1... | collective-permute-start | bytes 294920 | tf_op jit(solution)/shard_map/ppermute | solution.py:24
  62.8 7.5 %collective-permute-start.16 = (bf16[32,4,384]{2,1,0:T(4,128)(2,1)S(1)}, bf16[32,4,384]{2,1,0:T(4,128)(2,1)S(1)}, u32[]{:S(2)}, u32[]{:S(2)}) collective-permute-start(bf16[32,4,384]{2,1,0:T(4,128)(2,1)S(1)} %get-tuple-element.42), channel_id=1, source_target_pairs={{1,0},{2,1},{3,2},{4,3},{5,4},{6,5},{7,6},{0,7},{9,8},{10,9},{11,1... | collective-permute-start | bytes 294920 | tf_op jit(solution)/shard_map/ppermute | solution.py:25

commit v6 on v5

--- a/solution.py
+++ b/solution.py
@@ -10,61 +10,40 @@
 OV = 4
 ITERS = 2
 AHEAD = 2
+ORDER = range
 LANES = 128
-AXES = ("grp", "mem")
 EXACT = lax.Precision.HIGHEST
 F32 = jnp.float32
 BF16 = jnp.bfloat16
 
 
+def shifted(value, axis, distance):
+    count = lax.axis_size(axis)
+    return lax.ppermute(value, axis, [(i, (i + distance) % count) for i in range(count)])
+
+
 def edges(low_edge, high_edge, axis):
-    count = lax.axis_size(axis)
+    return beyond(shifted(high_edge, axis, 1), shifted(low_edge, axis, -1), axis)
+
+
+def beyond(low, high, axis):
     index = lax.axis_index(axis)
-    up = [(i, (i + 1) % count) for i in range(count)]
-    low = lax.ppermute(high_edge, axis, up)
-    high = lax.ppermute(low_edge, axis, [(j, i) for i, j in up])
-    return jnp.where(index == 0, 0, low), jnp.where(index == count - 1, 0, high)
-
-
-def masks():
-    members, groups = lax.axis_size("mem"), lax.axis_size("grp")
-    mem_bits = [1 << k for k in range(members.bit_length() - 1)]
-    grp_bits = [members << k for k in range(groups.bit_length() - 1)]
-    return mem_bits[:0:-1] + grp_bits[:1], mem_bits[:1] + grp_bits[1:]
-
-
-def swap(value, bit):
-    total = lax.axis_size("grp") * lax.axis_size("mem")
-    return lax.ppermute(value, AXES, [(i, i ^ bit) for i in range(total)])
-
-
-def gathered(value, bits):
-    for bit in bits:
-        value = jnp.concatenate([value, swap(value, bit)], axis=0)
-    return value
-
-
-def summed_shares(inverse_rows, sources, modes):
-    shares = lax.dot_general(
-        inverse_rows,
-        sources,
-        (((0,), (0,)), ((), ())),
-        precision=EXACT,
-        preferred_element_type=F32,
-    )
-    sum_bits = masks()[1]
-    me = lax.axis_index(AXES)
-    targets = [0]
-    for bit in sum_bits[::-1]:
-        targets = targets + [t ^ bit for t in targets]
-    parts = [
-        lax.dynamic_slice_in_dim(shares, (me ^ target) * modes, modes, 0) for target in targets
-    ]
-    for bit in sum_bits:
-        half = len(parts) // 2
-        got = swap(jnp.concatenate(parts[half:], axis=0), bit)
-        parts = [part + got[k * modes : (k + 1) * modes] for k, part in enumerate(parts[:half])]
-    return parts[0]
+    last = lax.axis_size(axis) - 1
+    return jnp.where(index == 0, 0, low), jnp.where(index == last, 0, high)
+
+
+def summed_over_members(shares):
+    members = lax.axis_size("mem")
+    sizes = [2] * (members.bit_length() - 1)
+    shares = shares.reshape(*sizes, shares.shape[0] // members, shares.shape[1])
+    for k in ORDER(len(sizes)):
+        bit = lax.axis_index("mem") >> k & 1
+        axis = len(sizes) - 1 - k
+        keep = lax.dynamic_slice_in_dim(shares, bit, 1, axis)
+        send = lax.dynamic_slice_in_dim(shares, 1 - bit, 1, axis)
+        pairs = [(i, i ^ 1 << k) for i in range(members)]
+        shares = keep + lax.ppermute(send, "mem", pairs)
+    return shares.reshape(shares.shape[-2:])
 
 
 def split(values):
@@ -93,12 +72,13 @@
     return one + (two[modes:] + three[2 * modes :]) + (two[:modes] + three[modes : 2 * modes]) + three[:modes]
 
 
-def survey(block, basis_ref, first, low_ref, high_ref, side_ref):
+def survey(block, basis_ref, first, down_ref, up_ref, side_ref):
     rows, own_y, columns = block.shape
+    count = OV * own_y
     if first == 0:
-        low_ref[...] = block[:OV].astype(BF16)
+        down_ref[:count] = block[:OV].reshape(count, columns).astype(BF16)
     if first + rows == side_ref.shape[0]:
-        high_ref[...] = block[rows - OV :].astype(BF16)
+        up_ref[:count] = block[rows - OV :].reshape(count, columns).astype(BF16)
     left = lax.broadcasted_iota(jnp.int32, (rows, 2 * OV, columns), 1) < OV
     side_ref[first : first + rows] = jnp.where(
         left, block[:, : 2 * OV], block[:, own_y - 2 * OV :]
@@ -106,8 +86,19 @@
     return restrict(basis_ref, first, block)
 
 
-def start_kernel(rhs_ref, basis_ref, low_ref, high_ref, side_ref, sum_ref, held, arrived):
-    own_x = held.shape[0]
+def finish(total, start, down_ref, up_ref, sum_ref):
+    sum_ref[...] = total
+    parts = jnp.concatenate(split(total), axis=0)
+    end = start + parts.shape[0]
+    down_ref[start:end] = parts
+    up_ref[start:end] = parts
+    return end
+
+
+def start_kernel(
+    rhs_ref, basis_ref, inverse_ref, down_ref, up_ref, side_ref, sum_ref, held, arrived
+):
+    own_x, own_y, columns = held.shape
     copies = [
         pltpu.make_async_copy(
             rhs_ref.at[pl.ds(first, OV)], held.at[pl.ds(first, OV)], arrived.at[first // OV]
@@ -116,12 +107,26 @@
     ]
     for copy in copies:
         copy.start()
+
+    groups = lax.axis_size("grp")
+    width = inverse_ref.shape[1] // groups
+    modes = inverse_ref.shape[0]
+    start = OV * own_y + 3 * modes
+    for ref, step in ((up_ref, 1), (down_ref, groups - 1)):
+        group = lax.rem(lax.axis_index("grp") + step, groups)
+        wanted = inverse_ref[:, pl.ds(pl.multiple_of(group * width, width), width)]
+        parts = jnp.concatenate(split(wanted), axis=1)
+        for k in range(3 * width // columns):
+            ref[start + k * modes : start + (k + 1) * modes] = parts[
+                :, k * columns : (k + 1) * columns
+            ]
+
     total = jnp.zeros(sum_ref.shape, F32)
     for first in range(0, own_x, OV):
         copies[first // OV].wait()
         block = held[first : first + OV]
-        total = total + survey(block, basis_ref, first, low_ref, high_ref, side_ref)
-    sum_ref[...] = total
+        total = total + survey(block, basis_ref, first, down_ref, up_ref, side_ref)
+    finish(total, OV * own_y, down_ref, up_ref, sum_ref)
 
 
 def residual_kernel(
@@ -134,8 +139,8 @@
     heat_ref,
     basis_ref,
     out_ref,
-    low_ref,
-    high_ref,
+    down_ref,
+    up_ref,
     side_ref,
     sum_ref,
 ):
@@ -172,8 +177,8 @@
         if index % OV == OV - 1:
             first = index + 1 - OV
             block = out_ref[first : first + OV]
-            total = total + survey(block, basis_ref, first, low_ref, high_ref, side_ref)
-    sum_ref[...] = total
+            total = total + survey(block, basis_ref, first, down_ref, up_ref, side_ref)
+    finish(total, OV * own_y, down_ref, up_ref, sum_ref)
 
 
 def fine_kernel(fetch, inverse_ref, block_ref, low_ref, high_ref, side_ref, out_ref, *refs):
@@ -288,41 +293,95 @@
     in_vmem = pl.BlockSpec(memory_space=pltpu.VMEM)
     in_hbm = pl.BlockSpec(memory_space=pltpu.HBM)
 
-    survey_shapes = [
-        shape_of((OV, own_y, columns), BF16),
-        shape_of((OV, own_y, columns), BF16),
-        shape_of((own_x, 2 * OV, columns), BF16),
-        shape_of((modes, columns), F32),
-    ]
+    members, groups = lax.axis_size("mem"), lax.axis_size("grp")
+    width = members * modes
+    edge_rows = OV * own_y
+    sum_rows = 3 * modes
+    inverse_rows = 3 * width // columns * modes
+
+    def survey_shapes(rows):
+        return [
+            shape_of((rows, columns), BF16),
+            shape_of((rows, columns), BF16),
+            shape_of((own_x, 2 * OV, columns), BF16),
+            shape_of((modes, columns), F32),
+        ]
 
     def surveyed_start():
         return pl.pallas_call(
             start_kernel,
-            in_specs=[in_hbm, in_vmem],
+            in_specs=[in_hbm, in_vmem, in_vmem],
             out_specs=[in_vmem] * 4,
-            out_shape=survey_shapes,
+            out_shape=survey_shapes(edge_rows + sum_rows + inverse_rows),
             scratch_shapes=[
                 pltpu.VMEM(rhs.shape, F32),
                 pltpu.SemaphoreType.DMA((own_x // OV,)),
             ],
             compiler_params=params(8),
-        )(pltpu.with_memory_space_constraint(rhs, pltpu.HBM), basis)
+        )(pltpu.with_memory_space_constraint(rhs, pltpu.HBM), basis, coarse_inverse)
 
     def surveyed_residual(now, around):
         return pl.pallas_call(
             residual_kernel,
             in_specs=[in_vmem] * 8,
             out_specs=[in_vmem] * 5,
-            out_shape=[shape_of(rhs.shape, F32)] + survey_shapes,
+            out_shape=[shape_of(rhs.shape, F32)] + survey_shapes(edge_rows + sum_rows),
             compiler_params=params(16),
         )(rhs, now, *around, heat, basis)
 
-    def window_margins(low_edge, high_edge, sides):
-        low, high = edges(low_edge, high_edge, "grp")
+    def added(parts):
+        high, middle, low = (part.astype(F32) for part in parts)
+        return high + middle + low
+
+    def sums_in(message):
+        return added(jnp.split(message[edge_rows : edge_rows + sum_rows], 3, axis=0))
+
+    def inverse_in(message):
+        pieces = message[edge_rows + sum_rows :]
+        pieces = jnp.concatenate(jnp.split(pieces, inverse_rows // modes, axis=0), axis=1)
+        return added(jnp.split(pieces, 3, axis=1))
+
+    def inverse_for(distance):
+        group = (lax.axis_index("grp") + distance) % groups
+        return lax.dynamic_slice_in_dim(coarse_inverse, group * width, width, 1)
+
+    def exchanged(down, up, sides, restricted, inverse):
+        first = inverse is None
+        from_below, from_above = shifted(up, "grp", 1), shifted(down, "grp", -1)
+        sums = [restricted]
+        rows = [inverse_for(0)]
+        for distance in range(2, groups - 1):
+            if first:
+                message = jnp.concatenate([restricted, inverse_for(distance)], axis=1)
+            else:
+                message = restricted
+            message = shifted(message, "grp", distance)
+            sums.append(message[:, :columns])
+            rows.append(message[:, columns:])
+        for message in (from_below, from_above):
+            sums.append(sums_in(message))
+            if first:
+                rows.append(inverse_in(message))
+        if first:
+            inverse = jnp.concatenate(rows, axis=0)
+        low, high = beyond(from_below[:edge_rows], from_above[:edge_rows], "grp")
+        low = low.reshape(OV, own_y, columns)
+        high = high.reshape(OV, own_y, columns)
         corners = [jnp.concatenate([m[:, :OV], m[:, -OV:]], axis=1) for m in (low, high)]
         sides = jnp.concatenate([corners[0], sides, corners[1]], axis=0)
         left, right = edges(sides[:, :OV], sides[:, OV:], "mem")
-        return low, high, jnp.concatenate([left, right], axis=1)
+        margins = low, high, jnp.concatenate([left, right], axis=1)
+        return margins, jnp.concatenate(sums, axis=0), inverse
+
+    def coarse_solve(inverse, sums):
+        shares = lax.dot_general(
+            inverse,
+            sums,
+            (((0,), (0,)), ((), ())),
+            precision=EXACT,
+            preferred_element_type=F32,
+        )
+        return summed_over_members(shares)
 
     held = (own_x * span_y, local)
 
@@ -374,21 +433,16 @@
             compiler_params=params(16),
         )(solved, basis, lifted, now if last else heat)
 
-    gather_bits = masks()[0]
-    *to_send, restricted = surveyed_start()
-    sources = gathered(jnp.concatenate([restricted, coarse_inverse], axis=1), gather_bits)
-    inverse_rows = sources[:, columns:]
-    margins = window_margins(*to_send)
+    margins, sums, inverse = exchanged(*surveyed_start(), None)
     solved, rows = fine(local_inverse, rhs, margins)
-    lifted = summed_shares(inverse_rows, sources[:, :columns], modes)
+    lifted = coarse_solve(inverse, sums)
     now, first, final, left, right = updated(solved, lifted, None)
     for sweep in range(ITERS - 1):
         around = edges(first, final, "grp") + edges(left, right, "mem")
-        residual, *to_send, restricted = surveyed_residual(now, around)
-        sources = gathered(restricted, gather_bits)
-        margins = window_margins(*to_send)
+        residual, *found = surveyed_residual(now, around)
+        margins, sums, inverse = exchanged(*found, inverse)
         solved, rows = fine(rows, residual, margins)
-        lifted = summed_shares(inverse_rows, sources, modes)
+        lifted = coarse_solve(inverse, sums)
         now = updated(solved, lifted, now)[0]
     return now
 

time: 76.1 us -> 68 us (0.89)
  waiting for transfers between devices: 28.2 us -> 16.7 us
  starting transfers between devices: 28.1 us -> 31.5 us
  matrix products: 1.66 us -> 0.74 us
  local copies, waits for them, and re-layouts: 1.41 us -> 2.22 us
    ppermute x22 -> x20, waiting for transfers between devices: 28.2 us -> 16.7 us  [the longest x14 15 us: shifted(): lax.ppermute(value, axis, [(i, (i + distance) % count) for i in range(cou...]
    ppermute x22 -> x20, starting transfers between devices: 28.1 us -> 31.5 us  [the longest x14 23.1 us: shifted(): lax.ppermute(value, axis, [(i, (i + distance) % count) for i in range(cou...]
    dot_general x2, matrix products: 1.66 us -> 0.74 us  [coarse_solve(): lax.dot_general(inverse, sums, (((0,), (0,)), ((), ())), precision=EXACT,...]
    unnamed x11 -> x12, local copies, waits for them, and re-layouts: 0.95 us -> 1.71 us
  transfers between devices with their start and end apart: 22 -> 20, of which waited for: 13 -> 14; matrix products, arithmetic and copies ran while one was open for 2% -> 1% of each run, Pallas kernels for 7% -> 14%
where the time goes in v6:
time: 68 us; the launch traced here: 67.8 us
  starting transfers between devices  31.5 us (46%)
  waiting for transfers between devices  16.7 us (25%)
  Pallas kernels  15.4 us (23%)
  local copies, waits for them, and re-layouts  2.22 us (3%)
  matrix products  0.74 us (1%)
  other arithmetic  0.71 us (1%)
    ppermute x14, starting transfers between devices, shifted(): lax.ppermute(value, axis, [(i, (i + distance) % count) for i in range(cou...  23.1 us
    ppermute x14, waiting for transfers between devices, shifted(): lax.ppermute(value, axis, [(i, (i + distance) % count) for i in range(cou...  15 us
    pallas_call x2, Pallas kernels, fine(): pl.pallas_call(functools.partial(fine_kernel, fetch), in_specs=[in_hbm if...  9.17 us
    ppermute x6, starting transfers between devices, summed_over_members(): shares = keep + lax.ppermute(send, 'mem', pairs)  8.38 us
    pallas_call x2, Pallas kernels, updated(): pl.pallas_call(functools.partial(update_kernel, last), in_specs=[in_vmem]...  2.33 us
    pallas_call x1, Pallas kernels, surveyed_start(): pl.pallas_call(start_kernel, in_specs=[in_hbm, in_vmem, in_vmem], out_spe...  2.05 us
    pallas_call x1, Pallas kernels, surveyed_residual(): pl.pallas_call(residual_kernel, in_specs=[in_vmem] * 8, out_specs=[in_vme...  1.81 us
    unnamed x12, local copies, waits for them, and re-layouts  1.71 us
  transfers between devices with their start and end apart: 20, of which 14 were waited for; matrix products, arithmetic and copies ran while one was open for 1% of the time, Pallas kernels for 14%

profile of v6, /device:TPU:0, one launch (start us, length us, event | category | flops | bytes accessed | tf_op | source)
XLA Modules:
  0.0 67.8 jit_solution(8244728254608493810)
XLA Ops:
  0.0 0.9 %copy-done.1 = f32[24,56,16]{1,2,0:T(8,128)S(1)} copy-done((f32[24,56,16]{1,2,0:T(8,128)S(1)}, f32[24,56,16]{1,2,0:T(8,128)}, u32[]{:S(2)}) %copy-start.1) | copy-done | bytes 86040
  0.9 0.8 %copy-done.3 = f32[16,512]{1,0:T(8,128)S(1)} copy-done((f32[16,512]{1,0:T(8,128)S(1)}, f32[16,512]{1,0:T(8,128)}, u32[]{:S(2)}) %copy-start.3) | copy-done | bytes 32792
  1.7 2.1 %shard_map.55 = (bf16[288,384]{1,0:T(8,128)(2,1)S(1)}, bf16[288,384]{1,0:T(8,128)(2,1)S(1)}, bf16[24,8,384]{2,1,0:T(8,128)(2,1)S(1)}, f32[16,384]{1,0:T(8,128)S(1)}) custom-call(f32[24,56,384]{2,1,0:T(8,128)} %rhs_ref.3, f32[24,16,56]{2,1,0:T(8,128)S(1)} %bitcast.11, f32[16,512]{1,0:T(8,128)S(1)} %copy-done.3), custom_call_target="tpu_custom_call" | custom-call | tf_op jit(solution)/shard_map/pallas_call | solution.py:311
  4.3 2.6 %collective-permute-start.4 = (f32[16,512]{1,0:T(8,128)S(1)}, f32[16,512]{1,0:T(8,128)S(1)}, u32[]{:S(2)}, u32[]{:S(2)}) collective-permute-start(f32[16,512]{1,0:T(8,128)S(1)} %pad_maximum_fusion.2), channel_id=1, source_target_pairs={{0,16},{8,24},{16,0},{24,8},{1,17},{9,25},{17,1},{25,9},{2,18},{10... | collective-permute-start | bytes 98312 | tf_op jit(solution)/shard_map/ppermute | solution.py:22
  6.9 1.4 %collective-permute-start.1 = (bf16[288,384]{1,0:T(8,128)(2,1)S(1)}, bf16[288,384]{1,0:T(8,128)(2,1)S(1)}, u32[]{:S(2)}, u32[]{:S(2)}) collective-permute-start(bf16[288,384]{1,0:T(8,128)(2,1)S(1)} %get-tuple-element.22), channel_id=1, source_target_pairs={{0,24},{8,0},{16,8},{24,16},{1,25},{9,1},{17,9},{25,17},{2,26},{10... | collective-permute-start | bytes 663560 | tf_op jit(solution)/shard_map/ppermute | solution.py:22
  8.3 0.8 %collective-permute-done.4 = f32[16,512]{1,0:T(8,128)S(1)} collective-permute-done((f32[16,512]{1,0:T(8,128)S(1)}, f32[16,512]{1,0:T(8,128)S(1)}, u32[]{:S(2)}, u32[]{:S(2)}) %collective-permute-start.4) | collective-permute-done | bytes 32800 | tf_op jit(solution)/shard_map/ppermute | solution.py:22
  9.2 1.0 %collective-permute-done = bf16[288,384]{1,0:T(8,128)(2,1)S(1)} collective-permute-done((bf16[288,384]{1,0:T(8,128)(2,1)S(1)}, bf16[288,384]{1,0:T(8,128)(2,1)S(1)}, u32[]{:S(2)}, u32[]{:S(2)}) %collective-permute-start) | collective-permute-done | bytes 221216 | tf_op jit(solution)/shard_map/ppermute | solution.py:22
  10.2 2.5 %collective-permute-done.1 = bf16[288,384]{1,0:T(8,128)(2,1)S(1)} collective-permute-done((bf16[288,384]{1,0:T(8,128)(2,1)S(1)}, bf16[288,384]{1,0:T(8,128)(2,1)S(1)}, u32[]{:S(2)}, u32[]{:S(2)}) %collective-permute-start.1) | collective-permute-done | bytes 221216 | tf_op jit(solution)/shard_map/ppermute | solution.py:22
  13.1 1.6 %collective-permute-start.5 = (f32[2,2,1,16,384]{4,3,2,1,0:T(8,128)S(1)}, f32[2,2,1,16,384]{4,3,2,1,0:T(8,128)S(1)}, u32[]{:S(2)}, u32[]{:S(2)}) collective-permute-start(f32[2,2,1,16,384]{4,3,2,1,0:T(8,128)S(1)} %constant_dynamic-slice_fusion.5), channel_id=1, source_target_pairs={{0,1},{1,0},{2,3},{3,2},{4,5},{5,4},{6,7},{7,6},{8,9},{9,8},{10,11... | collective-permute-start | bytes 294920 | tf_op jit(solution)/shard_map/ppermute | solution.py:45
  14.9 0.6 collective-permute-start.2
  15.5 4.2 %collective-permute-start.3 = (bf16[32,4,384]{2,1,0:T(4,128)(2,1)S(1)}, bf16[32,4,384]{2,1,0:T(4,128)(2,1)S(1)}, u32[]{:S(2)}, u32[]{:S(2)}) collective-permute-start(bf16[32,4,384]{2,1,0:T(4,128)(2,1)S(1)} %get-tuple-element.40), channel_id=1, source_target_pairs={{0,7},{1,0},{2,1},{3,2},{4,3},{5,4},{6,5},{7,6},{8,15},{9,8},{10,9... | collective-permute-start | bytes 294920 | tf_op jit(solution)/shard_map/ppermute | solution.py:22
  19.7 0.6 collective-permute-start.6
  20.4 2.7 %collective-permute-done.2 = bf16[32,4,384]{2,1,0:T(4,128)(2,1)S(1)} collective-permute-done((bf16[32,4,384]{2,1,0:T(4,128)(2,1)S(1)}, bf16[32,4,384]{2,1,0:T(4,128)(2,1)S(1)}, u32[]{:S(2)}, u32[]{:S(2)}) %collective-permute-start.2) | collective-permute-done | bytes 98336 | tf_op jit(solution)/shard_map/ppermute | solution.py:22
  24.0 2.3 %collective-permute-start.7 = (f32[1,1,1,16,384]{4,3,2,1,0:T(8,128)S(1)}, f32[1,1,1,16,384]{4,3,2,1,0:T(8,128)S(1)}, u32[]{:S(2)}, u32[]{:S(2)}) collective-permute-start(f32[1,1,1,16,384]{4,3,2,1,0:T(8,128)S(1)} %constant_dynamic-slice_fusion.3), channel_id=1, source_target_pairs={{0,4},{1,5},{2,6},{3,7},{4,0},{5,1},{6,2},{7,3},{8,12},{9,13},{10,... | collective-permute-start | bytes 73736 | tf_op jit(solution)/shard_map/ppermute | solution.py:45
  26.2 5.5 %shard_map.56 = (f32[24,56,384]{2,1,0:T(8,128)S(1)}, bf16[1536,2048]{1,0:T(8,128)(2,1)S(1)}) custom-call(bf16[2048,2048]{1,0:T(8,128)(2,1)} %inverse_ref.3, f32[24,56,384]{2,1,0:T(8,128)S(1)} %copy-done, bf16[4,56,384]{2,1,0:T(8,128)(2,1)S(1)} %bitcast.20, bf16[4,56,384]{2,1,0:T(8,128)(2,1)S(1)} %bitcast.22, bf16[32,8,384]{2,1,0:T(8,128)(2,1)S(1)} %pad_maximum_fusion.side_ref), custom_call_target="tpu_custom_call" | custom-call | flops 2415919104 | bytes 6291456 | tf_op jit(solution)/shard_map/pallas_call | solution.py:400
  32.0 0.6 shard_map.57
  32.6 1.2 %collective-permute-start.10 = (f32[6,4,512]{2,1,0:T(4,128)S(1)}, f32[6,4,512]{2,1,0:T(4,128)S(1)}, u32[]{:S(2)}, u32[]{:S(2)}) collective-permute-start(f32[6,4,512]{2,1,0:T(4,128)S(1)} %get-tuple-element.30), channel_id=1, source_target_pairs={{0,1},{1,2},{2,3},{3,4},{4,5},{5,6},{6,7},{7,0},{8,9},{9,10},{10,1... | collective-permute-start | bytes 147464 | tf_op jit(solution)/shard_map/ppermute | solution.py:22
  33.8 3.6 %collective-permute-start.11 = (f32[6,4,512]{2,1,0:T(4,128)S(1)}, f32[6,4,512]{2,1,0:T(4,128)S(1)}, u32[]{:S(2)}, u32[]{:S(2)}) collective-permute-start(f32[6,4,512]{2,1,0:T(4,128)S(1)} %get-tuple-element.31), channel_id=1, source_target_pairs={{0,7},{1,0},{2,1},{3,2},{4,3},{5,4},{6,5},{7,6},{8,15},{9,8},{10,9... | collective-permute-start | bytes 147464 | tf_op jit(solution)/shard_map/ppermute | solution.py:22
  37.4 1.7 %collective-permute-start.9 = (f32[1,56,512]{2,1,0:T(8,128)S(1)}, f32[1,56,512]{2,1,0:T(8,128)S(1)}, u32[]{:S(2)}, u32[]{:S(2)}) collective-permute-start(f32[1,56,512]{2,1,0:T(8,128)S(1)} %get-tuple-element.29), channel_id=1, source_target_pairs={{0,24},{8,0},{16,8},{24,16},{1,25},{9,1},{17,9},{25,17},{2,26},{10... | collective-permute-start | bytes 344072 | tf_op jit(solution)/shard_map/ppermute | solution.py:22
  39.5 2.1 %collective-permute-done.8 = f32[1,56,512]{2,1,0:T(8,128)S(1)} collective-permute-done((f32[1,56,512]{2,1,0:T(8,128)S(1)}, f32[1,56,512]{2,1,0:T(8,128)S(1)}, u32[]{:S(2)}, u32[]{:S(2)}) %collective-permute-start.8) | collective-permute-done | bytes 114720 | tf_op jit(solution)/shard_map/ppermute | solution.py:22
  41.7 1.8 %shard_map.58 = (f32[24,56,384]{2,1,0:T(8,128)S(1)}, bf16[272,384]{1,0:T(8,128)(2,1)S(1)}, bf16[272,384]{1,0:T(8,128)(2,1)S(1)}, bf16[24,8,384]{2,1,0:T(8,128)(2,1)S(1)}, f32[16,384]{1,0:T(8,128)S(1)}) custom-call(f32[24,56,384]{2,1,0:T(8,128)S(1)} %copy-done, f32[24,56,384]{2,1,0:T(8,128)S(1)} %get-tuple-element.27.now_ref.extra_ref, ...), custom_call_target="tpu_custom_call" | custom-call | tf_op jit(solution)/shard_map/pallas_call | solution.py:324
  43.5 1.1 %collective-permute-start.12 = (bf16[272,384]{1,0:T(8,128)(2,1)S(1)}, bf16[272,384]{1,0:T(8,128)(2,1)S(1)}, u32[]{:S(2)}, u32[]{:S(2)}) collective-permute-start(bf16[272,384]{1,0:T(8,128)(2,1)S(1)} %get-tuple-element.33), channel_id=1, source_target_pairs={{0,8},{8,16},{16,24},{24,0},{1,9},{9,17},{17,25},{25,1},{2,10},{10... | collective-permute-start | bytes 626696 | tf_op jit(solution)/shard_map/ppermute | solution.py:22
  44.6 1.1 %collective-permute-start.16 = (f32[16,384]{1,0:T(8,128)S(1)}, f32[16,384]{1,0:T(8,128)S(1)}, u32[]{:S(2)}, u32[]{:S(2)}) collective-permute-start(f32[16,384]{1,0:T(8,128)S(1)} %get-tuple-element.36), channel_id=1, source_target_pairs={{0,16},{8,24},{16,0},{24,8},{1,17},{9,25},{17,1},{25,9},{2,18},{10... | collective-permute-start | bytes 73736 | tf_op jit(solution)/shard_map/ppermute | solution.py:22
  46.0 3.3 %collective-permute-done.12 = bf16[272,384]{1,0:T(8,128)(2,1)S(1)} collective-permute-done((bf16[272,384]{1,0:T(8,128)(2,1)S(1)}, bf16[272,384]{1,0:T(8,128)(2,1)S(1)}, u32[]{:S(2)}, u32[]{:S(2)}) %collective-permute-start.12) | collective-permute-done | bytes 208928 | tf_op jit(solution)/shard_map/ppermute | solution.py:22
  49.3 0.7 collective-permute-done.13
  50.7 2.1 %collective-permute-start.14 = (bf16[32,4,384]{2,1,0:T(4,128)(2,1)S(1)}, bf16[32,4,384]{2,1,0:T(4,128)(2,1)S(1)}, u32[]{:S(2)}, u32[]{:S(2)}) collective-permute-start(bf16[32,4,384]{2,1,0:T(4,128)(2,1)S(1)} %get-tuple-element.37), channel_id=1, source_target_pairs={{0,1},{1,2},{2,3},{3,4},{4,5},{5,6},{6,7},{7,0},{8,9},{9,10},{10,1... | collective-permute-start | bytes 294920 | tf_op jit(solution)/shard_map/ppermute | solution.py:22
  52.8 2.7 %collective-permute-start.15 = (bf16[32,4,384]{2,1,0:T(4,128)(2,1)S(1)}, bf16[32,4,384]{2,1,0:T(4,128)(2,1)S(1)}, u32[]{:S(2)}, u32[]{:S(2)}) collective-permute-start(bf16[32,4,384]{2,1,0:T(4,128)(2,1)S(1)} %get-tuple-element.38), channel_id=1, source_target_pairs={{0,7},{1,0},{2,1},{3,2},{4,3},{5,4},{6,5},{7,6},{8,15},{9,8},{10,9... | collective-permute-start | bytes 294920 | tf_op jit(solution)/shard_map/ppermute | solution.py:22
  56.0 3.0 %collective-permute-start.18 = (f32[2,1,1,16,384]{4,3,2,1,0:T(8,128)S(1)}, f32[2,1,1,16,384]{4,3,2,1,0:T(8,128)S(1)}, u32[]{:S(2)}, u32[]{:S(2)}) collective-permute-start(f32[2,1,1,16,384]{4,3,2,1,0:T(8,128)S(1)} %constant_dynamic-slice_fusion.1), channel_id=1, source_target_pairs={{0,2},{1,3},{2,0},{3,1},{4,6},{5,7},{6,4},{7,5},{8,10},{9,11},{10,... | collective-permute-start | bytes 147464 | tf_op jit(solution)/shard_map/ppermute | solution.py:45
  59.0 1.4 %collective-permute-done.15 = bf16[32,4,384]{2,1,0:T(4,128)(2,1)S(1)} collective-permute-done((bf16[32,4,384]{2,1,0:T(4,128)(2,1)S(1)}, bf16[32,4,384]{2,1,0:T(4,128)(2,1)S(1)}, u32[]{:S(2)}, u32[]{:S(2)}) %collective-permute-start.15) | collective-permute-done | bytes 98336 | tf_op jit(solution)/shard_map/ppermute | solution.py:22
  61.2 0.8 %collective-permute-start.19 = (f32[1,1,1,16,384]{4,3,2,1,0:T(8,128)S(1)}, f32[1,1,1,16,384]{4,3,2,1,0:T(8,128)S(1)}, u32[]{:S(2)}, u32[]{:S(2)}) collective-permute-start(f32[1,1,1,16,384]{4,3,2,1,0:T(8,128)S(1)} %constant_dynamic-slice_fusion), channel_id=1, source_target_pairs={{0,4},{1,5},{2,6},{3,7},{4,0},{5,1},{6,2},{7,3},{8,12},{9,13},{10,... | collective-permute-start | bytes 73736 | tf_op jit(solution)/shard_map/ppermute | solution.py:45
  62.0 3.7 %shard_map.59.fine_ref = f32[24,56,384]{2,1,0:T(8,128)S(1)} custom-call(bf16[1536,2048]{1,0:T(8,128)(2,1)S(1)} %get-tuple-element.24.inverse_ref, f32[24,56,384]{2,1,0:T(8,128)S(1)} %get-tuple-element.32.block_ref, bf16[4,56,384]{2,1,0:T(8,128)(2,1)S(1)} %bitcast.16, bf16[4,56,384]{2,1,0:T(8,128)(2,1)S(1)} %bitcast.18, ...), custom_call_target="tpu_custom_call" | custom-call | flops 2415919104 | bytes 6291456 | tf_op jit(solution)/shard_map/pallas_call | solution.py:400
  66.0 1.7 %shard_map.60 = f32[24,56,384]{2,1,0:T(8,128)} custom-call(f32[24,56,384]{2,1,0:T(8,128)S(1)} %shard_map.59.fine_ref, f32[24,16,56]{2,1,0:T(8,128)S(1)} %bitcast.14, f32[16,384]{1,0:T(8,128)S(1)} %add_bitcast_fusion.lifted_ref, f32[24,56,384]{2,1,0:T(8,128)S(1)} %get-tuple-element.27.now_ref.extra_ref), custom_call_target="tpu_custom_call" | custom-call | tf_op jit(solution)/shard_map/pallas_call | solution.py:427
  (72 shorter events, 5.2 us)
Async XLA Ops:
  0.0 0.9 %copy-start.1 = (f32[24,56,16]{1,2,0:T(8,128)S(1)}, f32[24,56,16]{1,2,0:T(8,128)}, u32[]{:S(2)}) copy-start(f32[24,56,16]{1,2,0:T(8,128)} %param.8) | copy-start | bytes 258052
  0.9 0.8 %copy-start.3 = (f32[16,512]{1,0:T(8,128)S(1)}, f32[16,512]{1,0:T(8,128)}, u32[]{:S(2)}) copy-start(f32[16,512]{1,0:T(8,128)} %inverse_ref.2) | copy-start | bytes 98308
  1.7 2.6 %copy-start.4 = (f32[16,512]{1,0:T(8,128)S(1)}, f32[16,512]{1,0:T(8,128)}, u32[]{:S(2)}) copy-start(f32[16,512]{1,0:T(8,128)} %inverse_ref.2) | copy-start | bytes 98308
  3.7 22.5 %copy-start = (f32[24,56,384]{2,1,0:T(8,128)S(1)}, f32[24,56,384]{2,1,0:T(8,128)}, u32[]{:S(2)}) copy-start(f32[24,56,384]{2,1,0:T(8,128)} %rhs_ref.3) | copy-start | bytes 6193156
  3.8 6.4 %collective-permute-start = (bf16[288,384]{1,0:T(8,128)(2,1)S(1)}, bf16[288,384]{1,0:T(8,128)(2,1)S(1)}, u32[]{:S(2)}, u32[]{:S(2)}) collective-permute-start(bf16[288,384]{1,0:T(8,128)(2,1)S(1)} %get-tuple-element.21), channel_id=1, source_target_pairs={{0,8},{8,16},{16,24},{24,0},{1,9},{9,17},{17,25},{25,1},{2,10},{10... | collective-permute-start | bytes 663560 | tf_op jit(solution)/shard_map/ppermute | solution.py:22
  4.3 4.9 %collective-permute-start.4 = (f32[16,512]{1,0:T(8,128)S(1)}, f32[16,512]{1,0:T(8,128)S(1)}, u32[]{:S(2)}, u32[]{:S(2)}) collective-permute-start(f32[16,512]{1,0:T(8,128)S(1)} %pad_maximum_fusion.2), channel_id=1, source_target_pairs={{0,16},{8,24},{16,0},{24,8},{1,17},{9,25},{17,1},{25,9},{2,18},{10... | collective-permute-start | bytes 98312 | tf_op jit(solution)/shard_map/ppermute | solution.py:22
  6.9 5.8 %collective-permute-start.1 = (bf16[288,384]{1,0:T(8,128)(2,1)S(1)}, bf16[288,384]{1,0:T(8,128)(2,1)S(1)}, u32[]{:S(2)}, u32[]{:S(2)}) collective-permute-start(bf16[288,384]{1,0:T(8,128)(2,1)S(1)} %get-tuple-element.22), channel_id=1, source_target_pairs={{0,24},{8,0},{16,8},{24,16},{1,25},{9,1},{17,9},{25,17},{2,26},{10... | collective-permute-start | bytes 663560 | tf_op jit(solution)/shard_map/ppermute | solution.py:22
  13.1 6.6 %collective-permute-start.5 = (f32[2,2,1,16,384]{4,3,2,1,0:T(8,128)S(1)}, f32[2,2,1,16,384]{4,3,2,1,0:T(8,128)S(1)}, u32[]{:S(2)}, u32[]{:S(2)}) collective-permute-start(f32[2,2,1,16,384]{4,3,2,1,0:T(8,128)S(1)} %constant_dynamic-slice_fusion.5), channel_id=1, source_target_pairs={{0,1},{1,0},{2,3},{3,2},{4,5},{5,4},{6,7},{7,6},{8,9},{9,8},{10,11... | collective-permute-start | bytes 294920 | tf_op jit(solution)/shard_map/ppermute | solution.py:45
  14.9 8.1 %collective-permute-start.2 = (bf16[32,4,384]{2,1,0:T(4,128)(2,1)S(1)}, bf16[32,4,384]{2,1,0:T(4,128)(2,1)S(1)}, u32[]{:S(2)}, u32[]{:S(2)}) collective-permute-start(bf16[32,4,384]{2,1,0:T(4,128)(2,1)S(1)} %get-tuple-element.39), channel_id=1, source_target_pairs={{0,1},{1,2},{2,3},{3,4},{4,5},{5,6},{6,7},{7,0},{8,9},{9,10},{10,1... | collective-permute-start | bytes 294920 | tf_op jit(solution)/shard_map/ppermute | solution.py:22
  15.5 7.8 %collective-permute-start.3 = (bf16[32,4,384]{2,1,0:T(4,128)(2,1)S(1)}, bf16[32,4,384]{2,1,0:T(4,128)(2,1)S(1)}, u32[]{:S(2)}, u32[]{:S(2)}) collective-permute-start(bf16[32,4,384]{2,1,0:T(4,128)(2,1)S(1)} %get-tuple-element.40), channel_id=1, source_target_pairs={{0,7},{1,0},{2,1},{3,2},{4,3},{5,4},{6,5},{7,6},{8,15},{9,8},{10,9... | collective-permute-start | bytes 294920 | tf_op jit(solution)/shard_map/ppermute | solution.py:22
  19.7 4.2 %collective-permute-start.6 = (f32[2,1,1,16,384]{4,3,2,1,0:T(8,128)S(1)}, f32[2,1,1,16,384]{4,3,2,1,0:T(8,128)S(1)}, u32[]{:S(2)}, u32[]{:S(2)}) collective-permute-start(f32[2,1,1,16,384]{4,3,2,1,0:T(8,128)S(1)} %constant_dynamic-slice_fusion.4), channel_id=1, source_target_pairs={{0,2},{1,3},{2,0},{3,1},{4,6},{5,7},{6,4},{7,5},{8,10},{9,11},{10,... | collective-permute-start | bytes 147464 | tf_op jit(solution)/shard_map/ppermute | solution.py:45
  23.9 7.8 %copy-start.5 = (f32[24,56]{1,0:T(8,128)S(1)}, f32[24,56]{1,0:T(8,128)}, u32[]{:S(2)}) copy-start(f32[24,56]{1,0:T(8,128)} %param.6) | copy-start | bytes 16132
  23.9 8.0 %copy-start.2 = (f32[24,56,16]{1,2,0:T(8,128)S(1)}, f32[24,56,16]{1,2,0:T(8,128)}, u32[]{:S(2)}) copy-start(f32[24,56,16]{1,2,0:T(8,128)} %param.8) | copy-start | bytes 258052
  24.0 7.7 %collective-permute-start.7 = (f32[1,1,1,16,384]{4,3,2,1,0:T(8,128)S(1)}, f32[1,1,1,16,384]{4,3,2,1,0:T(8,128)S(1)}, u32[]{:S(2)}, u32[]{:S(2)}) collective-permute-start(f32[1,1,1,16,384]{4,3,2,1,0:T(8,128)S(1)} %constant_dynamic-slice_fusion.3), channel_id=1, source_target_pairs={{0,4},{1,5},{2,6},{3,7},{4,0},{5,1},{6,2},{7,3},{8,12},{9,13},{10,... | collective-permute-start | bytes 73736 | tf_op jit(solution)/shard_map/ppermute | solution.py:45
  32.6 6.8 %collective-permute-start.10 = (f32[6,4,512]{2,1,0:T(4,128)S(1)}, f32[6,4,512]{2,1,0:T(4,128)S(1)}, u32[]{:S(2)}, u32[]{:S(2)}) collective-permute-start(f32[6,4,512]{2,1,0:T(4,128)S(1)} %get-tuple-element.30), channel_id=1, source_target_pairs={{0,1},{1,2},{2,3},{3,4},{4,5},{5,6},{6,7},{7,0},{8,9},{9,10},{10,1... | collective-permute-start | bytes 147464 | tf_op jit(solution)/shard_map/ppermute | solution.py:22
  33.8 5.7 %collective-permute-start.11 = (f32[6,4,512]{2,1,0:T(4,128)S(1)}, f32[6,4,512]{2,1,0:T(4,128)S(1)}, u32[]{:S(2)}, u32[]{:S(2)}) collective-permute-start(f32[6,4,512]{2,1,0:T(4,128)S(1)} %get-tuple-element.31), channel_id=1, source_target_pairs={{0,7},{1,0},{2,1},{3,2},{4,3},{5,4},{6,5},{7,6},{8,15},{9,8},{10,9... | collective-permute-start | bytes 147464 | tf_op jit(solution)/shard_map/ppermute | solution.py:22
  37.4 4.2 %collective-permute-start.8 = (f32[1,56,512]{2,1,0:T(8,128)S(1)}, f32[1,56,512]{2,1,0:T(8,128)S(1)}, u32[]{:S(2)}, u32[]{:S(2)}) collective-permute-start(f32[1,56,512]{2,1,0:T(8,128)S(1)} %get-tuple-element.28), channel_id=1, source_target_pairs={{0,8},{8,16},{16,24},{24,0},{1,9},{9,17},{17,25},{25,1},{2,10},{10... | collective-permute-start | bytes 344072 | tf_op jit(solution)/shard_map/ppermute | solution.py:22
  37.4 4.2 %collective-permute-start.9 = (f32[1,56,512]{2,1,0:T(8,128)S(1)}, f32[1,56,512]{2,1,0:T(8,128)S(1)}, u32[]{:S(2)}, u32[]{:S(2)}) collective-permute-start(f32[1,56,512]{2,1,0:T(8,128)S(1)} %get-tuple-element.29), channel_id=1, source_target_pairs={{0,24},{8,0},{16,8},{24,16},{1,25},{9,1},{17,9},{25,17},{2,26},{10... | collective-permute-start | bytes 344072 | tf_op jit(solution)/shard_map/ppermute | solution.py:22
  43.5 5.8 %collective-permute-start.12 = (bf16[272,384]{1,0:T(8,128)(2,1)S(1)}, bf16[272,384]{1,0:T(8,128)(2,1)S(1)}, u32[]{:S(2)}, u32[]{:S(2)}) collective-permute-start(bf16[272,384]{1,0:T(8,128)(2,1)S(1)} %get-tuple-element.33), channel_id=1, source_target_pairs={{0,8},{8,16},{16,24},{24,0},{1,9},{9,17},{17,25},{25,1},{2,10},{10... | collective-permute-start | bytes 626696 | tf_op jit(solution)/shard_map/ppermute | solution.py:22
  44.6 5.5 %collective-permute-start.16 = (f32[16,384]{1,0:T(8,128)S(1)}, f32[16,384]{1,0:T(8,128)S(1)}, u32[]{:S(2)}, u32[]{:S(2)}) collective-permute-start(f32[16,384]{1,0:T(8,128)S(1)} %get-tuple-element.36), channel_id=1, source_target_pairs={{0,16},{8,24},{16,0},{24,8},{1,17},{9,25},{17,1},{25,9},{2,18},{10... | collective-permute-start | bytes 73736 | tf_op jit(solution)/shard_map/ppermute | solution.py:22
  45.6 4.4 %collective-permute-start.13 = (bf16[272,384]{1,0:T(8,128)(2,1)S(1)}, bf16[272,384]{1,0:T(8,128)(2,1)S(1)}, u32[]{:S(2)}, u32[]{:S(2)}) collective-permute-start(bf16[272,384]{1,0:T(8,128)(2,1)S(1)} %get-tuple-element.34), channel_id=1, source_target_pairs={{0,24},{8,0},{16,8},{24,16},{1,25},{9,1},{17,9},{25,17},{2,26},{10... | collective-permute-start | bytes 626696 | tf_op jit(solution)/shard_map/ppermute | solution.py:22
  50.5 5.5 %collective-permute-start.17 = (f32[2,2,1,16,384]{4,3,2,1,0:T(8,128)S(1)}, f32[2,2,1,16,384]{4,3,2,1,0:T(8,128)S(1)}, u32[]{:S(2)}, u32[]{:S(2)}) collective-permute-start(f32[2,2,1,16,384]{4,3,2,1,0:T(8,128)S(1)} %constant_dynamic-slice_fusion.2), channel_id=1, source_target_pairs={{0,1},{1,0},{2,3},{3,2},{4,5},{5,4},{6,7},{7,6},{8,9},{9,8},{10,11... | collective-permute-start | bytes 294920 | tf_op jit(solution)/shard_map/ppermute | solution.py:45
  50.7 8.3 %collective-permute-start.14 = (bf16[32,4,384]{2,1,0:T(4,128)(2,1)S(1)}, bf16[32,4,384]{2,1,0:T(4,128)(2,1)S(1)}, u32[]{:S(2)}, u32[]{:S(2)}) collective-permute-start(bf16[32,4,384]{2,1,0:T(4,128)(2,1)S(1)} %get-tuple-element.37), channel_id=1, source_target_pairs={{0,1},{1,2},{2,3},{3,4},{4,5},{5,6},{6,7},{7,0},{8,9},{9,10},{10,1... | collective-permute-start | bytes 294920 | tf_op jit(solution)/shard_map/ppermute | solution.py:22
  52.8 7.7 %collective-permute-start.15 = (bf16[32,4,384]{2,1,0:T(4,128)(2,1)S(1)}, bf16[32,4,384]{2,1,0:T(4,128)(2,1)S(1)}, u32[]{:S(2)}, u32[]{:S(2)}) collective-permute-start(bf16[32,4,384]{2,1,0:T(4,128)(2,1)S(1)} %get-tuple-element.38), channel_id=1, source_target_pairs={{0,7},{1,0},{2,1},{3,2},{4,3},{5,4},{6,5},{7,6},{8,15},{9,8},{10,9... | collective-permute-start | bytes 294920 | tf_op jit(solution)/shard_map/ppermute | solution.py:22
  56.0 5.1 %collective-permute-start.18 = (f32[2,1,1,16,384]{4,3,2,1,0:T(8,128)S(1)}, f32[2,1,1,16,384]{4,3,2,1,0:T(8,128)S(1)}, u32[]{:S(2)}, u32[]{:S(2)}) collective-permute-start(f32[2,1,1,16,384]{4,3,2,1,0:T(8,128)S(1)} %constant_dynamic-slice_fusion.1), channel_id=1, source_target_pairs={{0,2},{1,3},{2,0},{3,1},{4,6},{5,7},{6,4},{7,5},{8,10},{9,11},{10,... | collective-permute-start | bytes 147464 | tf_op jit(solution)/shard_map/ppermute | solution.py:45
  61.2 4.8 %collective-permute-start.19 = (f32[1,1,1,16,384]{4,3,2,1,0:T(8,128)S(1)}, f32[1,1,1,16,384]{4,3,2,1,0:T(8,128)S(1)}, u32[]{:S(2)}, u32[]{:S(2)}) collective-permute-start(f32[1,1,1,16,384]{4,3,2,1,0:T(8,128)S(1)} %constant_dynamic-slice_fusion), channel_id=1, source_target_pairs={{0,4},{1,5},{2,6},{3,7},{4,0},{5,1},{6,2},{7,3},{8,12},{9,13},{10,... | collective-permute-start | bytes 73736 | tf_op jit(solution)/shard_map/ppermute | solution.py:45

commit v7 on v6

--- a/solution.py
+++ b/solution.py
@@ -9,7 +9,7 @@
 
 OV = 4
 ITERS = 2
-AHEAD = 2
+HOLD = 6
 ORDER = range
 LANES = 128
 EXACT = lax.Precision.HIGHEST
@@ -96,17 +96,34 @@
 
 
 def start_kernel(
-    rhs_ref, basis_ref, inverse_ref, down_ref, up_ref, side_ref, sum_ref, held, arrived
+    rhs_ref,
+    basis_hbm,
+    inverse_hbm,
+    down_ref,
+    up_ref,
+    side_ref,
+    sum_ref,
+    held,
+    basis_ref,
+    inverse_ref,
+    arrived,
+    beside,
 ):
     own_x, own_y, columns = held.shape
+    small = [
+        pltpu.make_async_copy(inverse_hbm, inverse_ref, beside.at[0]),
+        pltpu.make_async_copy(basis_hbm, basis_ref, beside.at[1]),
+    ]
     copies = [
         pltpu.make_async_copy(
             rhs_ref.at[pl.ds(first, OV)], held.at[pl.ds(first, OV)], arrived.at[first // OV]
         )
         for first in range(0, own_x, OV)
     ]
-    for copy in copies:
+    for copy in small + copies:
         copy.start()
+    for copy in small:
+        copy.wait()
 
     groups = lax.axis_size("grp")
     width = inverse_ref.shape[1] // groups
@@ -181,28 +198,29 @@
     finish(total, OV * own_y, down_ref, up_ref, sum_ref)
 
 
-def fine_kernel(fetch, inverse_ref, block_ref, low_ref, high_ref, side_ref, out_ref, *refs):
+def hold_kernel(inverse_ref, heat_ref, order_ref, out_ref, arrived):
+    del heat_ref, order_ref
+    count = arrived.shape[0]
+    rows = out_ref.shape[0] // count
+    skipped = (inverse_ref.shape[0] - out_ref.shape[0]) // 2
+    copies = [
+        pltpu.make_async_copy(
+            inverse_ref.at[pl.ds(skipped + k * rows, rows)],
+            out_ref.at[pl.ds(k * rows, rows)],
+            arrived.at[k],
+        )
+        for k in range(count)
+    ]
+    for copy in copies:
+        copy.start()
+    for copy in copies:
+        copy.wait()
+
+
+def fine_kernel(rows_ref, block_ref, low_ref, high_ref, side_ref, out_ref, window, wide, solved):
     own_x, own_y, columns = block_ref.shape
     span_y = own_y + 2 * OV
-    copies = []
-    if fetch:
-        rows_held, window, wide, solved, arrived = refs
-        rows = solved.shape[0] // span_y
-        for first in range(0, own_x, rows):
-            count = rows * span_y
-            copies.append(
-                pltpu.make_async_copy(
-                    inverse_ref.at[pl.ds((OV + first) * span_y, count)],
-                    rows_held.at[pl.ds(first * span_y, count)],
-                    arrived.at[first // rows],
-                )
-            )
-        for copy in copies[:AHEAD]:
-            copy.start()
-    else:
-        rows_held = inverse_ref
-        window, wide, solved = refs
-        rows = solved.shape[0] // span_y
+    rows = solved.shape[0] // span_y
 
     def place(index, values):
         wide[OV : OV + own_y, :] = values
@@ -218,12 +236,8 @@
         place(OV + index, block_ref[index])
 
     for first in range(0, own_x, rows):
-        if fetch:
-            copies[first // rows].wait()
-            for copy in copies[first // rows + AHEAD : first // rows + AHEAD + 1]:
-                copy.start()
         solved[...] = product(
-            rows_held[first * span_y : (first + rows) * span_y, :], window[...]
+            rows_ref[first * span_y : (first + rows) * span_y, :], window[...]
         )
         for k in range(rows):
             out_ref[first + k] = solved[k * span_y + OV : k * span_y + OV + own_y, :]
@@ -310,15 +324,18 @@
     def surveyed_start():
         return pl.pallas_call(
             start_kernel,
-            in_specs=[in_hbm, in_vmem, in_vmem],
+            in_specs=[in_hbm] * 3,
             out_specs=[in_vmem] * 4,
             out_shape=survey_shapes(edge_rows + sum_rows + inverse_rows),
             scratch_shapes=[
                 pltpu.VMEM(rhs.shape, F32),
+                pltpu.VMEM(basis.shape, F32),
+                pltpu.VMEM(coarse_inverse.shape, F32),
                 pltpu.SemaphoreType.DMA((own_x // OV,)),
+                pltpu.SemaphoreType.DMA((2,)),
             ],
-            compiler_params=params(8),
-        )(pltpu.with_memory_space_constraint(rhs, pltpu.HBM), basis, coarse_inverse)
+            compiler_params=params(16),
+        )(*(pltpu.with_memory_space_constraint(a, pltpu.HBM) for a in (rhs, basis, coarse_inverse)))
 
     def surveyed_residual(now, around):
         return pl.pallas_call(
@@ -385,24 +402,30 @@
 
     held = (own_x * span_y, local)
 
+    def held_rows(order):
+        return pl.pallas_call(
+            hold_kernel,
+            in_specs=[in_hbm, pl.BlockSpec(memory_space=pl.ANY), pl.BlockSpec(memory_space=pl.ANY)],
+            out_specs=in_vmem,
+            out_shape=shape_of(held, BF16),
+            scratch_shapes=[pltpu.SemaphoreType.DMA((HOLD,))],
+            compiler_params=params(8),
+            cost_estimate=pl.CostEstimate(
+                flops=0, bytes_accessed=4 * held[0] * local, transcendentals=0
+            ),
+        )(pltpu.with_memory_space_constraint(local_inverse, pltpu.HBM), heat, order)
+
     def fine(rows, values, margins):
-        fetch = rows.shape != held
-        out_shape = [shape_of(rhs.shape, F32)]
-        scratch = [
-            pltpu.VMEM((local, columns), BF16),
-            pltpu.VMEM((span_y, columns), F32),
-            pltpu.VMEM((group * span_y, columns), F32),
-        ]
-        if fetch:
-            rows = pltpu.with_memory_space_constraint(rows, pltpu.HBM)
-            out_shape.append(shape_of(held, BF16))
-            scratch.append(pltpu.SemaphoreType.DMA((own_x // group,)))
-        result = pl.pallas_call(
-            functools.partial(fine_kernel, fetch),
-            in_specs=[in_hbm if fetch else in_vmem] + [in_vmem] * 4,
-            out_specs=[in_vmem] * len(out_shape),
-            out_shape=out_shape,
-            scratch_shapes=scratch,
+        return pl.pallas_call(
+            fine_kernel,
+            in_specs=[in_vmem] * 5,
+            out_specs=in_vmem,
+            out_shape=shape_of(rhs.shape, F32),
+            scratch_shapes=[
+                pltpu.VMEM((local, columns), BF16),
+                pltpu.VMEM((span_y, columns), F32),
+                pltpu.VMEM((group * span_y, columns), F32),
+            ],
             compiler_params=params(24),
             cost_estimate=pl.CostEstimate(
                 flops=2 * held[0] * local * columns,
@@ -410,7 +433,6 @@
                 transcendentals=0,
             ),
         )(rows, values, *margins)
-        return result if fetch else (*result, rows)
 
     def updated(solved, lifted, now):
         last = now is not None
@@ -433,15 +455,17 @@
             compiler_params=params(16),
         )(solved, basis, lifted, now if last else heat)
 
-    margins, sums, inverse = exchanged(*surveyed_start(), None)
-    solved, rows = fine(local_inverse, rhs, margins)
+    found = surveyed_start()
+    rows = held_rows(found[-1])
+    margins, sums, inverse = exchanged(*found, None)
+    solved = fine(rows, rhs, margins)
     lifted = coarse_solve(inverse, sums)
     now, first, final, left, right = updated(solved, lifted, None)
     for sweep in range(ITERS - 1):
         around = edges(first, final, "grp") + edges(left, right, "mem")
         residual, *found = surveyed_residual(now, around)
         margins, sums, inverse = exchanged(*found, inverse)
-        solved, rows = fine(rows, residual, margins)
+        solved = fine(rows, residual, margins)
         lifted = coarse_solve(inverse, sums)
         now = updated(solved, lifted, now)[0]
     return now

time: 68 us -> 64.8 us (0.953)
  waiting for transfers between devices: 16.7 us -> 13.6 us
  local copies, waits for them, and re-layouts: 2.22 us -> 0.54 us
  Pallas kernels: 15.4 us -> 17 us
    ppermute x14, waiting for transfers between devices: 15 us -> 11.9 us  [shifted(): lax.ppermute(value, axis, [(i, (i + distance) % count) for i in range(cou...]
    unnamed x12 -> x8, local copies, waits for them, and re-layouts: 1.71 us -> 0.02 us
    pallas_call x3 -> x4, Pallas kernels: 11.2 us -> 12.9 us  [the longest x2 7.44 us: fine(): pl.pallas_call(fine_kernel, in_specs=[in_vmem] * 5, out_specs=in_vmem, ou...]
  transfers between devices with their start and end apart: 20 -> 20, of which waited for: 14 -> 12; matrix products, arithmetic and copies ran while one was open for 1% -> 2% of each run, Pallas kernels for 14% -> 16%
where the time goes in v7:
time: 64.8 us; the launch traced here: 64.6 us
  starting transfers between devices  31.5 us (49%)
  Pallas kernels  17 us (26%)
  waiting for transfers between devices  13.6 us (21%)
  matrix products  0.74 us (1%)
  other arithmetic  0.71 us (1%)
    ppermute x14, starting transfers between devices, shifted(): lax.ppermute(value, axis, [(i, (i + distance) % count) for i in range(cou...  23.1 us
    ppermute x14, waiting for transfers between devices, shifted(): lax.ppermute(value, axis, [(i, (i + distance) % count) for i in range(cou...  11.9 us
    ppermute x6, starting transfers between devices, summed_over_members(): shares = keep + lax.ppermute(send, 'mem', pairs)  8.35 us
    pallas_call x2, Pallas kernels, fine(): pl.pallas_call(fine_kernel, in_specs=[in_vmem] * 5, out_specs=in_vmem, ou...  7.44 us
    pallas_call x1, Pallas kernels, held_rows(): pl.pallas_call(hold_kernel, in_specs=[in_hbm, pl.BlockSpec(memory_space=p...  2.86 us
    pallas_call x1, Pallas kernels, surveyed_start(): pl.pallas_call(start_kernel, in_specs=[in_hbm] * 3, out_specs=[in_vmem] *...  2.56 us
    pallas_call x2, Pallas kernels, updated(): pl.pallas_call(functools.partial(update_kernel, last), in_specs=[in_vmem]...  2.32 us
    pallas_call x1, Pallas kernels, surveyed_residual(): pl.pallas_call(residual_kernel, in_specs=[in_vmem] * 8, out_specs=[in_vme...  1.81 us
  transfers between devices with their start and end apart: 20, of which 12 were waited for; matrix products, arithmetic and copies ran while one was open for 2% of the time, Pallas kernels for 16%

profile of v7, /device:TPU:0, one launch (start us, length us, event | category | flops | bytes accessed | tf_op | source)
XLA Modules:
  0.0 64.6 jit_solution(11073860292918222369)
XLA Ops:
  0.0 2.6 %shard_map.55 = (bf16[288,384]{1,0:T(8,128)(2,1)S(1)}, bf16[288,384]{1,0:T(8,128)(2,1)S(1)}, bf16[24,8,384]{2,1,0:T(8,128)(2,1)S(1)}, f32[16,384]{1,0:T(8,128)S(1)}) custom-call(f32[24,56,384]{2,1,0:T(8,128)} %rhs_ref.3, f32[24,16,56]{2,1,0:T(8,128)} %bitcast.11, f32[16,512]{1,0:T(8,128)} %inverse_hbm.1), custom_call_target="tpu_custom_call" | custom-call | tf_op jit(solution)/shard_map/pallas_call | solution.py:325
  2.6 0.5 collective-permute-start
  3.1 2.6 %collective-permute-start.4 = (f32[16,512]{1,0:T(8,128)S(1)}, f32[16,512]{1,0:T(8,128)S(1)}, u32[]{:S(2)}, u32[]{:S(2)}) collective-permute-start(f32[16,512]{1,0:T(8,128)S(1)} %pad_maximum_fusion.2), channel_id=1, source_target_pairs={{0,16},{8,24},{16,0},{24,8},{1,17},{9,25},{17,1},{25,9},{2,18},{10... | collective-permute-start | bytes 98312 | tf_op jit(solution)/shard_map/ppermute | solution.py:22
  5.7 1.4 %collective-permute-start.1 = (bf16[288,384]{1,0:T(8,128)(2,1)S(1)}, bf16[288,384]{1,0:T(8,128)(2,1)S(1)}, u32[]{:S(2)}, u32[]{:S(2)}) collective-permute-start(bf16[288,384]{1,0:T(8,128)(2,1)S(1)} %get-tuple-element.21), channel_id=1, source_target_pairs={{0,24},{8,0},{16,8},{24,16},{1,25},{9,1},{17,9},{25,17},{2,26},{10... | collective-permute-start | bytes 663560 | tf_op jit(solution)/shard_map/ppermute | solution.py:22
  7.4 2.9 %shard_map.56.rows_ref = bf16[1536,2048]{1,0:T(8,128)(2,1)S(1)} custom-call(bf16[2048,2048]{1,0:T(8,128)(2,1)} %inverse_ref.1, f32[24,56,128]{2,1,0:T(8,128)S(1)} %broadcast_in_dim.30.heat_ref.extra_ref, f32[16,384]{1,0:T(8,128)S(1)} %get-tuple-element.19.order_ref), custom_call_target="tpu_custom_call" | custom-call | bytes 12582912 | tf_op jit(solution)/shard_map/pallas_call | solution.py:406
  10.3 1.2 %collective-permute-done.1 = bf16[288,384]{1,0:T(8,128)(2,1)S(1)} collective-permute-done((bf16[288,384]{1,0:T(8,128)(2,1)S(1)}, bf16[288,384]{1,0:T(8,128)(2,1)S(1)}, u32[]{:S(2)}, u32[]{:S(2)}) %collective-permute-start.1) | collective-permute-done | bytes 221216 | tf_op jit(solution)/shard_map/ppermute | solution.py:22
  11.9 1.6 %collective-permute-start.5 = (f32[2,2,1,16,384]{4,3,2,1,0:T(8,128)S(1)}, f32[2,2,1,16,384]{4,3,2,1,0:T(8,128)S(1)}, u32[]{:S(2)}, u32[]{:S(2)}) collective-permute-start(f32[2,2,1,16,384]{4,3,2,1,0:T(8,128)S(1)} %constant_dynamic-slice_fusion.5), channel_id=1, source_target_pairs={{0,1},{1,0},{2,3},{3,2},{4,5},{5,4},{6,7},{7,6},{8,9},{9,8},{10,11... | collective-permute-start | bytes 294920 | tf_op jit(solution)/shard_map/ppermute | solution.py:45
  13.7 0.6 collective-permute-start.2
  14.3 4.2 %collective-permute-start.3 = (bf16[32,4,384]{2,1,0:T(4,128)(2,1)S(1)}, bf16[32,4,384]{2,1,0:T(4,128)(2,1)S(1)}, u32[]{:S(2)}, u32[]{:S(2)}) collective-permute-start(bf16[32,4,384]{2,1,0:T(4,128)(2,1)S(1)} %get-tuple-element.36), channel_id=1, source_target_pairs={{0,7},{1,0},{2,1},{3,2},{4,3},{5,4},{6,5},{7,6},{8,15},{9,8},{10,9... | collective-permute-start | bytes 294920 | tf_op jit(solution)/shard_map/ppermute | solution.py:22
  18.6 0.6 collective-permute-start.6
  19.2 2.7 %collective-permute-done.2 = bf16[32,4,384]{2,1,0:T(4,128)(2,1)S(1)} collective-permute-done((bf16[32,4,384]{2,1,0:T(4,128)(2,1)S(1)}, bf16[32,4,384]{2,1,0:T(4,128)(2,1)S(1)}, u32[]{:S(2)}, u32[]{:S(2)}) %collective-permute-start.2) | collective-permute-done | bytes 98336 | tf_op jit(solution)/shard_map/ppermute | solution.py:22
  22.7 2.3 %collective-permute-start.7 = (f32[1,1,1,16,384]{4,3,2,1,0:T(8,128)S(1)}, f32[1,1,1,16,384]{4,3,2,1,0:T(8,128)S(1)}, u32[]{:S(2)}, u32[]{:S(2)}) collective-permute-start(f32[1,1,1,16,384]{4,3,2,1,0:T(8,128)S(1)} %constant_dynamic-slice_fusion.3), channel_id=1, source_target_pairs={{0,4},{1,5},{2,6},{3,7},{4,0},{5,1},{6,2},{7,3},{8,12},{9,13},{10,... | collective-permute-start | bytes 73736 | tf_op jit(solution)/shard_map/ppermute | solution.py:45
  25.0 3.7 %shard_map.57.fine_ref = f32[24,56,384]{2,1,0:T(8,128)S(1)} custom-call(bf16[1536,2048]{1,0:T(8,128)(2,1)S(1)} %shard_map.56.rows_ref, f32[24,56,384]{2,1,0:T(8,128)S(1)} %copy-done, bf16[4,56,384]{2,1,0:T(8,128)(2,1)S(1)} %bitcast.20, bf16[4,56,384]{2,1,0:T(8,128)(2,1)S(1)} %bitcast.22, bf16[32,8,384]{2,1,0:T(8,128)(2,1)S(1)} %pad_maximum_fusion.side_ref), custom_call_target="tpu_custom_call" | custom-call | flops 2415919104 | bytes 6291456 | tf_op jit(solution)/shard_map/pallas_call | solution.py:419
  28.8 0.6 shard_map.58
  29.4 1.2 %collective-permute-start.10 = (f32[6,4,512]{2,1,0:T(4,128)S(1)}, f32[6,4,512]{2,1,0:T(4,128)S(1)}, u32[]{:S(2)}, u32[]{:S(2)}) collective-permute-start(f32[6,4,512]{2,1,0:T(4,128)S(1)} %get-tuple-element.26), channel_id=1, source_target_pairs={{0,1},{1,2},{2,3},{3,4},{4,5},{5,6},{6,7},{7,0},{8,9},{9,10},{10,1... | collective-permute-start | bytes 147464 | tf_op jit(solution)/shard_map/ppermute | solution.py:22
  30.6 3.6 %collective-permute-start.11 = (f32[6,4,512]{2,1,0:T(4,128)S(1)}, f32[6,4,512]{2,1,0:T(4,128)S(1)}, u32[]{:S(2)}, u32[]{:S(2)}) collective-permute-start(f32[6,4,512]{2,1,0:T(4,128)S(1)} %get-tuple-element.27), channel_id=1, source_target_pairs={{0,7},{1,0},{2,1},{3,2},{4,3},{5,4},{6,5},{7,6},{8,15},{9,8},{10,9... | collective-permute-start | bytes 147464 | tf_op jit(solution)/shard_map/ppermute | solution.py:22
  34.2 1.7 %collective-permute-start.9 = (f32[1,56,512]{2,1,0:T(8,128)S(1)}, f32[1,56,512]{2,1,0:T(8,128)S(1)}, u32[]{:S(2)}, u32[]{:S(2)}) collective-permute-start(f32[1,56,512]{2,1,0:T(8,128)S(1)} %get-tuple-element.25), channel_id=1, source_target_pairs={{0,24},{8,0},{16,8},{24,16},{1,25},{9,1},{17,9},{25,17},{2,26},{10... | collective-permute-start | bytes 344072 | tf_op jit(solution)/shard_map/ppermute | solution.py:22
  36.3 2.1 %collective-permute-done.8 = f32[1,56,512]{2,1,0:T(8,128)S(1)} collective-permute-done((f32[1,56,512]{2,1,0:T(8,128)S(1)}, f32[1,56,512]{2,1,0:T(8,128)S(1)}, u32[]{:S(2)}, u32[]{:S(2)}) %collective-permute-start.8) | collective-permute-done | bytes 114720 | tf_op jit(solution)/shard_map/ppermute | solution.py:22
  38.5 1.8 %shard_map.59 = (f32[24,56,384]{2,1,0:T(8,128)S(1)}, bf16[272,384]{1,0:T(8,128)(2,1)S(1)}, bf16[272,384]{1,0:T(8,128)(2,1)S(1)}, bf16[24,8,384]{2,1,0:T(8,128)(2,1)S(1)}, f32[16,384]{1,0:T(8,128)S(1)}) custom-call(f32[24,56,384]{2,1,0:T(8,128)S(1)} %copy-done, f32[24,56,384]{2,1,0:T(8,128)S(1)} %get-tuple-element.23.now_ref.extra_ref, ...), custom_call_target="tpu_custom_call" | custom-call | tf_op jit(solution)/shard_map/pallas_call | solution.py:341
  40.3 1.1 %collective-permute-start.12 = (bf16[272,384]{1,0:T(8,128)(2,1)S(1)}, bf16[272,384]{1,0:T(8,128)(2,1)S(1)}, u32[]{:S(2)}, u32[]{:S(2)}) collective-permute-start(bf16[272,384]{1,0:T(8,128)(2,1)S(1)} %get-tuple-element.29), channel_id=1, source_target_pairs={{0,8},{8,16},{16,24},{24,0},{1,9},{9,17},{17,25},{25,1},{2,10},{10... | collective-permute-start | bytes 626696 | tf_op jit(solution)/shard_map/ppermute | solution.py:22
  41.4 1.1 %collective-permute-start.16 = (f32[16,384]{1,0:T(8,128)S(1)}, f32[16,384]{1,0:T(8,128)S(1)}, u32[]{:S(2)}, u32[]{:S(2)}) collective-permute-start(f32[16,384]{1,0:T(8,128)S(1)} %get-tuple-element.32), channel_id=1, source_target_pairs={{0,16},{8,24},{16,0},{24,8},{1,17},{9,25},{17,1},{25,9},{2,18},{10... | collective-permute-start | bytes 73736 | tf_op jit(solution)/shard_map/ppermute | solution.py:22
  42.8 3.3 %collective-permute-done.12 = bf16[272,384]{1,0:T(8,128)(2,1)S(1)} collective-permute-done((bf16[272,384]{1,0:T(8,128)(2,1)S(1)}, bf16[272,384]{1,0:T(8,128)(2,1)S(1)}, u32[]{:S(2)}, u32[]{:S(2)}) %collective-permute-start.12) | collective-permute-done | bytes 208928 | tf_op jit(solution)/shard_map/ppermute | solution.py:22
  46.1 0.7 %collective-permute-done.13 = bf16[272,384]{1,0:T(8,128)(2,1)S(1)} collective-permute-done((bf16[272,384]{1,0:T(8,128)(2,1)S(1)}, bf16[272,384]{1,0:T(8,128)(2,1)S(1)}, u32[]{:S(2)}, u32[]{:S(2)}) %collective-permute-start.13) | collective-permute-done | bytes 208928 | tf_op jit(solution)/shard_map/ppermute | solution.py:22
  47.5 2.1 %collective-permute-start.14 = (bf16[32,4,384]{2,1,0:T(4,128)(2,1)S(1)}, bf16[32,4,384]{2,1,0:T(4,128)(2,1)S(1)}, u32[]{:S(2)}, u32[]{:S(2)}) collective-permute-start(bf16[32,4,384]{2,1,0:T(4,128)(2,1)S(1)} %get-tuple-element.33), channel_id=1, source_target_pairs={{0,1},{1,2},{2,3},{3,4},{4,5},{5,6},{6,7},{7,0},{8,9},{9,10},{10,1... | collective-permute-start | bytes 294920 | tf_op jit(solution)/shard_map/ppermute | solution.py:22
  49.6 2.7 %collective-permute-start.15 = (bf16[32,4,384]{2,1,0:T(4,128)(2,1)S(1)}, bf16[32,4,384]{2,1,0:T(4,128)(2,1)S(1)}, u32[]{:S(2)}, u32[]{:S(2)}) collective-permute-start(bf16[32,4,384]{2,1,0:T(4,128)(2,1)S(1)} %get-tuple-element.34), channel_id=1, source_target_pairs={{0,7},{1,0},{2,1},{3,2},{4,3},{5,4},{6,5},{7,6},{8,15},{9,8},{10,9... | collective-permute-start | bytes 294920 | tf_op jit(solution)/shard_map/ppermute | solution.py:22
  52.3 0.5 collective-permute-done.17
  52.8 3.0 %collective-permute-start.18 = (f32[2,1,1,16,384]{4,3,2,1,0:T(8,128)S(1)}, f32[2,1,1,16,384]{4,3,2,1,0:T(8,128)S(1)}, u32[]{:S(2)}, u32[]{:S(2)}) collective-permute-start(f32[2,1,1,16,384]{4,3,2,1,0:T(8,128)S(1)} %constant_dynamic-slice_fusion.1), channel_id=1, source_target_pairs={{0,2},{1,3},{2,0},{3,1},{4,6},{5,7},{6,4},{7,5},{8,10},{9,11},{10,... | collective-permute-start | bytes 147464 | tf_op jit(solution)/shard_map/ppermute | solution.py:45
  55.8 1.4 %collective-permute-done.15 = bf16[32,4,384]{2,1,0:T(4,128)(2,1)S(1)} collective-permute-done((bf16[32,4,384]{2,1,0:T(4,128)(2,1)S(1)}, bf16[32,4,384]{2,1,0:T(4,128)(2,1)S(1)}, u32[]{:S(2)}, u32[]{:S(2)}) %collective-permute-start.15) | collective-permute-done | bytes 98336 | tf_op jit(solution)/shard_map/ppermute | solution.py:22
  57.4 0.5 collective-permute-done.18
  58.0 0.8 %collective-permute-start.19 = (f32[1,1,1,16,384]{4,3,2,1,0:T(8,128)S(1)}, f32[1,1,1,16,384]{4,3,2,1,0:T(8,128)S(1)}, u32[]{:S(2)}, u32[]{:S(2)}) collective-permute-start(f32[1,1,1,16,384]{4,3,2,1,0:T(8,128)S(1)} %constant_dynamic-slice_fusion), channel_id=1, source_target_pairs={{0,4},{1,5},{2,6},{3,7},{4,0},{5,1},{6,2},{7,3},{8,12},{9,13},{10,... | collective-permute-start | bytes 73736 | tf_op jit(solution)/shard_map/ppermute | solution.py:45
  58.8 3.7 %shard_map.60.fine_ref = f32[24,56,384]{2,1,0:T(8,128)S(1)} custom-call(bf16[1536,2048]{1,0:T(8,128)(2,1)S(1)} %shard_map.56.rows_ref, f32[24,56,384]{2,1,0:T(8,128)S(1)} %get-tuple-element.28.block_ref, bf16[4,56,384]{2,1,0:T(8,128)(2,1)S(1)} %bitcast.16, bf16[4,56,384]{2,1,0:T(8,128)(2,1)S(1)} %bitcast.18, bf16[32,8,384]{2,1,0:T(8,128)(2,1)S(1)} %pad_maximum_fusion.1.side_ref), custom_call_target="tpu_custom_call" | custom-call | flops 2415919104 | bytes 6291456 | tf_op jit(solution)/shard_map/pallas_call | solution.py:419
  62.8 1.7 %shard_map.61 = f32[24,56,384]{2,1,0:T(8,128)} custom-call(f32[24,56,384]{2,1,0:T(8,128)S(1)} %shard_map.60.fine_ref, f32[24,16,56]{2,1,0:T(8,128)S(1)} %bitcast.14, f32[16,384]{1,0:T(8,128)S(1)} %add_bitcast_fusion.lifted_ref, f32[24,56,384]{2,1,0:T(8,128)S(1)} %get-tuple-element.23.now_ref.extra_ref), custom_call_target="tpu_custom_call" | custom-call | tf_op jit(solution)/shard_map/pallas_call | solution.py:449
  (69 shorter events, 3.7 us)
Async XLA Ops:
  0.0 3.1 %copy-start.2 = (f32[16,512]{1,0:T(8,128)S(1)}, f32[16,512]{1,0:T(8,128)}, u32[]{:S(2)}) copy-start(f32[16,512]{1,0:T(8,128)} %inverse_hbm.1) | copy-start | bytes 98308
  0.0 7.1 %copy-start.3 = (f32[24,56]{1,0:T(8,128)S(1)}, f32[24,56]{1,0:T(8,128)}, u32[]{:S(2)}) copy-start(f32[24,56]{1,0:T(8,128)} %param.6) | copy-start | bytes 16132
  2.6 7.7 %collective-permute-start = (bf16[288,384]{1,0:T(8,128)(2,1)S(1)}, bf16[288,384]{1,0:T(8,128)(2,1)S(1)}, u32[]{:S(2)}, u32[]{:S(2)}) collective-permute-start(bf16[288,384]{1,0:T(8,128)(2,1)S(1)} %get-tuple-element.20), channel_id=1, source_target_pairs={{0,8},{8,16},{16,24},{24,0},{1,9},{9,17},{17,25},{25,1},{2,10},{10... | collective-permute-start | bytes 663560 | tf_op jit(solution)/shard_map/ppermute | solution.py:22
  3.1 7.1 %collective-permute-start.4 = (f32[16,512]{1,0:T(8,128)S(1)}, f32[16,512]{1,0:T(8,128)S(1)}, u32[]{:S(2)}, u32[]{:S(2)}) collective-permute-start(f32[16,512]{1,0:T(8,128)S(1)} %pad_maximum_fusion.2), channel_id=1, source_target_pairs={{0,16},{8,24},{16,0},{24,8},{1,17},{9,25},{17,1},{25,9},{2,18},{10... | collective-permute-start | bytes 98312 | tf_op jit(solution)/shard_map/ppermute | solution.py:22
  5.7 5.8 %collective-permute-start.1 = (bf16[288,384]{1,0:T(8,128)(2,1)S(1)}, bf16[288,384]{1,0:T(8,128)(2,1)S(1)}, u32[]{:S(2)}, u32[]{:S(2)}) collective-permute-start(bf16[288,384]{1,0:T(8,128)(2,1)S(1)} %get-tuple-element.21), channel_id=1, source_target_pairs={{0,24},{8,0},{16,8},{24,16},{1,25},{9,1},{17,9},{25,17},{2,26},{10... | collective-permute-start | bytes 663560 | tf_op jit(solution)/shard_map/ppermute | solution.py:22
  10.2 14.8 %copy-start = (f32[24,56,384]{2,1,0:T(8,128)S(1)}, f32[24,56,384]{2,1,0:T(8,128)}, u32[]{:S(2)}) copy-start(f32[24,56,384]{2,1,0:T(8,128)} %rhs_ref.3) | copy-start | bytes 6193156
  11.9 6.6 %collective-permute-start.5 = (f32[2,2,1,16,384]{4,3,2,1,0:T(8,128)S(1)}, f32[2,2,1,16,384]{4,3,2,1,0:T(8,128)S(1)}, u32[]{:S(2)}, u32[]{:S(2)}) collective-permute-start(f32[2,2,1,16,384]{4,3,2,1,0:T(8,128)S(1)} %constant_dynamic-slice_fusion.5), channel_id=1, source_target_pairs={{0,1},{1,0},{2,3},{3,2},{4,5},{5,4},{6,7},{7,6},{8,9},{9,8},{10,11... | collective-permute-start | bytes 294920 | tf_op jit(solution)/shard_map/ppermute | solution.py:45
  13.7 8.1 %collective-permute-start.2 = (bf16[32,4,384]{2,1,0:T(4,128)(2,1)S(1)}, bf16[32,4,384]{2,1,0:T(4,128)(2,1)S(1)}, u32[]{:S(2)}, u32[]{:S(2)}) collective-permute-start(bf16[32,4,384]{2,1,0:T(4,128)(2,1)S(1)} %get-tuple-element.35), channel_id=1, source_target_pairs={{0,1},{1,2},{2,3},{3,4},{4,5},{5,6},{6,7},{7,0},{8,9},{9,10},{10,1... | collective-permute-start | bytes 294920 | tf_op jit(solution)/shard_map/ppermute | solution.py:22
  14.3 7.8 %collective-permute-start.3 = (bf16[32,4,384]{2,1,0:T(4,128)(2,1)S(1)}, bf16[32,4,384]{2,1,0:T(4,128)(2,1)S(1)}, u32[]{:S(2)}, u32[]{:S(2)}) collective-permute-start(bf16[32,4,384]{2,1,0:T(4,128)(2,1)S(1)} %get-tuple-element.36), channel_id=1, source_target_pairs={{0,7},{1,0},{2,1},{3,2},{4,3},{5,4},{6,5},{7,6},{8,15},{9,8},{10,9... | collective-permute-start | bytes 294920 | tf_op jit(solution)/shard_map/ppermute | solution.py:22
  18.6 4.2 %collective-permute-start.6 = (f32[2,1,1,16,384]{4,3,2,1,0:T(8,128)S(1)}, f32[2,1,1,16,384]{4,3,2,1,0:T(8,128)S(1)}, u32[]{:S(2)}, u32[]{:S(2)}) collective-permute-start(f32[2,1,1,16,384]{4,3,2,1,0:T(8,128)S(1)} %constant_dynamic-slice_fusion.4), channel_id=1, source_target_pairs={{0,2},{1,3},{2,0},{3,1},{4,6},{5,7},{6,4},{7,5},{8,10},{9,11},{10,... | collective-permute-start | bytes 147464 | tf_op jit(solution)/shard_map/ppermute | solution.py:45
  22.7 6.0 %copy-start.1 = (f32[24,56,16]{1,2,0:T(8,128)S(1)}, f32[24,56,16]{1,2,0:T(8,128)}, u32[]{:S(2)}) copy-start(f32[24,56,16]{1,2,0:T(8,128)} %param.8) | copy-start | bytes 258052
  22.7 6.0 %collective-permute-start.7 = (f32[1,1,1,16,384]{4,3,2,1,0:T(8,128)S(1)}, f32[1,1,1,16,384]{4,3,2,1,0:T(8,128)S(1)}, u32[]{:S(2)}, u32[]{:S(2)}) collective-permute-start(f32[1,1,1,16,384]{4,3,2,1,0:T(8,128)S(1)} %constant_dynamic-slice_fusion.3), channel_id=1, source_target_pairs={{0,4},{1,5},{2,6},{3,7},{4,0},{5,1},{6,2},{7,3},{8,12},{9,13},{10,... | collective-permute-start | bytes 73736 | tf_op jit(solution)/shard_map/ppermute | solution.py:45
  29.4 6.8 %collective-permute-start.10 = (f32[6,4,512]{2,1,0:T(4,128)S(1)}, f32[6,4,512]{2,1,0:T(4,128)S(1)}, u32[]{:S(2)}, u32[]{:S(2)}) collective-permute-start(f32[6,4,512]{2,1,0:T(4,128)S(1)} %get-tuple-element.26), channel_id=1, source_target_pairs={{0,1},{1,2},{2,3},{3,4},{4,5},{5,6},{6,7},{7,0},{8,9},{9,10},{10,1... | collective-permute-start | bytes 147464 | tf_op jit(solution)/shard_map/ppermute | solution.py:22
  30.6 5.7 %collective-permute-start.11 = (f32[6,4,512]{2,1,0:T(4,128)S(1)}, f32[6,4,512]{2,1,0:T(4,128)S(1)}, u32[]{:S(2)}, u32[]{:S(2)}) collective-permute-start(f32[6,4,512]{2,1,0:T(4,128)S(1)} %get-tuple-element.27), channel_id=1, source_target_pairs={{0,7},{1,0},{2,1},{3,2},{4,3},{5,4},{6,5},{7,6},{8,15},{9,8},{10,9... | collective-permute-start | bytes 147464 | tf_op jit(solution)/shard_map/ppermute | solution.py:22
  34.2 4.2 %collective-permute-start.8 = (f32[1,56,512]{2,1,0:T(8,128)S(1)}, f32[1,56,512]{2,1,0:T(8,128)S(1)}, u32[]{:S(2)}, u32[]{:S(2)}) collective-permute-start(f32[1,56,512]{2,1,0:T(8,128)S(1)} %get-tuple-element.24), channel_id=1, source_target_pairs={{0,8},{8,16},{16,24},{24,0},{1,9},{9,17},{17,25},{25,1},{2,10},{10... | collective-permute-start | bytes 344072 | tf_op jit(solution)/shard_map/ppermute | solution.py:22
  34.2 4.2 %collective-permute-start.9 = (f32[1,56,512]{2,1,0:T(8,128)S(1)}, f32[1,56,512]{2,1,0:T(8,128)S(1)}, u32[]{:S(2)}, u32[]{:S(2)}) collective-permute-start(f32[1,56,512]{2,1,0:T(8,128)S(1)} %get-tuple-element.25), channel_id=1, source_target_pairs={{0,24},{8,0},{16,8},{24,16},{1,25},{9,1},{17,9},{25,17},{2,26},{10... | collective-permute-start | bytes 344072 | tf_op jit(solution)/shard_map/ppermute | solution.py:22
  40.3 5.8 %collective-permute-start.12 = (bf16[272,384]{1,0:T(8,128)(2,1)S(1)}, bf16[272,384]{1,0:T(8,128)(2,1)S(1)}, u32[]{:S(2)}, u32[]{:S(2)}) collective-permute-start(bf16[272,384]{1,0:T(8,128)(2,1)S(1)} %get-tuple-element.29), channel_id=1, source_target_pairs={{0,8},{8,16},{16,24},{24,0},{1,9},{9,17},{17,25},{25,1},{2,10},{10... | collective-permute-start | bytes 626696 | tf_op jit(solution)/shard_map/ppermute | solution.py:22
  41.4 5.5 %collective-permute-start.16 = (f32[16,384]{1,0:T(8,128)S(1)}, f32[16,384]{1,0:T(8,128)S(1)}, u32[]{:S(2)}, u32[]{:S(2)}) collective-permute-start(f32[16,384]{1,0:T(8,128)S(1)} %get-tuple-element.32), channel_id=1, source_target_pairs={{0,16},{8,24},{16,0},{24,8},{1,17},{9,25},{17,1},{25,9},{2,18},{10... | collective-permute-start | bytes 73736 | tf_op jit(solution)/shard_map/ppermute | solution.py:22
  42.4 4.4 %collective-permute-start.13 = (bf16[272,384]{1,0:T(8,128)(2,1)S(1)}, bf16[272,384]{1,0:T(8,128)(2,1)S(1)}, u32[]{:S(2)}, u32[]{:S(2)}) collective-permute-start(bf16[272,384]{1,0:T(8,128)(2,1)S(1)} %get-tuple-element.30), channel_id=1, source_target_pairs={{0,24},{8,0},{16,8},{24,16},{1,25},{9,1},{17,9},{25,17},{2,26},{10... | collective-permute-start | bytes 626696 | tf_op jit(solution)/shard_map/ppermute | solution.py:22
  47.3 5.5 %collective-permute-start.17 = (f32[2,2,1,16,384]{4,3,2,1,0:T(8,128)S(1)}, f32[2,2,1,16,384]{4,3,2,1,0:T(8,128)S(1)}, u32[]{:S(2)}, u32[]{:S(2)}) collective-permute-start(f32[2,2,1,16,384]{4,3,2,1,0:T(8,128)S(1)} %constant_dynamic-slice_fusion.2), channel_id=1, source_target_pairs={{0,1},{1,0},{2,3},{3,2},{4,5},{5,4},{6,7},{7,6},{8,9},{9,8},{10,11... | collective-permute-start | bytes 294920 | tf_op jit(solution)/shard_map/ppermute | solution.py:45
  47.5 8.3 %collective-permute-start.14 = (bf16[32,4,384]{2,1,0:T(4,128)(2,1)S(1)}, bf16[32,4,384]{2,1,0:T(4,128)(2,1)S(1)}, u32[]{:S(2)}, u32[]{:S(2)}) collective-permute-start(bf16[32,4,384]{2,1,0:T(4,128)(2,1)S(1)} %get-tuple-element.33), channel_id=1, source_target_pairs={{0,1},{1,2},{2,3},{3,4},{4,5},{5,6},{6,7},{7,0},{8,9},{9,10},{10,1... | collective-permute-start | bytes 294920 | tf_op jit(solution)/shard_map/ppermute | solution.py:22
  49.6 7.7 %collective-permute-start.15 = (bf16[32,4,384]{2,1,0:T(4,128)(2,1)S(1)}, bf16[32,4,384]{2,1,0:T(4,128)(2,1)S(1)}, u32[]{:S(2)}, u32[]{:S(2)}) collective-permute-start(bf16[32,4,384]{2,1,0:T(4,128)(2,1)S(1)} %get-tuple-element.34), channel_id=1, source_target_pairs={{0,7},{1,0},{2,1},{3,2},{4,3},{5,4},{6,5},{7,6},{8,15},{9,8},{10,9... | collective-permute-start | bytes 294920 | tf_op jit(solution)/shard_map/ppermute | solution.py:22
  52.8 5.1 %collective-permute-start.18 = (f32[2,1,1,16,384]{4,3,2,1,0:T(8,128)S(1)}, f32[2,1,1,16,384]{4,3,2,1,0:T(8,128)S(1)}, u32[]{:S(2)}, u32[]{:S(2)}) collective-permute-start(f32[2,1,1,16,384]{4,3,2,1,0:T(8,128)S(1)} %constant_dynamic-slice_fusion.1), channel_id=1, source_target_pairs={{0,2},{1,3},{2,0},{3,1},{4,6},{5,7},{6,4},{7,5},{8,10},{9,11},{10,... | collective-permute-start | bytes 147464 | tf_op jit(solution)/shard_map/ppermute | solution.py:45
  58.0 4.8 %collective-permute-start.19 = (f32[1,1,1,16,384]{4,3,2,1,0:T(8,128)S(1)}, f32[1,1,1,16,384]{4,3,2,1,0:T(8,128)S(1)}, u32[]{:S(2)}, u32[]{:S(2)}) collective-permute-start(f32[1,1,1,16,384]{4,3,2,1,0:T(8,128)S(1)} %constant_dynamic-slice_fusion), channel_id=1, source_target_pairs={{0,4},{1,5},{2,6},{3,7},{4,0},{5,1},{6,2},{7,3},{8,12},{9,13},{10,... | collective-permute-start | bytes 73736 | tf_op jit(solution)/shard_map/ppermute | solution.py:45

commit v8 on v7

--- a/solution.py
+++ b/solution.py
@@ -10,7 +10,6 @@
 OV = 4
 ITERS = 2
 HOLD = 6
-ORDER = range
 LANES = 128
 EXACT = lax.Precision.HIGHEST
 F32 = jnp.float32
@@ -36,7 +35,7 @@
     members = lax.axis_size("mem")
     sizes = [2] * (members.bit_length() - 1)
     shares = shares.reshape(*sizes, shares.shape[0] // members, shares.shape[1])
-    for k in ORDER(len(sizes)):
+    for k in (*range(1, len(sizes)), 0):
         bit = lax.axis_index("mem") >> k & 1
         axis = len(sizes) - 1 - k
         keep = lax.dynamic_slice_in_dim(shares, bit, 1, axis)
@@ -63,9 +62,13 @@
 
 def restrict(basis_ref, first, block):
     rows, own_y, columns = block.shape
-    high, middle, low = modes_of(basis_ref, first, rows)
+    return weighted(modes_of(basis_ref, first, rows), block.reshape(rows * own_y, columns))
+
+
+def weighted(weights, cells):
+    high, middle, low = weights
     modes = high.shape[0]
-    block_high, block_middle, block_low = split(block.reshape(rows * own_y, columns))
+    block_high, block_middle, block_low = split(cells)
     three = product(jnp.concatenate([high, middle, low], axis=0), block_high)
     two = product(jnp.concatenate([high, middle], axis=0), block_middle)
     one = product(high, block_low)
@@ -146,56 +149,88 @@
     finish(total, OV * own_y, down_ref, up_ref, sum_ref)
 
 
-def residual_kernel(
-    rhs_ref,
+def flux(values, heat, other, other_heat):
+    face = 0.5 * (heat + other_heat)
+    return jnp.concatenate([face] * (values.shape[1] // LANES), axis=1) * (values - other)
+
+
+def inner_kernel(rhs_ref, now_ref, heat_ref, basis_ref, out_ref, sum_ref, modes_ref):
+    own_x, own_y, columns = now_ref.shape
+    place = lax.broadcasted_iota(jnp.int32, (own_y, columns), 0)
+    here, heat = now_ref[0], heat_ref[0]
+    before = jnp.zeros((own_y, columns), F32)
+    total = jnp.zeros(sum_ref.shape, F32)
+    for index in range(own_x):
+        if index + 1 < own_x:
+            after, after_heat = now_ref[index + 1], heat_ref[index + 1]
+            across = flux(here, heat, after, after_heat)
+        else:
+            across = jnp.zeros((own_y, columns), F32)
+        along = flux(here, heat, pltpu.roll(here, own_y - 1, 0), pltpu.roll(heat, own_y - 1, 0))
+        along = jnp.where(place == own_y - 1, 0.0, along)
+        entering = pltpu.roll(along, 1, 0)
+        out_ref[index] = rhs_ref[index] - ((across - before) + (along - entering))
+        here, heat, before = after, after_heat, across
+        if index % OV == OV - 1:
+            first = index + 1 - OV
+            total = total + restrict(basis_ref, first, out_ref[first : first + OV])
+    sum_ref[...] = total
+    sides = []
+    for index in range(own_x):
+        row = basis_ref[index]
+        left = lax.broadcasted_iota(jnp.int32, (row.shape[0], 2 * OV), 1) < OV
+        sides.append(jnp.where(left, row[:, : 2 * OV], row[:, own_y - 2 * OV :]))
+    modes_ref[...] = jnp.concatenate([basis_ref[0], basis_ref[own_x - 1], *sides], axis=1)
+
+
+def edge_kernel(
+    part_ref,
     now_ref,
     below_ref,
     above_ref,
     left_ref,
     right_ref,
     heat_ref,
-    basis_ref,
+    part_sum_ref,
+    modes_ref,
     out_ref,
     down_ref,
     up_ref,
     side_ref,
     sum_ref,
+    changes,
 ):
+    del part_ref
     own_x, own_y, columns = now_ref.shape
-    place = lax.broadcasted_iota(jnp.int32, (own_y, columns), 0)
-    place_heat = place[:, :LANES]
-
-    def flux(values, heat, other, other_heat):
-        face = 0.5 * (heat + other_heat)
-        return jnp.concatenate([face] * (columns // LANES), axis=1) * (values - other)
+    count = OV * own_y
+    sides = 2 * OV
 
     def parts(row):
         return row[:, :columns], row[:, columns:]
 
-    here, heat = now_ref[0], heat_ref[0]
-    before = flux(*parts(below_ref[0]), here, heat)
-    total = jnp.zeros(sum_ref.shape, F32)
+    for at, index, ref in ((0, 0, below_ref), (own_y, own_x - 1, above_ref)):
+        change = flux(*parts(ref[0]), now_ref[index], heat_ref[index])
+        changes[at : at + own_y] = change
+        out_ref[index] = out_ref[index] + change
+    place = lax.broadcasted_iota(jnp.int32, (sides, columns), 0)
     for index in range(own_x):
-        if index + 1 < own_x:
-            after, after_heat = now_ref[index + 1], heat_ref[index + 1]
-        else:
-            after, after_heat = parts(above_ref[0])
-        across = flux(here, heat, after, after_heat)
-        right, right_heat = parts(right_ref[index // OV, index % OV : index % OV + 1])
-        left, left_heat = parts(left_ref[index // OV, index % OV : index % OV + 1])
-        right = jnp.where(place == own_y - 1, right, pltpu.roll(here, own_y - 1, 0))
-        right_heat = jnp.where(place_heat == own_y - 1, right_heat, pltpu.roll(heat, own_y - 1, 0))
-        along = flux(here, heat, right, right_heat)
-        entering = jnp.where(
-            place == 0, flux(left, left_heat, here[:1], heat[:1]), pltpu.roll(along, 1, 0)
-        )
-        out_ref[index] = rhs_ref[index] - ((across - before) + (along - entering))
-        here, heat, before = after, after_heat, across
-        if index % OV == OV - 1:
-            first = index + 1 - OV
-            block = out_ref[first : first + OV]
-            total = total + survey(block, basis_ref, first, down_ref, up_ref, side_ref)
-    finish(total, OV * own_y, down_ref, up_ref, sum_ref)
+        tiles = []
+        for ref, start, cell in ((left_ref, 0, 0), (right_ref, own_y - sides, sides - 1)):
+            other = parts(ref[index // OV, index % OV : index % OV + 1])
+            tile = slice(start, start + sides)
+            change = flux(*other, now_ref[index, tile], heat_ref[index, tile])
+            change = jnp.where(place == cell, change, 0.0)
+            tiles.append(change)
+            out_ref[index, tile] = out_ref[index, tile] + change
+        at = 2 * own_y + index * sides
+        changes[at : at + sides] = tiles[0] + tiles[1]
+        side_ref[index] = jnp.where(
+            place < OV, out_ref[index, :sides], out_ref[index, own_y - sides :]
+        ).astype(BF16)
+    down_ref[:count] = out_ref[:OV].reshape(count, columns).astype(BF16)
+    up_ref[:count] = out_ref[own_x - OV :].reshape(count, columns).astype(BF16)
+    total = part_sum_ref[...] + weighted(split(modes_ref[...]), changes[...])
+    finish(total, count, down_ref, up_ref, sum_ref)
 
 
 def hold_kernel(inverse_ref, heat_ref, order_ref, out_ref, arrived):
@@ -337,14 +372,35 @@
             compiler_params=params(16),
         )(*(pltpu.with_memory_space_constraint(a, pltpu.HBM) for a in (rhs, basis, coarse_inverse)))
 
+    edge_cells = 2 * own_y + 2 * OV * own_x
+
+    def inner(now):
+        return pl.pallas_call(
+            inner_kernel,
+            in_specs=[in_vmem] * 4,
+            out_specs=[in_vmem] * 3,
+            out_shape=[
+                shape_of(rhs.shape, F32),
+                shape_of((modes, columns), F32),
+                shape_of((modes, edge_cells), F32),
+            ],
+            compiler_params=params(16),
+            cost_estimate=pl.CostEstimate(
+                flops=0, bytes_accessed=12 * own_x * own_y * columns, transcendentals=0
+            ),
+        )(rhs, now, heat, basis)
+
     def surveyed_residual(now, around):
+        part, part_sum, edge_modes = inner(now)
         return pl.pallas_call(
-            residual_kernel,
-            in_specs=[in_vmem] * 8,
+            edge_kernel,
+            in_specs=[in_vmem] * 9,
             out_specs=[in_vmem] * 5,
             out_shape=[shape_of(rhs.shape, F32)] + survey_shapes(edge_rows + sum_rows),
+            scratch_shapes=[pltpu.VMEM((edge_cells, columns), F32)],
+            input_output_aliases={0: 0},
             compiler_params=params(16),
-        )(rhs, now, *around, heat, basis)
+        )(part, now, *around, heat, part_sum, edge_modes)
 
     def added(parts):
         high, middle, low = (part.astype(F32) for part in parts)

time: 64.8 us -> 63 us (0.972)
  starting transfers between devices: 31.5 us -> 27.3 us
  waiting for transfers between devices: 13.6 us -> 15.7 us
    ppermute x6, starting transfers between devices: 8.35 us -> 4.07 us  [summed_over_members(): shares = keep + lax.ppermute(send, 'mem', pairs)]
    ppermute x6, waiting for transfers between devices: 1.68 us -> 3.66 us  [summed_over_members(): shares = keep + lax.ppermute(send, 'mem', pairs)]
    pallas_call x1 -> x2, Pallas kernels: 1.81 us -> 2.1 us  [the longest x1 1.67 us: inner(): pl.pallas_call(inner_kernel, in_specs=[in_vmem] * 4, out_specs=[in_vmem]...]
  transfers between devices with their start and end apart: 20 -> 20, of which waited for: 12 -> 10; matrix products, arithmetic and copies ran while one was open for 2% -> 2% of each run, Pallas kernels for 16% -> 19%
where the time goes in v8:
time: 63 us; the launch traced here: 62.9 us
  starting transfers between devices  27.3 us (43%)
  Pallas kernels  17.3 us (27%)
  waiting for transfers between devices  15.7 us (25%)
  matrix products  0.74 us (1%)
  other arithmetic  0.72 us (1%)
    ppermute x14, starting transfers between devices, shifted(): lax.ppermute(value, axis, [(i, (i + distance) % count) for i in range(cou...  23.3 us
    ppermute x14, waiting for transfers between devices, shifted(): lax.ppermute(value, axis, [(i, (i + distance) % count) for i in range(cou...  12 us
    pallas_call x2, Pallas kernels, fine(): pl.pallas_call(fine_kernel, in_specs=[in_vmem] * 5, out_specs=in_vmem, ou...  7.44 us
    ppermute x6, starting transfers between devices, summed_over_members(): shares = keep + lax.ppermute(send, 'mem', pairs)  4.07 us
    ppermute x6, waiting for transfers between devices, summed_over_members(): shares = keep + lax.ppermute(send, 'mem', pairs)  3.66 us
    pallas_call x1, Pallas kernels, held_rows(): pl.pallas_call(hold_kernel, in_specs=[in_hbm, pl.BlockSpec(memory_space=p...  2.86 us
    pallas_call x1, Pallas kernels, surveyed_start(): pl.pallas_call(start_kernel, in_specs=[in_hbm] * 3, out_specs=[in_vmem] *...  2.56 us
    pallas_call x2, Pallas kernels, updated(): pl.pallas_call(functools.partial(update_kernel, last), in_specs=[in_vmem]...  2.32 us
  transfers between devices with their start and end apart: 20, of which 10 were waited for; matrix products, arithmetic and copies ran while one was open for 2% of the time, Pallas kernels for 19%

profile of v8, /device:TPU:0, one launch (start us, length us, event | category | flops | bytes accessed | tf_op | source)
XLA Modules:
  0.0 62.9 jit_solution(16650180027783070039)
XLA Ops:
  0.0 2.6 %shard_map.55 = (bf16[288,384]{1,0:T(8,128)(2,1)S(1)}, bf16[288,384]{1,0:T(8,128)(2,1)S(1)}, bf16[24,8,384]{2,1,0:T(8,128)(2,1)S(1)}, f32[16,384]{1,0:T(8,128)S(1)}) custom-call(f32[24,56,384]{2,1,0:T(8,128)} %rhs_ref.3, f32[24,16,56]{2,1,0:T(8,128)} %bitcast.11, f32[16,512]{1,0:T(8,128)} %inverse_hbm.1), custom_call_target="tpu_custom_call" | custom-call | tf_op jit(solution)/shard_map/pallas_call | solution.py:360
  2.6 0.5 collective-permute-start
  3.1 2.6 %collective-permute-start.4 = (f32[16,512]{1,0:T(8,128)S(1)}, f32[16,512]{1,0:T(8,128)S(1)}, u32[]{:S(2)}, u32[]{:S(2)}) collective-permute-start(f32[16,512]{1,0:T(8,128)S(1)} %pad_maximum_fusion.2), channel_id=1, source_target_pairs={{0,16},{8,24},{16,0},{24,8},{1,17},{9,25},{17,1},{25,9},{2,18},{10... | collective-permute-start | bytes 98312 | tf_op jit(solution)/shard_map/ppermute | solution.py:21
  5.7 1.4 %collective-permute-start.1 = (bf16[288,384]{1,0:T(8,128)(2,1)S(1)}, bf16[288,384]{1,0:T(8,128)(2,1)S(1)}, u32[]{:S(2)}, u32[]{:S(2)}) collective-permute-start(bf16[288,384]{1,0:T(8,128)(2,1)S(1)} %get-tuple-element.24), channel_id=1, source_target_pairs={{0,24},{8,0},{16,8},{24,16},{1,25},{9,1},{17,9},{25,17},{2,26},{10... | collective-permute-start | bytes 663560 | tf_op jit(solution)/shard_map/ppermute | solution.py:21
  7.4 2.9 %shard_map.56.rows_ref = bf16[1536,2048]{1,0:T(8,128)(2,1)S(1)} custom-call(bf16[2048,2048]{1,0:T(8,128)(2,1)} %inverse_ref.1, f32[24,56,128]{2,1,0:T(8,128)S(1)} %broadcast_in_dim.30.heat_ref.extra_ref, f32[16,384]{1,0:T(8,128)S(1)} %get-tuple-element.22.order_ref), custom_call_target="tpu_custom_call" | custom-call | bytes 12582912 | tf_op jit(solution)/shard_map/pallas_call | solution.py:462
  10.3 1.2 %collective-permute-done.1 = bf16[288,384]{1,0:T(8,128)(2,1)S(1)} collective-permute-done((bf16[288,384]{1,0:T(8,128)(2,1)S(1)}, bf16[288,384]{1,0:T(8,128)(2,1)S(1)}, u32[]{:S(2)}, u32[]{:S(2)}) %collective-permute-start.1) | collective-permute-done | bytes 221216 | tf_op jit(solution)/shard_map/ppermute | solution.py:21
  11.9 1.6 %collective-permute-start.5 = (f32[2,1,2,16,384]{4,3,2,1,0:T(8,128)S(1)}, f32[2,1,2,16,384]{4,3,2,1,0:T(8,128)S(1)}, u32[]{:S(2)}, u32[]{:S(2)}) collective-permute-start(f32[2,1,2,16,384]{4,3,2,1,0:T(8,128)S(1)} %constant_dynamic-slice_fusion.5), channel_id=1, source_target_pairs={{0,2},{1,3},{2,0},{3,1},{4,6},{5,7},{6,4},{7,5},{8,10},{9,11},{10,... | collective-permute-start | bytes 294920 | tf_op jit(solution)/shard_map/ppermute | solution.py:44
  13.8 1.6 %collective-permute-start.2 = (bf16[32,4,384]{2,1,0:T(4,128)(2,1)S(1)}, bf16[32,4,384]{2,1,0:T(4,128)(2,1)S(1)}, u32[]{:S(2)}, u32[]{:S(2)}) collective-permute-start(bf16[32,4,384]{2,1,0:T(4,128)(2,1)S(1)} %get-tuple-element.41), channel_id=1, source_target_pairs={{0,1},{1,2},{2,3},{3,4},{4,5},{5,6},{6,7},{7,0},{8,9},{9,10},{10,1... | collective-permute-start | bytes 294920 | tf_op jit(solution)/shard_map/ppermute | solution.py:21
  15.4 3.2 %collective-permute-start.3 = (bf16[32,4,384]{2,1,0:T(4,128)(2,1)S(1)}, bf16[32,4,384]{2,1,0:T(4,128)(2,1)S(1)}, u32[]{:S(2)}, u32[]{:S(2)}) collective-permute-start(bf16[32,4,384]{2,1,0:T(4,128)(2,1)S(1)} %get-tuple-element.42), channel_id=1, source_target_pairs={{0,7},{1,0},{2,1},{3,2},{4,3},{5,4},{6,5},{7,6},{8,15},{9,8},{10,9... | collective-permute-start | bytes 294920 | tf_op jit(solution)/shard_map/ppermute | solution.py:21
  18.6 1.6 %collective-permute-start.6 = (f32[1,1,2,16,384]{4,3,2,1,0:T(8,128)S(1)}, f32[1,1,2,16,384]{4,3,2,1,0:T(8,128)S(1)}, u32[]{:S(2)}, u32[]{:S(2)}) collective-permute-start(f32[1,1,2,16,384]{4,3,2,1,0:T(8,128)S(1)} %constant_dynamic-slice_fusion.4), channel_id=1, source_target_pairs={{0,4},{1,5},{2,6},{3,7},{4,0},{5,1},{6,2},{7,3},{8,12},{9,13},{10,... | collective-permute-start | bytes 147464 | tf_op jit(solution)/shard_map/ppermute | solution.py:44
  20.2 2.4 %collective-permute-done.2 = bf16[32,4,384]{2,1,0:T(4,128)(2,1)S(1)} collective-permute-done((bf16[32,4,384]{2,1,0:T(4,128)(2,1)S(1)}, bf16[32,4,384]{2,1,0:T(4,128)(2,1)S(1)}, u32[]{:S(2)}, u32[]{:S(2)}) %collective-permute-start.2) | collective-permute-done | bytes 98336 | tf_op jit(solution)/shard_map/ppermute | solution.py:21
  22.9 1.5 %collective-permute-done.6 = f32[1,1,2,16,384]{4,3,2,1,0:T(8,128)S(1)} collective-permute-done((f32[1,1,2,16,384]{4,3,2,1,0:T(8,128)S(1)}, f32[1,1,2,16,384]{4,3,2,1,0:T(8,128)S(1)}, u32[]{:S(2)}, u32[]{:S(2)}) %collective-permute-start.6) | collective-permute-done | bytes 49184 | tf_op jit(solution)/shard_map/ppermute | solution.py:44
  24.9 3.7 %shard_map.57.fine_ref = f32[24,56,384]{2,1,0:T(8,128)S(1)} custom-call(bf16[1536,2048]{1,0:T(8,128)(2,1)S(1)} %shard_map.56.rows_ref, f32[24,56,384]{2,1,0:T(8,128)S(1)} %copy-done, bf16[4,56,384]{2,1,0:T(8,128)(2,1)S(1)} %bitcast.20, bf16[4,56,384]{2,1,0:T(8,128)(2,1)S(1)} %bitcast.22, bf16[32,8,384]{2,1,0:T(8,128)(2,1)S(1)} %pad_maximum_fusion.side_ref), custom_call_target="tpu_custom_call" | custom-call | flops 2415919104 | bytes 6291456 | tf_op jit(solution)/shard_map/pallas_call | solution.py:475
  28.6 0.6 %shard_map.58 = (f32[24,56,384]{2,1,0:T(8,128)S(1)}, f32[1,56,512]{2,1,0:T(8,128)S(1)}, f32[1,56,512]{2,1,0:T(8,128)S(1)}, f32[6,4,512]{2,1,0:T(4,128)S(1)}, f32[6,4,512]{2,1,0:T(4,128)S(1)}) custom-call(f32[24,56,384]{2,1,0:T(8,128)S(1)} %shard_map.57.fine_ref, f32[24,16,56]{2,1,0:T(8,128)S(1)} %bitcast.12, f32[16,384]{1,0:T(8,128)S(1)} %add_bitcast_fusion.1.lifted_ref, ...), custom_call_target="tpu_custom_call" | custom-call | tf_op jit(solution)/shard_map/pallas_call | solution.py:505
  29.3 1.7 %collective-permute-start.10 = (f32[6,4,512]{2,1,0:T(4,128)S(1)}, f32[6,4,512]{2,1,0:T(4,128)S(1)}, u32[]{:S(2)}, u32[]{:S(2)}) collective-permute-start(f32[6,4,512]{2,1,0:T(4,128)S(1)} %get-tuple-element.30), channel_id=1, source_target_pairs={{0,1},{1,2},{2,3},{3,4},{4,5},{5,6},{6,7},{7,0},{8,9},{9,10},{10,1... | collective-permute-start | bytes 147464 | tf_op jit(solution)/shard_map/ppermute | solution.py:21
  31.0 3.0 %collective-permute-start.11 = (f32[6,4,512]{2,1,0:T(4,128)S(1)}, f32[6,4,512]{2,1,0:T(4,128)S(1)}, u32[]{:S(2)}, u32[]{:S(2)}) collective-permute-start(f32[6,4,512]{2,1,0:T(4,128)S(1)} %get-tuple-element.31), channel_id=1, source_target_pairs={{0,7},{1,0},{2,1},{3,2},{4,3},{5,4},{6,5},{7,6},{8,15},{9,8},{10,9... | collective-permute-start | bytes 147464 | tf_op jit(solution)/shard_map/ppermute | solution.py:21
  34.0 1.7 %collective-permute-start.9 = (f32[1,56,512]{2,1,0:T(8,128)S(1)}, f32[1,56,512]{2,1,0:T(8,128)S(1)}, u32[]{:S(2)}, u32[]{:S(2)}) collective-permute-start(f32[1,56,512]{2,1,0:T(8,128)S(1)} %get-tuple-element.29), channel_id=1, source_target_pairs={{0,24},{8,0},{16,8},{24,16},{1,25},{9,1},{17,9},{25,17},{2,26},{10... | collective-permute-start | bytes 344072 | tf_op jit(solution)/shard_map/ppermute | solution.py:21
  35.8 1.7 %shard_map.59 = (f32[24,56,384]{2,1,0:T(8,128)S(1)}, f32[16,384]{1,0:T(8,128)S(1)}, f32[16,304]{1,0:T(8,128)S(1)}) custom-call(f32[24,56,384]{2,1,0:T(8,128)S(1)} %copy-done, f32[24,56,384]{2,1,0:T(8,128)S(1)} %get-tuple-element.26.now_ref.extra_ref, f32[24,56,128]{2,1,0:T(8,128)S(1)} %broadcast_in_dim.30.heat_ref.extra_ref, f32[24,16,56]{2,1,0:T(8,128)S(1)} %bitcast.13), custom_call_target="tpu_custom_call" | custom-call | bytes 6193152 | tf_op jit(solution)/shard_map/pallas_call | solution.py:378
  37.5 0.7 %collective-permute-done.8 = f32[1,56,512]{2,1,0:T(8,128)S(1)} collective-permute-done((f32[1,56,512]{2,1,0:T(8,128)S(1)}, f32[1,56,512]{2,1,0:T(8,128)S(1)}, u32[]{:S(2)}, u32[]{:S(2)}) %collective-permute-start.8) | collective-permute-done | bytes 114720 | tf_op jit(solution)/shard_map/ppermute | solution.py:21
  38.3 0.4 shard_map.60
  38.7 1.2 %collective-permute-start.12 = (bf16[272,384]{1,0:T(8,128)(2,1)S(1)}, bf16[272,384]{1,0:T(8,128)(2,1)S(1)}, u32[]{:S(2)}, u32[]{:S(2)}) collective-permute-start(bf16[272,384]{1,0:T(8,128)(2,1)S(1)} %get-tuple-element.35), channel_id=1, source_target_pairs={{0,8},{8,16},{16,24},{24,0},{1,9},{9,17},{17,25},{25,1},{2,10},{10... | collective-permute-start | bytes 626696 | tf_op jit(solution)/shard_map/ppermute | solution.py:21
  40.0 0.9 %collective-permute-start.16 = (f32[16,384]{1,0:T(8,128)S(1)}, f32[16,384]{1,0:T(8,128)S(1)}, u32[]{:S(2)}, u32[]{:S(2)}) collective-permute-start(f32[16,384]{1,0:T(8,128)S(1)} %get-tuple-element.38), channel_id=1, source_target_pairs={{0,16},{8,24},{16,0},{24,8},{1,17},{9,25},{17,1},{25,9},{2,18},{10... | collective-permute-start | bytes 73736 | tf_op jit(solution)/shard_map/ppermute | solution.py:21
  40.9 0.5 collective-permute-start.13
  41.4 3.0 %collective-permute-done.12 = bf16[272,384]{1,0:T(8,128)(2,1)S(1)} collective-permute-done((bf16[272,384]{1,0:T(8,128)(2,1)S(1)}, bf16[272,384]{1,0:T(8,128)(2,1)S(1)}, u32[]{:S(2)}, u32[]{:S(2)}) %collective-permute-start.12) | collective-permute-done | bytes 208928 | tf_op jit(solution)/shard_map/ppermute | solution.py:21
  44.5 0.9 %collective-permute-done.13 = bf16[272,384]{1,0:T(8,128)(2,1)S(1)} collective-permute-done((bf16[272,384]{1,0:T(8,128)(2,1)S(1)}, bf16[272,384]{1,0:T(8,128)(2,1)S(1)}, u32[]{:S(2)}, u32[]{:S(2)}) %collective-permute-start.13) | collective-permute-done | bytes 208928 | tf_op jit(solution)/shard_map/ppermute | solution.py:21
  46.2 4.7 %collective-permute-start.15 = (bf16[32,4,384]{2,1,0:T(4,128)(2,1)S(1)}, bf16[32,4,384]{2,1,0:T(4,128)(2,1)S(1)}, u32[]{:S(2)}, u32[]{:S(2)}) collective-permute-start(bf16[32,4,384]{2,1,0:T(4,128)(2,1)S(1)} %get-tuple-element.40), channel_id=1, source_target_pairs={{0,7},{1,0},{2,1},{3,2},{4,3},{5,4},{6,5},{7,6},{8,15},{9,8},{10,9... | collective-permute-start | bytes 294920 | tf_op jit(solution)/shard_map/ppermute | solution.py:21
  50.9 0.5 collective-permute-done.17
  51.6 2.8 %collective-permute-done.14 = bf16[32,4,384]{2,1,0:T(4,128)(2,1)S(1)} collective-permute-done((bf16[32,4,384]{2,1,0:T(4,128)(2,1)S(1)}, bf16[32,4,384]{2,1,0:T(4,128)(2,1)S(1)}, u32[]{:S(2)}, u32[]{:S(2)}) %collective-permute-start.14) | collective-permute-done | bytes 98336 | tf_op jit(solution)/shard_map/ppermute | solution.py:21
  54.5 0.9 %collective-permute-done.15 = bf16[32,4,384]{2,1,0:T(4,128)(2,1)S(1)} collective-permute-done((bf16[32,4,384]{2,1,0:T(4,128)(2,1)S(1)}, bf16[32,4,384]{2,1,0:T(4,128)(2,1)S(1)}, u32[]{:S(2)}, u32[]{:S(2)}) %collective-permute-start.15) | collective-permute-done | bytes 98336 | tf_op jit(solution)/shard_map/ppermute | solution.py:21
  55.5 1.6 %collective-permute-done.18 = f32[1,1,2,16,384]{4,3,2,1,0:T(8,128)S(1)} collective-permute-done((f32[1,1,2,16,384]{4,3,2,1,0:T(8,128)S(1)}, f32[1,1,2,16,384]{4,3,2,1,0:T(8,128)S(1)}, u32[]{:S(2)}, u32[]{:S(2)}) %collective-permute-start.18) | collective-permute-done | bytes 49184 | tf_op jit(solution)/shard_map/ppermute | solution.py:44
  57.3 3.7 %shard_map.61.fine_ref = f32[24,56,384]{2,1,0:T(8,128)S(1)} custom-call(bf16[1536,2048]{1,0:T(8,128)(2,1)S(1)} %shard_map.56.rows_ref, f32[24,56,384]{2,1,0:T(8,128)S(1)} %get-tuple-element.34.block_ref, bf16[4,56,384]{2,1,0:T(8,128)(2,1)S(1)} %bitcast.16, bf16[4,56,384]{2,1,0:T(8,128)(2,1)S(1)} %bitcast.18, bf16[32,8,384]{2,1,0:T(8,128)(2,1)S(1)} %pad_maximum_fusion.1.side_ref), custom_call_target="tpu_custom_call" | custom-call | flops 2415919104 | bytes 6291456 | tf_op jit(solution)/shard_map/pallas_call | solution.py:475
  61.0 1.7 %shard_map.62 = f32[24,56,384]{2,1,0:T(8,128)} custom-call(f32[24,56,384]{2,1,0:T(8,128)S(1)} %shard_map.61.fine_ref, f32[24,16,56]{2,1,0:T(8,128)S(1)} %bitcast.14, f32[16,384]{1,0:T(8,128)S(1)} %add_bitcast_fusion.lifted_ref, f32[24,56,384]{2,1,0:T(8,128)S(1)} %get-tuple-element.26.now_ref.extra_ref), custom_call_target="tpu_custom_call" | custom-call | tf_op jit(solution)/shard_map/pallas_call | solution.py:505
  (70 shorter events, 2.9 us)
Async XLA Ops:
  0.0 3.1 %copy-start.2 = (f32[16,512]{1,0:T(8,128)S(1)}, f32[16,512]{1,0:T(8,128)}, u32[]{:S(2)}) copy-start(f32[16,512]{1,0:T(8,128)} %inverse_hbm.1) | copy-start | bytes 98308
  0.0 7.1 %copy-start.3 = (f32[24,56]{1,0:T(8,128)S(1)}, f32[24,56]{1,0:T(8,128)}, u32[]{:S(2)}) copy-start(f32[24,56]{1,0:T(8,128)} %param.6) | copy-start | bytes 16132
  2.6 7.7 %collective-permute-start = (bf16[288,384]{1,0:T(8,128)(2,1)S(1)}, bf16[288,384]{1,0:T(8,128)(2,1)S(1)}, u32[]{:S(2)}, u32[]{:S(2)}) collective-permute-start(bf16[288,384]{1,0:T(8,128)(2,1)S(1)} %get-tuple-element.23), channel_id=1, source_target_pairs={{0,8},{8,16},{16,24},{24,0},{1,9},{9,17},{17,25},{25,1},{2,10},{10... | collective-permute-start | bytes 663560 | tf_op jit(solution)/shard_map/ppermute | solution.py:21
  3.1 7.1 %collective-permute-start.4 = (f32[16,512]{1,0:T(8,128)S(1)}, f32[16,512]{1,0:T(8,128)S(1)}, u32[]{:S(2)}, u32[]{:S(2)}) collective-permute-start(f32[16,512]{1,0:T(8,128)S(1)} %pad_maximum_fusion.2), channel_id=1, source_target_pairs={{0,16},{8,24},{16,0},{24,8},{1,17},{9,25},{17,1},{25,9},{2,18},{10... | collective-permute-start | bytes 98312 | tf_op jit(solution)/shard_map/ppermute | solution.py:21
  5.7 5.8 %collective-permute-start.1 = (bf16[288,384]{1,0:T(8,128)(2,1)S(1)}, bf16[288,384]{1,0:T(8,128)(2,1)S(1)}, u32[]{:S(2)}, u32[]{:S(2)}) collective-permute-start(bf16[288,384]{1,0:T(8,128)(2,1)S(1)} %get-tuple-element.24), channel_id=1, source_target_pairs={{0,24},{8,0},{16,8},{24,16},{1,25},{9,1},{17,9},{25,17},{2,26},{10... | collective-permute-start | bytes 663560 | tf_op jit(solution)/shard_map/ppermute | solution.py:21
  10.2 14.6 %copy-start = (f32[24,56,384]{2,1,0:T(8,128)S(1)}, f32[24,56,384]{2,1,0:T(8,128)}, u32[]{:S(2)}) copy-start(f32[24,56,384]{2,1,0:T(8,128)} %rhs_ref.3) | copy-start | bytes 6193156
  11.9 6.6 %collective-permute-start.5 = (f32[2,1,2,16,384]{4,3,2,1,0:T(8,128)S(1)}, f32[2,1,2,16,384]{4,3,2,1,0:T(8,128)S(1)}, u32[]{:S(2)}, u32[]{:S(2)}) collective-permute-start(f32[2,1,2,16,384]{4,3,2,1,0:T(8,128)S(1)} %constant_dynamic-slice_fusion.5), channel_id=1, source_target_pairs={{0,2},{1,3},{2,0},{3,1},{4,6},{5,7},{6,4},{7,5},{8,10},{9,11},{10,... | collective-permute-start | bytes 294920 | tf_op jit(solution)/shard_map/ppermute | solution.py:44
  13.8 8.9 %collective-permute-start.2 = (bf16[32,4,384]{2,1,0:T(4,128)(2,1)S(1)}, bf16[32,4,384]{2,1,0:T(4,128)(2,1)S(1)}, u32[]{:S(2)}, u32[]{:S(2)}) collective-permute-start(bf16[32,4,384]{2,1,0:T(4,128)(2,1)S(1)} %get-tuple-element.41), channel_id=1, source_target_pairs={{0,1},{1,2},{2,3},{3,4},{4,5},{5,6},{6,7},{7,0},{8,9},{9,10},{10,1... | collective-permute-start | bytes 294920 | tf_op jit(solution)/shard_map/ppermute | solution.py:21
  15.4 7.3 %collective-permute-start.3 = (bf16[32,4,384]{2,1,0:T(4,128)(2,1)S(1)}, bf16[32,4,384]{2,1,0:T(4,128)(2,1)S(1)}, u32[]{:S(2)}, u32[]{:S(2)}) collective-permute-start(bf16[32,4,384]{2,1,0:T(4,128)(2,1)S(1)} %get-tuple-element.42), channel_id=1, source_target_pairs={{0,7},{1,0},{2,1},{3,2},{4,3},{5,4},{6,5},{7,6},{8,15},{9,8},{10,9... | collective-permute-start | bytes 294920 | tf_op jit(solution)/shard_map/ppermute | solution.py:21
  18.6 5.8 %collective-permute-start.6 = (f32[1,1,2,16,384]{4,3,2,1,0:T(8,128)S(1)}, f32[1,1,2,16,384]{4,3,2,1,0:T(8,128)S(1)}, u32[]{:S(2)}, u32[]{:S(2)}) collective-permute-start(f32[1,1,2,16,384]{4,3,2,1,0:T(8,128)S(1)} %constant_dynamic-slice_fusion.4), channel_id=1, source_target_pairs={{0,4},{1,5},{2,6},{3,7},{4,0},{5,1},{6,2},{7,3},{8,12},{9,13},{10,... | collective-permute-start | bytes 147464 | tf_op jit(solution)/shard_map/ppermute | solution.py:44
  24.4 4.2 %copy-start.1 = (f32[24,56,16]{1,2,0:T(8,128)S(1)}, f32[24,56,16]{1,2,0:T(8,128)}, u32[]{:S(2)}) copy-start(f32[24,56,16]{1,2,0:T(8,128)} %param.8) | copy-start | bytes 258052
  24.4 4.1 %collective-permute-start.7 = (f32[1,1,1,16,384]{4,3,2,1,0:T(8,128)S(1)}, f32[1,1,1,16,384]{4,3,2,1,0:T(8,128)S(1)}, u32[]{:S(2)}, u32[]{:S(2)}) collective-permute-start(f32[1,1,1,16,384]{4,3,2,1,0:T(8,128)S(1)} %constant_dynamic-slice_fusion.3), channel_id=1, source_target_pairs={{0,1},{1,0},{2,3},{3,2},{4,5},{5,4},{6,7},{7,6},{8,9},{9,8},{10,11... | collective-permute-start | bytes 73736 | tf_op jit(solution)/shard_map/ppermute | solution.py:44
  29.3 8.2 %collective-permute-start.10 = (f32[6,4,512]{2,1,0:T(4,128)S(1)}, f32[6,4,512]{2,1,0:T(4,128)S(1)}, u32[]{:S(2)}, u32[]{:S(2)}) collective-permute-start(f32[6,4,512]{2,1,0:T(4,128)S(1)} %get-tuple-element.30), channel_id=1, source_target_pairs={{0,1},{1,2},{2,3},{3,4},{4,5},{5,6},{6,7},{7,0},{8,9},{9,10},{10,1... | collective-permute-start | bytes 147464 | tf_op jit(solution)/shard_map/ppermute | solution.py:21
  31.0 6.5 %collective-permute-start.11 = (f32[6,4,512]{2,1,0:T(4,128)S(1)}, f32[6,4,512]{2,1,0:T(4,128)S(1)}, u32[]{:S(2)}, u32[]{:S(2)}) collective-permute-start(f32[6,4,512]{2,1,0:T(4,128)S(1)} %get-tuple-element.31), channel_id=1, source_target_pairs={{0,7},{1,0},{2,1},{3,2},{4,3},{5,4},{6,5},{7,6},{8,15},{9,8},{10,9... | collective-permute-start | bytes 147464 | tf_op jit(solution)/shard_map/ppermute | solution.py:21
  34.0 4.2 %collective-permute-start.8 = (f32[1,56,512]{2,1,0:T(8,128)S(1)}, f32[1,56,512]{2,1,0:T(8,128)S(1)}, u32[]{:S(2)}, u32[]{:S(2)}) collective-permute-start(f32[1,56,512]{2,1,0:T(8,128)S(1)} %get-tuple-element.28), channel_id=1, source_target_pairs={{0,8},{8,16},{16,24},{24,0},{1,9},{9,17},{17,25},{25,1},{2,10},{10... | collective-permute-start | bytes 344072 | tf_op jit(solution)/shard_map/ppermute | solution.py:21
  34.0 4.2 %collective-permute-start.9 = (f32[1,56,512]{2,1,0:T(8,128)S(1)}, f32[1,56,512]{2,1,0:T(8,128)S(1)}, u32[]{:S(2)}, u32[]{:S(2)}) collective-permute-start(f32[1,56,512]{2,1,0:T(8,128)S(1)} %get-tuple-element.29), channel_id=1, source_target_pairs={{0,24},{8,0},{16,8},{24,16},{1,25},{9,1},{17,9},{25,17},{2,26},{10... | collective-permute-start | bytes 344072 | tf_op jit(solution)/shard_map/ppermute | solution.py:21
  38.7 5.7 %collective-permute-start.12 = (bf16[272,384]{1,0:T(8,128)(2,1)S(1)}, bf16[272,384]{1,0:T(8,128)(2,1)S(1)}, u32[]{:S(2)}, u32[]{:S(2)}) collective-permute-start(bf16[272,384]{1,0:T(8,128)(2,1)S(1)} %get-tuple-element.35), channel_id=1, source_target_pairs={{0,8},{8,16},{16,24},{24,0},{1,9},{9,17},{17,25},{25,1},{2,10},{10... | collective-permute-start | bytes 626696 | tf_op jit(solution)/shard_map/ppermute | solution.py:21
  40.0 5.5 %collective-permute-start.16 = (f32[16,384]{1,0:T(8,128)S(1)}, f32[16,384]{1,0:T(8,128)S(1)}, u32[]{:S(2)}, u32[]{:S(2)}) collective-permute-start(f32[16,384]{1,0:T(8,128)S(1)} %get-tuple-element.38), channel_id=1, source_target_pairs={{0,16},{8,24},{16,0},{24,8},{1,17},{9,25},{17,1},{25,9},{2,18},{10... | collective-permute-start | bytes 73736 | tf_op jit(solution)/shard_map/ppermute | solution.py:21
  40.9 4.5 %collective-permute-start.13 = (bf16[272,384]{1,0:T(8,128)(2,1)S(1)}, bf16[272,384]{1,0:T(8,128)(2,1)S(1)}, u32[]{:S(2)}, u32[]{:S(2)}) collective-permute-start(bf16[272,384]{1,0:T(8,128)(2,1)S(1)} %get-tuple-element.36), channel_id=1, source_target_pairs={{0,24},{8,0},{16,8},{24,16},{1,25},{9,1},{17,9},{25,17},{2,26},{10... | collective-permute-start | bytes 626696 | tf_op jit(solution)/shard_map/ppermute | solution.py:21
  45.9 5.5 %collective-permute-start.17 = (f32[2,1,2,16,384]{4,3,2,1,0:T(8,128)S(1)}, f32[2,1,2,16,384]{4,3,2,1,0:T(8,128)S(1)}, u32[]{:S(2)}, u32[]{:S(2)}) collective-permute-start(f32[2,1,2,16,384]{4,3,2,1,0:T(8,128)S(1)} %constant_dynamic-slice_fusion.2), channel_id=1, source_target_pairs={{0,2},{1,3},{2,0},{3,1},{4,6},{5,7},{6,4},{7,5},{8,10},{9,11},{10,... | collective-permute-start | bytes 294920 | tf_op jit(solution)/shard_map/ppermute | solution.py:44
  46.1 8.3 %collective-permute-start.14 = (bf16[32,4,384]{2,1,0:T(4,128)(2,1)S(1)}, bf16[32,4,384]{2,1,0:T(4,128)(2,1)S(1)}, u32[]{:S(2)}, u32[]{:S(2)}) collective-permute-start(bf16[32,4,384]{2,1,0:T(4,128)(2,1)S(1)} %get-tuple-element.39), channel_id=1, source_target_pairs={{0,1},{1,2},{2,3},{3,4},{4,5},{5,6},{6,7},{7,0},{8,9},{9,10},{10,1... | collective-permute-start | bytes 294920 | tf_op jit(solution)/shard_map/ppermute | solution.py:21
  46.2 9.2 %collective-permute-start.15 = (bf16[32,4,384]{2,1,0:T(4,128)(2,1)S(1)}, bf16[32,4,384]{2,1,0:T(4,128)(2,1)S(1)}, u32[]{:S(2)}, u32[]{:S(2)}) collective-permute-start(bf16[32,4,384]{2,1,0:T(4,128)(2,1)S(1)} %get-tuple-element.40), channel_id=1, source_target_pairs={{0,7},{1,0},{2,1},{3,2},{4,3},{5,4},{6,5},{7,6},{8,15},{9,8},{10,9... | collective-permute-start | bytes 294920 | tf_op jit(solution)/shard_map/ppermute | solution.py:21
  51.4 5.7 %collective-permute-start.18 = (f32[1,1,2,16,384]{4,3,2,1,0:T(8,128)S(1)}, f32[1,1,2,16,384]{4,3,2,1,0:T(8,128)S(1)}, u32[]{:S(2)}, u32[]{:S(2)}) collective-permute-start(f32[1,1,2,16,384]{4,3,2,1,0:T(8,128)S(1)} %constant_dynamic-slice_fusion.1), channel_id=1, source_target_pairs={{0,4},{1,5},{2,6},{3,7},{4,0},{5,1},{6,2},{7,3},{8,12},{9,13},{10,... | collective-permute-start | bytes 147464 | tf_op jit(solution)/shard_map/ppermute | solution.py:44
  57.1 3.9 %collective-permute-start.19 = (f32[1,1,1,16,384]{4,3,2,1,0:T(8,128)S(1)}, f32[1,1,1,16,384]{4,3,2,1,0:T(8,128)S(1)}, u32[]{:S(2)}, u32[]{:S(2)}) collective-permute-start(f32[1,1,1,16,384]{4,3,2,1,0:T(8,128)S(1)} %constant_dynamic-slice_fusion), channel_id=1, source_target_pairs={{0,1},{1,0},{2,3},{3,2},{4,5},{5,4},{6,7},{7,6},{8,9},{9,8},{10,11... | collective-permute-start | bytes 73736 | tf_op jit(solution)/shard_map/ppermute | solution.py:44

commit v9 on v8

--- a/solution.py
+++ b/solution.py
@@ -9,7 +9,6 @@
 
 OV = 4
 ITERS = 2
-HOLD = 6
 LANES = 128
 EXACT = lax.Precision.HIGHEST
 F32 = jnp.float32
@@ -91,11 +90,10 @@
 
 def finish(total, start, down_ref, up_ref, sum_ref):
     sum_ref[...] = total
-    parts = jnp.concatenate(split(total), axis=0)
+    parts = jnp.concatenate(split(total)[:2], axis=0)
     end = start + parts.shape[0]
     down_ref[start:end] = parts
     up_ref[start:end] = parts
-    return end
 
 
 def start_kernel(
@@ -131,7 +129,7 @@
     groups = lax.axis_size("grp")
     width = inverse_ref.shape[1] // groups
     modes = inverse_ref.shape[0]
-    start = OV * own_y + 3 * modes
+    start = OV * own_y + 2 * modes
     for ref, step in ((up_ref, 1), (down_ref, groups - 1)):
         group = lax.rem(lax.axis_index("grp") + step, groups)
         wanted = inverse_ref[:, pl.ds(pl.multiple_of(group * width, width), width)]
@@ -345,7 +343,7 @@
     members, groups = lax.axis_size("mem"), lax.axis_size("grp")
     width = members * modes
     edge_rows = OV * own_y
-    sum_rows = 3 * modes
+    sum_rows = 2 * modes
     inverse_rows = 3 * width // columns * modes
 
     def survey_shapes(rows):
@@ -403,11 +401,10 @@
         )(part, now, *around, heat, part_sum, edge_modes)
 
     def added(parts):
-        high, middle, low = (part.astype(F32) for part in parts)
-        return high + middle + low
+        return sum(part.astype(F32) for part in parts)
 
     def sums_in(message):
-        return added(jnp.split(message[edge_rows : edge_rows + sum_rows], 3, axis=0))
+        return added(jnp.split(message[edge_rows : edge_rows + sum_rows], 2, axis=0))
 
     def inverse_in(message):
         pieces = message[edge_rows + sum_rows :]
@@ -464,7 +461,7 @@
             in_specs=[in_hbm, pl.BlockSpec(memory_space=pl.ANY), pl.BlockSpec(memory_space=pl.ANY)],
             out_specs=in_vmem,
             out_shape=shape_of(held, BF16),
-            scratch_shapes=[pltpu.SemaphoreType.DMA((HOLD,))],
+            scratch_shapes=[pltpu.SemaphoreType.DMA((own_x // OV,))],
             compiler_params=params(8),
             cost_estimate=pl.CostEstimate(
                 flops=0, bytes_accessed=4 * held[0] * local, transcendentals=0

time: 63 us -> 62.5 us (level)
  no operation moved by 1% of the time
where the time goes in v9:
time: 62.5 us; the launch traced here: 62.3 us
  starting transfers between devices  27.3 us (44%)
  Pallas kernels  17.3 us (28%)
  waiting for transfers between devices  15.2 us (24%)
  matrix products  0.74 us (1%)
  other arithmetic  0.71 us (1%)
    ppermute x14, starting transfers between devices, shifted(): lax.ppermute(value, axis, [(i, (i + distance) % count) for i in range(cou...  23.2 us
    ppermute x14, waiting for transfers between devices, shifted(): lax.ppermute(value, axis, [(i, (i + distance) % count) for i in range(cou...  11.5 us
    pallas_call x2, Pallas kernels, fine(): pl.pallas_call(fine_kernel, in_specs=[in_vmem] * 5, out_specs=in_vmem, ou...  7.44 us
    ppermute x6, starting transfers between devices, summed_over_members(): shares = keep + lax.ppermute(send, 'mem', pairs)  4.08 us
    ppermute x6, waiting for transfers between devices, summed_over_members(): shares = keep + lax.ppermute(send, 'mem', pairs)  3.66 us
    pallas_call x1, Pallas kernels, held_rows(): pl.pallas_call(hold_kernel, in_specs=[in_hbm, pl.BlockSpec(memory_space=p...  2.86 us
    pallas_call x1, Pallas kernels, surveyed_start(): pl.pallas_call(start_kernel, in_specs=[in_hbm] * 3, out_specs=[in_vmem] *...  2.56 us
    pallas_call x2, Pallas kernels, updated(): pl.pallas_call(functools.partial(update_kernel, last), in_specs=[in_vmem]...  2.33 us
  transfers between devices with their start and end apart: 20, of which 10 were waited for; matrix products, arithmetic and copies ran while one was open for 2% of the time, Pallas kernels for 19%

profile of v9, /device:TPU:0, one launch (start us, length us, event | category | flops | bytes accessed | tf_op | source)
XLA Modules:
  0.0 62.3 jit_solution(4591354214682412367)
XLA Ops:
  0.0 2.6 %shard_map.55 = (bf16[272,384]{1,0:T(8,128)(2,1)S(1)}, bf16[272,384]{1,0:T(8,128)(2,1)S(1)}, bf16[24,8,384]{2,1,0:T(8,128)(2,1)S(1)}, f32[16,384]{1,0:T(8,128)S(1)}) custom-call(f32[24,56,384]{2,1,0:T(8,128)} %rhs_ref.3, f32[24,16,56]{2,1,0:T(8,128)} %bitcast.11, f32[16,512]{1,0:T(8,128)} %inverse_hbm.1), custom_call_target="tpu_custom_call" | custom-call | tf_op jit(solution)/shard_map/pallas_call | solution.py:358
  2.6 0.5 collective-permute-start
  3.1 2.6 %collective-permute-start.4 = (f32[16,512]{1,0:T(8,128)S(1)}, f32[16,512]{1,0:T(8,128)S(1)}, u32[]{:S(2)}, u32[]{:S(2)}) collective-permute-start(f32[16,512]{1,0:T(8,128)S(1)} %pad_maximum_fusion.2), channel_id=1, source_target_pairs={{0,16},{8,24},{16,0},{24,8},{1,17},{9,25},{17,1},{25,9},{2,18},{10... | collective-permute-start | bytes 98312 | tf_op jit(solution)/shard_map/ppermute | solution.py:20
  5.7 1.4 %collective-permute-start.1 = (bf16[272,384]{1,0:T(8,128)(2,1)S(1)}, bf16[272,384]{1,0:T(8,128)(2,1)S(1)}, u32[]{:S(2)}, u32[]{:S(2)}) collective-permute-start(bf16[272,384]{1,0:T(8,128)(2,1)S(1)} %get-tuple-element.24), channel_id=1, source_target_pairs={{0,24},{8,0},{16,8},{24,16},{1,25},{9,1},{17,9},{25,17},{2,26},{10... | collective-permute-start | bytes 626696 | tf_op jit(solution)/shard_map/ppermute | solution.py:20
  7.4 2.9 %shard_map.56.rows_ref = bf16[1536,2048]{1,0:T(8,128)(2,1)S(1)} custom-call(bf16[2048,2048]{1,0:T(8,128)(2,1)} %inverse_ref.1, f32[24,56,128]{2,1,0:T(8,128)S(1)} %broadcast_in_dim.30.heat_ref.extra_ref, f32[16,384]{1,0:T(8,128)S(1)} %get-tuple-element.22.order_ref), custom_call_target="tpu_custom_call" | custom-call | bytes 12582912 | tf_op jit(solution)/shard_map/pallas_call | solution.py:459
  10.3 0.9 %collective-permute-done.1 = bf16[272,384]{1,0:T(8,128)(2,1)S(1)} collective-permute-done((bf16[272,384]{1,0:T(8,128)(2,1)S(1)}, bf16[272,384]{1,0:T(8,128)(2,1)S(1)}, u32[]{:S(2)}, u32[]{:S(2)}) %collective-permute-start.1) | collective-permute-done | bytes 208928 | tf_op jit(solution)/shard_map/ppermute | solution.py:20
  11.7 1.6 %collective-permute-start.5 = (f32[2,1,2,16,384]{4,3,2,1,0:T(8,128)S(1)}, f32[2,1,2,16,384]{4,3,2,1,0:T(8,128)S(1)}, u32[]{:S(2)}, u32[]{:S(2)}) collective-permute-start(f32[2,1,2,16,384]{4,3,2,1,0:T(8,128)S(1)} %constant_dynamic-slice_fusion.5), channel_id=1, source_target_pairs={{0,2},{1,3},{2,0},{3,1},{4,6},{5,7},{6,4},{7,5},{8,10},{9,11},{10,... | collective-permute-start | bytes 294920 | tf_op jit(solution)/shard_map/ppermute | solution.py:43
  13.5 1.6 %collective-permute-start.2 = (bf16[32,4,384]{2,1,0:T(4,128)(2,1)S(1)}, bf16[32,4,384]{2,1,0:T(4,128)(2,1)S(1)}, u32[]{:S(2)}, u32[]{:S(2)}) collective-permute-start(bf16[32,4,384]{2,1,0:T(4,128)(2,1)S(1)} %get-tuple-element.41), channel_id=1, source_target_pairs={{0,1},{1,2},{2,3},{3,4},{4,5},{5,6},{6,7},{7,0},{8,9},{9,10},{10,1... | collective-permute-start | bytes 294920 | tf_op jit(solution)/shard_map/ppermute | solution.py:20
  15.1 3.2 %collective-permute-start.3 = (bf16[32,4,384]{2,1,0:T(4,128)(2,1)S(1)}, bf16[32,4,384]{2,1,0:T(4,128)(2,1)S(1)}, u32[]{:S(2)}, u32[]{:S(2)}) collective-permute-start(bf16[32,4,384]{2,1,0:T(4,128)(2,1)S(1)} %get-tuple-element.42), channel_id=1, source_target_pairs={{0,7},{1,0},{2,1},{3,2},{4,3},{5,4},{6,5},{7,6},{8,15},{9,8},{10,9... | collective-permute-start | bytes 294920 | tf_op jit(solution)/shard_map/ppermute | solution.py:20
  18.3 1.6 %collective-permute-start.6 = (f32[1,1,2,16,384]{4,3,2,1,0:T(8,128)S(1)}, f32[1,1,2,16,384]{4,3,2,1,0:T(8,128)S(1)}, u32[]{:S(2)}, u32[]{:S(2)}) collective-permute-start(f32[1,1,2,16,384]{4,3,2,1,0:T(8,128)S(1)} %constant_dynamic-slice_fusion.4), channel_id=1, source_target_pairs={{0,4},{1,5},{2,6},{3,7},{4,0},{5,1},{6,2},{7,3},{8,12},{9,13},{10,... | collective-permute-start | bytes 147464 | tf_op jit(solution)/shard_map/ppermute | solution.py:43
  19.9 2.4 %collective-permute-done.2 = bf16[32,4,384]{2,1,0:T(4,128)(2,1)S(1)} collective-permute-done((bf16[32,4,384]{2,1,0:T(4,128)(2,1)S(1)}, bf16[32,4,384]{2,1,0:T(4,128)(2,1)S(1)}, u32[]{:S(2)}, u32[]{:S(2)}) %collective-permute-start.2) | collective-permute-done | bytes 98336 | tf_op jit(solution)/shard_map/ppermute | solution.py:20
  22.6 1.5 %collective-permute-done.6 = f32[1,1,2,16,384]{4,3,2,1,0:T(8,128)S(1)} collective-permute-done((f32[1,1,2,16,384]{4,3,2,1,0:T(8,128)S(1)}, f32[1,1,2,16,384]{4,3,2,1,0:T(8,128)S(1)}, u32[]{:S(2)}, u32[]{:S(2)}) %collective-permute-start.6) | collective-permute-done | bytes 49184 | tf_op jit(solution)/shard_map/ppermute | solution.py:43
  24.6 3.7 %shard_map.57.fine_ref = f32[24,56,384]{2,1,0:T(8,128)S(1)} custom-call(bf16[1536,2048]{1,0:T(8,128)(2,1)S(1)} %shard_map.56.rows_ref, f32[24,56,384]{2,1,0:T(8,128)S(1)} %copy-done, bf16[4,56,384]{2,1,0:T(8,128)(2,1)S(1)} %bitcast.20, bf16[4,56,384]{2,1,0:T(8,128)(2,1)S(1)} %bitcast.22, bf16[32,8,384]{2,1,0:T(8,128)(2,1)S(1)} %pad_maximum_fusion.side_ref), custom_call_target="tpu_custom_call" | custom-call | flops 2415919104 | bytes 6291456 | tf_op jit(solution)/shard_map/pallas_call | solution.py:472
  28.4 0.6 %shard_map.58 = (f32[24,56,384]{2,1,0:T(8,128)S(1)}, f32[1,56,512]{2,1,0:T(8,128)S(1)}, f32[1,56,512]{2,1,0:T(8,128)S(1)}, f32[6,4,512]{2,1,0:T(4,128)S(1)}, f32[6,4,512]{2,1,0:T(4,128)S(1)}) custom-call(f32[24,56,384]{2,1,0:T(8,128)S(1)} %shard_map.57.fine_ref, f32[24,16,56]{2,1,0:T(8,128)S(1)} %bitcast.12, f32[16,384]{1,0:T(8,128)S(1)} %add_bitcast_fusion.1.lifted_ref, ...), custom_call_target="tpu_custom_call" | custom-call | tf_op jit(solution)/shard_map/pallas_call | solution.py:502
  29.0 1.7 %collective-permute-start.10 = (f32[6,4,512]{2,1,0:T(4,128)S(1)}, f32[6,4,512]{2,1,0:T(4,128)S(1)}, u32[]{:S(2)}, u32[]{:S(2)}) collective-permute-start(f32[6,4,512]{2,1,0:T(4,128)S(1)} %get-tuple-element.30), channel_id=1, source_target_pairs={{0,1},{1,2},{2,3},{3,4},{4,5},{5,6},{6,7},{7,0},{8,9},{9,10},{10,1... | collective-permute-start | bytes 147464 | tf_op jit(solution)/shard_map/ppermute | solution.py:20
  30.7 3.0 %collective-permute-start.11 = (f32[6,4,512]{2,1,0:T(4,128)S(1)}, f32[6,4,512]{2,1,0:T(4,128)S(1)}, u32[]{:S(2)}, u32[]{:S(2)}) collective-permute-start(f32[6,4,512]{2,1,0:T(4,128)S(1)} %get-tuple-element.31), channel_id=1, source_target_pairs={{0,7},{1,0},{2,1},{3,2},{4,3},{5,4},{6,5},{7,6},{8,15},{9,8},{10,9... | collective-permute-start | bytes 147464 | tf_op jit(solution)/shard_map/ppermute | solution.py:20
  33.8 1.7 %collective-permute-start.9 = (f32[1,56,512]{2,1,0:T(8,128)S(1)}, f32[1,56,512]{2,1,0:T(8,128)S(1)}, u32[]{:S(2)}, u32[]{:S(2)}) collective-permute-start(f32[1,56,512]{2,1,0:T(8,128)S(1)} %get-tuple-element.29), channel_id=1, source_target_pairs={{0,24},{8,0},{16,8},{24,16},{1,25},{9,1},{17,9},{25,17},{2,26},{10... | collective-permute-start | bytes 344072 | tf_op jit(solution)/shard_map/ppermute | solution.py:20
  35.5 1.7 %shard_map.59 = (f32[24,56,384]{2,1,0:T(8,128)S(1)}, f32[16,384]{1,0:T(8,128)S(1)}, f32[16,304]{1,0:T(8,128)S(1)}) custom-call(f32[24,56,384]{2,1,0:T(8,128)S(1)} %copy-done, f32[24,56,384]{2,1,0:T(8,128)S(1)} %get-tuple-element.26.now_ref.extra_ref, f32[24,56,128]{2,1,0:T(8,128)S(1)} %broadcast_in_dim.30.heat_ref.extra_ref, f32[24,16,56]{2,1,0:T(8,128)S(1)} %bitcast.13), custom_call_target="tpu_custom_call" | custom-call | bytes 6193152 | tf_op jit(solution)/shard_map/pallas_call | solution.py:376
  37.2 0.7 %collective-permute-done.8 = f32[1,56,512]{2,1,0:T(8,128)S(1)} collective-permute-done((f32[1,56,512]{2,1,0:T(8,128)S(1)}, f32[1,56,512]{2,1,0:T(8,128)S(1)}, u32[]{:S(2)}, u32[]{:S(2)}) %collective-permute-start.8) | collective-permute-done | bytes 114720 | tf_op jit(solution)/shard_map/ppermute | solution.py:20
  38.0 0.4 shard_map.60
  38.5 1.2 %collective-permute-start.12 = (bf16[256,384]{1,0:T(8,128)(2,1)S(1)}, bf16[256,384]{1,0:T(8,128)(2,1)S(1)}, u32[]{:S(2)}, u32[]{:S(2)}) collective-permute-start(bf16[256,384]{1,0:T(8,128)(2,1)S(1)} %get-tuple-element.35), channel_id=1, source_target_pairs={{0,8},{8,16},{16,24},{24,0},{1,9},{9,17},{17,25},{25,1},{2,10},{10... | collective-permute-start | bytes 589832 | tf_op jit(solution)/shard_map/ppermute | solution.py:20
  39.7 0.9 %collective-permute-start.16 = (f32[16,384]{1,0:T(8,128)S(1)}, f32[16,384]{1,0:T(8,128)S(1)}, u32[]{:S(2)}, u32[]{:S(2)}) collective-permute-start(f32[16,384]{1,0:T(8,128)S(1)} %get-tuple-element.38), channel_id=1, source_target_pairs={{0,16},{8,24},{16,0},{24,8},{1,17},{9,25},{17,1},{25,9},{2,18},{10... | collective-permute-start | bytes 73736 | tf_op jit(solution)/shard_map/ppermute | solution.py:20
  40.6 0.5 collective-permute-start.13
  41.1 2.8 %collective-permute-done.12 = bf16[256,384]{1,0:T(8,128)(2,1)S(1)} collective-permute-done((bf16[256,384]{1,0:T(8,128)(2,1)S(1)}, bf16[256,384]{1,0:T(8,128)(2,1)S(1)}, u32[]{:S(2)}, u32[]{:S(2)}) %collective-permute-start.12) | collective-permute-done | bytes 196640 | tf_op jit(solution)/shard_map/ppermute | solution.py:20
  43.9 0.9 %collective-permute-done.13 = bf16[256,384]{1,0:T(8,128)(2,1)S(1)} collective-permute-done((bf16[256,384]{1,0:T(8,128)(2,1)S(1)}, bf16[256,384]{1,0:T(8,128)(2,1)S(1)}, u32[]{:S(2)}, u32[]{:S(2)}) %collective-permute-start.13) | collective-permute-done | bytes 196640 | tf_op jit(solution)/shard_map/ppermute | solution.py:20
  45.6 4.7 %collective-permute-start.15 = (bf16[32,4,384]{2,1,0:T(4,128)(2,1)S(1)}, bf16[32,4,384]{2,1,0:T(4,128)(2,1)S(1)}, u32[]{:S(2)}, u32[]{:S(2)}) collective-permute-start(bf16[32,4,384]{2,1,0:T(4,128)(2,1)S(1)} %get-tuple-element.40), channel_id=1, source_target_pairs={{0,7},{1,0},{2,1},{3,2},{4,3},{5,4},{6,5},{7,6},{8,15},{9,8},{10,9... | collective-permute-start | bytes 294920 | tf_op jit(solution)/shard_map/ppermute | solution.py:20
  50.3 0.5 collective-permute-done.17
  51.1 2.8 %collective-permute-done.14 = bf16[32,4,384]{2,1,0:T(4,128)(2,1)S(1)} collective-permute-done((bf16[32,4,384]{2,1,0:T(4,128)(2,1)S(1)}, bf16[32,4,384]{2,1,0:T(4,128)(2,1)S(1)}, u32[]{:S(2)}, u32[]{:S(2)}) %collective-permute-start.14) | collective-permute-done | bytes 98336 | tf_op jit(solution)/shard_map/ppermute | solution.py:20
  53.9 0.9 %collective-permute-done.15 = bf16[32,4,384]{2,1,0:T(4,128)(2,1)S(1)} collective-permute-done((bf16[32,4,384]{2,1,0:T(4,128)(2,1)S(1)}, bf16[32,4,384]{2,1,0:T(4,128)(2,1)S(1)}, u32[]{:S(2)}, u32[]{:S(2)}) %collective-permute-start.15) | collective-permute-done | bytes 98336 | tf_op jit(solution)/shard_map/ppermute | solution.py:20
  54.9 1.6 %collective-permute-done.18 = f32[1,1,2,16,384]{4,3,2,1,0:T(8,128)S(1)} collective-permute-done((f32[1,1,2,16,384]{4,3,2,1,0:T(8,128)S(1)}, f32[1,1,2,16,384]{4,3,2,1,0:T(8,128)S(1)}, u32[]{:S(2)}, u32[]{:S(2)}) %collective-permute-start.18) | collective-permute-done | bytes 49184 | tf_op jit(solution)/shard_map/ppermute | solution.py:43
  56.7 3.7 %shard_map.61.fine_ref = f32[24,56,384]{2,1,0:T(8,128)S(1)} custom-call(bf16[1536,2048]{1,0:T(8,128)(2,1)S(1)} %shard_map.56.rows_ref, f32[24,56,384]{2,1,0:T(8,128)S(1)} %get-tuple-element.34.block_ref, bf16[4,56,384]{2,1,0:T(8,128)(2,1)S(1)} %bitcast.16, bf16[4,56,384]{2,1,0:T(8,128)(2,1)S(1)} %bitcast.18, bf16[32,8,384]{2,1,0:T(8,128)(2,1)S(1)} %pad_maximum_fusion.1.side_ref), custom_call_target="tpu_custom_call" | custom-call | flops 2415919104 | bytes 6291456 | tf_op jit(solution)/shard_map/pallas_call | solution.py:472
  60.5 1.7 %shard_map.62 = f32[24,56,384]{2,1,0:T(8,128)} custom-call(f32[24,56,384]{2,1,0:T(8,128)S(1)} %shard_map.61.fine_ref, f32[24,16,56]{2,1,0:T(8,128)S(1)} %bitcast.14, f32[16,384]{1,0:T(8,128)S(1)} %add_bitcast_fusion.lifted_ref, f32[24,56,384]{2,1,0:T(8,128)S(1)} %get-tuple-element.26.now_ref.extra_ref), custom_call_target="tpu_custom_call" | custom-call | tf_op jit(solution)/shard_map/pallas_call | solution.py:502
  (70 shorter events, 2.9 us)
Async XLA Ops:
  0.0 3.1 %copy-start.2 = (f32[16,512]{1,0:T(8,128)S(1)}, f32[16,512]{1,0:T(8,128)}, u32[]{:S(2)}) copy-start(f32[16,512]{1,0:T(8,128)} %inverse_hbm.1) | copy-start | bytes 98308
  0.0 7.1 %copy-start.3 = (f32[24,56]{1,0:T(8,128)S(1)}, f32[24,56]{1,0:T(8,128)}, u32[]{:S(2)}) copy-start(f32[24,56]{1,0:T(8,128)} %param.6) | copy-start | bytes 16132
  2.6 7.7 %collective-permute-start = (bf16[272,384]{1,0:T(8,128)(2,1)S(1)}, bf16[272,384]{1,0:T(8,128)(2,1)S(1)}, u32[]{:S(2)}, u32[]{:S(2)}) collective-permute-start(bf16[272,384]{1,0:T(8,128)(2,1)S(1)} %get-tuple-element.23), channel_id=1, source_target_pairs={{0,8},{8,16},{16,24},{24,0},{1,9},{9,17},{17,25},{25,1},{2,10},{10... | collective-permute-start | bytes 626696 | tf_op jit(solution)/shard_map/ppermute | solution.py:20
  3.1 7.1 %collective-permute-start.4 = (f32[16,512]{1,0:T(8,128)S(1)}, f32[16,512]{1,0:T(8,128)S(1)}, u32[]{:S(2)}, u32[]{:S(2)}) collective-permute-start(f32[16,512]{1,0:T(8,128)S(1)} %pad_maximum_fusion.2), channel_id=1, source_target_pairs={{0,16},{8,24},{16,0},{24,8},{1,17},{9,25},{17,1},{25,9},{2,18},{10... | collective-permute-start | bytes 98312 | tf_op jit(solution)/shard_map/ppermute | solution.py:20
  5.7 5.5 %collective-permute-start.1 = (bf16[272,384]{1,0:T(8,128)(2,1)S(1)}, bf16[272,384]{1,0:T(8,128)(2,1)S(1)}, u32[]{:S(2)}, u32[]{:S(2)}) collective-permute-start(bf16[272,384]{1,0:T(8,128)(2,1)S(1)} %get-tuple-element.24), channel_id=1, source_target_pairs={{0,24},{8,0},{16,8},{24,16},{1,25},{9,1},{17,9},{25,17},{2,26},{10... | collective-permute-start | bytes 626696 | tf_op jit(solution)/shard_map/ppermute | solution.py:20
  10.2 14.4 %copy-start = (f32[24,56,384]{2,1,0:T(8,128)S(1)}, f32[24,56,384]{2,1,0:T(8,128)}, u32[]{:S(2)}) copy-start(f32[24,56,384]{2,1,0:T(8,128)} %rhs_ref.3) | copy-start | bytes 6193156
  11.7 6.6 %collective-permute-start.5 = (f32[2,1,2,16,384]{4,3,2,1,0:T(8,128)S(1)}, f32[2,1,2,16,384]{4,3,2,1,0:T(8,128)S(1)}, u32[]{:S(2)}, u32[]{:S(2)}) collective-permute-start(f32[2,1,2,16,384]{4,3,2,1,0:T(8,128)S(1)} %constant_dynamic-slice_fusion.5), channel_id=1, source_target_pairs={{0,2},{1,3},{2,0},{3,1},{4,6},{5,7},{6,4},{7,5},{8,10},{9,11},{10,... | collective-permute-start | bytes 294920 | tf_op jit(solution)/shard_map/ppermute | solution.py:43
  13.5 8.9 %collective-permute-start.2 = (bf16[32,4,384]{2,1,0:T(4,128)(2,1)S(1)}, bf16[32,4,384]{2,1,0:T(4,128)(2,1)S(1)}, u32[]{:S(2)}, u32[]{:S(2)}) collective-permute-start(bf16[32,4,384]{2,1,0:T(4,128)(2,1)S(1)} %get-tuple-element.41), channel_id=1, source_target_pairs={{0,1},{1,2},{2,3},{3,4},{4,5},{5,6},{6,7},{7,0},{8,9},{9,10},{10,1... | collective-permute-start | bytes 294920 | tf_op jit(solution)/shard_map/ppermute | solution.py:20
  15.1 7.3 %collective-permute-start.3 = (bf16[32,4,384]{2,1,0:T(4,128)(2,1)S(1)}, bf16[32,4,384]{2,1,0:T(4,128)(2,1)S(1)}, u32[]{:S(2)}, u32[]{:S(2)}) collective-permute-start(bf16[32,4,384]{2,1,0:T(4,128)(2,1)S(1)} %get-tuple-element.42), channel_id=1, source_target_pairs={{0,7},{1,0},{2,1},{3,2},{4,3},{5,4},{6,5},{7,6},{8,15},{9,8},{10,9... | collective-permute-start | bytes 294920 | tf_op jit(solution)/shard_map/ppermute | solution.py:20
  18.3 5.8 %collective-permute-start.6 = (f32[1,1,2,16,384]{4,3,2,1,0:T(8,128)S(1)}, f32[1,1,2,16,384]{4,3,2,1,0:T(8,128)S(1)}, u32[]{:S(2)}, u32[]{:S(2)}) collective-permute-start(f32[1,1,2,16,384]{4,3,2,1,0:T(8,128)S(1)} %constant_dynamic-slice_fusion.4), channel_id=1, source_target_pairs={{0,4},{1,5},{2,6},{3,7},{4,0},{5,1},{6,2},{7,3},{8,12},{9,13},{10,... | collective-permute-start | bytes 147464 | tf_op jit(solution)/shard_map/ppermute | solution.py:43
  24.2 4.2 %copy-start.1 = (f32[24,56,16]{1,2,0:T(8,128)S(1)}, f32[24,56,16]{1,2,0:T(8,128)}, u32[]{:S(2)}) copy-start(f32[24,56,16]{1,2,0:T(8,128)} %param.8) | copy-start | bytes 258052
  24.2 4.1 %collective-permute-start.7 = (f32[1,1,1,16,384]{4,3,2,1,0:T(8,128)S(1)}, f32[1,1,1,16,384]{4,3,2,1,0:T(8,128)S(1)}, u32[]{:S(2)}, u32[]{:S(2)}) collective-permute-start(f32[1,1,1,16,384]{4,3,2,1,0:T(8,128)S(1)} %constant_dynamic-slice_fusion.3), channel_id=1, source_target_pairs={{0,1},{1,0},{2,3},{3,2},{4,5},{5,4},{6,7},{7,6},{8,9},{9,8},{10,11... | collective-permute-start | bytes 73736 | tf_op jit(solution)/shard_map/ppermute | solution.py:43
  29.0 8.2 %collective-permute-start.10 = (f32[6,4,512]{2,1,0:T(4,128)S(1)}, f32[6,4,512]{2,1,0:T(4,128)S(1)}, u32[]{:S(2)}, u32[]{:S(2)}) collective-permute-start(f32[6,4,512]{2,1,0:T(4,128)S(1)} %get-tuple-element.30), channel_id=1, source_target_pairs={{0,1},{1,2},{2,3},{3,4},{4,5},{5,6},{6,7},{7,0},{8,9},{9,10},{10,1... | collective-permute-start | bytes 147464 | tf_op jit(solution)/shard_map/ppermute | solution.py:20
  30.7 6.5 %collective-permute-start.11 = (f32[6,4,512]{2,1,0:T(4,128)S(1)}, f32[6,4,512]{2,1,0:T(4,128)S(1)}, u32[]{:S(2)}, u32[]{:S(2)}) collective-permute-start(f32[6,4,512]{2,1,0:T(4,128)S(1)} %get-tuple-element.31), channel_id=1, source_target_pairs={{0,7},{1,0},{2,1},{3,2},{4,3},{5,4},{6,5},{7,6},{8,15},{9,8},{10,9... | collective-permute-start | bytes 147464 | tf_op jit(solution)/shard_map/ppermute | solution.py:20
  33.8 4.2 %collective-permute-start.8 = (f32[1,56,512]{2,1,0:T(8,128)S(1)}, f32[1,56,512]{2,1,0:T(8,128)S(1)}, u32[]{:S(2)}, u32[]{:S(2)}) collective-permute-start(f32[1,56,512]{2,1,0:T(8,128)S(1)} %get-tuple-element.28), channel_id=1, source_target_pairs={{0,8},{8,16},{16,24},{24,0},{1,9},{9,17},{17,25},{25,1},{2,10},{10... | collective-permute-start | bytes 344072 | tf_op jit(solution)/shard_map/ppermute | solution.py:20
  33.8 4.2 %collective-permute-start.9 = (f32[1,56,512]{2,1,0:T(8,128)S(1)}, f32[1,56,512]{2,1,0:T(8,128)S(1)}, u32[]{:S(2)}, u32[]{:S(2)}) collective-permute-start(f32[1,56,512]{2,1,0:T(8,128)S(1)} %get-tuple-element.29), channel_id=1, source_target_pairs={{0,24},{8,0},{16,8},{24,16},{1,25},{9,1},{17,9},{25,17},{2,26},{10... | collective-permute-start | bytes 344072 | tf_op jit(solution)/shard_map/ppermute | solution.py:20
  38.5 5.4 %collective-permute-start.12 = (bf16[256,384]{1,0:T(8,128)(2,1)S(1)}, bf16[256,384]{1,0:T(8,128)(2,1)S(1)}, u32[]{:S(2)}, u32[]{:S(2)}) collective-permute-start(bf16[256,384]{1,0:T(8,128)(2,1)S(1)} %get-tuple-element.35), channel_id=1, source_target_pairs={{0,8},{8,16},{16,24},{24,0},{1,9},{9,17},{17,25},{25,1},{2,10},{10... | collective-permute-start | bytes 589832 | tf_op jit(solution)/shard_map/ppermute | solution.py:20
  39.7 5.2 %collective-permute-start.16 = (f32[16,384]{1,0:T(8,128)S(1)}, f32[16,384]{1,0:T(8,128)S(1)}, u32[]{:S(2)}, u32[]{:S(2)}) collective-permute-start(f32[16,384]{1,0:T(8,128)S(1)} %get-tuple-element.38), channel_id=1, source_target_pairs={{0,16},{8,24},{16,0},{24,8},{1,17},{9,25},{17,1},{25,9},{2,18},{10... | collective-permute-start | bytes 73736 | tf_op jit(solution)/shard_map/ppermute | solution.py:20
  40.6 4.2 %collective-permute-start.13 = (bf16[256,384]{1,0:T(8,128)(2,1)S(1)}, bf16[256,384]{1,0:T(8,128)(2,1)S(1)}, u32[]{:S(2)}, u32[]{:S(2)}) collective-permute-start(bf16[256,384]{1,0:T(8,128)(2,1)S(1)} %get-tuple-element.36), channel_id=1, source_target_pairs={{0,24},{8,0},{16,8},{24,16},{1,25},{9,1},{17,9},{25,17},{2,26},{10... | collective-permute-start | bytes 589832 | tf_op jit(solution)/shard_map/ppermute | solution.py:20
  45.4 5.5 %collective-permute-start.17 = (f32[2,1,2,16,384]{4,3,2,1,0:T(8,128)S(1)}, f32[2,1,2,16,384]{4,3,2,1,0:T(8,128)S(1)}, u32[]{:S(2)}, u32[]{:S(2)}) collective-permute-start(f32[2,1,2,16,384]{4,3,2,1,0:T(8,128)S(1)} %constant_dynamic-slice_fusion.2), channel_id=1, source_target_pairs={{0,2},{1,3},{2,0},{3,1},{4,6},{5,7},{6,4},{7,5},{8,10},{9,11},{10,... | collective-permute-start | bytes 294920 | tf_op jit(solution)/shard_map/ppermute | solution.py:43
  45.6 8.3 %collective-permute-start.14 = (bf16[32,4,384]{2,1,0:T(4,128)(2,1)S(1)}, bf16[32,4,384]{2,1,0:T(4,128)(2,1)S(1)}, u32[]{:S(2)}, u32[]{:S(2)}) collective-permute-start(bf16[32,4,384]{2,1,0:T(4,128)(2,1)S(1)} %get-tuple-element.39), channel_id=1, source_target_pairs={{0,1},{1,2},{2,3},{3,4},{4,5},{5,6},{6,7},{7,0},{8,9},{9,10},{10,1... | collective-permute-start | bytes 294920 | tf_op jit(solution)/shard_map/ppermute | solution.py:20
  45.6 9.2 %collective-permute-start.15 = (bf16[32,4,384]{2,1,0:T(4,128)(2,1)S(1)}, bf16[32,4,384]{2,1,0:T(4,128)(2,1)S(1)}, u32[]{:S(2)}, u32[]{:S(2)}) collective-permute-start(bf16[32,4,384]{2,1,0:T(4,128)(2,1)S(1)} %get-tuple-element.40), channel_id=1, source_target_pairs={{0,7},{1,0},{2,1},{3,2},{4,3},{5,4},{6,5},{7,6},{8,15},{9,8},{10,9... | collective-permute-start | bytes 294920 | tf_op jit(solution)/shard_map/ppermute | solution.py:20
  50.9 5.7 %collective-permute-start.18 = (f32[1,1,2,16,384]{4,3,2,1,0:T(8,128)S(1)}, f32[1,1,2,16,384]{4,3,2,1,0:T(8,128)S(1)}, u32[]{:S(2)}, u32[]{:S(2)}) collective-permute-start(f32[1,1,2,16,384]{4,3,2,1,0:T(8,128)S(1)} %constant_dynamic-slice_fusion.1), channel_id=1, source_target_pairs={{0,4},{1,5},{2,6},{3,7},{4,0},{5,1},{6,2},{7,3},{8,12},{9,13},{10,... | collective-permute-start | bytes 147464 | tf_op jit(solution)/shard_map/ppermute | solution.py:43
  56.6 3.9 %collective-permute-start.19 = (f32[1,1,1,16,384]{4,3,2,1,0:T(8,128)S(1)}, f32[1,1,1,16,384]{4,3,2,1,0:T(8,128)S(1)}, u32[]{:S(2)}, u32[]{:S(2)}) collective-permute-start(f32[1,1,1,16,384]{4,3,2,1,0:T(8,128)S(1)} %constant_dynamic-slice_fusion), channel_id=1, source_target_pairs={{0,1},{1,0},{2,3},{3,2},{4,5},{5,4},{6,7},{7,6},{8,9},{9,8},{10,11... | collective-permute-start | bytes 73736 | tf_op jit(solution)/shard_map/ppermute | solution.py:43

commit v10 on v9

--- a/solution.py
+++ b/solution.py
@@ -10,7 +10,6 @@
 OV = 4
 ITERS = 2
 LANES = 128
-EXACT = lax.Precision.HIGHEST
 F32 = jnp.float32
 BF16 = jnp.bfloat16
 
@@ -65,13 +64,12 @@
 
 
 def weighted(weights, cells):
-    high, middle, low = weights
+    high, middle, _ = weights
     modes = high.shape[0]
-    block_high, block_middle, block_low = split(cells)
-    three = product(jnp.concatenate([high, middle, low], axis=0), block_high)
-    two = product(jnp.concatenate([high, middle], axis=0), block_middle)
-    one = product(high, block_low)
-    return one + (two[modes:] + three[2 * modes :]) + (two[:modes] + three[modes : 2 * modes]) + three[:modes]
+    cells_high = cells.astype(BF16)
+    cells_middle = (cells - cells_high.astype(F32)).astype(BF16)
+    two = product(jnp.concatenate([high, middle], axis=0), cells_high)
+    return (product(high, cells_middle) + two[modes:]) + two[:modes]
 
 
 def survey(block, basis_ref, first, down_ref, up_ref, side_ref):
@@ -448,7 +446,7 @@
             inverse,
             sums,
             (((0,), (0,)), ((), ())),
-            precision=EXACT,
+            precision=lax.Precision.HIGH,
             preferred_element_type=F32,
         )
         return summed_over_members(shares)

time: 62.5 us -> 61.9 us (level)
  no operation moved by 1% of the time
where the time goes in v10:
time: 61.9 us; the launch traced here: 61.8 us
  starting transfers between devices  27.3 us (44%)
  Pallas kernels  16.8 us (27%)
  waiting for transfers between devices  15.3 us (25%)
  other arithmetic  0.71 us (1%)
    ppermute x14, starting transfers between devices, shifted(): lax.ppermute(value, axis, [(i, (i + distance) % count) for i in range(cou...  23.2 us
    ppermute x14, waiting for transfers between devices, shifted(): lax.ppermute(value, axis, [(i, (i + distance) % count) for i in range(cou...  11.7 us
    pallas_call x2, Pallas kernels, fine(): pl.pallas_call(fine_kernel, in_specs=[in_vmem] * 5, out_specs=in_vmem, ou...  7.44 us
    ppermute x6, starting transfers between devices, summed_over_members(): shares = keep + lax.ppermute(send, 'mem', pairs)  4.09 us
    ppermute x6, waiting for transfers between devices, summed_over_members(): shares = keep + lax.ppermute(send, 'mem', pairs)  3.62 us
    pallas_call x1, Pallas kernels, held_rows(): pl.pallas_call(hold_kernel, in_specs=[in_hbm, pl.BlockSpec(memory_space=p...  2.86 us
    pallas_call x1, Pallas kernels, surveyed_start(): pl.pallas_call(start_kernel, in_specs=[in_hbm] * 3, out_specs=[in_vmem] *...  2.34 us
    pallas_call x2, Pallas kernels, updated(): pl.pallas_call(functools.partial(update_kernel, last), in_specs=[in_vmem]...  2.33 us
  transfers between devices with their start and end apart: 20, of which 10 were waited for; matrix products, arithmetic and copies ran while one was open for 2% of the time, Pallas kernels for 19%

profile of v10, /device:TPU:0, one launch (start us, length us, event | category | flops | bytes accessed | tf_op | source)
XLA Modules:
  0.0 61.8 jit_solution(4166708294185556745)
XLA Ops:
  0.0 2.3 %shard_map.55 = (bf16[272,384]{1,0:T(8,128)(2,1)S(1)}, bf16[272,384]{1,0:T(8,128)(2,1)S(1)}, bf16[24,8,384]{2,1,0:T(8,128)(2,1)S(1)}, f32[16,384]{1,0:T(8,128)S(1)}) custom-call(f32[24,56,384]{2,1,0:T(8,128)} %rhs_ref.3, f32[24,16,56]{2,1,0:T(8,128)} %bitcast.11, f32[16,512]{1,0:T(8,128)} %inverse_hbm.1), custom_call_target="tpu_custom_call" | custom-call | tf_op jit(solution)/shard_map/pallas_call | solution.py:356
  2.3 0.5 collective-permute-start
  2.9 2.6 %collective-permute-start.4 = (f32[16,512]{1,0:T(8,128)S(1)}, f32[16,512]{1,0:T(8,128)S(1)}, u32[]{:S(2)}, u32[]{:S(2)}) collective-permute-start(f32[16,512]{1,0:T(8,128)S(1)} %pad_maximum_fusion.2), channel_id=1, source_target_pairs={{0,16},{8,24},{16,0},{24,8},{1,17},{9,25},{17,1},{25,9},{2,18},{10... | collective-permute-start | bytes 98312 | tf_op jit(solution)/shard_map/ppermute | solution.py:19
  5.5 1.4 %collective-permute-start.1 = (bf16[272,384]{1,0:T(8,128)(2,1)S(1)}, bf16[272,384]{1,0:T(8,128)(2,1)S(1)}, u32[]{:S(2)}, u32[]{:S(2)}) collective-permute-start(bf16[272,384]{1,0:T(8,128)(2,1)S(1)} %get-tuple-element.24), channel_id=1, source_target_pairs={{0,24},{8,0},{16,8},{24,16},{1,25},{9,1},{17,9},{25,17},{2,26},{10... | collective-permute-start | bytes 626696 | tf_op jit(solution)/shard_map/ppermute | solution.py:19
  7.1 2.9 %shard_map.56.rows_ref = bf16[1536,2048]{1,0:T(8,128)(2,1)S(1)} custom-call(bf16[2048,2048]{1,0:T(8,128)(2,1)} %inverse_ref.1, f32[24,56,128]{2,1,0:T(8,128)S(1)} %broadcast_in_dim.30.heat_ref.extra_ref, f32[16,384]{1,0:T(8,128)S(1)} %get-tuple-element.22.order_ref), custom_call_target="tpu_custom_call" | custom-call | bytes 12582912 | tf_op jit(solution)/shard_map/pallas_call | solution.py:457
  10.1 0.9 %collective-permute-done.1 = bf16[272,384]{1,0:T(8,128)(2,1)S(1)} collective-permute-done((bf16[272,384]{1,0:T(8,128)(2,1)S(1)}, bf16[272,384]{1,0:T(8,128)(2,1)S(1)}, u32[]{:S(2)}, u32[]{:S(2)}) %collective-permute-start.1) | collective-permute-done | bytes 208928 | tf_op jit(solution)/shard_map/ppermute | solution.py:19
  11.4 1.6 %collective-permute-start.5 = (f32[2,1,2,16,384]{4,3,2,1,0:T(8,128)S(1)}, f32[2,1,2,16,384]{4,3,2,1,0:T(8,128)S(1)}, u32[]{:S(2)}, u32[]{:S(2)}) collective-permute-start(f32[2,1,2,16,384]{4,3,2,1,0:T(8,128)S(1)} %constant_dynamic-slice_fusion.5), channel_id=1, source_target_pairs={{0,2},{1,3},{2,0},{3,1},{4,6},{5,7},{6,4},{7,5},{8,10},{9,11},{10,... | collective-permute-start | bytes 294920 | tf_op jit(solution)/shard_map/ppermute | solution.py:42
  13.2 1.6 %collective-permute-start.2 = (bf16[32,4,384]{2,1,0:T(4,128)(2,1)S(1)}, bf16[32,4,384]{2,1,0:T(4,128)(2,1)S(1)}, u32[]{:S(2)}, u32[]{:S(2)}) collective-permute-start(bf16[32,4,384]{2,1,0:T(4,128)(2,1)S(1)} %get-tuple-element.41), channel_id=1, source_target_pairs={{0,1},{1,2},{2,3},{3,4},{4,5},{5,6},{6,7},{7,0},{8,9},{9,10},{10,1... | collective-permute-start | bytes 294920 | tf_op jit(solution)/shard_map/ppermute | solution.py:19
  14.8 3.2 %collective-permute-start.3 = (bf16[32,4,384]{2,1,0:T(4,128)(2,1)S(1)}, bf16[32,4,384]{2,1,0:T(4,128)(2,1)S(1)}, u32[]{:S(2)}, u32[]{:S(2)}) collective-permute-start(bf16[32,4,384]{2,1,0:T(4,128)(2,1)S(1)} %get-tuple-element.42), channel_id=1, source_target_pairs={{0,7},{1,0},{2,1},{3,2},{4,3},{5,4},{6,5},{7,6},{8,15},{9,8},{10,9... | collective-permute-start | bytes 294920 | tf_op jit(solution)/shard_map/ppermute | solution.py:19
  18.0 1.6 %collective-permute-start.6 = (f32[1,1,2,16,384]{4,3,2,1,0:T(8,128)S(1)}, f32[1,1,2,16,384]{4,3,2,1,0:T(8,128)S(1)}, u32[]{:S(2)}, u32[]{:S(2)}) collective-permute-start(f32[1,1,2,16,384]{4,3,2,1,0:T(8,128)S(1)} %constant_dynamic-slice_fusion.4), channel_id=1, source_target_pairs={{0,4},{1,5},{2,6},{3,7},{4,0},{5,1},{6,2},{7,3},{8,12},{9,13},{10,... | collective-permute-start | bytes 147464 | tf_op jit(solution)/shard_map/ppermute | solution.py:42
  19.6 2.5 %collective-permute-done.2 = bf16[32,4,384]{2,1,0:T(4,128)(2,1)S(1)} collective-permute-done((bf16[32,4,384]{2,1,0:T(4,128)(2,1)S(1)}, bf16[32,4,384]{2,1,0:T(4,128)(2,1)S(1)}, u32[]{:S(2)}, u32[]{:S(2)}) %collective-permute-start.2) | collective-permute-done | bytes 98336 | tf_op jit(solution)/shard_map/ppermute | solution.py:19
  22.3 1.5 %collective-permute-done.6 = f32[1,1,2,16,384]{4,3,2,1,0:T(8,128)S(1)} collective-permute-done((f32[1,1,2,16,384]{4,3,2,1,0:T(8,128)S(1)}, f32[1,1,2,16,384]{4,3,2,1,0:T(8,128)S(1)}, u32[]{:S(2)}, u32[]{:S(2)}) %collective-permute-start.6) | collective-permute-done | bytes 49184 | tf_op jit(solution)/shard_map/ppermute | solution.py:42
  23.9 0.4 collective-permute-start.7
  24.3 3.7 %shard_map.57.fine_ref = f32[24,56,384]{2,1,0:T(8,128)S(1)} custom-call(bf16[1536,2048]{1,0:T(8,128)(2,1)S(1)} %shard_map.56.rows_ref, f32[24,56,384]{2,1,0:T(8,128)S(1)} %copy-done, bf16[4,56,384]{2,1,0:T(8,128)(2,1)S(1)} %bitcast.20, bf16[4,56,384]{2,1,0:T(8,128)(2,1)S(1)} %bitcast.22, bf16[32,8,384]{2,1,0:T(8,128)(2,1)S(1)} %pad_maximum_fusion.side_ref), custom_call_target="tpu_custom_call" | custom-call | flops 2415919104 | bytes 6291456 | tf_op jit(solution)/shard_map/pallas_call | solution.py:470
  28.1 0.6 %shard_map.58 = (f32[24,56,384]{2,1,0:T(8,128)S(1)}, f32[1,56,512]{2,1,0:T(8,128)S(1)}, f32[1,56,512]{2,1,0:T(8,128)S(1)}, f32[6,4,512]{2,1,0:T(4,128)S(1)}, f32[6,4,512]{2,1,0:T(4,128)S(1)}) custom-call(f32[24,56,384]{2,1,0:T(8,128)S(1)} %shard_map.57.fine_ref, f32[24,16,56]{2,1,0:T(8,128)S(1)} %bitcast.12, f32[16,384]{1,0:T(8,128)S(1)} %add_bitcast_fusion.1.lifted_ref, ...), custom_call_target="tpu_custom_call" | custom-call | tf_op jit(solution)/shard_map/pallas_call | solution.py:500
  28.7 1.7 %collective-permute-start.10 = (f32[6,4,512]{2,1,0:T(4,128)S(1)}, f32[6,4,512]{2,1,0:T(4,128)S(1)}, u32[]{:S(2)}, u32[]{:S(2)}) collective-permute-start(f32[6,4,512]{2,1,0:T(4,128)S(1)} %get-tuple-element.30), channel_id=1, source_target_pairs={{0,1},{1,2},{2,3},{3,4},{4,5},{5,6},{6,7},{7,0},{8,9},{9,10},{10,1... | collective-permute-start | bytes 147464 | tf_op jit(solution)/shard_map/ppermute | solution.py:19
  30.4 3.1 %collective-permute-start.11 = (f32[6,4,512]{2,1,0:T(4,128)S(1)}, f32[6,4,512]{2,1,0:T(4,128)S(1)}, u32[]{:S(2)}, u32[]{:S(2)}) collective-permute-start(f32[6,4,512]{2,1,0:T(4,128)S(1)} %get-tuple-element.31), channel_id=1, source_target_pairs={{0,7},{1,0},{2,1},{3,2},{4,3},{5,4},{6,5},{7,6},{8,15},{9,8},{10,9... | collective-permute-start | bytes 147464 | tf_op jit(solution)/shard_map/ppermute | solution.py:19
  33.5 1.7 %collective-permute-start.9 = (f32[1,56,512]{2,1,0:T(8,128)S(1)}, f32[1,56,512]{2,1,0:T(8,128)S(1)}, u32[]{:S(2)}, u32[]{:S(2)}) collective-permute-start(f32[1,56,512]{2,1,0:T(8,128)S(1)} %get-tuple-element.29), channel_id=1, source_target_pairs={{0,24},{8,0},{16,8},{24,16},{1,25},{9,1},{17,9},{25,17},{2,26},{10... | collective-permute-start | bytes 344072 | tf_op jit(solution)/shard_map/ppermute | solution.py:19
  35.2 1.5 %shard_map.59 = (f32[24,56,384]{2,1,0:T(8,128)S(1)}, f32[16,384]{1,0:T(8,128)S(1)}, f32[16,304]{1,0:T(8,128)S(1)}) custom-call(f32[24,56,384]{2,1,0:T(8,128)S(1)} %copy-done, f32[24,56,384]{2,1,0:T(8,128)S(1)} %get-tuple-element.26.now_ref.extra_ref, f32[24,56,128]{2,1,0:T(8,128)S(1)} %broadcast_in_dim.30.heat_ref.extra_ref, f32[24,16,56]{2,1,0:T(8,128)S(1)} %bitcast.13), custom_call_target="tpu_custom_call" | custom-call | bytes 6193152 | tf_op jit(solution)/shard_map/pallas_call | solution.py:374
  36.8 0.9 %collective-permute-done.8 = f32[1,56,512]{2,1,0:T(8,128)S(1)} collective-permute-done((f32[1,56,512]{2,1,0:T(8,128)S(1)}, f32[1,56,512]{2,1,0:T(8,128)S(1)}, u32[]{:S(2)}, u32[]{:S(2)}) %collective-permute-start.8) | collective-permute-done | bytes 114720 | tf_op jit(solution)/shard_map/ppermute | solution.py:19
  38.1 1.2 %collective-permute-start.12 = (bf16[256,384]{1,0:T(8,128)(2,1)S(1)}, bf16[256,384]{1,0:T(8,128)(2,1)S(1)}, u32[]{:S(2)}, u32[]{:S(2)}) collective-permute-start(bf16[256,384]{1,0:T(8,128)(2,1)S(1)} %get-tuple-element.35), channel_id=1, source_target_pairs={{0,8},{8,16},{16,24},{24,0},{1,9},{9,17},{17,25},{25,1},{2,10},{10... | collective-permute-start | bytes 589832 | tf_op jit(solution)/shard_map/ppermute | solution.py:19
  39.3 0.9 %collective-permute-start.16 = (f32[16,384]{1,0:T(8,128)S(1)}, f32[16,384]{1,0:T(8,128)S(1)}, u32[]{:S(2)}, u32[]{:S(2)}) collective-permute-start(f32[16,384]{1,0:T(8,128)S(1)} %get-tuple-element.38), channel_id=1, source_target_pairs={{0,16},{8,24},{16,0},{24,8},{1,17},{9,25},{17,1},{25,9},{2,18},{10... | collective-permute-start | bytes 73736 | tf_op jit(solution)/shard_map/ppermute | solution.py:19
  40.3 0.5 collective-permute-start.13
  40.8 2.8 %collective-permute-done.12 = bf16[256,384]{1,0:T(8,128)(2,1)S(1)} collective-permute-done((bf16[256,384]{1,0:T(8,128)(2,1)S(1)}, bf16[256,384]{1,0:T(8,128)(2,1)S(1)}, u32[]{:S(2)}, u32[]{:S(2)}) %collective-permute-start.12) | collective-permute-done | bytes 196640 | tf_op jit(solution)/shard_map/ppermute | solution.py:19
  43.6 0.9 %collective-permute-done.13 = bf16[256,384]{1,0:T(8,128)(2,1)S(1)} collective-permute-done((bf16[256,384]{1,0:T(8,128)(2,1)S(1)}, bf16[256,384]{1,0:T(8,128)(2,1)S(1)}, u32[]{:S(2)}, u32[]{:S(2)}) %collective-permute-start.13) | collective-permute-done | bytes 196640 | tf_op jit(solution)/shard_map/ppermute | solution.py:19
  45.2 4.7 %collective-permute-start.15 = (bf16[32,4,384]{2,1,0:T(4,128)(2,1)S(1)}, bf16[32,4,384]{2,1,0:T(4,128)(2,1)S(1)}, u32[]{:S(2)}, u32[]{:S(2)}) collective-permute-start(bf16[32,4,384]{2,1,0:T(4,128)(2,1)S(1)} %get-tuple-element.40), channel_id=1, source_target_pairs={{0,7},{1,0},{2,1},{3,2},{4,3},{5,4},{6,5},{7,6},{8,15},{9,8},{10,9... | collective-permute-start | bytes 294920 | tf_op jit(solution)/shard_map/ppermute | solution.py:19
  49.9 0.5 collective-permute-done.17
  50.6 2.8 %collective-permute-done.14 = bf16[32,4,384]{2,1,0:T(4,128)(2,1)S(1)} collective-permute-done((bf16[32,4,384]{2,1,0:T(4,128)(2,1)S(1)}, bf16[32,4,384]{2,1,0:T(4,128)(2,1)S(1)}, u32[]{:S(2)}, u32[]{:S(2)}) %collective-permute-start.14) | collective-permute-done | bytes 98336 | tf_op jit(solution)/shard_map/ppermute | solution.py:19
  53.5 0.9 %collective-permute-done.15 = bf16[32,4,384]{2,1,0:T(4,128)(2,1)S(1)} collective-permute-done((bf16[32,4,384]{2,1,0:T(4,128)(2,1)S(1)}, bf16[32,4,384]{2,1,0:T(4,128)(2,1)S(1)}, u32[]{:S(2)}, u32[]{:S(2)}) %collective-permute-start.15) | collective-permute-done | bytes 98336 | tf_op jit(solution)/shard_map/ppermute | solution.py:19
  54.5 1.6 %collective-permute-done.18 = f32[1,1,2,16,384]{4,3,2,1,0:T(8,128)S(1)} collective-permute-done((f32[1,1,2,16,384]{4,3,2,1,0:T(8,128)S(1)}, f32[1,1,2,16,384]{4,3,2,1,0:T(8,128)S(1)}, u32[]{:S(2)}, u32[]{:S(2)}) %collective-permute-start.18) | collective-permute-done | bytes 49184 | tf_op jit(solution)/shard_map/ppermute | solution.py:42
  56.3 3.7 %shard_map.61.fine_ref = f32[24,56,384]{2,1,0:T(8,128)S(1)} custom-call(bf16[1536,2048]{1,0:T(8,128)(2,1)S(1)} %shard_map.56.rows_ref, f32[24,56,384]{2,1,0:T(8,128)S(1)} %get-tuple-element.34.block_ref, bf16[4,56,384]{2,1,0:T(8,128)(2,1)S(1)} %bitcast.16, bf16[4,56,384]{2,1,0:T(8,128)(2,1)S(1)} %bitcast.18, bf16[32,8,384]{2,1,0:T(8,128)(2,1)S(1)} %pad_maximum_fusion.1.side_ref), custom_call_target="tpu_custom_call" | custom-call | flops 2415919104 | bytes 6291456 | tf_op jit(solution)/shard_map/pallas_call | solution.py:470
  60.1 1.7 %shard_map.62 = f32[24,56,384]{2,1,0:T(8,128)} custom-call(f32[24,56,384]{2,1,0:T(8,128)S(1)} %shard_map.61.fine_ref, f32[24,16,56]{2,1,0:T(8,128)S(1)} %bitcast.14, f32[16,384]{1,0:T(8,128)S(1)} %add_bitcast_fusion.lifted_ref, f32[24,56,384]{2,1,0:T(8,128)S(1)} %get-tuple-element.26.now_ref.extra_ref), custom_call_target="tpu_custom_call" | custom-call | tf_op jit(solution)/shard_map/pallas_call | solution.py:500
  (70 shorter events, 2.7 us)
Async XLA Ops:
  0.0 2.9 %copy-start.2 = (f32[16,512]{1,0:T(8,128)S(1)}, f32[16,512]{1,0:T(8,128)}, u32[]{:S(2)}) copy-start(f32[16,512]{1,0:T(8,128)} %inverse_hbm.1) | copy-start | bytes 98308
  0.0 6.9 %copy-start.3 = (f32[24,56]{1,0:T(8,128)S(1)}, f32[24,56]{1,0:T(8,128)}, u32[]{:S(2)}) copy-start(f32[24,56]{1,0:T(8,128)} %param.6) | copy-start | bytes 16132
  2.3 7.7 %collective-permute-start = (bf16[272,384]{1,0:T(8,128)(2,1)S(1)}, bf16[272,384]{1,0:T(8,128)(2,1)S(1)}, u32[]{:S(2)}, u32[]{:S(2)}) collective-permute-start(bf16[272,384]{1,0:T(8,128)(2,1)S(1)} %get-tuple-element.23), channel_id=1, source_target_pairs={{0,8},{8,16},{16,24},{24,0},{1,9},{9,17},{17,25},{25,1},{2,10},{10... | collective-permute-start | bytes 626696 | tf_op jit(solution)/shard_map/ppermute | solution.py:19
  2.9 7.1 %collective-permute-start.4 = (f32[16,512]{1,0:T(8,128)S(1)}, f32[16,512]{1,0:T(8,128)S(1)}, u32[]{:S(2)}, u32[]{:S(2)}) collective-permute-start(f32[16,512]{1,0:T(8,128)S(1)} %pad_maximum_fusion.2), channel_id=1, source_target_pairs={{0,16},{8,24},{16,0},{24,8},{1,17},{9,25},{17,1},{25,9},{2,18},{10... | collective-permute-start | bytes 98312 | tf_op jit(solution)/shard_map/ppermute | solution.py:19
  5.5 5.5 %collective-permute-start.1 = (bf16[272,384]{1,0:T(8,128)(2,1)S(1)}, bf16[272,384]{1,0:T(8,128)(2,1)S(1)}, u32[]{:S(2)}, u32[]{:S(2)}) collective-permute-start(bf16[272,384]{1,0:T(8,128)(2,1)S(1)} %get-tuple-element.24), channel_id=1, source_target_pairs={{0,24},{8,0},{16,8},{24,16},{1,25},{9,1},{17,9},{25,17},{2,26},{10... | collective-permute-start | bytes 626696 | tf_op jit(solution)/shard_map/ppermute | solution.py:19
  10.0 14.3 %copy-start = (f32[24,56,384]{2,1,0:T(8,128)S(1)}, f32[24,56,384]{2,1,0:T(8,128)}, u32[]{:S(2)}) copy-start(f32[24,56,384]{2,1,0:T(8,128)} %rhs_ref.3) | copy-start | bytes 6193156
  11.4 6.6 %collective-permute-start.5 = (f32[2,1,2,16,384]{4,3,2,1,0:T(8,128)S(1)}, f32[2,1,2,16,384]{4,3,2,1,0:T(8,128)S(1)}, u32[]{:S(2)}, u32[]{:S(2)}) collective-permute-start(f32[2,1,2,16,384]{4,3,2,1,0:T(8,128)S(1)} %constant_dynamic-slice_fusion.5), channel_id=1, source_target_pairs={{0,2},{1,3},{2,0},{3,1},{4,6},{5,7},{6,4},{7,5},{8,10},{9,11},{10,... | collective-permute-start | bytes 294920 | tf_op jit(solution)/shard_map/ppermute | solution.py:42
  13.2 8.9 %collective-permute-start.2 = (bf16[32,4,384]{2,1,0:T(4,128)(2,1)S(1)}, bf16[32,4,384]{2,1,0:T(4,128)(2,1)S(1)}, u32[]{:S(2)}, u32[]{:S(2)}) collective-permute-start(bf16[32,4,384]{2,1,0:T(4,128)(2,1)S(1)} %get-tuple-element.41), channel_id=1, source_target_pairs={{0,1},{1,2},{2,3},{3,4},{4,5},{5,6},{6,7},{7,0},{8,9},{9,10},{10,1... | collective-permute-start | bytes 294920 | tf_op jit(solution)/shard_map/ppermute | solution.py:19
  14.8 7.4 %collective-permute-start.3 = (bf16[32,4,384]{2,1,0:T(4,128)(2,1)S(1)}, bf16[32,4,384]{2,1,0:T(4,128)(2,1)S(1)}, u32[]{:S(2)}, u32[]{:S(2)}) collective-permute-start(bf16[32,4,384]{2,1,0:T(4,128)(2,1)S(1)} %get-tuple-element.42), channel_id=1, source_target_pairs={{0,7},{1,0},{2,1},{3,2},{4,3},{5,4},{6,5},{7,6},{8,15},{9,8},{10,9... | collective-permute-start | bytes 294920 | tf_op jit(solution)/shard_map/ppermute | solution.py:19
  18.0 5.8 %collective-permute-start.6 = (f32[1,1,2,16,384]{4,3,2,1,0:T(8,128)S(1)}, f32[1,1,2,16,384]{4,3,2,1,0:T(8,128)S(1)}, u32[]{:S(2)}, u32[]{:S(2)}) collective-permute-start(f32[1,1,2,16,384]{4,3,2,1,0:T(8,128)S(1)} %constant_dynamic-slice_fusion.4), channel_id=1, source_target_pairs={{0,4},{1,5},{2,6},{3,7},{4,0},{5,1},{6,2},{7,3},{8,12},{9,13},{10,... | collective-permute-start | bytes 147464 | tf_op jit(solution)/shard_map/ppermute | solution.py:42
  23.9 4.2 %copy-start.1 = (f32[24,56,16]{1,2,0:T(8,128)S(1)}, f32[24,56,16]{1,2,0:T(8,128)}, u32[]{:S(2)}) copy-start(f32[24,56,16]{1,2,0:T(8,128)} %param.8) | copy-start | bytes 258052
  23.9 4.2 %collective-permute-start.7 = (f32[1,1,1,16,384]{4,3,2,1,0:T(8,128)S(1)}, f32[1,1,1,16,384]{4,3,2,1,0:T(8,128)S(1)}, u32[]{:S(2)}, u32[]{:S(2)}) collective-permute-start(f32[1,1,1,16,384]{4,3,2,1,0:T(8,128)S(1)} %constant_dynamic-slice_fusion.3), channel_id=1, source_target_pairs={{0,1},{1,0},{2,3},{3,2},{4,5},{5,4},{6,7},{7,6},{8,9},{9,8},{10,11... | collective-permute-start | bytes 73736 | tf_op jit(solution)/shard_map/ppermute | solution.py:42
  28.7 8.0 %collective-permute-start.10 = (f32[6,4,512]{2,1,0:T(4,128)S(1)}, f32[6,4,512]{2,1,0:T(4,128)S(1)}, u32[]{:S(2)}, u32[]{:S(2)}) collective-permute-start(f32[6,4,512]{2,1,0:T(4,128)S(1)} %get-tuple-element.30), channel_id=1, source_target_pairs={{0,1},{1,2},{2,3},{3,4},{4,5},{5,6},{6,7},{7,0},{8,9},{9,10},{10,1... | collective-permute-start | bytes 147464 | tf_op jit(solution)/shard_map/ppermute | solution.py:19
  30.4 6.3 %collective-permute-start.11 = (f32[6,4,512]{2,1,0:T(4,128)S(1)}, f32[6,4,512]{2,1,0:T(4,128)S(1)}, u32[]{:S(2)}, u32[]{:S(2)}) collective-permute-start(f32[6,4,512]{2,1,0:T(4,128)S(1)} %get-tuple-element.31), channel_id=1, source_target_pairs={{0,7},{1,0},{2,1},{3,2},{4,3},{5,4},{6,5},{7,6},{8,15},{9,8},{10,9... | collective-permute-start | bytes 147464 | tf_op jit(solution)/shard_map/ppermute | solution.py:19
  33.5 4.2 %collective-permute-start.8 = (f32[1,56,512]{2,1,0:T(8,128)S(1)}, f32[1,56,512]{2,1,0:T(8,128)S(1)}, u32[]{:S(2)}, u32[]{:S(2)}) collective-permute-start(f32[1,56,512]{2,1,0:T(8,128)S(1)} %get-tuple-element.28), channel_id=1, source_target_pairs={{0,8},{8,16},{16,24},{24,0},{1,9},{9,17},{17,25},{25,1},{2,10},{10... | collective-permute-start | bytes 344072 | tf_op jit(solution)/shard_map/ppermute | solution.py:19
  33.5 4.2 %collective-permute-start.9 = (f32[1,56,512]{2,1,0:T(8,128)S(1)}, f32[1,56,512]{2,1,0:T(8,128)S(1)}, u32[]{:S(2)}, u32[]{:S(2)}) collective-permute-start(f32[1,56,512]{2,1,0:T(8,128)S(1)} %get-tuple-element.29), channel_id=1, source_target_pairs={{0,24},{8,0},{16,8},{24,16},{1,25},{9,1},{17,9},{25,17},{2,26},{10... | collective-permute-start | bytes 344072 | tf_op jit(solution)/shard_map/ppermute | solution.py:19
  38.1 5.4 %collective-permute-start.12 = (bf16[256,384]{1,0:T(8,128)(2,1)S(1)}, bf16[256,384]{1,0:T(8,128)(2,1)S(1)}, u32[]{:S(2)}, u32[]{:S(2)}) collective-permute-start(bf16[256,384]{1,0:T(8,128)(2,1)S(1)} %get-tuple-element.35), channel_id=1, source_target_pairs={{0,8},{8,16},{16,24},{24,0},{1,9},{9,17},{17,25},{25,1},{2,10},{10... | collective-permute-start | bytes 589832 | tf_op jit(solution)/shard_map/ppermute | solution.py:19
  39.3 5.2 %collective-permute-start.16 = (f32[16,384]{1,0:T(8,128)S(1)}, f32[16,384]{1,0:T(8,128)S(1)}, u32[]{:S(2)}, u32[]{:S(2)}) collective-permute-start(f32[16,384]{1,0:T(8,128)S(1)} %get-tuple-element.38), channel_id=1, source_target_pairs={{0,16},{8,24},{16,0},{24,8},{1,17},{9,25},{17,1},{25,9},{2,18},{10... | collective-permute-start | bytes 73736 | tf_op jit(solution)/shard_map/ppermute | solution.py:19
  40.3 4.2 %collective-permute-start.13 = (bf16[256,384]{1,0:T(8,128)(2,1)S(1)}, bf16[256,384]{1,0:T(8,128)(2,1)S(1)}, u32[]{:S(2)}, u32[]{:S(2)}) collective-permute-start(bf16[256,384]{1,0:T(8,128)(2,1)S(1)} %get-tuple-element.36), channel_id=1, source_target_pairs={{0,24},{8,0},{16,8},{24,16},{1,25},{9,1},{17,9},{25,17},{2,26},{10... | collective-permute-start | bytes 589832 | tf_op jit(solution)/shard_map/ppermute | solution.py:19
  44.9 5.5 %collective-permute-start.17 = (f32[2,1,2,16,384]{4,3,2,1,0:T(8,128)S(1)}, f32[2,1,2,16,384]{4,3,2,1,0:T(8,128)S(1)}, u32[]{:S(2)}, u32[]{:S(2)}) collective-permute-start(f32[2,1,2,16,384]{4,3,2,1,0:T(8,128)S(1)} %constant_dynamic-slice_fusion.2), channel_id=1, source_target_pairs={{0,2},{1,3},{2,0},{3,1},{4,6},{5,7},{6,4},{7,5},{8,10},{9,11},{10,... | collective-permute-start | bytes 294920 | tf_op jit(solution)/shard_map/ppermute | solution.py:42
  45.1 8.3 %collective-permute-start.14 = (bf16[32,4,384]{2,1,0:T(4,128)(2,1)S(1)}, bf16[32,4,384]{2,1,0:T(4,128)(2,1)S(1)}, u32[]{:S(2)}, u32[]{:S(2)}) collective-permute-start(bf16[32,4,384]{2,1,0:T(4,128)(2,1)S(1)} %get-tuple-element.39), channel_id=1, source_target_pairs={{0,1},{1,2},{2,3},{3,4},{4,5},{5,6},{6,7},{7,0},{8,9},{9,10},{10,1... | collective-permute-start | bytes 294920 | tf_op jit(solution)/shard_map/ppermute | solution.py:19
  45.2 9.2 %collective-permute-start.15 = (bf16[32,4,384]{2,1,0:T(4,128)(2,1)S(1)}, bf16[32,4,384]{2,1,0:T(4,128)(2,1)S(1)}, u32[]{:S(2)}, u32[]{:S(2)}) collective-permute-start(bf16[32,4,384]{2,1,0:T(4,128)(2,1)S(1)} %get-tuple-element.40), channel_id=1, source_target_pairs={{0,7},{1,0},{2,1},{3,2},{4,3},{5,4},{6,5},{7,6},{8,15},{9,8},{10,9... | collective-permute-start | bytes 294920 | tf_op jit(solution)/shard_map/ppermute | solution.py:19
  50.5 5.7 %collective-permute-start.18 = (f32[1,1,2,16,384]{4,3,2,1,0:T(8,128)S(1)}, f32[1,1,2,16,384]{4,3,2,1,0:T(8,128)S(1)}, u32[]{:S(2)}, u32[]{:S(2)}) collective-permute-start(f32[1,1,2,16,384]{4,3,2,1,0:T(8,128)S(1)} %constant_dynamic-slice_fusion.1), channel_id=1, source_target_pairs={{0,4},{1,5},{2,6},{3,7},{4,0},{5,1},{6,2},{7,3},{8,12},{9,13},{10,... | collective-permute-start | bytes 147464 | tf_op jit(solution)/shard_map/ppermute | solution.py:42
  56.1 3.9 %collective-permute-start.19 = (f32[1,1,1,16,384]{4,3,2,1,0:T(8,128)S(1)}, f32[1,1,1,16,384]{4,3,2,1,0:T(8,128)S(1)}, u32[]{:S(2)}, u32[]{:S(2)}) collective-permute-start(f32[1,1,1,16,384]{4,3,2,1,0:T(8,128)S(1)} %constant_dynamic-slice_fusion), channel_id=1, source_target_pairs={{0,1},{1,0},{2,3},{3,2},{4,5},{5,4},{6,7},{7,6},{8,9},{9,8},{10,11... | collective-permute-start | bytes 73736 | tf_op jit(solution)/shard_map/ppermute | solution.py:42

commit v11 on v10

--- a/solution.py
+++ b/solution.py
@@ -281,13 +281,13 @@
     else:
         first_ref, last_ref, left_ref, right_ref = refs
         result = out_ref
-    high, middle, low = split(lifted_ref[...])
-    lifted = jnp.concatenate([high, middle, high, low, middle, high], axis=0)
+    high, middle, _ = split(lifted_ref[...])
+    lifted = jnp.concatenate([high, middle, high], axis=0)
     sends = []
     for first in range(0, own_x, OV):
-        high, middle, low = modes_of(basis_ref, first, OV)
+        high, middle, _ = modes_of(basis_ref, first, OV)
         coarse = lax.dot_general(
-            jnp.concatenate([high, high, middle, high, middle, low], axis=0),
+            jnp.concatenate([high, high, middle], axis=0),
             lifted,
             (((0,), (0,)), ((), ())),
             preferred_element_type=F32,

time: 61.9 us -> 62.2 us (level)
  no operation moved by 1% of the time
where the time goes in v11:
time: 62.2 us; the launch traced here: 62.1 us
  starting transfers between devices  27.3 us (44%)
  Pallas kernels  17 us (27%)
  waiting for transfers between devices  15.3 us (25%)
  other arithmetic  0.71 us (1%)
    ppermute x14, starting transfers between devices, shifted(): lax.ppermute(value, axis, [(i, (i + distance) % count) for i in range(cou...  23.2 us
    ppermute x14, waiting for transfers between devices, shifted(): lax.ppermute(value, axis, [(i, (i + distance) % count) for i in range(cou...  11.7 us
    pallas_call x2, Pallas kernels, fine(): pl.pallas_call(fine_kernel, in_specs=[in_vmem] * 5, out_specs=in_vmem, ou...  7.44 us
    ppermute x6, starting transfers between devices, summed_over_members(): shares = keep + lax.ppermute(send, 'mem', pairs)  4.08 us
    ppermute x6, waiting for transfers between devices, summed_over_members(): shares = keep + lax.ppermute(send, 'mem', pairs)  3.62 us
    pallas_call x1, Pallas kernels, held_rows(): pl.pallas_call(hold_kernel, in_specs=[in_hbm, pl.BlockSpec(memory_space=p...  2.86 us
    pallas_call x2, Pallas kernels, updated(): pl.pallas_call(functools.partial(update_kernel, last), in_specs=[in_vmem]...  2.47 us
    pallas_call x1, Pallas kernels, surveyed_start(): pl.pallas_call(start_kernel, in_specs=[in_hbm] * 3, out_specs=[in_vmem] *...  2.34 us
  transfers between devices with their start and end apart: 20, of which 10 were waited for; matrix products, arithmetic and copies ran while one was open for 2% of the time, Pallas kernels for 19%

profile of v11, /device:TPU:0, one launch (start us, length us, event | category | flops | bytes accessed | tf_op | source)
XLA Modules:
  0.0 62.1 jit_solution(15336173292724194409)
XLA Ops:
  0.0 2.3 %shard_map.55 = (bf16[272,384]{1,0:T(8,128)(2,1)S(1)}, bf16[272,384]{1,0:T(8,128)(2,1)S(1)}, bf16[24,8,384]{2,1,0:T(8,128)(2,1)S(1)}, f32[16,384]{1,0:T(8,128)S(1)}) custom-call(f32[24,56,384]{2,1,0:T(8,128)} %rhs_ref.3, f32[24,16,56]{2,1,0:T(8,128)} %bitcast.11, f32[16,512]{1,0:T(8,128)} %inverse_hbm.1), custom_call_target="tpu_custom_call" | custom-call | tf_op jit(solution)/shard_map/pallas_call | solution.py:356
  2.3 0.5 collective-permute-start
  2.9 2.6 %collective-permute-start.4 = (f32[16,512]{1,0:T(8,128)S(1)}, f32[16,512]{1,0:T(8,128)S(1)}, u32[]{:S(2)}, u32[]{:S(2)}) collective-permute-start(f32[16,512]{1,0:T(8,128)S(1)} %pad_maximum_fusion.2), channel_id=1, source_target_pairs={{0,16},{8,24},{16,0},{24,8},{1,17},{9,25},{17,1},{25,9},{2,18},{10... | collective-permute-start | bytes 98312 | tf_op jit(solution)/shard_map/ppermute | solution.py:19
  5.5 1.4 %collective-permute-start.1 = (bf16[272,384]{1,0:T(8,128)(2,1)S(1)}, bf16[272,384]{1,0:T(8,128)(2,1)S(1)}, u32[]{:S(2)}, u32[]{:S(2)}) collective-permute-start(bf16[272,384]{1,0:T(8,128)(2,1)S(1)} %get-tuple-element.24), channel_id=1, source_target_pairs={{0,24},{8,0},{16,8},{24,16},{1,25},{9,1},{17,9},{25,17},{2,26},{10... | collective-permute-start | bytes 626696 | tf_op jit(solution)/shard_map/ppermute | solution.py:19
  7.1 2.9 %shard_map.56.rows_ref = bf16[1536,2048]{1,0:T(8,128)(2,1)S(1)} custom-call(bf16[2048,2048]{1,0:T(8,128)(2,1)} %inverse_ref.1, f32[24,56,128]{2,1,0:T(8,128)S(1)} %broadcast_in_dim.30.heat_ref.extra_ref, f32[16,384]{1,0:T(8,128)S(1)} %get-tuple-element.22.order_ref), custom_call_target="tpu_custom_call" | custom-call | bytes 12582912 | tf_op jit(solution)/shard_map/pallas_call | solution.py:457
  10.1 0.9 %collective-permute-done.1 = bf16[272,384]{1,0:T(8,128)(2,1)S(1)} collective-permute-done((bf16[272,384]{1,0:T(8,128)(2,1)S(1)}, bf16[272,384]{1,0:T(8,128)(2,1)S(1)}, u32[]{:S(2)}, u32[]{:S(2)}) %collective-permute-start.1) | collective-permute-done | bytes 208928 | tf_op jit(solution)/shard_map/ppermute | solution.py:19
  11.4 1.6 %collective-permute-start.5 = (f32[2,1,2,16,384]{4,3,2,1,0:T(8,128)S(1)}, f32[2,1,2,16,384]{4,3,2,1,0:T(8,128)S(1)}, u32[]{:S(2)}, u32[]{:S(2)}) collective-permute-start(f32[2,1,2,16,384]{4,3,2,1,0:T(8,128)S(1)} %constant_dynamic-slice_fusion.5), channel_id=1, source_target_pairs={{0,2},{1,3},{2,0},{3,1},{4,6},{5,7},{6,4},{7,5},{8,10},{9,11},{10,... | collective-permute-start | bytes 294920 | tf_op jit(solution)/shard_map/ppermute | solution.py:42
  13.2 1.6 %collective-permute-start.2 = (bf16[32,4,384]{2,1,0:T(4,128)(2,1)S(1)}, bf16[32,4,384]{2,1,0:T(4,128)(2,1)S(1)}, u32[]{:S(2)}, u32[]{:S(2)}) collective-permute-start(bf16[32,4,384]{2,1,0:T(4,128)(2,1)S(1)} %get-tuple-element.41), channel_id=1, source_target_pairs={{0,1},{1,2},{2,3},{3,4},{4,5},{5,6},{6,7},{7,0},{8,9},{9,10},{10,1... | collective-permute-start | bytes 294920 | tf_op jit(solution)/shard_map/ppermute | solution.py:19
  14.8 3.2 %collective-permute-start.3 = (bf16[32,4,384]{2,1,0:T(4,128)(2,1)S(1)}, bf16[32,4,384]{2,1,0:T(4,128)(2,1)S(1)}, u32[]{:S(2)}, u32[]{:S(2)}) collective-permute-start(bf16[32,4,384]{2,1,0:T(4,128)(2,1)S(1)} %get-tuple-element.42), channel_id=1, source_target_pairs={{0,7},{1,0},{2,1},{3,2},{4,3},{5,4},{6,5},{7,6},{8,15},{9,8},{10,9... | collective-permute-start | bytes 294920 | tf_op jit(solution)/shard_map/ppermute | solution.py:19
  18.0 1.6 %collective-permute-start.6 = (f32[1,1,2,16,384]{4,3,2,1,0:T(8,128)S(1)}, f32[1,1,2,16,384]{4,3,2,1,0:T(8,128)S(1)}, u32[]{:S(2)}, u32[]{:S(2)}) collective-permute-start(f32[1,1,2,16,384]{4,3,2,1,0:T(8,128)S(1)} %constant_dynamic-slice_fusion.4), channel_id=1, source_target_pairs={{0,4},{1,5},{2,6},{3,7},{4,0},{5,1},{6,2},{7,3},{8,12},{9,13},{10,... | collective-permute-start | bytes 147464 | tf_op jit(solution)/shard_map/ppermute | solution.py:42
  19.6 2.5 %collective-permute-done.2 = bf16[32,4,384]{2,1,0:T(4,128)(2,1)S(1)} collective-permute-done((bf16[32,4,384]{2,1,0:T(4,128)(2,1)S(1)}, bf16[32,4,384]{2,1,0:T(4,128)(2,1)S(1)}, u32[]{:S(2)}, u32[]{:S(2)}) %collective-permute-start.2) | collective-permute-done | bytes 98336 | tf_op jit(solution)/shard_map/ppermute | solution.py:19
  22.3 1.5 %collective-permute-done.6 = f32[1,1,2,16,384]{4,3,2,1,0:T(8,128)S(1)} collective-permute-done((f32[1,1,2,16,384]{4,3,2,1,0:T(8,128)S(1)}, f32[1,1,2,16,384]{4,3,2,1,0:T(8,128)S(1)}, u32[]{:S(2)}, u32[]{:S(2)}) %collective-permute-start.6) | collective-permute-done | bytes 49184 | tf_op jit(solution)/shard_map/ppermute | solution.py:42
  23.9 0.4 collective-permute-start.7
  24.3 3.7 %shard_map.57.fine_ref = f32[24,56,384]{2,1,0:T(8,128)S(1)} custom-call(bf16[1536,2048]{1,0:T(8,128)(2,1)S(1)} %shard_map.56.rows_ref, f32[24,56,384]{2,1,0:T(8,128)S(1)} %copy-done, bf16[4,56,384]{2,1,0:T(8,128)(2,1)S(1)} %bitcast.20, bf16[4,56,384]{2,1,0:T(8,128)(2,1)S(1)} %bitcast.22, bf16[32,8,384]{2,1,0:T(8,128)(2,1)S(1)} %pad_maximum_fusion.side_ref), custom_call_target="tpu_custom_call" | custom-call | flops 2415919104 | bytes 6291456 | tf_op jit(solution)/shard_map/pallas_call | solution.py:470
  28.1 0.8 %shard_map.58 = (f32[24,56,384]{2,1,0:T(8,128)S(1)}, f32[1,56,512]{2,1,0:T(8,128)S(1)}, f32[1,56,512]{2,1,0:T(8,128)S(1)}, f32[6,4,512]{2,1,0:T(4,128)S(1)}, f32[6,4,512]{2,1,0:T(4,128)S(1)}) custom-call(f32[24,56,384]{2,1,0:T(8,128)S(1)} %shard_map.57.fine_ref, f32[24,16,56]{2,1,0:T(8,128)S(1)} %bitcast.12, f32[16,384]{1,0:T(8,128)S(1)} %add_bitcast_fusion.1.lifted_ref, ...), custom_call_target="tpu_custom_call" | custom-call | tf_op jit(solution)/shard_map/pallas_call | solution.py:500
  28.8 1.7 %collective-permute-start.10 = (f32[6,4,512]{2,1,0:T(4,128)S(1)}, f32[6,4,512]{2,1,0:T(4,128)S(1)}, u32[]{:S(2)}, u32[]{:S(2)}) collective-permute-start(f32[6,4,512]{2,1,0:T(4,128)S(1)} %get-tuple-element.30), channel_id=1, source_target_pairs={{0,1},{1,2},{2,3},{3,4},{4,5},{5,6},{6,7},{7,0},{8,9},{9,10},{10,1... | collective-permute-start | bytes 147464 | tf_op jit(solution)/shard_map/ppermute | solution.py:19
  30.6 3.0 %collective-permute-start.11 = (f32[6,4,512]{2,1,0:T(4,128)S(1)}, f32[6,4,512]{2,1,0:T(4,128)S(1)}, u32[]{:S(2)}, u32[]{:S(2)}) collective-permute-start(f32[6,4,512]{2,1,0:T(4,128)S(1)} %get-tuple-element.31), channel_id=1, source_target_pairs={{0,7},{1,0},{2,1},{3,2},{4,3},{5,4},{6,5},{7,6},{8,15},{9,8},{10,9... | collective-permute-start | bytes 147464 | tf_op jit(solution)/shard_map/ppermute | solution.py:19
  33.6 1.7 %collective-permute-start.9 = (f32[1,56,512]{2,1,0:T(8,128)S(1)}, f32[1,56,512]{2,1,0:T(8,128)S(1)}, u32[]{:S(2)}, u32[]{:S(2)}) collective-permute-start(f32[1,56,512]{2,1,0:T(8,128)S(1)} %get-tuple-element.29), channel_id=1, source_target_pairs={{0,24},{8,0},{16,8},{24,16},{1,25},{9,1},{17,9},{25,17},{2,26},{10... | collective-permute-start | bytes 344072 | tf_op jit(solution)/shard_map/ppermute | solution.py:19
  35.4 1.5 %shard_map.59 = (f32[24,56,384]{2,1,0:T(8,128)S(1)}, f32[16,384]{1,0:T(8,128)S(1)}, f32[16,304]{1,0:T(8,128)S(1)}) custom-call(f32[24,56,384]{2,1,0:T(8,128)S(1)} %copy-done, f32[24,56,384]{2,1,0:T(8,128)S(1)} %get-tuple-element.26.now_ref.extra_ref, f32[24,56,128]{2,1,0:T(8,128)S(1)} %broadcast_in_dim.30.heat_ref.extra_ref, f32[24,16,56]{2,1,0:T(8,128)S(1)} %bitcast.13), custom_call_target="tpu_custom_call" | custom-call | bytes 6193152 | tf_op jit(solution)/shard_map/pallas_call | solution.py:374
  36.9 0.9 %collective-permute-done.8 = f32[1,56,512]{2,1,0:T(8,128)S(1)} collective-permute-done((f32[1,56,512]{2,1,0:T(8,128)S(1)}, f32[1,56,512]{2,1,0:T(8,128)S(1)}, u32[]{:S(2)}, u32[]{:S(2)}) %collective-permute-start.8) | collective-permute-done | bytes 114720 | tf_op jit(solution)/shard_map/ppermute | solution.py:19
  38.3 1.2 %collective-permute-start.12 = (bf16[256,384]{1,0:T(8,128)(2,1)S(1)}, bf16[256,384]{1,0:T(8,128)(2,1)S(1)}, u32[]{:S(2)}, u32[]{:S(2)}) collective-permute-start(bf16[256,384]{1,0:T(8,128)(2,1)S(1)} %get-tuple-element.35), channel_id=1, source_target_pairs={{0,8},{8,16},{16,24},{24,0},{1,9},{9,17},{17,25},{25,1},{2,10},{10... | collective-permute-start | bytes 589832 | tf_op jit(solution)/shard_map/ppermute | solution.py:19
  39.5 0.9 %collective-permute-start.16 = (f32[16,384]{1,0:T(8,128)S(1)}, f32[16,384]{1,0:T(8,128)S(1)}, u32[]{:S(2)}, u32[]{:S(2)}) collective-permute-start(f32[16,384]{1,0:T(8,128)S(1)} %get-tuple-element.38), channel_id=1, source_target_pairs={{0,16},{8,24},{16,0},{24,8},{1,17},{9,25},{17,1},{25,9},{2,18},{10... | collective-permute-start | bytes 73736 | tf_op jit(solution)/shard_map/ppermute | solution.py:19
  40.4 0.5 collective-permute-start.13
  40.9 2.8 %collective-permute-done.12 = bf16[256,384]{1,0:T(8,128)(2,1)S(1)} collective-permute-done((bf16[256,384]{1,0:T(8,128)(2,1)S(1)}, bf16[256,384]{1,0:T(8,128)(2,1)S(1)}, u32[]{:S(2)}, u32[]{:S(2)}) %collective-permute-start.12) | collective-permute-done | bytes 196640 | tf_op jit(solution)/shard_map/ppermute | solution.py:19
  43.7 0.9 %collective-permute-done.13 = bf16[256,384]{1,0:T(8,128)(2,1)S(1)} collective-permute-done((bf16[256,384]{1,0:T(8,128)(2,1)S(1)}, bf16[256,384]{1,0:T(8,128)(2,1)S(1)}, u32[]{:S(2)}, u32[]{:S(2)}) %collective-permute-start.13) | collective-permute-done | bytes 196640 | tf_op jit(solution)/shard_map/ppermute | solution.py:19
  45.3 4.7 %collective-permute-start.15 = (bf16[32,4,384]{2,1,0:T(4,128)(2,1)S(1)}, bf16[32,4,384]{2,1,0:T(4,128)(2,1)S(1)}, u32[]{:S(2)}, u32[]{:S(2)}) collective-permute-start(bf16[32,4,384]{2,1,0:T(4,128)(2,1)S(1)} %get-tuple-element.40), channel_id=1, source_target_pairs={{0,7},{1,0},{2,1},{3,2},{4,3},{5,4},{6,5},{7,6},{8,15},{9,8},{10,9... | collective-permute-start | bytes 294920 | tf_op jit(solution)/shard_map/ppermute | solution.py:19
  50.1 0.5 collective-permute-done.17
  50.8 2.8 %collective-permute-done.14 = bf16[32,4,384]{2,1,0:T(4,128)(2,1)S(1)} collective-permute-done((bf16[32,4,384]{2,1,0:T(4,128)(2,1)S(1)}, bf16[32,4,384]{2,1,0:T(4,128)(2,1)S(1)}, u32[]{:S(2)}, u32[]{:S(2)}) %collective-permute-start.14) | collective-permute-done | bytes 98336 | tf_op jit(solution)/shard_map/ppermute | solution.py:19
  53.6 0.9 %collective-permute-done.15 = bf16[32,4,384]{2,1,0:T(4,128)(2,1)S(1)} collective-permute-done((bf16[32,4,384]{2,1,0:T(4,128)(2,1)S(1)}, bf16[32,4,384]{2,1,0:T(4,128)(2,1)S(1)}, u32[]{:S(2)}, u32[]{:S(2)}) %collective-permute-start.15) | collective-permute-done | bytes 98336 | tf_op jit(solution)/shard_map/ppermute | solution.py:19
  54.7 1.6 %collective-permute-done.18 = f32[1,1,2,16,384]{4,3,2,1,0:T(8,128)S(1)} collective-permute-done((f32[1,1,2,16,384]{4,3,2,1,0:T(8,128)S(1)}, f32[1,1,2,16,384]{4,3,2,1,0:T(8,128)S(1)}, u32[]{:S(2)}, u32[]{:S(2)}) %collective-permute-start.18) | collective-permute-done | bytes 49184 | tf_op jit(solution)/shard_map/ppermute | solution.py:42
  56.5 3.7 %shard_map.61.fine_ref = f32[24,56,384]{2,1,0:T(8,128)S(1)} custom-call(bf16[1536,2048]{1,0:T(8,128)(2,1)S(1)} %shard_map.56.rows_ref, f32[24,56,384]{2,1,0:T(8,128)S(1)} %get-tuple-element.34.block_ref, bf16[4,56,384]{2,1,0:T(8,128)(2,1)S(1)} %bitcast.16, bf16[4,56,384]{2,1,0:T(8,128)(2,1)S(1)} %bitcast.18, bf16[32,8,384]{2,1,0:T(8,128)(2,1)S(1)} %pad_maximum_fusion.1.side_ref), custom_call_target="tpu_custom_call" | custom-call | flops 2415919104 | bytes 6291456 | tf_op jit(solution)/shard_map/pallas_call | solution.py:470
  60.2 1.7 %shard_map.62 = f32[24,56,384]{2,1,0:T(8,128)} custom-call(f32[24,56,384]{2,1,0:T(8,128)S(1)} %shard_map.61.fine_ref, f32[24,16,56]{2,1,0:T(8,128)S(1)} %bitcast.14, f32[16,384]{1,0:T(8,128)S(1)} %add_bitcast_fusion.lifted_ref, f32[24,56,384]{2,1,0:T(8,128)S(1)} %get-tuple-element.26.now_ref.extra_ref), custom_call_target="tpu_custom_call" | custom-call | tf_op jit(solution)/shard_map/pallas_call | solution.py:500
  (70 shorter events, 2.7 us)
Async XLA Ops:
  0.0 2.9 %copy-start.2 = (f32[16,512]{1,0:T(8,128)S(1)}, f32[16,512]{1,0:T(8,128)}, u32[]{:S(2)}) copy-start(f32[16,512]{1,0:T(8,128)} %inverse_hbm.1) | copy-start | bytes 98308
  0.0 6.9 %copy-start.3 = (f32[24,56]{1,0:T(8,128)S(1)}, f32[24,56]{1,0:T(8,128)}, u32[]{:S(2)}) copy-start(f32[24,56]{1,0:T(8,128)} %param.6) | copy-start | bytes 16132
  2.3 7.7 %collective-permute-start = (bf16[272,384]{1,0:T(8,128)(2,1)S(1)}, bf16[272,384]{1,0:T(8,128)(2,1)S(1)}, u32[]{:S(2)}, u32[]{:S(2)}) collective-permute-start(bf16[272,384]{1,0:T(8,128)(2,1)S(1)} %get-tuple-element.23), channel_id=1, source_target_pairs={{0,8},{8,16},{16,24},{24,0},{1,9},{9,17},{17,25},{25,1},{2,10},{10... | collective-permute-start | bytes 626696 | tf_op jit(solution)/shard_map/ppermute | solution.py:19
  2.9 7.1 %collective-permute-start.4 = (f32[16,512]{1,0:T(8,128)S(1)}, f32[16,512]{1,0:T(8,128)S(1)}, u32[]{:S(2)}, u32[]{:S(2)}) collective-permute-start(f32[16,512]{1,0:T(8,128)S(1)} %pad_maximum_fusion.2), channel_id=1, source_target_pairs={{0,16},{8,24},{16,0},{24,8},{1,17},{9,25},{17,1},{25,9},{2,18},{10... | collective-permute-start | bytes 98312 | tf_op jit(solution)/shard_map/ppermute | solution.py:19
  5.5 5.5 %collective-permute-start.1 = (bf16[272,384]{1,0:T(8,128)(2,1)S(1)}, bf16[272,384]{1,0:T(8,128)(2,1)S(1)}, u32[]{:S(2)}, u32[]{:S(2)}) collective-permute-start(bf16[272,384]{1,0:T(8,128)(2,1)S(1)} %get-tuple-element.24), channel_id=1, source_target_pairs={{0,24},{8,0},{16,8},{24,16},{1,25},{9,1},{17,9},{25,17},{2,26},{10... | collective-permute-start | bytes 626696 | tf_op jit(solution)/shard_map/ppermute | solution.py:19
  10.0 14.3 %copy-start = (f32[24,56,384]{2,1,0:T(8,128)S(1)}, f32[24,56,384]{2,1,0:T(8,128)}, u32[]{:S(2)}) copy-start(f32[24,56,384]{2,1,0:T(8,128)} %rhs_ref.3) | copy-start | bytes 6193156
  11.4 6.6 %collective-permute-start.5 = (f32[2,1,2,16,384]{4,3,2,1,0:T(8,128)S(1)}, f32[2,1,2,16,384]{4,3,2,1,0:T(8,128)S(1)}, u32[]{:S(2)}, u32[]{:S(2)}) collective-permute-start(f32[2,1,2,16,384]{4,3,2,1,0:T(8,128)S(1)} %constant_dynamic-slice_fusion.5), channel_id=1, source_target_pairs={{0,2},{1,3},{2,0},{3,1},{4,6},{5,7},{6,4},{7,5},{8,10},{9,11},{10,... | collective-permute-start | bytes 294920 | tf_op jit(solution)/shard_map/ppermute | solution.py:42
  13.2 8.9 %collective-permute-start.2 = (bf16[32,4,384]{2,1,0:T(4,128)(2,1)S(1)}, bf16[32,4,384]{2,1,0:T(4,128)(2,1)S(1)}, u32[]{:S(2)}, u32[]{:S(2)}) collective-permute-start(bf16[32,4,384]{2,1,0:T(4,128)(2,1)S(1)} %get-tuple-element.41), channel_id=1, source_target_pairs={{0,1},{1,2},{2,3},{3,4},{4,5},{5,6},{6,7},{7,0},{8,9},{9,10},{10,1... | collective-permute-start | bytes 294920 | tf_op jit(solution)/shard_map/ppermute | solution.py:19
  14.8 7.4 %collective-permute-start.3 = (bf16[32,4,384]{2,1,0:T(4,128)(2,1)S(1)}, bf16[32,4,384]{2,1,0:T(4,128)(2,1)S(1)}, u32[]{:S(2)}, u32[]{:S(2)}) collective-permute-start(bf16[32,4,384]{2,1,0:T(4,128)(2,1)S(1)} %get-tuple-element.42), channel_id=1, source_target_pairs={{0,7},{1,0},{2,1},{3,2},{4,3},{5,4},{6,5},{7,6},{8,15},{9,8},{10,9... | collective-permute-start | bytes 294920 | tf_op jit(solution)/shard_map/ppermute | solution.py:19
  18.0 5.8 %collective-permute-start.6 = (f32[1,1,2,16,384]{4,3,2,1,0:T(8,128)S(1)}, f32[1,1,2,16,384]{4,3,2,1,0:T(8,128)S(1)}, u32[]{:S(2)}, u32[]{:S(2)}) collective-permute-start(f32[1,1,2,16,384]{4,3,2,1,0:T(8,128)S(1)} %constant_dynamic-slice_fusion.4), channel_id=1, source_target_pairs={{0,4},{1,5},{2,6},{3,7},{4,0},{5,1},{6,2},{7,3},{8,12},{9,13},{10,... | collective-permute-start | bytes 147464 | tf_op jit(solution)/shard_map/ppermute | solution.py:42
  23.9 4.2 %copy-start.1 = (f32[24,56,16]{1,2,0:T(8,128)S(1)}, f32[24,56,16]{1,2,0:T(8,128)}, u32[]{:S(2)}) copy-start(f32[24,56,16]{1,2,0:T(8,128)} %param.8) | copy-start | bytes 258052
  23.9 4.2 %collective-permute-start.7 = (f32[1,1,1,16,384]{4,3,2,1,0:T(8,128)S(1)}, f32[1,1,1,16,384]{4,3,2,1,0:T(8,128)S(1)}, u32[]{:S(2)}, u32[]{:S(2)}) collective-permute-start(f32[1,1,1,16,384]{4,3,2,1,0:T(8,128)S(1)} %constant_dynamic-slice_fusion.3), channel_id=1, source_target_pairs={{0,1},{1,0},{2,3},{3,2},{4,5},{5,4},{6,7},{7,6},{8,9},{9,8},{10,11... | collective-permute-start | bytes 73736 | tf_op jit(solution)/shard_map/ppermute | solution.py:42
  28.8 8.0 %collective-permute-start.10 = (f32[6,4,512]{2,1,0:T(4,128)S(1)}, f32[6,4,512]{2,1,0:T(4,128)S(1)}, u32[]{:S(2)}, u32[]{:S(2)}) collective-permute-start(f32[6,4,512]{2,1,0:T(4,128)S(1)} %get-tuple-element.30), channel_id=1, source_target_pairs={{0,1},{1,2},{2,3},{3,4},{4,5},{5,6},{6,7},{7,0},{8,9},{9,10},{10,1... | collective-permute-start | bytes 147464 | tf_op jit(solution)/shard_map/ppermute | solution.py:19
  30.6 6.3 %collective-permute-start.11 = (f32[6,4,512]{2,1,0:T(4,128)S(1)}, f32[6,4,512]{2,1,0:T(4,128)S(1)}, u32[]{:S(2)}, u32[]{:S(2)}) collective-permute-start(f32[6,4,512]{2,1,0:T(4,128)S(1)} %get-tuple-element.31), channel_id=1, source_target_pairs={{0,7},{1,0},{2,1},{3,2},{4,3},{5,4},{6,5},{7,6},{8,15},{9,8},{10,9... | collective-permute-start | bytes 147464 | tf_op jit(solution)/shard_map/ppermute | solution.py:19
  33.6 4.2 %collective-permute-start.8 = (f32[1,56,512]{2,1,0:T(8,128)S(1)}, f32[1,56,512]{2,1,0:T(8,128)S(1)}, u32[]{:S(2)}, u32[]{:S(2)}) collective-permute-start(f32[1,56,512]{2,1,0:T(8,128)S(1)} %get-tuple-element.28), channel_id=1, source_target_pairs={{0,8},{8,16},{16,24},{24,0},{1,9},{9,17},{17,25},{25,1},{2,10},{10... | collective-permute-start | bytes 344072 | tf_op jit(solution)/shard_map/ppermute | solution.py:19
  33.6 4.2 %collective-permute-start.9 = (f32[1,56,512]{2,1,0:T(8,128)S(1)}, f32[1,56,512]{2,1,0:T(8,128)S(1)}, u32[]{:S(2)}, u32[]{:S(2)}) collective-permute-start(f32[1,56,512]{2,1,0:T(8,128)S(1)} %get-tuple-element.29), channel_id=1, source_target_pairs={{0,24},{8,0},{16,8},{24,16},{1,25},{9,1},{17,9},{25,17},{2,26},{10... | collective-permute-start | bytes 344072 | tf_op jit(solution)/shard_map/ppermute | solution.py:19
  38.3 5.4 %collective-permute-start.12 = (bf16[256,384]{1,0:T(8,128)(2,1)S(1)}, bf16[256,384]{1,0:T(8,128)(2,1)S(1)}, u32[]{:S(2)}, u32[]{:S(2)}) collective-permute-start(bf16[256,384]{1,0:T(8,128)(2,1)S(1)} %get-tuple-element.35), channel_id=1, source_target_pairs={{0,8},{8,16},{16,24},{24,0},{1,9},{9,17},{17,25},{25,1},{2,10},{10... | collective-permute-start | bytes 589832 | tf_op jit(solution)/shard_map/ppermute | solution.py:19
  39.5 5.2 %collective-permute-start.16 = (f32[16,384]{1,0:T(8,128)S(1)}, f32[16,384]{1,0:T(8,128)S(1)}, u32[]{:S(2)}, u32[]{:S(2)}) collective-permute-start(f32[16,384]{1,0:T(8,128)S(1)} %get-tuple-element.38), channel_id=1, source_target_pairs={{0,16},{8,24},{16,0},{24,8},{1,17},{9,25},{17,1},{25,9},{2,18},{10... | collective-permute-start | bytes 73736 | tf_op jit(solution)/shard_map/ppermute | solution.py:19
  40.4 4.2 %collective-permute-start.13 = (bf16[256,384]{1,0:T(8,128)(2,1)S(1)}, bf16[256,384]{1,0:T(8,128)(2,1)S(1)}, u32[]{:S(2)}, u32[]{:S(2)}) collective-permute-start(bf16[256,384]{1,0:T(8,128)(2,1)S(1)} %get-tuple-element.36), channel_id=1, source_target_pairs={{0,24},{8,0},{16,8},{24,16},{1,25},{9,1},{17,9},{25,17},{2,26},{10... | collective-permute-start | bytes 589832 | tf_op jit(solution)/shard_map/ppermute | solution.py:19
  45.1 5.5 %collective-permute-start.17 = (f32[2,1,2,16,384]{4,3,2,1,0:T(8,128)S(1)}, f32[2,1,2,16,384]{4,3,2,1,0:T(8,128)S(1)}, u32[]{:S(2)}, u32[]{:S(2)}) collective-permute-start(f32[2,1,2,16,384]{4,3,2,1,0:T(8,128)S(1)} %constant_dynamic-slice_fusion.2), channel_id=1, source_target_pairs={{0,2},{1,3},{2,0},{3,1},{4,6},{5,7},{6,4},{7,5},{8,10},{9,11},{10,... | collective-permute-start | bytes 294920 | tf_op jit(solution)/shard_map/ppermute | solution.py:42
  45.3 8.3 %collective-permute-start.14 = (bf16[32,4,384]{2,1,0:T(4,128)(2,1)S(1)}, bf16[32,4,384]{2,1,0:T(4,128)(2,1)S(1)}, u32[]{:S(2)}, u32[]{:S(2)}) collective-permute-start(bf16[32,4,384]{2,1,0:T(4,128)(2,1)S(1)} %get-tuple-element.39), channel_id=1, source_target_pairs={{0,1},{1,2},{2,3},{3,4},{4,5},{5,6},{6,7},{7,0},{8,9},{9,10},{10,1... | collective-permute-start | bytes 294920 | tf_op jit(solution)/shard_map/ppermute | solution.py:19
  45.3 9.2 %collective-permute-start.15 = (bf16[32,4,384]{2,1,0:T(4,128)(2,1)S(1)}, bf16[32,4,384]{2,1,0:T(4,128)(2,1)S(1)}, u32[]{:S(2)}, u32[]{:S(2)}) collective-permute-start(bf16[32,4,384]{2,1,0:T(4,128)(2,1)S(1)} %get-tuple-element.40), channel_id=1, source_target_pairs={{0,7},{1,0},{2,1},{3,2},{4,3},{5,4},{6,5},{7,6},{8,15},{9,8},{10,9... | collective-permute-start | bytes 294920 | tf_op jit(solution)/shard_map/ppermute | solution.py:19
  50.6 5.6 %collective-permute-start.18 = (f32[1,1,2,16,384]{4,3,2,1,0:T(8,128)S(1)}, f32[1,1,2,16,384]{4,3,2,1,0:T(8,128)S(1)}, u32[]{:S(2)}, u32[]{:S(2)}) collective-permute-start(f32[1,1,2,16,384]{4,3,2,1,0:T(8,128)S(1)} %constant_dynamic-slice_fusion.1), channel_id=1, source_target_pairs={{0,4},{1,5},{2,6},{3,7},{4,0},{5,1},{6,2},{7,3},{8,12},{9,13},{10,... | collective-permute-start | bytes 147464 | tf_op jit(solution)/shard_map/ppermute | solution.py:42
  56.3 3.9 %collective-permute-start.19 = (f32[1,1,1,16,384]{4,3,2,1,0:T(8,128)S(1)}, f32[1,1,1,16,384]{4,3,2,1,0:T(8,128)S(1)}, u32[]{:S(2)}, u32[]{:S(2)}) collective-permute-start(f32[1,1,1,16,384]{4,3,2,1,0:T(8,128)S(1)} %constant_dynamic-slice_fusion), channel_id=1, source_target_pairs={{0,1},{1,0},{2,3},{3,2},{4,5},{5,4},{6,7},{7,6},{8,9},{9,8},{10,11... | collective-permute-start | bytes 73736 | tf_op jit(solution)/shard_map/ppermute | solution.py:42
